TPU v7x, 32 devices: a whole 2x2x4 slice. The times are simulated.
32 devices in a mesh: shard: 4 (over y, x), ctx: 4 (over z), tp: 2 (over core).
Axes of the slice: x: 2, y: 2, z: 4, core: 2. Of those that a mesh axis runs over, the one named last changes fastest.
Arguments:
- tokens: bfloat16 [8, 2560, 768], P('shard', 'ctx'), may hold values from -6 to 6
- gate_res: float32 [8, 2560, 12], P('shard', 'ctx'), may hold values from -3 to 3
- cotangent: bfloat16 [8, 2560, 768], P('shard', 'ctx'), may hold values from -6 to 6
- parents: int32 [8, 20], P('shard'), may hold values from 0 to 11, as said below
- expert_ids: int32 [8, 2560, 2], P('shard', 'ctx'), may hold values from 0 to 11, all different within a row
- priority: int32 [4, 4, 1280], P('shard', 'ctx'), may hold values from 0 to 1279, each once within a row
- w_qkv: bfloat16 [768, 3, 768], P('ctx', None, 'tp'), may hold values from -0.3125 to 0.3125
- w_out: bfloat16 [768, 768], P('ctx', 'tp'), may hold values from -0.875 to 0.875
- w_router: bfloat16 [768, 12], P('ctx'), may hold values from -0.15625 to 0.15625
- attn_gain: bfloat16 [768], P('ctx'), may hold values from 0.5 to 1.5
- ffn_gain: bfloat16 [768], P('ctx'), may hold values from 0.5 to 1.5
- const_vec: bfloat16 [768, 2], P('ctx'), may hold values from -4 to 4
- w_gate_up: bfloat16 [768, 8, 2, 2048], P('ctx', 'shard', None, 'tp'), may hold values from -0.21875 to 0.21875
- w_down: bfloat16 [768, 8, 2048], P('ctx', 'shard', 'tp'), may hold values from -0.25 to 0.25
Outputs:
- mixed_out: float32 [8, 2560, 768], P('shard', 'ctx')
- d_tokens: float32 [8, 2560, 768], P('shard', 'ctx')
- d_gate_res: float32 [8, 2560, 12], P('shard', 'ctx')
- d_w_qkv: float32 [768, 3, 768], P('ctx', None, 'tp')
- d_w_out: float32 [768, 768], P('ctx', 'tp')
- d_w_router: float32 [768, 12], P('ctx')
- d_attn_gain: float32 [768], P('ctx')
- d_ffn_gain: float32 [768], P('ctx')
- d_const_vec: float32 [768, 2], P('ctx')
- d_w_gate_up: float32 [768, 8, 2, 2048], P('ctx', 'shard', None, 'tp')
- d_w_down: float32 [768, 8, 2048], P('ctx', 'shard', 'tp')
Inputs may be any that keep to these rules, and one draw needn't show every extreme that they name: `parents`: segment 0 is its own parent and segments 1 to 7 have parent s - 1; the next 4 segments have parent 8 - 1; each of the last 8 segments has one of those branch segments as parent, exactly 2 under each branch.
All inputs are finite; a program needn't handle non-finite values.
Results may differ from a plain program's by a relative error of at most 0.023.
Values may be sent and summed in bfloat16 or wider, within the bound.
No kernel may reach another device: no remote copies, remote signals or barrier semaphores. Data moves between devices by JAX's collectives and lax.ppermute only.
A program may use at most 256 MiB of HBM per device.

v0:
```python
import math

import jax
import jax.numpy as jnp
from jax import lax
from jax.sharding import PartitionSpec as P

HEAD_DIM = 64


eps = 1e-06
score_scale = 0.125


def ancestry(parent_row):
    seg_count = parent_row.shape[0]
    position = jnp.arange(seg_count, dtype=jnp.int32)
    linked = (parent_row[:, None] == position[None, :]) | (position[:, None] == position[None, :])
    reach = linked.astype(jnp.float32)
    for repeat in range(seg_count.bit_length()):
        reach = jnp.minimum(jnp.dot(reach, reach, precision=lax.Precision.HIGHEST), 1.0)
    return reach


def path_rows(positions, seg_len, ancestors):
    onehot = (
        (positions // seg_len)[:, None] == jnp.arange(ancestors.shape[0], dtype=jnp.int32)[None, :]
    ).astype(jnp.float32)
    return jnp.dot(onehot, ancestors)


def allowed_block(query_rows, query_pos, key_start, key_count, seg_len):
    key_pos = key_start + jnp.arange(key_count, dtype=jnp.int32)
    key_onehot = (
        (key_pos // seg_len)[:, None] == jnp.arange(query_rows.shape[1], dtype=jnp.int32)[None, :]
    ).astype(jnp.float32)
    linked = jnp.dot(query_rows, key_onehot.T) > 0.5
    return (linked & (key_pos[None, :] <= query_pos[:, None]))[None]


def slot_table(picked_ids, ranking, experts, capacity):
    count_rows = picked_ids.shape[0]
    flat_ids = picked_ids.reshape(-1)
    rank_key = (2 * ranking[:, None] + jnp.arange(2, dtype=jnp.int32)[None, :]).reshape(-1)
    earlier = (flat_ids[:, None] == flat_ids[None, :]) & (rank_key[None, :] < rank_key[:, None])
    ranks = jnp.sum(earlier.astype(jnp.int32), axis=1)
    kept = (flat_ids < experts) & (ranks < capacity)
    target = jnp.where(kept, flat_ids * capacity + ranks, -1).reshape(count_rows, 2)
    slot_index = jnp.arange(experts * capacity, dtype=jnp.int32)
    return slot_index[None, :, None] == target.T[:, None, :]


def block_scores(queries, keys_blk):
    return (
        jnp.einsum("qhe,khe->hqk", queries, keys_blk, preferred_element_type=jnp.float32)
        * score_scale
    )


def softmax_grads(queries, grads_out, stat_lse, stat_delta, keys_blk, values_blk, mask):
    prob = jnp.where(mask, jnp.exp(block_scores(queries, keys_blk) - stat_lse[:, :, None]), 0.0)
    dprob = jnp.einsum("qhe,khe->hqk", grads_out, values_blk, preferred_element_type=jnp.float32)
    dscore = (prob * (dprob - stat_delta[:, :, None])).astype(jnp.bfloat16)
    return (prob.astype(jnp.bfloat16), dscore)


def shards(
    tokens,
    gate_res,
    cotangent,
    parents,
    expert_ids,
    priority,
    w_qkv,
    w_out,
    w_router,
    attn_gain,
    ffn_gain,
    const_vec,
    w_gate_up,
    w_down,
):
    full_qkv, full_out, full_router, full_again, full_fgain, full_const, full_gu, full_down = (
        lax.all_gather(w_qkv, "ctx", axis=0, tiled=True),
        lax.all_gather(w_out, "ctx", axis=0, tiled=True),
        lax.all_gather(w_router, "ctx", axis=0, tiled=True),
        lax.all_gather(attn_gain, "ctx", axis=0, tiled=True),
        lax.all_gather(ffn_gain, "ctx", axis=0, tiled=True),
        lax.all_gather(const_vec, "ctx", axis=0, tiled=True),
        lax.all_gather(w_gate_up, "ctx", axis=0, tiled=True),
        lax.all_gather(w_down, "ctx", axis=0, tiled=True),
    )
    tree_count, rows, model_width = tokens.shape
    tok_rows = tree_count * rows
    inputs = tokens.reshape(tok_rows, model_width).astype(jnp.float32)
    local_width = full_out.shape[1]
    local_heads = local_width // HEAD_DIM
    ctx_index = lax.axis_index("ctx")
    tree_len = rows * lax.axis_size("ctx")
    ancestors_all = jax.vmap(ancestry)(parents)
    seg_len = tree_len // parents.shape[1]
    key_block = math.gcd(tree_len, 512)
    starts = jnp.arange(tree_len // key_block, dtype=jnp.int32) * key_block
    key_start_own = ctx_index * rows
    query_pos = key_start_own + jnp.arange(rows, dtype=jnp.int32)
    query_rows_all = jax.vmap(lambda anc: path_rows(query_pos, seg_len, anc))(ancestors_all)
    inv_first = lax.rsqrt(jnp.mean(inputs * inputs, axis=-1, keepdims=True) + eps)
    first_unit = inputs * inv_first
    first_gain = full_again.astype(jnp.float32)
    normed = (first_unit * first_gain).astype(jnp.bfloat16)
    projected = jnp.einsum("nd,dke->nke", normed, full_qkv, preferred_element_type=jnp.float32)
    q_low = projected[:, 0].astype(jnp.bfloat16)
    k_low = projected[:, 1].astype(jnp.bfloat16)
    v_low = projected[:, 2].astype(jnp.bfloat16)
    keys_all, values_all = (
        lax.all_gather(k_low.reshape(tree_count, rows, local_width), "ctx", axis=1, tiled=True),
        lax.all_gather(v_low.reshape(tree_count, rows, local_width), "ctx", axis=1, tiled=True),
    )
    q_heads = q_low.reshape(tree_count, rows, local_heads, HEAD_DIM)
    k_heads = keys_all.reshape(tree_count, tree_len, local_heads, HEAD_DIM)
    v_heads = values_all.reshape(tree_count, tree_len, local_heads, HEAD_DIM)

    def tree_forward(q_one, k_one, v_one, rows_one):

        def stat_step(carry, start):
            running_top, running_sum = carry
            keys_blk = lax.dynamic_slice_in_dim(k_one, start, key_block, 0)
            mask = allowed_block(rows_one, query_pos, start, key_block, seg_len)
            masked = jnp.where(mask, block_scores(q_one, keys_blk), -1e30)
            new_top = jnp.maximum(running_top, jnp.max(masked, axis=2))
            expo = jnp.where(mask, jnp.exp(masked - new_top[:, :, None]), 0.0)
            running_sum = running_sum * jnp.exp(running_top - new_top) + jnp.sum(expo, axis=2)
            return ((new_top, running_sum), None)

        start_top = jnp.full((local_heads, rows), -1e30, jnp.float32)
        (final_top, final_sum), unused = lax.scan(
            stat_step, (start_top, jnp.zeros_like(start_top)), starts
        )
        lse_one = final_top + jnp.log(final_sum)

        def out_step(accum, start):
            keys_blk = lax.dynamic_slice_in_dim(k_one, start, key_block, 0)
            values_blk = lax.dynamic_slice_in_dim(v_one, start, key_block, 0)
            mask = allowed_block(rows_one, query_pos, start, key_block, seg_len)
            prob = jnp.where(
                mask, jnp.exp(block_scores(q_one, keys_blk) - lse_one[:, :, None]), 0.0
            ).astype(jnp.bfloat16)
            return (
                accum
                + jnp.einsum("hqk,khe->qhe", prob, values_blk, preferred_element_type=jnp.float32),
                None,
            )

        attended_one, unused = lax.scan(
            out_step, jnp.zeros((rows, local_heads, HEAD_DIM), jnp.float32), starts
        )
        return (attended_one, lse_one)

    attended, lse = jax.vmap(tree_forward)(q_heads, k_heads, v_heads, query_rows_all)
    attended_low = attended.reshape(tok_rows, local_width).astype(jnp.bfloat16)
    attn_part = jnp.einsum("nh,dh->nd", attended_low, full_out, preferred_element_type=jnp.float32)
    attn_sum = lax.psum(attn_part.astype(jnp.bfloat16), "tp").astype(jnp.float32)
    mixed = inputs + attn_sum
    inv_second = lax.rsqrt(jnp.mean(mixed * mixed, axis=-1, keepdims=True) + eps)
    second_unit = mixed * inv_second
    second_gain = full_fgain.astype(jnp.float32)
    second_low = (second_unit * second_gain).astype(jnp.bfloat16)
    second_float = second_low.astype(jnp.float32)
    logits = jnp.dot(
        second_low, full_router, preferred_element_type=jnp.float32
    ) + gate_res.reshape(tok_rows, -1)
    expo_logits = jnp.exp(logits - jnp.max(logits, axis=-1, keepdims=True))
    probs = expo_logits / jnp.sum(expo_logits, axis=-1, keepdims=True)
    experts = lax.axis_size("shard") * w_gate_up.shape[1]
    every_expert = experts + 4
    capacity = tok_rows * 2 // every_expert
    picked_ids = expert_ids.reshape(tok_rows, 2)
    selector = (picked_ids[:, :, None] == jnp.arange(every_expert, dtype=jnp.int32)).astype(
        jnp.float32
    )
    picked = jnp.sum(selector * probs[:, None, :], axis=-1)
    picked_total = jnp.sum(picked, axis=-1, keepdims=True)
    gates = picked / picked_total
    table = slot_table(picked_ids, priority[0, 0], experts, capacity).astype(jnp.bfloat16)
    routed = table[0] + table[1]
    send_slots = jnp.einsum(
        "et,td->ed", routed, second_low, preferred_element_type=jnp.float32
    ).astype(jnp.bfloat16)
    send_slots = send_slots.reshape(experts, 1, capacity, model_width)
    arrived = lax.all_to_all(send_slots, "shard", split_axis=0, concat_axis=1, tiled=True)
    gate_up = jnp.einsum("jsrd,djgf->jsrgf", arrived, full_gu, preferred_element_type=jnp.float32)
    hidden_low = (jax.nn.silu(gate_up[:, :, :, 0]) * gate_up[:, :, :, 1]).astype(jnp.bfloat16)
    partial_out = jnp.einsum(
        "jsrf,djf->jsrd", hidden_low, full_down, preferred_element_type=jnp.float32
    )
    summed = lax.psum(partial_out.astype(jnp.bfloat16), "tp")
    returned = lax.all_to_all(summed, "shard", split_axis=1, concat_axis=0, tiled=True)
    returned, kept_slots = (returned, arrived)
    out_slots = returned.reshape(experts * capacity, model_width)
    ffn_values = jnp.einsum("cet,ed->ctd", table, out_slots, preferred_element_type=jnp.float32)
    copy_flag = selector[:, :, experts + 1]
    const_flags = selector[:, :, experts + 2 :]
    const_float = full_const.astype(jnp.float32)
    fixed_terms = jnp.einsum(
        "nck,dk->cnd", const_flags, const_float, precision=lax.Precision.HIGHEST
    )
    values_pair = ffn_values + copy_flag.T[:, :, None] * second_float[None] + fixed_terms
    mixed_out = mixed + jnp.sum(gates.T[:, :, None] * values_pair, axis=0)
    grad_out = cotangent.reshape(tok_rows, model_width).astype(jnp.float32)
    weighted = gates.T[:, :, None] * grad_out[None]
    d_gates = jnp.einsum("cnd,nd->nc", values_pair, grad_out)
    d_const = jnp.einsum("nck,cnd->dk", const_flags, weighted, precision=lax.Precision.HIGHEST)
    d_out_slots = jnp.einsum(
        "cet,ctd->ed", table.astype(jnp.float32), weighted, precision=lax.Precision.HIGHEST
    )
    d_out_low = d_out_slots.astype(jnp.bfloat16).reshape(experts, 1, capacity, model_width)
    d_picked = (d_gates - jnp.sum(d_gates * gates, axis=-1, keepdims=True)) / picked_total
    d_probs = jnp.einsum("nc,nck->nk", d_picked, selector)
    d_logits = probs * (d_probs - jnp.sum(probs * d_probs, axis=-1, keepdims=True))
    d_router_w = jnp.dot(second_float.T, d_logits, precision=lax.Precision.HIGHEST)
    d_second = jnp.sum(copy_flag.T[:, :, None] * weighted, axis=0)
    d_second = d_second + jnp.dot(
        d_logits, full_router.astype(jnp.float32).T, precision=lax.Precision.HIGHEST
    )
    arrived_grad = lax.all_to_all(d_out_low, "shard", split_axis=0, concat_axis=1, tiled=True)
    gate_up = jnp.einsum(
        "jsrd,djgf->jsrgf", kept_slots, full_gu, preferred_element_type=jnp.float32
    )
    gate_part = gate_up[:, :, :, 0]
    up_part = gate_up[:, :, :, 1]
    sigma = jax.nn.sigmoid(gate_part)
    silu_part = gate_part * sigma
    hidden_low = (silu_part * up_part).astype(jnp.bfloat16)
    d_hidden = jnp.einsum(
        "jsrd,djf->jsrf", arrived_grad, full_down, preferred_element_type=jnp.float32
    )
    d_gate_part = d_hidden * up_part * sigma * (1.0 + gate_part * (1.0 - sigma))
    d_up_part = d_hidden * silu_part
    d_gate_up_low = jnp.stack([d_gate_part, d_up_part], axis=3).astype(jnp.bfloat16)
    d_slot_part = jnp.einsum(
        "jsrgf,djgf->jsrd", d_gate_up_low, full_gu, preferred_element_type=jnp.float32
    )
    d_slot_sum = lax.psum(d_slot_part.astype(jnp.bfloat16), "tp")
    d_slot_back = lax.all_to_all(d_slot_sum, "shard", split_axis=1, concat_axis=0, tiled=True)
    d_gate_up_w = jnp.einsum(
        "jsrd,jsrgf->djgf", kept_slots, d_gate_up_low, preferred_element_type=jnp.float32
    )
    d_down_w = jnp.einsum(
        "jsrd,jsrf->djf", arrived_grad, hidden_low, preferred_element_type=jnp.float32
    )
    d_second = d_second + jnp.einsum(
        "et,ed->td",
        routed,
        d_slot_back.reshape(experts * capacity, model_width),
        preferred_element_type=jnp.float32,
    )
    d_second_gain = jnp.sum(d_second * second_unit, axis=0)
    d_second_unit = d_second * second_gain
    d_mixed = grad_out + inv_second * (
        d_second_unit - second_unit * jnp.mean(d_second_unit * second_unit, axis=-1, keepdims=True)
    )
    d_attn_low = d_mixed.astype(jnp.bfloat16)
    d_out_w = jnp.einsum("nd,nh->dh", d_attn_low, attended_low, preferred_element_type=jnp.float32)
    d_attended = jnp.einsum("nd,dh->nh", d_attn_low, full_out, preferred_element_type=jnp.float32)
    do_low = d_attended.astype(jnp.bfloat16)
    do_heads = do_low.reshape(tree_count, rows, local_heads, HEAD_DIM)
    delta = jnp.einsum("tqhe,tqhe->thq", do_heads.astype(jnp.float32), attended)

    def tree_both(q_one, k_one, v_one, do_one, lse_one, delta_one, rows_one):

        def both_step(dq_accum, start):
            keys_blk = lax.dynamic_slice_in_dim(k_one, start, key_block, 0)
            values_blk = lax.dynamic_slice_in_dim(v_one, start, key_block, 0)
            mask = allowed_block(rows_one, query_pos, start, key_block, seg_len)
            prob_low, dscore = softmax_grads(
                q_one, do_one, lse_one, delta_one, keys_blk, values_blk, mask
            )
            dq_accum = dq_accum + jnp.einsum(
                "hqk,khe->qhe", dscore, keys_blk, preferred_element_type=jnp.float32
            )
            dkey = (
                jnp.einsum("hqk,qhe->khe", dscore, q_one, preferred_element_type=jnp.float32)
                * score_scale
            )
            dval = jnp.einsum("hqk,qhe->khe", prob_low, do_one, preferred_element_type=jnp.float32)
            return (
                dq_accum,
                jnp.stack(
                    [dkey.reshape(key_block, local_width), dval.reshape(key_block, local_width)],
                    axis=1,
                ),
            )

        dq_one, terms_one = lax.scan(
            both_step, jnp.zeros((rows, local_heads, HEAD_DIM), jnp.float32), starts
        )
        return (dq_one, terms_one.reshape(tree_len, 2, local_width))

    dq_total, key_terms = jax.vmap(tree_both)(
        q_heads, k_heads, v_heads, do_heads, lse, delta, query_rows_all
    )
    key_sums = lax.psum_scatter(
        key_terms.astype(jnp.bfloat16), "ctx", scatter_dimension=1, tiled=True
    ).astype(jnp.float32)
    key_grad = key_sums[:, :, 0].reshape(tok_rows, local_width)
    value_grad = key_sums[:, :, 1].reshape(tok_rows, local_width)
    query_grad = (dq_total * score_scale).reshape(tok_rows, local_width)
    d_qkv_low = jnp.stack([query_grad, key_grad, value_grad], axis=1).astype(jnp.bfloat16)
    d_qkv_w = jnp.einsum("nd,nke->dke", normed, d_qkv_low, preferred_element_type=jnp.float32)
    d_normed_part = jnp.einsum(
        "nke,dke->nd", d_qkv_low, full_qkv, preferred_element_type=jnp.float32
    )
    d_normed = lax.psum(d_normed_part.astype(jnp.bfloat16), "tp").astype(jnp.float32)
    d_first_gain = jnp.sum(d_normed * first_unit, axis=0)
    d_first_unit = d_normed * first_gain
    d_inputs = d_mixed + inv_first * (
        d_first_unit - first_unit * jnp.mean(d_first_unit * first_unit, axis=-1, keepdims=True)
    )
    summed_grads = (
        lax.psum_scatter(
            d_qkv_w.astype(jnp.bfloat16), "ctx", scatter_dimension=0, tiled=True
        ).astype(jnp.float32),
        lax.psum_scatter(
            d_out_w.astype(jnp.bfloat16), "ctx", scatter_dimension=0, tiled=True
        ).astype(jnp.float32),
        lax.psum_scatter(
            d_router_w.astype(jnp.bfloat16), "ctx", scatter_dimension=0, tiled=True
        ).astype(jnp.float32),
        lax.psum_scatter(
            d_first_gain.astype(jnp.bfloat16), "ctx", scatter_dimension=0, tiled=True
        ).astype(jnp.float32),
        lax.psum_scatter(
            d_second_gain.astype(jnp.bfloat16), "ctx", scatter_dimension=0, tiled=True
        ).astype(jnp.float32),
        lax.psum_scatter(
            d_const.astype(jnp.bfloat16), "ctx", scatter_dimension=0, tiled=True
        ).astype(jnp.float32),
        lax.psum_scatter(
            d_gate_up_w.astype(jnp.bfloat16), "ctx", scatter_dimension=0, tiled=True
        ).astype(jnp.float32),
        lax.psum_scatter(
            d_down_w.astype(jnp.bfloat16), "ctx", scatter_dimension=0, tiled=True
        ).astype(jnp.float32),
    )
    shared = (
        lax.psum(summed_grads[0].astype(jnp.bfloat16), "shard").astype(jnp.float32),
        lax.psum(summed_grads[1].astype(jnp.bfloat16), "shard").astype(jnp.float32),
        lax.psum(summed_grads[2].astype(jnp.bfloat16), "shard").astype(jnp.float32),
        lax.psum(summed_grads[3].astype(jnp.bfloat16), "shard").astype(jnp.float32),
        lax.psum(summed_grads[4].astype(jnp.bfloat16), "shard").astype(jnp.float32),
        lax.psum(summed_grads[5].astype(jnp.bfloat16), "shard").astype(jnp.float32),
    )
    out_rows = mixed_out.reshape(tree_count, rows, model_width)
    grad_rows = d_inputs.reshape(tree_count, rows, model_width)
    logit_rows = d_logits.reshape(tree_count, rows, every_expert)
    return (
        out_rows,
        grad_rows,
        logit_rows,
        shared[0],
        shared[1],
        shared[2],
        shared[3],
        shared[4],
        shared[5],
        summed_grads[6],
        summed_grads[7],
    )


def solution(mesh):
    return jax.shard_map(
        shards,
        mesh=mesh,
        in_specs=(
            P("shard", "ctx", None),
            P("shard", "ctx", None),
            P("shard", "ctx", None),
            P("shard", None),
            P("shard", "ctx", None),
            P("shard", "ctx", None),
            P("ctx", None, "tp"),
            P("ctx", "tp"),
            P("ctx", None),
            P("ctx"),
            P("ctx"),
            P("ctx", None),
            P("ctx", "shard", None, "tp"),
            P("ctx", "shard", "tp"),
        ),
        out_specs=(
            P("shard", "ctx", None),
            P("shard", "ctx", None),
            P("shard", "ctx", None),
            P("ctx", None, "tp"),
            P("ctx", "tp"),
            P("ctx", None),
            P("ctx"),
            P("ctx"),
            P("ctx", None),
            P("ctx", "shard", None, "tp"),
            P("ctx", "shard", "tp"),
        ),
        check_vma=False,
    )
```

profile of v0, /device:TPU:0, one launch (start us, length us, event | category | flops | bytes accessed | tf_op | source)
XLA Modules:
  0.0 1618.9 jit_solution(13005266278389709842)
XLA Ops:
  11.6 13.5 all-reduce.10
  29.3 23.3 %all-gather.8.cloned.1.call-done = bf16[768,3,384]{2,0,1:T(8,128)(2,1)} async-done(((bf16[192,3,384]{2,0,1:T(8,128)(2,1)}), bf16[768,3,384]{2,0,1:T(8,128)(2,1)}) %all-gather.8.cloned.1.call-update) | async-done | bytes 1769488 | tf_op jit(solution)/shard_map/all_gather | solution.py:84
  58.8 19.9 %all_gather.34 = bf16[768,384]{1,0:T(8,128)(2,1)S(1)} all-gather(bf16[192,384]{1,0:T(8,128)(2,1)S(1)} %copy-done.34), channel_id=1, replica_groups=mesh['shard'=4,'ctx'=4,'tp'=2] {'ctx'}, dimensions={0}, use_global_device_ids=true | all-gather | bytes 737280 | tf_op jit(solution)/shard_map/all_gather | solution.py:85
  83.6 53.5 %all-gather.12.cloned.1.call-done = bf16[2,2560,384]{2,1,0:T(8,128)(2,1)} async-done(((bf16[2,640,384]{2,1,0:T(8,128)(2,1)}), bf16[2,2560,384]{2,1,0:T(8,128)(2,1)}) %all-gather.12.cloned.1.call-update) | async-done | bytes 3932176 | tf_op jit(solution)/shard_map/all_gather | solution.py:116
  143.4 109.1 %while.48 = (s32[]{:T(128)}, f32[2,6,640]{2,1,0:T(8,128)S(1)}, f32[2,6,640]{2,1,0:T(8,128)S(1)}, s32[5]{0:T(128)S(1)}, bf16[2,640,20]{1,2,0:T(8,128)(2,1)S(1)}, ...) while((s32[]{:T(128)}, f32[2,6,640]{2,1,0:T(8,128)S(1)}, ...), condition=%wide.region_4.5_spmd.clone, body=%wide.region_1.4_spmd.clone.sunk | while | flops 562684032 | bytes 36312256 | solution.py:136
  260.2 62.9 %while.49 = (s32[]{:T(128)}, f32[2,640,6,64]{1,3,2,0:T(8,128)S(1)}, s32[5]{0:T(128)S(1)}, bf16[2,2560,6,64]{1,3,2,0:T(8,128)(2,1)}, bf16[2,640,20]{1,2,0:T(8,128...) while((s32[]{:T(128)}, f32[2,640,6,64]{1,3,2,0:T(8,128)S(1)}, ...), condition=%wide.region_6.7_spmd.clone, body=%wide.region_5.6_spmd.clone.sunk | while | flops 1051216512 | bytes 8560837 | solution.py:154
  351.2 13.2 all-gather
  390.8 26.9 %bitcast_convert_fusion.3 = bf16[1704,768]{1,0:T(8,128)(2,1)} fusion(f32[1280,768]{1,0:T(8,128)} %bitcast_convert_fusion.5, f32[2,1280]{1,0:T(2,128)S(1)} %fusion.202, pred[2,1704,1280]{2,1,0:T(8,128)(4,1)} %iota_compare_fusion.17), kind=kOutput, calls=%fused_computation.125 | convolution fusion | flops 40205680640 | bytes 10921984 | tf_op jit(solution)/shard_map/cet,ctd->ed/dot_general | solution.py:213
  426.4 40.2 %all-gather.14.cloned.1.call-done = bf16[768,2,2,1024]{3,0,2,1:T(8,128)(2,1)} async-done(((bf16[192,2,2,1024]{3,0,2,1:T(8,128)(2,1)}), bf16[768,2,2,1024]{3,0,2,1:T(8,128)(2,1)}) %all-gather.14.cloned.1.call-update) | async-done | bytes 6291472 | tf_op jit(solution)/shard_map/all_gather | solution.py:90
  478.3 52.1 %all-gather.16.cloned.1.call-done = bf16[768,2,1024]{2,0,1:T(8,128)(2,1)} async-done(((bf16[192,2,1024]{2,0,1:T(8,128)(2,1)}), bf16[768,2,1024]{2,0,1:T(8,128)(2,1)}) %all-gather.16.cloned.1.call-update) | async-done | bytes 3145744 | tf_op jit(solution)/shard_map/all_gather | solution.py:91
  530.4 12.3 fusion.96
  562.6 29.1 %all-reduce.29.cloned.1.call-done = (bf16[2,4,213,768]{3,2,1,0:T(8,128)(2,1)}, bf16[2,4,213,768]{3,2,1,0:T(8,128)(2,1)}) async-done(((bf16[2,4,213,768]{3,2,1,0:T(8,128)(2,1)}, bf16[2,4,213,768]{3,2,1,0:T(8,128)(2,1)}), (bf16[2,4,213,768]{3,2,1,0:T(8,128)(2,1)}, bf16[2,4,213,768]{3,2,1,0:T(8,128)(2,1)})) %all-reduce.29.cloned.1.call-update) | async-done | bytes 5234704 | tf_op jit(solution)/shard_map/psum | solution.py:196
  645.8 20.2 %fusion.66 = (f32[1280,768]{1,0:T(8,128)}, f32[1280,768]{1,0:T(8,128)}, bf16[2,1280,768]{2,1,0:T(8,128)(2,1)}) fusion(f32[1280,768]{1,0:T(8,128)} %bitcast_convert_fusion.5, f32[2,1280]{1,0:T(2,128)S(1)} %bitcast.447, f32[2,1280]{1,0:T(2,128)S(1)} %fusion.202, f32[1280,2,768]{2,0,1:T(8,128)} %fusion.144, f32[1280,768]{1,0:T(8,128)} %get-tuple-element.762, ...), kind=kOutput, calls=%fused_computation.102 | convolution fusion | flops 6720491520 | bytes 30173184 | tf_op jit(solution)/shard_map/cet,ed->ctd/dot_general | solution.py:200
  666.0 25.2 %fusion.67 = f32[1280,1,2]{2,1,0:T(1,128)S(1)} fusion(bf16[2,1280,768]{2,1,0:T(8,128)(2,1)} %get-tuple-element.786, bf16[1280,768,1]{1,0,2:T(8,128)(2,1)} %bitcast.427), kind=kOutput, calls=%fused_computation.105 | convolution fusion | flops 3932160 | bytes 5908480 | tf_op jit(solution)/shard_map/cnd,nd->nc/dot_general | solution.py:211
  721.8 242.8 %while.50 = (s32[]{:T(128)}, f32[2,640,6,64]{1,3,2,0:T(8,128)}, bf16[5,2,512,2,384]{4,2,0,3,1:T(8,128)(2,1)}, s32[5]{0:T(128)S(1)}, bf16[2,2560,6,64]{1,3,2,0:T(...) while((s32[]{:T(128)}, f32[2,640,6,64]{1,3,2,0:T(8,128)}, ...), condition=%wide.region_22.23_spmd.clone, body=%wide.region_21.22_spmd.clone.sunk | while | flops 2586331648 | bytes 141977424 | solution.py:294
  971.3 13.2 fusion.74
  992.8 16.4 %copy.157 = bf16[768,2,2,1024]{3,2,1,0:T(2,128)(2,1)} copy(bf16[768,2,2,1024]{0,3,2,1:T(8,128)(2,1)} %fusion.74) | data formatting | bytes 12582912 | tf_op jit(solution)/shard_map/convert_element_type | solution.py:339
  1019.0 83.6 %reduce-scatter.10.cloned.1.call-done = bf16[2,640,2,384]{3,1,2,0:T(8,128)(2,1)} async-done(((bf16[2,2560,2,384]{3,1,2,0:T(8,128)(2,1)}), bf16[2,640,2,384]{3,1,2,0:T(8,128)(2,1)}) %reduce-scatter.10.cloned.1.call-update) | async-done | bytes 1966096 | tf_op jit(solution)/shard_map/reduce_scatter | solution.py:302
  1126.4 18.7 %reduce-scatter.16.cloned.1.call-done = bf16[192,12]{1,0:T(8,128)(2,1)} async-done(((bf16[768,12]{1,0:T(8,128)(2,1)}), bf16[192,12]{1,0:T(8,128)(2,1)}) %reduce-scatter.16.cloned.1.call-update) | async-done | bytes 4624
  1146.0 326.1 %all-reduce.25.cloned.1.call-done = (bf16[768,2,2,1024]{3,2,1,0:T(2,128)(2,1)}, bf16[768,2,1024]{2,1,0:T(2,128)(2,1)}) async-done(((bf16[768,2,2,1024]{3,2,1,0:T(2,128)(2,1)}, bf16[768,2,1024]{2,1,0:T(2,128)(2,1)}), (bf16[768,2,2,1024]{3,2,1,0:T(2,128)(2,1)}, bf16[768,2,1024]{2,1,0:T(2,128)(2,1)})) %all-reduce.25.cloned.1.call-update) | async-done | bytes 9437200
  1479.8 15.2 all-reduce.23.cloned.1.call-done
  1510.2 16.0 all-reduce.12
  1528.5 31.6 %reduce-scatter.12.cloned.1.call-done = bf16[192,3,384]{2,0,1:T(8,128)(2,1)} async-done(((bf16[768,3,384]{2,0,1:T(8,128)(2,1)}), bf16[192,3,384]{2,0,1:T(8,128)(2,1)}) %reduce-scatter.12.cloned.1.call-update) | async-done | bytes 442384 | tf_op jit(solution)/shard_map/reduce_scatter | solution.py:320
  1564.7 43.9 %all-reduce.27.cloned.1.call-done = (bf16[192,3,384]{2,0,1:T(8,128)(2,1)}, bf16[192,384]{1,0:T(8,128)(2,1)}) async-done(((bf16[192,3,384]{2,0,1:T(8,128)(2,1)}, bf16[192,384]{1,0:T(8,128)(2,1)}), (bf16[192,3,384]{2,0,1:T(8,128)(2,1)}, bf16[192,384]{1,0:T(8,128)(2,1)})) %all-reduce.27.cloned.1.call-update) | async-done | bytes 589840 | tf_op jit(solution)/shard_map/psum | solution.py:346
  (467 shorter events, 677.1 us)
Async XLA Ops:
  7.2 45.5 %all-gather.8.cloned.1.call-start = ((), (), s32[]{:S(2)}) async-start(), calls=%async_computation.9 | async-start | bytes 2211840 | tf_op jit(solution)/shard_map/all_gather | solution.py:84
  7.9 129.2 %all-gather.12.cloned.1.call-start = ((), (), s32[]{:S(2)}) async-start(), calls=%async_computation.11 | async-start | bytes 4915200 | tf_op jit(solution)/shard_map/all_gather | solution.py:116
  58.7 195.1 %all-gather.10.cloned.1.call-start = ((), (), s32[]{:S(2)}) async-start(), calls=%async_computation.10 | async-start | bytes 4915200 | tf_op jit(solution)/shard_map/all_gather | solution.py:117
  78.8 245.6 %copy-start.22 = (bf16[768,384]{1,0:T(8,128)(2,1)}, bf16[768,384]{1,0:T(8,128)(2,1)S(1)}, u32[]{:S(2)}) copy-start(bf16[768,384]{1,0:T(8,128)(2,1)S(1)} %all_gather.34) | copy-start | bytes 1769476
  83.1 285.6 %all-reduce.21.cloned.1.call-start = ((), (), s32[]{:S(2)}) async-start(), calls=%async_computation.12 | async-start | bytes 3932160 | tf_op jit(solution)/shard_map/psum | solution.py:162
  327.9 138.7 %all-gather.14.cloned.1.call-start = ((), (), s32[]{:S(2)}) async-start(), calls=%async_computation.13 | async-start | bytes 7864320 | tf_op jit(solution)/shard_map/all_gather | solution.py:90
  331.0 199.3 %all-gather.16.cloned.1.call-start = ((), (), s32[]{:S(2)}) async-start(), calls=%async_computation.14 | async-start | bytes 3932160 | tf_op jit(solution)/shard_map/all_gather | solution.py:91
  386.1 35.7 %all-to-all-start = ((bf16[8,1,213,768]{3,2,1,0:T(8,128)(2,1)}), bf16[8,1,213,768]{3,2,1,0:T(8,128)(2,1)}, u32[]{:S(2)}, u32[]{:S(2)}) async-start(bf16[8,1,213,768]{3,2,1,0:T(8,128)(2,1)} %bitcast.423), calls=%async_computation | async-start | bytes 5308416 | tf_op jit(solution)/shard_map/all_to_all | solution.py:190
  390.8 255.0 %copy-start.42 = (f32[2,1280]{1,0:T(2,128)}, f32[2,1280]{1,0:T(2,128)S(1)}, u32[]{:S(2)}) copy-start(f32[2,1280]{1,0:T(2,128)S(1)} %fusion.202) | copy-start | bytes 30724
  421.8 108.6 %all-to-all-start.2 = ((bf16[8,1,213,768]{3,2,1,0:T(8,128)(2,1)}), bf16[8,1,213,768]{3,2,1,0:T(8,128)(2,1)}, u32[]{:S(2)}, u32[]{:S(2)}) async-start(bf16[8,1,213,768]{3,2,1,0:T(8,128)(2,1)} %bitcast.422), calls=%async_computation.2 | async-start | bytes 5308416 | tf_op jit(solution)/shard_map/all_to_all | solution.py:225
  426.4 165.4 %all-reduce.29.cloned.1.call-start = ((), (), s32[]{:S(2)}) async-start(), calls=%async_computation.23 | async-start | bytes 10616832 | tf_op jit(solution)/shard_map/psum | solution.py:196
  597.7 35.9 %all-to-all-start.1 = ((bf16[2,4,213,768]{3,0,2,1:T(2,128)(2,1)}), bf16[2,4,213,768]{3,0,2,1:T(2,128)(2,1)}, u32[]{:S(2)}, u32[]{:S(2)}) async-start(bf16[2,4,213,768]{3,0,2,1:T(2,128)(2,1)} %copy.141), calls=%async_computation.1 | async-start | bytes 5234688 | tf_op jit(solution)/shard_map/all_to_all | solution.py:197
  633.6 58.3 %all-to-all-start.3 = ((bf16[2,4,213,768]{3,0,2,1:T(2,128)(2,1)}), bf16[2,4,213,768]{3,0,2,1:T(2,128)(2,1)}, u32[]{:S(2)}, u32[]{:S(2)}) async-start(bf16[2,4,213,768]{3,0,2,1:T(2,128)(2,1)} %copy.147), calls=%async_computation.3 | async-start | bytes 5234688 | tf_op jit(solution)/shard_map/all_to_all | solution.py:244
  638.1 464.5 %reduce-scatter.10.cloned.1.call-start = ((), (), s32[]{:S(2)}) async-start(), calls=%async_computation.15 | async-start | bytes 9830400 | tf_op jit(solution)/shard_map/reduce_scatter | solution.py:302
  964.6 160.3 %reduce-scatter.18.cloned.1.call-start = ((), (), s32[]{:S(2)}) async-start(), calls=%async_computation.20 | async-start | bytes 245760
  971.2 173.9 %reduce-scatter.16.cloned.1.call-start = ((), (), s32[]{:S(2)}) async-start(), calls=%async_computation.19 | async-start | bytes 245760
  986.2 485.9 %all-reduce.25.cloned.1.call-start = ((), (), s32[]{:S(2)}) async-start(), calls=%async_computation.21 | async-start | bytes 18874368
  1015.0 480.0 %all-reduce.23.cloned.1.call-start = ((), (), s32[]{:S(2)}) async-start(), calls=%async_computation.16 | async-start | bytes 3932160 | tf_op jit(solution)/shard_map/psum | solution.py:313
  1109.3 419.1 %reduce-scatter.14.cloned.1.call-start = ((), (), s32[]{:S(2)}) async-start(), calls=%async_computation.18 | async-start | bytes 737280 | tf_op jit(solution)/shard_map/reduce_scatter | solution.py:323
  1113.7 446.3 %reduce-scatter.12.cloned.1.call-start = ((), (), s32[]{:S(2)}) async-start(), calls=%async_computation.17 | async-start | bytes 2211840 | tf_op jit(solution)/shard_map/reduce_scatter | solution.py:320
  1119.6 375.5 %copy-start.4 = (bf16[2,640,768]{2,1,0:T(8,128)(2,1)S(1)}, bf16[2,640,768]{2,1,0:T(8,128)(2,1)}, u32[]{:S(2)}) copy-start(bf16[2,640,768]{2,1,0:T(8,128)(2,1)} %param.20) | copy-start | bytes 5898244
  1119.6 375.5 %copy-start.36 = (f32[1280]{0:T(1024)S(1)}, f32[1280]{0:T(1024)}, u32[]{:S(2)}) copy-start(f32[1280]{0:T(1024)} %copy-done.35) | copy-start | bytes 15364
  1119.6 375.4 %copy-start.38 = (f32[768]{0:T(1024)S(1)}, f32[768]{0:T(1024)}, u32[]{:S(2)}) copy-start(f32[768]{0:T(1024)} %copy-done.37) | copy-start | bytes 9220
  1119.6 489.0 %all-reduce.27.cloned.1.call-start = ((), (), s32[]{:S(2)}) async-start(), calls=%async_computation.22 | async-start | bytes 1179648 | tf_op jit(solution)/shard_map/psum | solution.py:346
  (62 other events, 469.2 us)
Sparse Core Ops, SparseCore 0:
  9.6 43.0 all-gather.7
  58.8 78.2 all-gather.11
  139.2 75.4 all-gather.9
  328.0 19.9 all-reduce.20
  350.1 116.5 all-gather.13
  468.7 61.6 all-gather.15
  562.7 28.9 all-reduce.28
  964.7 137.8 reduce-scatter.9
  1105.0 19.8 reduce-scatter.17
  1127.5 17.5 reduce-scatter.15
  1148.5 323.5 all-reduce.24
  1475.0 19.9 all-reduce.22
  1497.9 23.1 reduce-scatter.13
  1523.3 36.7 reduce-scatter.11
  1563.2 45.3 all-reduce.26
where the time goes:
time: 1630 us; the launch traced here: 1620 us
  waiting for transfers between devices  734 us (45%)
  matrix products  469 us (29%)
  local copies, waits for them, and re-layouts  146 us (9%)
  other arithmetic  117 us (7%)
  blocking collectives  86.2 us (5%)
  loops' own time  31 us (2%)
  starting transfers between devices  19.6 us (1%)
  between operations  16.5 us (1%)
    unnamed x18, waiting for transfers between devices  350 us
    dot_general x10, matrix products, block_scores(): jnp.einsum('qhe,khe->hqk', queries, keys_blk, preferred_element_type=jnp....  95.4 us
    reduce_scatter x1, waiting for transfers between devices, shards(): lax.psum_scatter(key_terms.astype(jnp.bfloat16), 'ctx', scatter_dimension...  83.6 us
    all_gather x1, waiting for transfers between devices, shards(): lax.all_gather(k_low.reshape(tree_count, rows, local_width), 'ctx', axis=...  53.5 us
    all_gather x1, waiting for transfers between devices, shards(): lax.all_gather(w_down, 'ctx', axis=0, tiled=True)  52.1 us
    dot_general x5, matrix products, both_step(): jnp.einsum('hqk,qhe->khe', prob_low, do_one, preferred_element_type=jnp.f...  49.3 us
    dot_general x5, matrix products, softmax_grads(): jnp.einsum('qhe,khe->hqk', grads_out, values_blk, preferred_element_type=...  48.3 us
    psum x1, waiting for transfers between devices, shards(): lax.psum(summed_grads[0].astype(jnp.bfloat16), 'shard').astype(jnp.float32)  43.9 us
  transfers between devices with their start and end apart: 19, of which 13 were waited for; matrix products, arithmetic and copies ran while one was open for 22% of the time, Pallas kernels for 0%

commit v1 on v0

--- a/solution.py
+++ b/solution.py
@@ -1,8 +1,11 @@
+import functools
 import math
 
 import jax
 import jax.numpy as jnp
 from jax import lax
+from jax.experimental import pallas as pl
+from jax.experimental.pallas import tpu as pltpu
 from jax.sharding import PartitionSpec as P
 
 HEAD_DIM = 64
@@ -368,9 +371,593 @@
     )
 
 
+NT = (((1,), (1,)), ((), ()))
+NN = (((1,), (0,)), ((), ()))
+TRUNK = 8
+KEY_SEGS = 12
+PIECE = 256
+
+
+def mm(a, b, dims=NN):
+    return lax.dot_general(a, b, dims, preferred_element_type=jnp.float32)
+
+
+def stacked(rows, half):
+    first = lax.broadcasted_iota(jnp.int32, rows.shape, 1) < half
+    blank = jnp.zeros_like(rows)
+    return jnp.concatenate([jnp.where(first, rows, blank), jnp.where(first, blank, rows)], axis=0)
+
+
+def unstack(wide, half, seg):
+    return jnp.concatenate([wide[:half, :seg], wide[half:, seg:]], axis=0)
+
+
+def causal(seg):
+    row = lax.broadcasted_iota(jnp.int32, (seg, 2 * seg), 0)
+    col = lax.broadcasted_iota(jnp.int32, (seg, 2 * seg), 1)
+    return row <= jnp.where(col >= seg, col - seg, col)
+
+
+def attend_kernel(own, seg, half, info, q_ref, k_ref, v_ref, o_ref, lse_ref, s_ref, p_ref):
+    trunk = TRUNK * seg
+    allowed = causal(seg)
+    v_trunk = v_ref[own : own + trunk, :].T
+
+    def one(i, unused):
+        count, branch, leaf = info[i, 0], info[i, 1], info[i, 2]
+        here = pl.ds(pl.multiple_of(i * seg, seg), seg)
+        there = pl.ds(pl.multiple_of(own + branch * seg, seg), seg)
+        qs = stacked(q_ref[here, :] * 0.125, half)
+        s_ref[:trunk, :] = mm(k_ref[own : own + trunk, :], qs, NT)
+        s_branch = mm(k_ref[there, :], qs, NT)
+        s_own = jnp.where(allowed, mm(k_ref[here, :], qs, NT), -1e30)
+        biases = [jnp.where(kb < count, 0.0, -1e30) for kb in range(TRUNK)]
+        leaf_bias = jnp.where(leaf > 0, 0.0, -1e30)
+        top = jnp.max(s_own, axis=0, keepdims=True)
+        top = jnp.maximum(top, jnp.max(s_branch, axis=0, keepdims=True) + leaf_bias)
+        for kb in range(TRUNK):
+            part = jnp.max(s_ref[kb * seg : (kb + 1) * seg, :], axis=0, keepdims=True)
+            top = jnp.maximum(top, part + biases[kb])
+        e_own = jnp.exp(s_own - top)
+        e_branch = jnp.exp(s_branch - (top - leaf_bias))
+        total = jnp.sum(e_own + e_branch, axis=0, keepdims=True)
+        for kb in range(TRUNK):
+            e = jnp.exp(s_ref[kb * seg : (kb + 1) * seg, :] - (top - biases[kb]))
+            total = total + jnp.sum(e, axis=0, keepdims=True)
+            p_ref[kb * seg : (kb + 1) * seg, :] = e.astype(jnp.bfloat16)
+        out = mm(v_trunk, p_ref[...])
+        out = out + mm(v_ref[there, :].T, e_branch.astype(jnp.bfloat16))
+        out = out + mm(v_ref[here, :].T, e_own.astype(jnp.bfloat16))
+        out = unstack(out * (1.0 / total), half, seg)
+        o_ref[here, :] = out.T.astype(jnp.bfloat16)
+        lse_ref[pl.ds(i, 1), :] = top + jnp.log(total)
+        return 0
+
+    lax.fori_loop(0, own // seg, one, 0)
+
+
+def attend_back_kernel(
+    own, seg, half, info, q_ref, k_ref, v_ref, o_ref, do_ref, lse_ref, dq_ref, dk_ref, dv_ref, ak, av
+):
+    trunk = TRUNK * seg
+    allowed = causal(seg)
+    low = jnp.bfloat16
+    tk = slice(own, own + trunk)
+    k_trunk = k_ref[tk, :].T
+    ak[...] = jnp.zeros_like(ak)
+    av[...] = jnp.zeros_like(av)
+
+    def one(i, unused):
+        count, branch, leaf = info[i, 0], info[i, 1], info[i, 2]
+        here = pl.ds(pl.multiple_of(i * seg, seg), seg)
+        there = pl.ds(pl.multiple_of(own + branch * seg, seg), seg)
+        qs = stacked(q_ref[here, :] * 0.125, half)
+        do = do_ref[here, :]
+        dos = stacked(do, half)
+        prod = (do.astype(jnp.float32) * o_ref[here, :].astype(jnp.float32)).T
+        delta = jnp.concatenate(
+            [jnp.sum(prod[:half], axis=0, keepdims=True), jnp.sum(prod[half:], axis=0, keepdims=True)],
+            axis=1,
+        )
+        lse = lse_ref[pl.ds(i, 1), :]
+        leaf_bias = jnp.where(leaf > 0, 0.0, -1e30)
+
+        def piece(keys, values, shift, mask):
+            s = mm(keys, qs, NT)
+            if mask:
+                s = jnp.where(allowed, s, -1e30)
+            if isinstance(shift, list):
+                p = jnp.concatenate(
+                    [jnp.exp(s[kb * seg : (kb + 1) * seg] - shift[kb]) for kb in range(TRUNK)], axis=0
+                )
+            else:
+                p = jnp.exp(s - shift)
+            ds = (p * (mm(values, dos, NT) - delta)).astype(low)
+            p = p.astype(low)
+            return (mm(p, dos), mm(ds, qs), ds)
+
+        shifts = [lse - jnp.where(kb < count, 0.0, -1e30) for kb in range(TRUNK)]
+        dv, dk, ds = piece(k_ref[tk, :], v_ref[tk, :], shifts, False)
+        av[tk, :] += dv
+        ak[tk, :] += dk
+        dq = mm(k_trunk, ds)
+        keys = k_ref[there, :]
+        dv, dk, ds = piece(keys, v_ref[there, :], lse - leaf_bias, False)
+        av[there, :] += dv
+        ak[there, :] += dk
+        dq = dq + mm(keys.T, ds)
+        keys = k_ref[here, :]
+        dv, dk, ds = piece(keys, v_ref[here, :], lse, True)
+        av[here, :] += dv
+        ak[here, :] += dk
+        dq = dq + mm(keys.T, ds)
+        dq_ref[here, :] = (unstack(dq, half, seg) * 0.125).T.astype(low)
+        return 0
+
+    lax.fori_loop(0, own // seg, one, 0)
+    dk_ref[...] = ak[...].astype(low)
+    dv_ref[...] = av[...].astype(low)
+
+
+def attend(info, q, kv, seg):
+    own, width = q.shape
+    total = kv.shape[0]
+    pairs = width // 128
+    segs = own // seg
+    lane = pl.BlockSpec((own, 128), lambda h: (0, h))
+    return pl.pallas_call(
+        functools.partial(attend_kernel, own, seg, HEAD_DIM),
+        grid=(pairs,),
+        in_specs=[
+            pl.BlockSpec(memory_space=pltpu.SMEM),
+            lane,
+            pl.BlockSpec((total, 128), lambda h: (0, h)),
+            pl.BlockSpec((total, 128), lambda h: (0, pairs + h)),
+        ],
+        out_specs=[lane, pl.BlockSpec((None, 8, 2 * seg), lambda h: (h, 0, 0))],
+        out_shape=[
+            jax.ShapeDtypeStruct((own, width), jnp.bfloat16),
+            jax.ShapeDtypeStruct((pairs, 8, 2 * seg), jnp.float32),
+        ],
+        scratch_shapes=[
+            pltpu.VMEM((TRUNK * seg, 2 * seg), jnp.float32),
+            pltpu.VMEM((TRUNK * seg, 2 * seg), jnp.bfloat16),
+        ],
+        compiler_params=pltpu.CompilerParams(vmem_limit_bytes=32 << 20),
+        cost_estimate=pl.CostEstimate(
+            flops=4 * segs * 10 * seg * seg * width, bytes_accessed=8 << 20, transcendentals=0
+        ),
+        name="attend",
+    )(info, q, kv, kv)
+
+
+def attend_back(info, q, kv, o, do, lse, seg):
+    own, width = q.shape
+    total = kv.shape[0]
+    pairs = width // 128
+    segs = own // seg
+    lane = pl.BlockSpec((own, 128), lambda h: (0, h))
+    keys = pl.BlockSpec((total, 128), lambda h: (0, h))
+    return pl.pallas_call(
+        functools.partial(attend_back_kernel, own, seg, HEAD_DIM),
+        grid=(pairs,),
+        in_specs=[
+            pl.BlockSpec(memory_space=pltpu.SMEM),
+            lane,
+            keys,
+            pl.BlockSpec((total, 128), lambda h: (0, pairs + h)),
+            lane,
+            lane,
+            pl.BlockSpec((None, 8, 2 * seg), lambda h: (h, 0, 0)),
+        ],
+        out_specs=[lane, keys, keys],
+        out_shape=[
+            jax.ShapeDtypeStruct((own, width), jnp.bfloat16),
+            jax.ShapeDtypeStruct((total, width), jnp.bfloat16),
+            jax.ShapeDtypeStruct((total, width), jnp.bfloat16),
+        ],
+        scratch_shapes=[
+            pltpu.VMEM((total, 128), jnp.float32),
+            pltpu.VMEM((total, 128), jnp.float32),
+        ],
+        compiler_params=pltpu.CompilerParams(vmem_limit_bytes=40 << 20),
+        cost_estimate=pl.CostEstimate(
+            flops=10 * segs * 10 * seg * seg * width, bytes_accessed=16 << 20, transcendentals=0
+        ),
+        name="attend_back",
+    )(info, q, kv, kv, o, do, lse)
+
+
+def expert_kernel(x_ref, xt_ref, d_ref, dt_ref, w_ref, o0_ref, s0_ref, o_ref, s_ref, dw_ref):
+    low = jnp.bfloat16
+
+    @pl.when(pl.program_id(0) == 0)
+    def start():
+        o_ref[...] = o0_ref[...]
+        s_ref[...] = s0_ref[...]
+
+    wg = w_ref[:, :PIECE]
+    wu = w_ref[:, PIECE : 2 * PIECE]
+    wd = w_ref[:, 2 * PIECE :]
+    u = mm(x_ref[...], wg)
+    up = mm(x_ref[...], wu)
+    sigma = 1.0 / (1.0 + jnp.exp(-u))
+    silu = u * sigma
+    hidden = (silu * up).astype(low)
+    o_ref[...] += mm(hidden, wd, NT)
+    dh = mm(d_ref[...], wd)
+    du = (dh * up * sigma * (1.0 + u * (1.0 - sigma))).astype(low)
+    dup = (dh * silu).astype(low)
+    s_ref[...] += mm(du, wg, NT) + mm(dup, wu, NT)
+    dw_ref[:, :PIECE] = mm(xt_ref[...], du).astype(low)
+    dw_ref[:, PIECE : 2 * PIECE] = mm(xt_ref[...], dup).astype(low)
+    dw_ref[:, 2 * PIECE :] = mm(dt_ref[...], hidden).astype(low)
+
+
+def expert_pass(x, xt, d, dt, w, o0, s0):
+    rows, width = x.shape
+    pieces = w.shape[1] // (3 * PIECE)
+    whole = pl.BlockSpec((rows, width), lambda j: (0, 0))
+    turned = pl.BlockSpec((width, rows), lambda j: (0, 0))
+    strip = pl.BlockSpec((width, 3 * PIECE), lambda j: (0, j))
+    return pl.pallas_call(
+        expert_kernel,
+        grid=(pieces,),
+        in_specs=[whole, turned, whole, turned, strip, whole, whole],
+        out_specs=[whole, whole, strip],
+        out_shape=[
+            jax.ShapeDtypeStruct((rows, width), jnp.float32),
+            jax.ShapeDtypeStruct((rows, width), jnp.float32),
+            jax.ShapeDtypeStruct(w.shape, jnp.bfloat16),
+        ],
+        compiler_params=pltpu.CompilerParams(vmem_limit_bytes=56 << 20),
+        cost_estimate=pl.CostEstimate(
+            flops=2 * 3 * rows * w.shape[0] * w.shape[1], bytes_accessed=30 << 20, transcendentals=0
+        ),
+        name="expert_pass",
+    )(x, xt, d, dt, w, o0, s0)
+
+
+def flip(x, axis, bit, size):
+    return lax.ppermute(x, axis, [(i, i ^ bit) for i in range(size)])
+
+
+def line_gather(x, size, position):
+    after, before = [x], [x]
+    for t in range(1, size):
+        after.append(lax.ppermute(after[-1], "ctx", [(i, i + 1) for i in range(t - 1, size - 1)]))
+        before.append(lax.ppermute(before[-1], "ctx", [(i, i - 1) for i in range(1, size - t + 1)]))
+    out = jnp.zeros((size,) + x.shape, x.dtype)
+    for k in range(size):
+        block = x if k == 0 else jnp.where(position >= k, after[k], before[size - k])
+        out = lax.dynamic_update_index_in_dim(out, block, (position - k) % size, 0)
+    return out
+
+
+def turn_gather(x, size, position):
+    out = jnp.zeros((size,) + x.shape, x.dtype)
+    out = lax.dynamic_update_index_in_dim(out, x, position, 0)
+    for k in range(1, size):
+        block = lax.ppermute(x, "ctx", [(i, (i + k) % size) for i in range(size)])
+        out = lax.dynamic_update_index_in_dim(out, block, (position - k) % size, 0)
+    return out
+
+
+def line_sum(x, size, position):
+    def part(index):
+        index = jnp.clip(index, 0, size - 1)
+        return lax.dynamic_index_in_dim(x, index, 0, keepdims=False)
+
+    def add(a, b):
+        return (a.astype(jnp.float32) + b.astype(jnp.float32)).astype(x.dtype)
+
+    down = up = None
+    for t in range(1, size):
+        low = part(position - size + t)
+        high = part(position + size - t)
+        if t > 1:
+            low, high = add(low, down), add(high, up)
+        down = lax.ppermute(low, "ctx", [(i, i - 1) for i in range(size - t, size)])
+        up = lax.ppermute(high, "ctx", [(i, i + 1) for i in range(0, t)])
+    return part(position).astype(jnp.float32) + down.astype(jnp.float32) + up.astype(jnp.float32)
+
+
+def turn_sum(x, size, position):
+    total = lax.dynamic_index_in_dim(x, position, 0, keepdims=False).astype(jnp.float32)
+    for k in range(1, size):
+        block = lax.dynamic_index_in_dim(x, (position + k) % size, 0, keepdims=False)
+        got = lax.ppermute(block, "ctx", [(i, (i + k) % size) for i in range(size)])
+        total = total + got.astype(jnp.float32)
+    return total
+
+
+def by_core(
+    tokens, gate_res, cotangent, parents, expert_ids, priority, w_qkv, w_out, w_router, attn_gain,
+    ffn_gain, const_vec, w_gate_up, w_down,
+):
+    low, full = jnp.bfloat16, jnp.float32
+    shard, ctx, tp = lax.axis_index("shard"), lax.axis_index("ctx"), lax.axis_index("tp")
+    shards_n, ctx_n = lax.axis_size("shard"), lax.axis_size("ctx")
+    trees, rows, width = tokens.shape
+    rows_d = w_qkv.shape[0]
+    seg = rows * ctx_n // parents.shape[1]
+    own_segs = rows // seg
+    edge = KEY_SEGS * seg - 2 * rows
+
+    def own_tree(x):
+        return lax.dynamic_index_in_dim(x, tp, 0, keepdims=False)
+
+    def both_trees(x, other):
+        ordered = jnp.stack([x, other])
+        return jnp.where(tp == 0, ordered, ordered[::-1])
+
+    def swap(x):
+        return flip(x, "tp", 1, 2)
+
+    x_own = own_tree(tokens)
+    ends = [(i, i + 1) for i in range(ctx_n - 1)]
+    near_head = lax.ppermute(x_own[:edge], "ctx", ends)
+    near_tail = lax.ppermute(x_own[edge:], "ctx", ends[:-1])
+    near = jnp.concatenate([near_head, near_tail], axis=0)
+    mid = lax.ppermute(near, "ctx", ends[1:])
+    far = lax.ppermute(mid, "ctx", ends[2:])
+
+    mine = jnp.stack([w_qkv[:, 0], w_qkv[:, 1], w_qkv[:, 2], w_out])
+    matrix = turn_gather(lax.dynamic_index_in_dim(mine, shard, 0, keepdims=False), ctx_n, ctx)
+    matrix = matrix.reshape(width, -1)
+    plane = [matrix] + [flip(matrix, "shard", k, shards_n) for k in range(1, shards_n)]
+    plane = [jnp.concatenate([m, swap(m)], axis=1) for m in plane]
+    plane = jnp.stack(plane)
+    weight_q, weight_k, weight_v, weight_o = [
+        lax.dynamic_index_in_dim(plane, m ^ shard, 0, keepdims=False) for m in range(4)
+    ]
+    weight_kv = jnp.concatenate([weight_k, weight_v], axis=1)
+
+    small = jnp.concatenate(
+        [w_router.T, attn_gain[None], ffn_gain[None], const_vec.T], axis=0
+    )
+    small = turn_gather(small, ctx_n, ctx).transpose(1, 0, 2).reshape(small.shape[0], width)
+    all_experts = w_router.shape[1]
+    router_t = small[:all_experts]
+    gain_a = small[all_experts].astype(full)
+    gain_f = small[all_experts + 1].astype(full)
+    const_t = small[all_experts + 2 :].astype(full)
+
+    units = w_down.shape[2]
+    pieces = units // PIECE
+
+    def packed(e):
+        gu = lax.dynamic_index_in_dim(w_gate_up, e, 1, keepdims=False)
+        dn = lax.dynamic_index_in_dim(w_down, e, 1, keepdims=False)
+        three = jnp.concatenate([gu, dn[:, None]], axis=1).reshape(rows_d, 3, pieces, PIECE)
+        return three.transpose(0, 2, 1, 3).reshape(rows_d, 3 * units)
+
+    half_near = packed(tp)
+    half_far = swap(packed(1 - tp))
+    expert_near = line_gather(half_near, ctx_n, ctx).reshape(width, 3 * units)
+    expert_far = line_gather(half_far, ctx_n, ctx).reshape(width, 3 * units)
+
+    capacity = trees * rows * 2 // all_experts
+    experts = shards_n * w_gate_up.shape[1]
+    padded = -(-capacity // 16) * 16
+    ids_block = expert_ids.reshape(trees * rows, 2)
+    flat = ids_block.reshape(-1)
+    order = (2 * priority[0, 0][:, None] + jnp.arange(2, dtype=jnp.int32)[None, :]).reshape(-1)
+    earlier = (flat[:, None] == flat[None, :]) & (order[None, :] < order[:, None])
+    ranks = jnp.sum(earlier.astype(jnp.int32), axis=1)
+    kept = (flat < experts) & (ranks < capacity) & (flat % 2 == tp)
+    place = jnp.where(kept, ((flat // 2) ^ shard) * padded + ranks, -1).reshape(trees, rows, 2)
+    place = jnp.where(tp == 0, place, place[::-1]).reshape(trees * rows, 2).T
+    slot = jnp.arange(shards_n * padded, dtype=jnp.int32)
+    table = slot[None, :, None] == place[:, None, :]
+    routed = (table[0] | table[1]).astype(low)
+
+    block0 = jnp.where(ctx == 0, x_own, jnp.where(ctx == 1, near, jnp.where(ctx == 2, mid, far)))
+    block1 = jnp.where(ctx == 1, x_own, jnp.where(ctx == 2, near, mid))
+    block2 = jnp.where(ctx == 2, x_own[:edge], near[:edge])
+    x_all = jnp.concatenate([x_own, block0, block1, block2], axis=0).astype(full)
+    inv_all = lax.rsqrt(jnp.mean(x_all * x_all, axis=-1, keepdims=True) + eps)
+    unit_all = x_all * inv_all
+    normed = (unit_all * gain_a).astype(low)
+    q = mm(normed[:rows], weight_q).astype(low)
+    kv = mm(normed, weight_kv).astype(low)
+
+    seg_id = ctx * own_segs + jnp.arange(own_segs, dtype=jnp.int32)
+    parent = jnp.take(own_tree(parents), seg_id)
+    leaf = (seg_id >= KEY_SEGS).astype(jnp.int32)
+    info = jnp.stack([jnp.minimum(seg_id, TRUNK), jnp.where(leaf > 0, parent, TRUNK), leaf], axis=1)
+    o_low, lse = attend(info, q, kv, seg)
+
+    inputs = x_own.astype(full)
+    mixed = inputs + mm(o_low, weight_o, NT)
+    inv_second = lax.rsqrt(jnp.mean(mixed * mixed, axis=-1, keepdims=True) + eps)
+    second_unit = mixed * inv_second
+    second = (second_unit * gain_f).astype(low)
+
+    logits = mm(second, router_t, NT) + own_tree(gate_res)
+    expo = jnp.exp(logits - jnp.max(logits, axis=-1, keepdims=True))
+    probs = expo / jnp.sum(expo, axis=-1, keepdims=True)
+    ids = own_tree(expert_ids)
+    selector = (ids[:, :, None] == jnp.arange(all_experts, dtype=jnp.int32)).astype(full)
+    picked = jnp.sum(selector * probs[:, None, :], axis=-1)
+    picked_total = jnp.sum(picked, axis=-1, keepdims=True)
+    gates = picked / picked_total
+
+    second_both = jnp.concatenate([second, swap(second)], axis=0)
+    gates_both = jnp.concatenate([gates.T, swap(gates.T)], axis=1)
+    g_own = own_tree(cotangent)
+    g_other = lax.dynamic_index_in_dim(cotangent, 1 - tp, 0, keepdims=False)
+    slots = mm(routed, second_both).astype(low).reshape(shards_n, padded, width)
+    g_slots = mm(routed, jnp.concatenate([g_own, g_other], axis=0))
+    weighted = jnp.where(table[0], gates_both[0][None, :], 0.0) + jnp.where(
+        table[1], gates_both[1][None, :], 0.0
+    )
+    gate_slots = jnp.sum(weighted, axis=1, keepdims=True)
+    d_slots = (g_slots * gate_slots).astype(low).reshape(shards_n, padded, width)
+    x_in = [slots[0]] + [flip(slots[k], "shard", k, shards_n) for k in range(1, shards_n)]
+    d_in = [d_slots[0]] + [flip(d_slots[k], "shard", k, shards_n) for k in range(1, shards_n)]
+    x_in = jnp.concatenate(x_in, axis=0)
+    d_in = jnp.concatenate(d_in, axis=0)
+
+    blank = jnp.zeros(x_in.shape, full)
+    xt, dt = x_in.T, d_in.T
+    out_sum, ds_sum, dw_near = expert_pass(x_in, xt, d_in, dt, expert_near, blank, blank)
+    out_sum, ds_sum, dw_far = expert_pass(x_in, xt, d_in, dt, expert_far, out_sum, ds_sum)
+    out_low = out_sum.astype(low).reshape(shards_n, padded, width)
+    ds_low = ds_sum.astype(low).reshape(shards_n, padded, width)
+    out_back = [out_low[0]] + [flip(out_low[k], "shard", k, shards_n) for k in range(1, shards_n)]
+    ds_back = [ds_low[0]] + [flip(ds_low[k], "shard", k, shards_n) for k in range(1, shards_n)]
+    out_back = jnp.concatenate(out_back, axis=0)
+    ds_back = jnp.concatenate(ds_back, axis=0)
+
+    rows_tn = (((0,), (0,)), ((), ()))
+    combined = mm(weighted.astype(low), out_back, rows_tn)
+    d_routed = mm(routed, ds_back, rows_tn)
+    gate_dots = jnp.sum(g_slots * out_back.astype(full), axis=1)
+    d_gate_pairs = jnp.sum(jnp.where(table, gate_dots[None, :, None], 0.0), axis=1)
+    combined = combined[:rows] + swap(combined[rows:].astype(low)).astype(full)
+    d_routed = d_routed[:rows] + swap(d_routed[rows:].astype(low)).astype(full)
+    d_gate_pairs = d_gate_pairs[:, :rows] + swap(d_gate_pairs[:, rows:])
+
+    second_f = second.astype(full)
+    g = g_own.astype(full)
+    copy_flag = selector[:, :, experts + 1]
+    const_flags = selector[:, :, experts + 2 :]
+    copy_gate = jnp.sum(gates * copy_flag, axis=1, keepdims=True)
+    const_gate = jnp.sum(gates[:, :, None] * const_flags, axis=1)
+    mixed_out = (
+        mixed
+        + combined
+        + copy_gate * second_f
+        + const_gate[:, :1] * const_t[0][None]
+        + const_gate[:, 1:] * const_t[1][None]
+    )
+    g_second = jnp.sum(g * second_f, axis=1, keepdims=True)
+    g_const = jnp.stack([jnp.sum(g * const_t[k][None], axis=1) for k in range(2)], axis=1)
+    d_gates = (
+        d_gate_pairs.T
+        + copy_flag * g_second
+        + jnp.sum(const_flags * g_const[:, None, :], axis=-1)
+    )
+    d_picked = (d_gates - jnp.sum(d_gates * gates, axis=-1, keepdims=True)) / picked_total
+    d_probs = jnp.sum(d_picked[:, :, None] * selector, axis=1)
+    d_logits = probs * (d_probs - jnp.sum(probs * d_probs, axis=-1, keepdims=True))
+    high = lax.Precision.HIGHEST
+    d_router = jnp.einsum("tk,td->kd", d_logits, second_f, precision=high)
+    d_const = jnp.einsum("tk,td->kd", const_gate, g, precision=high)
+    d_second = copy_gate * g + d_routed + jnp.dot(d_logits, router_t.astype(full), precision=high)
+    d_gain_f = jnp.sum(d_second * second_unit, axis=0)
+    d_unit = d_second * gain_f
+    d_mixed = g + inv_second * (
+        d_unit - second_unit * jnp.mean(d_unit * second_unit, axis=-1, keepdims=True)
+    )
+    d_attn = d_mixed.astype(low)
+    d_o = mm(d_attn, weight_o).astype(low)
+    d_weight_o = mm(d_attn, o_low, rows_tn)
+
+    dq, dk, dv = attend_back(info, q, kv, o_low, d_o, lse, seg)
+    d_weight_q = mm(normed[:rows], dq, rows_tn)
+    d_weight_k = mm(normed, dk, rows_tn)
+    d_weight_v = mm(normed, dv, rows_tn)
+    d_keys = mm(dk, weight_k, NT) + mm(dv, weight_v, NT)
+    d_near = d_keys[:rows] + mm(dq, weight_q, NT)
+    d_gain_a = jnp.sum(d_near * unit_all[:rows], axis=0) + jnp.sum(
+        d_keys[rows:] * unit_all[rows:], axis=0
+    )
+
+    def send(x, pairs):
+        return lax.ppermute(x.astype(low), "ctx", pairs).astype(full)
+
+    part0 = d_keys[rows : 2 * rows]
+    part1 = d_keys[2 * rows : 3 * rows]
+    part2 = d_keys[3 * rows :]
+    for hop in range(ctx_n - 1, 0, -1):
+        part0 = part0 + send(part0, [(hop, hop - 1)])
+        if hop >= 2:
+            part1 = part1 + send(part1, [(hop, hop - 1)])
+        if hop >= 3:
+            part2 = part2 + send(part2, [(hop, hop - 1)])
+    part2 = jnp.concatenate([part2, jnp.zeros((rows - edge, width), full)], axis=0)
+    extra = jnp.where(ctx == 0, part0, jnp.where(ctx == 1, part1, jnp.where(ctx == 2, part2, 0.0)))
+    d_normed = d_near + extra
+    unit_own, inv_own = unit_all[:rows], inv_all[:rows]
+    d_first = d_normed * gain_a
+    d_tokens = d_mixed + inv_own * (
+        d_first - unit_own * jnp.mean(d_first * unit_own, axis=-1, keepdims=True)
+    )
+
+    shared = jnp.stack([d_weight_q, d_weight_k, d_weight_v, d_weight_o]).astype(low)
+    part = width // 2
+    shared = shared[:, :, :part].astype(full) + swap(shared[:, :, part:]).astype(full)
+    shared = shared.astype(low)
+
+    def numbered(k):
+        return lax.dynamic_index_in_dim(shared, shard ^ k, 0, keepdims=False)
+
+    total = numbered(0).astype(full)
+    for k in range(1, shards_n):
+        total = total + flip(numbered(k), "shard", k, shards_n).astype(full)
+    total = turn_sum(total.astype(low).reshape(ctx_n, rows_d, part), ctx_n, ctx).astype(low)
+    pieces4 = jnp.stack([total] + [flip(total, "shard", k, shards_n) for k in range(1, shards_n)])
+    d_q, d_k, d_v, d_w_out = [
+        lax.dynamic_index_in_dim(pieces4, m ^ shard, 0, keepdims=False).astype(full) for m in range(4)
+    ]
+    d_w_qkv = jnp.stack([d_q, d_k, d_v], axis=1)
+
+    tiny = jnp.concatenate([d_router, d_gain_a[None], d_gain_f[None], d_const], axis=0)
+    tiny = tiny + swap(tiny)
+    for axis, size in (("shard", shards_n), ("ctx", ctx_n)):
+        bit = 1
+        while bit < size:
+            tiny = tiny + flip(tiny, axis, bit, size)
+            bit *= 2
+    tiny = lax.dynamic_slice_in_dim(tiny, ctx * rows_d, rows_d, 1)
+
+    g_near = line_sum(dw_near.reshape(ctx_n, rows_d, 3 * units), ctx_n, ctx)
+    g_far = line_sum(dw_far.reshape(ctx_n, rows_d, 3 * units), ctx_n, ctx)
+    g_far = swap(g_far.astype(low)).astype(full)
+
+    def unpacked(x):
+        return x.reshape(rows_d, pieces, 3, PIECE).transpose(0, 2, 1, 3).reshape(rows_d, 3, units)
+
+    both = jnp.stack([unpacked(g_near), unpacked(g_far)], axis=1)
+    both = jnp.where(tp == 0, both, both[:, ::-1])
+    return (
+        both_trees(mixed_out, swap(mixed_out)),
+        both_trees(d_tokens, swap(d_tokens)),
+        both_trees(d_logits, swap(d_logits)),
+        d_w_qkv,
+        d_w_out,
+        tiny[:all_experts].T,
+        tiny[all_experts],
+        tiny[all_experts + 1],
+        tiny[all_experts + 2 :].T,
+        both[:, :, :2],
+        both[:, :, 2],
+    )
+
+
+def program(tokens, gate_res, cotangent, parents, expert_ids, priority, w_qkv, *weights):
+    trees, rows, width = tokens.shape
+    ctx_n = lax.axis_size("ctx")
+    seg = rows * ctx_n // parents.shape[1]
+    fits = (
+        ctx_n == 4
+        and lax.axis_size("shard") == 4
+        and lax.axis_size("tp") == 2
+        and trees == 2
+        and seg == 128
+        and rows % seg == 0
+        and 2 * rows < KEY_SEGS * seg <= 3 * rows
+        and weights[-1].shape[1] == 2
+    )
+    chosen = by_core if fits else shards
+    return chosen(tokens, gate_res, cotangent, parents, expert_ids, priority, w_qkv, *weights)
+
+
 def solution(mesh):
     return jax.shard_map(
-        shards,
+        program,
         mesh=mesh,
         in_specs=(
             P("shard", "ctx", None),

time: 1630 us -> 810 us (0.50)
  waiting for transfers between devices: 734 us -> 180 us
  matrix products: 469 us -> 47 us
  starting transfers between devices: 19.6 us -> 234 us
  Pallas kernels: 0 us -> 116 us
  blocking collectives: 86.2 us -> 0 us
  local copies, waits for them, and re-layouts: 146 us -> 97.1 us
  loops' own time: 31 us -> 0 us
    dot_general x78 -> x19, matrix products: 469 us -> 47 us  [the longest x16 45.1 us: mm(): return lax.dot_general(a, b, dims, preferred_element_type=jnp.float32)]
    unnamed x18 -> x0, waiting for transfers between devices: 350 us -> none
    ppermute x0 -> x84, starting transfers between devices: none -> 234 us  [the longest x6 133 us: line_sum(): up = lax.ppermute(high, 'ctx', [(i, i + 1) for i in range(0, t)])]
    ppermute x0 -> x84, waiting for transfers between devices: none -> 180 us  [the longest x41 96.1 us: flip(): return lax.ppermute(x, axis, [(i, i ^ bit) for i in range(size)])]
    all_gather x5 -> x0, waiting for transfers between devices: 169 us -> none  [the longest x1 53.5 us: shards(): lax.all_gather(k_low.reshape(tree_count, rows, local_width), 'ctx', axis=...]
    pallas_call x0 -> x4, Pallas kernels: none -> 116 us  [the longest x2 45.3 us: expert_pass(): pl.pallas_call(expert_kernel, grid=(pieces,), in_specs=[whole, turned, wh...]
    reduce_scatter x3 -> x0, waiting for transfers between devices: 115 us -> none  [the longest x1 83.6 us: shards(): lax.psum_scatter(key_terms.astype(jnp.bfloat16), 'ctx', scatter_dimension...]
    psum x4 -> x0, waiting for transfers between devices: 88.2 us -> none  [the longest x1 43.9 us: shards(): lax.psum(summed_grads[0].astype(jnp.bfloat16), 'shard').astype(jnp.float32)]
  transfers between devices with their start and end apart: 19 -> 84, of which waited for: 13 -> 24; matrix products, arithmetic and copies ran while one was open for 22% -> 30% of each run, Pallas kernels for 0% -> 9%
where the time goes in v1:
time: 810 us; the launch traced here: 802 us
  starting transfers between devices  234 us (29%)
  waiting for transfers between devices  180 us (22%)
  other arithmetic  125 us (15%)
  Pallas kernels  116 us (14%)
  local copies, waits for them, and re-layouts  97.1 us (12%)
  matrix products  47 us (6%)
    ppermute x6, starting transfers between devices, line_sum(): up = lax.ppermute(high, 'ctx', [(i, i + 1) for i in range(0, t)])  133 us
    ppermute x41, waiting for transfers between devices, flip(): return lax.ppermute(x, axis, [(i, i ^ bit) for i in range(size)])  96.1 us
    ppermute x6, waiting for transfers between devices, line_gather(): lax.ppermute(before[-1], 'ctx', [(i, i - 1) for i in range(1, size - t +...  51 us
    pallas_call x2, Pallas kernels, expert_pass(): pl.pallas_call(expert_kernel, grid=(pieces,), in_specs=[whole, turned, wh...  45.3 us
    dot_general x16, matrix products, mm(): return lax.dot_general(a, b, dims, preferred_element_type=jnp.float32)  45.1 us
    pallas_call x1, Pallas kernels, attend_back(): pl.pallas_call(functools.partial(attend_back_kernel, own, seg, HEAD_DIM),...  41.1 us
    ppermute x41, starting transfers between devices, flip(): return lax.ppermute(x, axis, [(i, i ^ bit) for i in range(size)])  37.2 us
    pallas_call x1, Pallas kernels, attend(): pl.pallas_call(functools.partial(attend_kernel, own, seg, HEAD_DIM), grid...  29.9 us
  transfers between devices with their start and end apart: 84, of which 24 were waited for; matrix products, arithmetic and copies ran while one was open for 30% of the time, Pallas kernels for 9%

profile of v1, /device:TPU:0, one launch (start us, length us, event | category | flops | bytes accessed | tf_op | source)
XLA Modules:
  0.0 802.5 jit_solution(13879107879505302882)
XLA Ops:
  71.6 10.7 %collective-permute-done.1 = bf16[384,768]{1,0:T(8,128)(2,1)S(1)} collective-permute-done((bf16[384,768]{1,0:T(8,128)(2,1)S(1)}, bf16[384,768]{1,0:T(8,128)(2,1)S(1)}, u32[]{:S(2)}, u32[]{:S(2)}) %collective-permute-start.1) | collective-permute-done | bytes 589856 | tf_op jit(solution)/shard_map/ppermute | solution.py:700
  91.5 6.2 collective-permute-done.13
  110.4 6.8 collective-permute-done.33
  117.2 7.9 collective-permute-start.26
  131.8 10.1 %convert_multiply_fusion = (f32[2176,768]{1,0:T(8,128)}, bf16[2176,768]{1,0:T(8,128)(2,1)S(1)}) fusion(f32[2176]{0:T(1024)S(1)} %add_rsqrt_fusion, bf16[256,768]{1,0:T(8,128)(2,1)S(1)} %get-tuple-element.164, bf16[640,768]{1,0:T(8,128)(2,1)S(1)} %select_select_fusion, bf16[640,768]{1,0:T(8,128)(2,1)S(1)} %get-tuple-element.110, ...), kind=kLoop, calls=%fused_computation.5 | loop fusion | flops 18382848 | bytes 13381120 | tf_op jit(solution)/shard_map/mul | solution.py:760
  143.6 5.9 convolution_convert_fusion.k_ref.v_ref
  149.4 29.9 %attend.1 = (bf16[640,768]{1,0:T(8,128)(2,1)S(1)}, f32[6,8,256]{2,1,0:T(8,128)S(1)}) custom-call(s32[5,3]{1,0:T(8,128)S(1)} %pad_add_fusion.info, bf16[640,768]{1,0:T(8,128)(2,1)S(1)} %convolution_convert_fusion.6.q_ref, bf16[2176,1536]{1,0:T(8,128)(2,1)S(1)} %convolution_convert_fusion.k_ref.v_ref, bf16[2176,1536]{1,0:T(8,128)(2,1)S(1)} %convolution_convert_fusion.k_ref.v_ref), custom_call_target="tpu_custom_call" | custom-call | flops 2516582400 | bytes 8388608 | tf_op jit(solution)/shard_map/attend/pallas_call | solution.py:508
  203.7 5.8 collective-permute-done.22
  211.4 6.8 collective-permute-done.23
  237.9 24.0 %collective-permute-done.35 = bf16[192,3072]{1,0:T(8,128)(2,1)} collective-permute-done((bf16[192,3072]{1,0:T(8,128)(2,1)}, bf16[192,3072]{1,0:T(8,128)(2,1)}, u32[]{:S(2)}, u32[]{:S(2)}) %collective-permute-start.35) | collective-permute-done | bytes 1179680 | tf_op jit(solution)/shard_map/ppermute | solution.py:629
  285.1 17.8 %collective-permute-done.29 = bf16[192,3072]{1,0:T(8,128)(2,1)} collective-permute-done((bf16[192,3072]{1,0:T(8,128)(2,1)}, bf16[192,3072]{1,0:T(8,128)(2,1)}, u32[]{:S(2)}, u32[]{:S(2)}) %collective-permute-start.29) | collective-permute-done | bytes 1179680 | tf_op jit(solution)/shard_map/ppermute | solution.py:629
  314.1 22.7 %expert_pass.2 = (f32[896,768]{1,0:T(8,128)}, f32[896,768]{1,0:T(8,128)}, bf16[768,3072]{1,0:T(8,128)(2,1)}) custom-call(bf16[896,768]{1,0:T(8,128)(2,1)} %copy.131.x_ref, bf16[768,896]{1,0:T(8,128)(2,1)} %fusion.150.xt_ref, bf16[896,768]{1,0:T(8,128)(2,1)} %copy.132.d_ref, bf16[768,896]{1,0:T(8,128)(2,1)} %fusion.148.dt_ref, ...), custom_call_target="tpu_custom_call" | custom-call | flops 12683575296 | bytes 31457280 | tf_op jit(solution)/shard_map/expert_pass/pallas_call | solution.py:603
  336.8 22.5 %expert_pass.3 = (f32[896,768]{1,0:T(8,128)}, f32[896,768]{1,0:T(8,128)}, bf16[768,3072]{1,0:T(8,128)(2,1)}) custom-call(bf16[896,768]{1,0:T(8,128)(2,1)} %copy.131.x_ref, bf16[768,896]{1,0:T(8,128)(2,1)} %fusion.150.xt_ref, bf16[896,768]{1,0:T(8,128)(2,1)} %copy.132.d_ref, bf16[768,896]{1,0:T(8,128)(2,1)} %fusion.148.dt_ref, bf16[768,3072]{1,0:T(8,128)(2,1)} %bitcast.282, ...), custom_call_target="tpu_custom_call" | custom-call | flops 12683575296 | bytes 31457280 | tf_op jit(solution)/shard_map/expert_pass/pallas_call | solution.py:603
  363.1 19.8 %collective-permute-start.80 = (bf16[192,3072]{1,0:T(8,128)(2,1)}, bf16[192,3072]{1,0:T(8,128)(2,1)}, u32[]{:S(2)}, u32[]{:S(2)}) collective-permute-start(bf16[192,3072]{1,0:T(8,128)(2,1)} %get-tuple-element.121), channel_id=1, source_target_pairs={{0,2},{1,3},{8,10},{9,11},{16,18},{17,19},{24,26},{25,27}} | collective-permute-start | bytes 3538952 | tf_op jit(solution)/shard_map/ppermute | solution.py:661
  390.1 6.1 collective-permute-done.38
  397.5 5.9 collective-permute-done.39
  443.6 41.1 %attend_back.1 = (bf16[640,768]{1,0:T(8,128)(2,1)S(1)}, bf16[2176,768]{1,0:T(8,128)(2,1)S(1)}, bf16[2176,768]{1,0:T(8,128)(2,1)S(1)}) custom-call(s32[5,3]{1,0:T(8,128)S(1)} %pad_add_fusion.info, bf16[640,768]{1,0:T(8,128)(2,1)S(1)} %convolution_convert_fusion.6.q_ref, bf16[2176,1536]{1,0:T(8,128)(2,1)} %copy-done.2, bf16[2176,1536]{1,0:T(8,128)(2,1)} %copy-done.2, ...), custom_call_target="tpu_custom_call" | custom-call | flops 6291456000 | bytes 16777216 | tf_op jit(solution)/shard_map/attend_back/pallas_call | solution.py:541
  520.7 84.1 %collective-permute-start.81 = (bf16[192,3072]{1,0:T(8,128)(2,1)}, bf16[192,3072]{1,0:T(8,128)(2,1)S(1)}, u32[]{:S(2)}, u32[]{:S(2)}) collective-permute-start(bf16[192,3072]{1,0:T(8,128)(2,1)} %get-tuple-element.119), channel_id=1, source_target_pairs={{0,2},{2,4},{1,3},{3,5},{8,10},{10,12},{9,11},{11,13},{16,18},{18,... | collective-permute-start | bytes 3538952 | tf_op jit(solution)/shard_map/ppermute | solution.py:661
  609.6 10.1 %collective-permute-start.75 = (bf16[192,3072]{1,0:T(8,128)(2,1)}, bf16[192,3072]{1,0:T(8,128)(2,1)}, u32[]{:S(2)}, u32[]{:S(2)}) collective-permute-start(bf16[192,3072]{1,0:T(8,128)(2,1)} %get-tuple-element.123), channel_id=1, source_target_pairs={{0,2},{2,4},{1,3},{3,5},{8,10},{10,12},{9,11},{11,13},{16,18},{18,... | collective-permute-start | bytes 3538952 | tf_op jit(solution)/shard_map/ppermute | solution.py:661
  635.7 12.0 %collective-permute-done.50 = bf16[640,768]{1,0:T(8,128)(2,1)} collective-permute-done((bf16[640,768]{1,0:T(8,128)(2,1)}, bf16[640,768]{1,0:T(8,128)(2,1)}, u32[]{:S(2)}, u32[]{:S(2)}) %collective-permute-start.50) | collective-permute-done | bytes 983072 | tf_op jit(solution)/shard_map/ppermute | solution.py:869
  661.6 15.1 %collective-permute-start.82 = (bf16[192,3072]{1,0:T(8,128)(2,1)S(1)}, bf16[192,3072]{1,0:T(8,128)(2,1)S(1)}, u32[]{:S(2)}, u32[]{:S(2)}) collective-permute-start(bf16[192,3072]{1,0:T(8,128)(2,1)S(1)} %copy-done.36), channel_id=1, source_target_pairs={{0,2},{2,4},{4,6},{1,3},{3,5},{5,7},{8,10},{10,12},{12,14},{9,11},... | collective-permute-start | bytes 3538952 | tf_op jit(solution)/shard_map/ppermute | solution.py:661
  683.1 20.9 %collective-permute-done.69 = f32[16,768]{1,0:T(8,128)S(1)} collective-permute-done((f32[16,768]{1,0:T(8,128)S(1)}, f32[16,768]{1,0:T(8,128)S(1)}, u32[]{:S(2)}, u32[]{:S(2)}) %collective-permute-start.69) | collective-permute-done | bytes 49184 | tf_op jit(solution)/shard_map/ppermute | solution.py:622
  715.5 23.4 %collective-permute-done.70 = f32[16,768]{1,0:T(8,128)S(1)} collective-permute-done((f32[16,768]{1,0:T(8,128)S(1)}, f32[16,768]{1,0:T(8,128)S(1)}, u32[]{:S(2)}, u32[]{:S(2)}) %collective-permute-start.70) | collective-permute-done | bytes 49184 | tf_op jit(solution)/shard_map/ppermute | solution.py:622
  756.7 7.2 collective-permute-done.76
  (497 shorter events, 377.2 us)
Async XLA Ops:
  2.7 51.1 %collective-permute-start.4 = (bf16[16,192]{1,0:T(8,128)(2,1)S(1)}, bf16[16,192]{1,0:T(8,128)(2,1)}, u32[]{:S(2)}, u32[]{:S(2)}) collective-permute-start(bf16[16,192]{1,0:T(8,128)(2,1)S(1)} %pad_maximum_fusion.12), channel_id=1, source_target_pairs={{0,2},{2,4},{4,6},{6,0},{1,3},{3,5},{5,7},{7,1},{8,10},{10,12},{12... | collective-permute-start | bytes 18440 | tf_op jit(solution)/shard_map/ppermute | solution.py:641
  5.8 51.4 %collective-permute-start.5 = (bf16[16,192]{1,0:T(8,128)(2,1)S(1)}, bf16[16,192]{1,0:T(8,128)(2,1)}, u32[]{:S(2)}, u32[]{:S(2)}) collective-permute-start(bf16[16,192]{1,0:T(8,128)(2,1)S(1)} %pad_maximum_fusion.12), channel_id=1, source_target_pairs={{0,4},{2,6},{4,0},{6,2},{1,5},{3,7},{5,1},{7,3},{8,12},{10,14},{12... | collective-permute-start | bytes 18440 | tf_op jit(solution)/shard_map/ppermute | solution.py:641
  8.4 49.7 %collective-permute-start.6 = (bf16[16,192]{1,0:T(8,128)(2,1)S(1)}, bf16[16,192]{1,0:T(8,128)(2,1)}, u32[]{:S(2)}, u32[]{:S(2)}) collective-permute-start(bf16[16,192]{1,0:T(8,128)(2,1)S(1)} %pad_maximum_fusion.12), channel_id=1, source_target_pairs={{0,6},{2,0},{4,2},{6,4},{1,7},{3,1},{5,3},{7,5},{8,14},{10,8},{12,... | collective-permute-start | bytes 18440 | tf_op jit(solution)/shard_map/ppermute | solution.py:641
  12.6 49.0 %collective-permute-start.7 = (bf16[192,384]{1,0:T(8,128)(2,1)}, bf16[192,384]{1,0:T(8,128)(2,1)S(1)}, u32[]{:S(2)}, u32[]{:S(2)}) collective-permute-start(bf16[192,384]{1,0:T(8,128)(2,1)} %bitcast.16), channel_id=1, source_target_pairs={{0,2},{2,4},{4,6},{6,0},{1,3},{3,5},{5,7},{7,1},{8,10},{10,12},{12... | collective-permute-start | bytes 442376 | tf_op jit(solution)/shard_map/ppermute | solution.py:641
  13.2 53.0 %collective-permute-start.8 = (bf16[192,384]{1,0:T(8,128)(2,1)}, bf16[192,384]{1,0:T(8,128)(2,1)S(1)}, u32[]{:S(2)}, u32[]{:S(2)}) collective-permute-start(bf16[192,384]{1,0:T(8,128)(2,1)} %bitcast.16), channel_id=1, source_target_pairs={{0,4},{2,6},{4,0},{6,2},{1,5},{3,7},{5,1},{7,3},{8,12},{10,14},{12... | collective-permute-start | bytes 442376 | tf_op jit(solution)/shard_map/ppermute | solution.py:641
  101.5 95.9 %collective-permute-start.32 = (bf16[192,3072]{1,0:T(8,128)(2,1)}, bf16[192,3072]{1,0:T(8,128)(2,1)}, u32[]{:S(2)}, u32[]{:S(2)}) collective-permute-start(bf16[192,3072]{1,0:T(8,128)(2,1)} %reshape.372), channel_id=1, source_target_pairs={{0,2},{2,4},{4,6},{1,3},{3,5},{5,7},{8,10},{10,12},{12,14},{9,11},... | collective-permute-start | bytes 3538952 | tf_op jit(solution)/shard_map/ppermute | solution.py:628
  107.9 90.5 %collective-permute-start.27 = (bf16[192,3072]{1,0:T(8,128)(2,1)}, bf16[192,3072]{1,0:T(8,128)(2,1)}, u32[]{:S(2)}, u32[]{:S(2)}) collective-permute-start(bf16[192,3072]{1,0:T(8,128)(2,1)} %collective-permute-done.25), channel_id=1, source_target_pairs={{2,0},{4,2},{6,4},{3,1},{5,3},{7,5},{10,8},{12,10},{14,12},{11,9},... | collective-permute-start | bytes 3538952 | tf_op jit(solution)/shard_map/ppermute | solution.py:629
  117.2 81.7 %collective-permute-start.26 = (bf16[192,3072]{1,0:T(8,128)(2,1)}, bf16[192,3072]{1,0:T(8,128)(2,1)}, u32[]{:S(2)}, u32[]{:S(2)}) collective-permute-start(bf16[192,3072]{1,0:T(8,128)(2,1)} %collective-permute-done.25), channel_id=1, source_target_pairs={{0,2},{2,4},{4,6},{1,3},{3,5},{5,7},{8,10},{10,12},{12,14},{9,11},... | collective-permute-start | bytes 3538952 | tf_op jit(solution)/shard_map/ppermute | solution.py:628
  125.1 77.3 %collective-permute-start.34 = (bf16[192,3072]{1,0:T(8,128)(2,1)}, bf16[192,3072]{1,0:T(8,128)(2,1)}, u32[]{:S(2)}, u32[]{:S(2)}) collective-permute-start(bf16[192,3072]{1,0:T(8,128)(2,1)} %collective-permute-done.33), channel_id=1, source_target_pairs={{2,0},{4,2},{3,1},{5,3},{10,8},{12,10},{11,9},{13,11},{18,16},{20,... | collective-permute-start | bytes 3538952 | tf_op jit(solution)/shard_map/ppermute | solution.py:629
  209.5 52.4 %collective-permute-start.35 = (bf16[192,3072]{1,0:T(8,128)(2,1)}, bf16[192,3072]{1,0:T(8,128)(2,1)}, u32[]{:S(2)}, u32[]{:S(2)}) collective-permute-start(bf16[192,3072]{1,0:T(8,128)(2,1)} %collective-permute-done.34), channel_id=1, source_target_pairs={{2,0},{3,1},{10,8},{11,9},{18,16},{19,17},{26,24},{27,25}} | collective-permute-start | bytes 3538952 | tf_op jit(solution)/shard_map/ppermute | solution.py:629
  218.2 47.7 %collective-permute-start.36 = (bf16[192,3072]{1,0:T(8,128)(2,1)}, bf16[192,3072]{1,0:T(8,128)(2,1)}, u32[]{:S(2)}, u32[]{:S(2)}) collective-permute-start(bf16[192,3072]{1,0:T(8,128)(2,1)} %collective-permute-done.32), channel_id=1, source_target_pairs={{2,4},{4,6},{3,5},{5,7},{10,12},{12,14},{11,13},{13,15},{18,20},{2... | collective-permute-start | bytes 3538952 | tf_op jit(solution)/shard_map/ppermute | solution.py:628
  219.9 49.0 %collective-permute-start.30 = (bf16[192,3072]{1,0:T(8,128)(2,1)}, bf16[192,3072]{1,0:T(8,128)(2,1)}, u32[]{:S(2)}, u32[]{:S(2)}) collective-permute-start(bf16[192,3072]{1,0:T(8,128)(2,1)} %collective-permute-done.26), channel_id=1, source_target_pairs={{2,4},{4,6},{3,5},{5,7},{10,12},{12,14},{11,13},{13,15},{18,20},{2... | collective-permute-start | bytes 3538952 | tf_op jit(solution)/shard_map/ppermute | solution.py:628
  362.3 65.0 %collective-permute-start.77 = (bf16[192,3072]{1,0:T(8,128)(2,1)S(1)}, bf16[192,3072]{1,0:T(8,128)(2,1)S(1)}, u32[]{:S(2)}, u32[]{:S(2)}) collective-permute-start(bf16[192,3072]{1,0:T(8,128)(2,1)S(1)} %get-tuple-element.120), channel_id=1, source_target_pairs={{6,4},{7,5},{14,12},{15,13},{22,20},{23,21},{30,28},{31,29}} | collective-permute-start | bytes 3538952 | tf_op jit(solution)/shard_map/ppermute | solution.py:660
  363.1 151.5 %collective-permute-start.80 = (bf16[192,3072]{1,0:T(8,128)(2,1)}, bf16[192,3072]{1,0:T(8,128)(2,1)}, u32[]{:S(2)}, u32[]{:S(2)}) collective-permute-start(bf16[192,3072]{1,0:T(8,128)(2,1)} %get-tuple-element.121), channel_id=1, source_target_pairs={{0,2},{1,3},{8,10},{9,11},{16,18},{17,19},{24,26},{25,27}} | collective-permute-start | bytes 3538952 | tf_op jit(solution)/shard_map/ppermute | solution.py:661
  417.2 103.0 %collective-permute-start.74 = (bf16[192,3072]{1,0:T(8,128)(2,1)}, bf16[192,3072]{1,0:T(8,128)(2,1)}, u32[]{:S(2)}, u32[]{:S(2)}) collective-permute-start(bf16[192,3072]{1,0:T(8,128)(2,1)} %get-tuple-element.125), channel_id=1, source_target_pairs={{0,2},{1,3},{8,10},{9,11},{16,18},{17,19},{24,26},{25,27}} | collective-permute-start | bytes 3538952 | tf_op jit(solution)/shard_map/ppermute | solution.py:661
  430.5 84.2 %collective-permute-start.78 = (bf16[192,3072]{1,0:T(8,128)(2,1)}, bf16[192,3072]{1,0:T(8,128)(2,1)}, u32[]{:S(2)}, u32[]{:S(2)}) collective-permute-start(bf16[192,3072]{1,0:T(8,128)(2,1)} %fusion.10), channel_id=1, source_target_pairs={{4,2},{6,4},{5,3},{7,5},{12,10},{14,12},{13,11},{15,13},{20,18},{2... | collective-permute-start | bytes 3538952 | tf_op jit(solution)/shard_map/ppermute | solution.py:660
  511.3 97.0 %collective-permute-start.51 = (bf16[640,768]{1,0:T(8,128)(2,1)S(1)}, bf16[640,768]{1,0:T(8,128)(2,1)}, u32[]{:S(2)}, u32[]{:S(2)}) collective-permute-start(bf16[640,768]{1,0:T(8,128)(2,1)S(1)} %copy-done.41), channel_id=1, source_target_pairs={{6,4},{7,5},{14,12},{15,13},{22,20},{23,21},{30,28},{31,29}} | collective-permute-start | bytes 2949128 | tf_op jit(solution)/shard_map/ppermute | solution.py:869
  514.6 108.7 %collective-permute-start.42 = (f32[640,768]{1,0:T(8,128)S(1)}, f32[640,768]{1,0:T(8,128)}, u32[]{:S(2)}, u32[]{:S(2)}) collective-permute-start(f32[640,768]{1,0:T(8,128)S(1)} %copy-done.14), channel_id=1, source_target_pairs={{0,1},{1,0},{2,3},{3,2},{4,5},{5,4},{6,7},{7,6},{8,9},{9,8},{10,11... | collective-permute-start | bytes 5898248 | tf_op jit(solution)/shard_map/ppermute | solution.py:622
  514.7 94.8 %collective-permute-start.49 = (bf16[640,768]{1,0:T(8,128)(2,1)S(1)}, bf16[640,768]{1,0:T(8,128)(2,1)}, u32[]{:S(2)}, u32[]{:S(2)}) collective-permute-start(bf16[640,768]{1,0:T(8,128)(2,1)S(1)} %fusion.71), channel_id=1, source_target_pairs={{4,2},{5,3},{12,10},{13,11},{20,18},{21,19},{28,26},{29,27}} | collective-permute-start | bytes 2949128 | tf_op jit(solution)/shard_map/ppermute | solution.py:869
  520.2 110.6 %collective-permute-start.56 = (bf16[4,768,384]{2,1,0:T(8,128)(2,1)}, bf16[4,768,384]{2,1,0:T(8,128)(2,1)}, u32[]{:S(2)}, u32[]{:S(2)}) collective-permute-start(bf16[4,768,384]{2,1,0:T(8,128)(2,1)} %slice.321), channel_id=1, source_target_pairs={{0,1},{1,0},{2,3},{3,2},{4,5},{5,4},{6,7},{7,6},{8,9},{9,8},{10,11... | collective-permute-start | bytes 7077896 | tf_op jit(solution)/shard_map/ppermute | solution.py:622
  520.7 107.9 %collective-permute-start.81 = (bf16[192,3072]{1,0:T(8,128)(2,1)}, bf16[192,3072]{1,0:T(8,128)(2,1)S(1)}, u32[]{:S(2)}, u32[]{:S(2)}) collective-permute-start(bf16[192,3072]{1,0:T(8,128)(2,1)} %get-tuple-element.119), channel_id=1, source_target_pairs={{0,2},{2,4},{1,3},{3,5},{8,10},{10,12},{9,11},{11,13},{16,18},{18,... | collective-permute-start | bytes 3538952 | tf_op jit(solution)/shard_map/ppermute | solution.py:661
  608.3 143.4 %collective-permute-start.79 = (bf16[192,3072]{1,0:T(8,128)(2,1)}, bf16[192,3072]{1,0:T(8,128)(2,1)}, u32[]{:S(2)}, u32[]{:S(2)}) collective-permute-start(bf16[192,3072]{1,0:T(8,128)(2,1)} %get-tuple-element.118), channel_id=1, source_target_pairs={{2,0},{4,2},{6,4},{3,1},{5,3},{7,5},{10,8},{12,10},{14,12},{11,9},... | collective-permute-start | bytes 3538952 | tf_op jit(solution)/shard_map/ppermute | solution.py:660
  661.6 90.1 %collective-permute-start.82 = (bf16[192,3072]{1,0:T(8,128)(2,1)S(1)}, bf16[192,3072]{1,0:T(8,128)(2,1)S(1)}, u32[]{:S(2)}, u32[]{:S(2)}) collective-permute-start(bf16[192,3072]{1,0:T(8,128)(2,1)S(1)} %copy-done.36), channel_id=1, source_target_pairs={{0,2},{2,4},{4,6},{1,3},{3,5},{5,7},{8,10},{10,12},{12,14},{9,11},... | collective-permute-start | bytes 3538952 | tf_op jit(solution)/shard_map/ppermute | solution.py:661
  707.2 49.5 %collective-permute-start.73 = (bf16[192,3072]{1,0:T(8,128)(2,1)S(1)}, bf16[192,3072]{1,0:T(8,128)(2,1)S(1)}, u32[]{:S(2)}, u32[]{:S(2)}) collective-permute-start(bf16[192,3072]{1,0:T(8,128)(2,1)S(1)} %copy-done.37), channel_id=1, source_target_pairs={{2,0},{4,2},{6,4},{3,1},{5,3},{7,5},{10,8},{12,10},{14,12},{11,9},... | collective-permute-start | bytes 3538952 | tf_op jit(solution)/shard_map/ppermute | solution.py:660
  (132 other events, 1953.5 us)

commit v2 on v1

--- a/solution.py
+++ b/solution.py
@@ -376,6 +376,7 @@
 TRUNK = 8
 KEY_SEGS = 12
 PIECE = 256
+SENT = (0, 2, 1, 3)
 
 
 def mm(a, b, dims=NN):
@@ -398,7 +399,8 @@
     return row <= jnp.where(col >= seg, col - seg, col)
 
 
-def attend_kernel(own, seg, half, info, q_ref, k_ref, v_ref, o_ref, lse_ref, s_ref, p_ref):
+def attend_kernel(own, seg, half, more, info, q_ref, k_ref, v_ref, *rest):
+    o_ref, lse_ref, s_ref, p_ref = rest[2 * more :]
     trunk = TRUNK * seg
     allowed = causal(seg)
     v_trunk = v_ref[own : own + trunk, :].T
@@ -437,8 +439,9 @@
 
 
 def attend_back_kernel(
-    own, seg, half, info, q_ref, k_ref, v_ref, o_ref, do_ref, lse_ref, dq_ref, dk_ref, dv_ref, ak, av
+    own, seg, half, more, info, q_ref, k_ref, v_ref, o_ref, do_ref, lse_ref, *rest
 ):
+    dq_ref, dk_ref, dv_ref, ak, av = rest[3 * more :]
     trunk = TRUNK * seg
     allowed = causal(seg)
     low = jnp.bfloat16
@@ -499,139 +502,252 @@
     dv_ref[...] = av[...].astype(low)
 
 
-def attend(info, q, kv, seg):
+def attend(info, q, kv, seg, begin, count, prev=()):
     own, width = q.shape
     total = kv.shape[0]
     pairs = width // 128
-    segs = own // seg
-    lane = pl.BlockSpec((own, 128), lambda h: (0, h))
+    lane = pl.BlockSpec((own, 128), lambda h: (0, begin + h))
     return pl.pallas_call(
-        functools.partial(attend_kernel, own, seg, HEAD_DIM),
-        grid=(pairs,),
+        functools.partial(attend_kernel, own, seg, HEAD_DIM, len(prev) > 0),
+        grid=(count,),
         in_specs=[
             pl.BlockSpec(memory_space=pltpu.SMEM),
             lane,
-            pl.BlockSpec((total, 128), lambda h: (0, h)),
-            pl.BlockSpec((total, 128), lambda h: (0, pairs + h)),
-        ],
-        out_specs=[lane, pl.BlockSpec((None, 8, 2 * seg), lambda h: (h, 0, 0))],
+            pl.BlockSpec((total, 128), lambda h: (0, begin + h)),
+            pl.BlockSpec((total, 128), lambda h: (0, pairs + begin + h)),
+        ]
+        + [pl.BlockSpec(memory_space=pl.ANY)] * len(prev),
+        out_specs=[lane, pl.BlockSpec((None, 8, 2 * seg), lambda h: (begin + h, 0, 0))],
         out_shape=[
             jax.ShapeDtypeStruct((own, width), jnp.bfloat16),
             jax.ShapeDtypeStruct((pairs, 8, 2 * seg), jnp.float32),
         ],
+        input_output_aliases={4 + i: i for i in range(len(prev))},
         scratch_shapes=[
             pltpu.VMEM((TRUNK * seg, 2 * seg), jnp.float32),
             pltpu.VMEM((TRUNK * seg, 2 * seg), jnp.bfloat16),
         ],
         compiler_params=pltpu.CompilerParams(vmem_limit_bytes=32 << 20),
         cost_estimate=pl.CostEstimate(
-            flops=4 * segs * 10 * seg * seg * width, bytes_accessed=8 << 20, transcendentals=0
+            flops=count * 5 * 10**9, bytes_accessed=count << 20, transcendentals=0
         ),
         name="attend",
-    )(info, q, kv, kv)
-
-
-def attend_back(info, q, kv, o, do, lse, seg):
+    )(info, q, kv, kv, *prev)
+
+
+def attend_back(info, q, kv, o, do, lse, seg, begin, count, prev=()):
     own, width = q.shape
     total = kv.shape[0]
     pairs = width // 128
-    segs = own // seg
-    lane = pl.BlockSpec((own, 128), lambda h: (0, h))
-    keys = pl.BlockSpec((total, 128), lambda h: (0, h))
+    lane = pl.BlockSpec((own, 128), lambda h: (0, begin + h))
+    keys = pl.BlockSpec((total, 128), lambda h: (0, begin + h))
     return pl.pallas_call(
-        functools.partial(attend_back_kernel, own, seg, HEAD_DIM),
-        grid=(pairs,),
+        functools.partial(attend_back_kernel, own, seg, HEAD_DIM, len(prev) > 0),
+        grid=(count,),
         in_specs=[
             pl.BlockSpec(memory_space=pltpu.SMEM),
             lane,
             keys,
-            pl.BlockSpec((total, 128), lambda h: (0, pairs + h)),
+            pl.BlockSpec((total, 128), lambda h: (0, pairs + begin + h)),
             lane,
             lane,
-            pl.BlockSpec((None, 8, 2 * seg), lambda h: (h, 0, 0)),
-        ],
+            pl.BlockSpec((None, 8, 2 * seg), lambda h: (begin + h, 0, 0)),
+        ]
+        + [pl.BlockSpec(memory_space=pl.ANY)] * len(prev),
         out_specs=[lane, keys, keys],
         out_shape=[
             jax.ShapeDtypeStruct((own, width), jnp.bfloat16),
             jax.ShapeDtypeStruct((total, width), jnp.bfloat16),
             jax.ShapeDtypeStruct((total, width), jnp.bfloat16),
         ],
+        input_output_aliases={7 + i: i for i in range(len(prev))},
         scratch_shapes=[
             pltpu.VMEM((total, 128), jnp.float32),
             pltpu.VMEM((total, 128), jnp.float32),
         ],
         compiler_params=pltpu.CompilerParams(vmem_limit_bytes=40 << 20),
         cost_estimate=pl.CostEstimate(
-            flops=10 * segs * 10 * seg * seg * width, bytes_accessed=16 << 20, transcendentals=0
+            flops=count * 7 * 10**9, bytes_accessed=2 * count << 20, transcendentals=0
         ),
         name="attend_back",
-    )(info, q, kv, kv, o, do, lse)
-
-
-def expert_kernel(x_ref, xt_ref, d_ref, dt_ref, w_ref, o0_ref, s0_ref, o_ref, s_ref, dw_ref):
+    )(info, q, kv, kv, o, do, lse, *prev)
+
+
+def pin(x, *after):
+    return lax.optimization_barrier((x,) + after)[0]
+
+
+def expert_kernel(more, place, x_ref, g_ref, gate_ref, w0, w1, w2, w3, *rest):
     low = jnp.bfloat16
+    if more:
+        prev_ref, o_ref, o2_ref, s_ref, s2_ref, dot_ref, dw_ref, xt, dt, d_ref, oa, sa, wb, gb = rest
+    else:
+        o_ref, o2_ref, s_ref, s2_ref, dot_ref, dw_ref, xt, dt, d_ref, oa, sa, wb, gb = rest
+    part = w0.shape[1]
 
     @pl.when(pl.program_id(0) == 0)
     def start():
-        o_ref[...] = o0_ref[...]
-        s_ref[...] = s0_ref[...]
-
-    wg = w_ref[:, :PIECE]
-    wu = w_ref[:, PIECE : 2 * PIECE]
-    wd = w_ref[:, 2 * PIECE :]
-    u = mm(x_ref[...], wg)
-    up = mm(x_ref[...], wu)
+        xt[...] = x_ref[...].T
+        d_ref[...] = (g_ref[...].astype(jnp.float32) * gate_ref[...]).astype(low)
+        dt[...] = d_ref[...].T
+        oa[...] = jnp.zeros_like(oa)
+        sa[...] = jnp.zeros_like(sa)
+
+    def rows_of(r):
+        return pl.ds(pl.multiple_of((place[0] ^ r) * part, 64), part)
+
+    for r, w in enumerate((w0, w1, w2, w3)):
+        wb[:, rows_of(r), :] = w[...]
+    u = mm(x_ref[...], wb[0])
+    up = mm(x_ref[...], wb[1])
     sigma = 1.0 / (1.0 + jnp.exp(-u))
     silu = u * sigma
     hidden = (silu * up).astype(low)
-    o_ref[...] += mm(hidden, wd, NT)
-    dh = mm(d_ref[...], wd)
+    oa[...] += mm(hidden, wb[2], NT)
+    dh = mm(d_ref[...], wb[2])
     du = (dh * up * sigma * (1.0 + u * (1.0 - sigma))).astype(low)
     dup = (dh * silu).astype(low)
-    s_ref[...] += mm(du, wg, NT) + mm(dup, wu, NT)
-    dw_ref[:, :PIECE] = mm(xt_ref[...], du).astype(low)
-    dw_ref[:, PIECE : 2 * PIECE] = mm(xt_ref[...], dup).astype(low)
-    dw_ref[:, 2 * PIECE :] = mm(dt_ref[...], hidden).astype(low)
-
-
-def expert_pass(x, xt, d, dt, w, o0, s0):
+    sa[...] += mm(du, wb[0], NT) + mm(dup, wb[1], NT)
+    gb[0] = mm(xt[...], du).astype(low)
+    gb[1] = mm(xt[...], dup).astype(low)
+    gb[2] = mm(dt[...], hidden).astype(low)
+    for at, r in enumerate(SENT):
+        got = gb[:, rows_of(r), :]
+        if more:
+            got = (got.astype(jnp.float32) + prev_ref[at].astype(jnp.float32)).astype(low)
+        dw_ref[at] = got
+
+    @pl.when(pl.program_id(0) == pl.num_programs(0) - 1)
+    def finish():
+        dot_ref[...] = jnp.sum(g_ref[...].astype(jnp.float32) * oa[...], axis=1, keepdims=True)
+        wide = o_ref.shape[1]
+        here = pl.ds(pl.multiple_of(place[1] * wide, 128), wide)
+        there = pl.ds(pl.multiple_of((1 - place[1]) * wide, 128), wide)
+        o_ref[...] = oa[:, here].astype(low)
+        o2_ref[...] = oa[:, there].astype(low)
+        s_ref[...] = sa[:, here].astype(low)
+        s2_ref[...] = sa[:, there].astype(low)
+
+
+def expert_pass(place, x, g, gate, weights, prev):
     rows, width = x.shape
-    pieces = w.shape[1] // (3 * PIECE)
+    three, part, units = weights[0].shape
+    low = jnp.bfloat16
     whole = pl.BlockSpec((rows, width), lambda j: (0, 0))
-    turned = pl.BlockSpec((width, rows), lambda j: (0, 0))
-    strip = pl.BlockSpec((width, 3 * PIECE), lambda j: (0, j))
+    strip = pl.BlockSpec((three, part, PIECE), lambda j: (0, 0, j))
+    strips = pl.BlockSpec((4, three, part, PIECE), lambda j: (0, 0, 0, j))
+    column = pl.BlockSpec((rows, 1), lambda j: (0, 0))
+    half = pl.BlockSpec((rows, width // 2), lambda j: (0, 0))
+    more = prev is not None
     return pl.pallas_call(
-        expert_kernel,
-        grid=(pieces,),
-        in_specs=[whole, turned, whole, turned, strip, whole, whole],
-        out_specs=[whole, whole, strip],
+        functools.partial(expert_kernel, more),
+        grid=(units // PIECE,),
+        in_specs=[pl.BlockSpec(memory_space=pltpu.SMEM), whole, whole, column]
+        + [strip] * 4
+        + [strips] * more,
+        out_specs=[half] * 4 + [column, strips],
         out_shape=[
-            jax.ShapeDtypeStruct((rows, width), jnp.float32),
-            jax.ShapeDtypeStruct((rows, width), jnp.float32),
-            jax.ShapeDtypeStruct(w.shape, jnp.bfloat16),
+            *[jax.ShapeDtypeStruct((rows, width // 2), low)] * 4,
+            jax.ShapeDtypeStruct((rows, 1), jnp.float32),
+            jax.ShapeDtypeStruct((4, three, part, units), low),
         ],
-        compiler_params=pltpu.CompilerParams(vmem_limit_bytes=56 << 20),
+        scratch_shapes=[
+            pltpu.VMEM((width, rows), low),
+            pltpu.VMEM((width, rows), low),
+            pltpu.VMEM((rows, width), low),
+            pltpu.VMEM((rows, width), jnp.float32),
+            pltpu.VMEM((rows, width), jnp.float32),
+            pltpu.VMEM((three, width, PIECE), low),
+            pltpu.VMEM((three, width, PIECE), low),
+        ],
+        compiler_params=pltpu.CompilerParams(vmem_limit_bytes=60 << 20),
         cost_estimate=pl.CostEstimate(
-            flops=2 * 3 * rows * w.shape[0] * w.shape[1], bytes_accessed=30 << 20, transcendentals=0
+            flops=22 * 10**9, bytes_accessed=20 << 20, transcendentals=0
         ),
         name="expert_pass",
-    )(x, xt, d, dt, w, o0, s0)
+    )(place, x, g, gate, *weights, *([prev] if more else []))
+
+
+def spread_kernel(pieces, padded, capacity, gated, place_ref, rows_ref, *rest):
+    low = jnp.bfloat16
+    outs = rest[1:] if gated else rest
+    tokens = rows_ref.shape[0]
+    for p in range(pieces):
+        slot = lax.broadcasted_iota(jnp.int32, (padded, tokens), 0) + p * padded
+        hits = [slot == place_ref[c : c + 1, :] for c in range(2)]
+        out = mm(jnp.where(hits[0] | hits[1], 1.0, 0.0).astype(low), rows_ref[...]).astype(low)
+        if gated:
+            parts = sum(
+                mm(rest[0][c], jnp.where(hits[c], 1.0, 0.0).astype(low), NT) for c in range(2)
+            ).astype(low)
+            blank = jnp.zeros((parts.shape[0], out.shape[1] - padded), low)
+            parts = jnp.concatenate([parts, blank], axis=1)
+            row = lax.broadcasted_iota(jnp.int32, out.shape, 0)
+            for i in range(3):
+                out = jnp.where(row == capacity + i, parts[i : i + 1, :], out)
+        outs[p][...] = out
+
+
+def spread(place, rows, pieces, padded, capacity, parts=None):
+    shape = jax.ShapeDtypeStruct((padded, rows.shape[1]), jnp.bfloat16)
+    gated = parts is not None
+    return pl.pallas_call(
+        functools.partial(spread_kernel, pieces, padded, capacity, gated),
+        out_shape=[shape] * pieces,
+        compiler_params=pltpu.CompilerParams(vmem_limit_bytes=40 << 20),
+        cost_estimate=pl.CostEstimate(flops=4 * 10**9, bytes_accessed=2 << 20, transcendentals=0),
+        name="spread",
+    )(place, rows, *([parts] if gated else []))
+
+
+def gather_kernel(pieces, padded, capacity, dots, place_ref, *rest):
+    low = jnp.bfloat16
+    if dots:
+        ins, (out_ref, dot_ref) = rest[:pieces], rest[pieces:]
+    else:
+        gate_ref, ins, out_ref = rest[0], rest[1 : 1 + pieces], rest[1 + pieces]
+    tokens = place_ref.shape[0]
+    total = None
+    sums = [0.0, 0.0]
+    for p in range(pieces):
+        slot = lax.broadcasted_iota(jnp.int32, (tokens, padded), 1) + p * padded
+        hits = [slot == place_ref[:, c : c + 1] for c in range(2)]
+        if dots:
+            picks = [jnp.where(h, 1.0, 0.0).astype(low) for h in hits]
+            values = ins[p][capacity : capacity + 3, :padded]
+            values = jnp.concatenate([values, jnp.zeros((13, padded), low)], axis=0)
+            for c in range(2):
+                sums[c] = sums[c] + mm(picks[c], values, NT)
+            pick = picks[0] + picks[1]
+        else:
+            pick = jnp.where(hits[0], gate_ref[:, 0:1], jnp.where(hits[1], gate_ref[:, 1:2], 0.0))
+            pick = pick.astype(low)
+        part = mm(pick, ins[p][...])
+        total = part if total is None else total + part
+    out_ref[...] = total.astype(low)
+    if dots:
+        for c in range(2):
+            dot_ref[:, c : c + 1] = jnp.sum(sums[c], axis=1, keepdims=True)
+
+
+def gather(place, pieces, capacity, gate=None):
+    padded, width = pieces[0].shape
+    tokens = place.shape[0]
+    dots = gate is None
+    shapes = [jax.ShapeDtypeStruct((tokens, width), jnp.bfloat16)]
+    if dots:
+        shapes.append(jax.ShapeDtypeStruct((tokens, 2), jnp.float32))
+    return pl.pallas_call(
+        functools.partial(gather_kernel, len(pieces), padded, capacity, dots),
+        out_shape=shapes,
+        compiler_params=pltpu.CompilerParams(vmem_limit_bytes=40 << 20),
+        cost_estimate=pl.CostEstimate(flops=4 * 10**9, bytes_accessed=2 << 20, transcendentals=0),
+        name="gather",
+    )(place, *([] if dots else [gate]), *pieces)
 
 
 def flip(x, axis, bit, size):
     return lax.ppermute(x, axis, [(i, i ^ bit) for i in range(size)])
-
-
-def line_gather(x, size, position):
-    after, before = [x], [x]
-    for t in range(1, size):
-        after.append(lax.ppermute(after[-1], "ctx", [(i, i + 1) for i in range(t - 1, size - 1)]))
-        before.append(lax.ppermute(before[-1], "ctx", [(i, i - 1) for i in range(1, size - t + 1)]))
-    out = jnp.zeros((size,) + x.shape, x.dtype)
-    for k in range(size):
-        block = x if k == 0 else jnp.where(position >= k, after[k], before[size - k])
-        out = lax.dynamic_update_index_in_dim(out, block, (position - k) % size, 0)
-    return out
 
 
 def turn_gather(x, size, position):
@@ -643,25 +759,6 @@
     return out
 
 
-def line_sum(x, size, position):
-    def part(index):
-        index = jnp.clip(index, 0, size - 1)
-        return lax.dynamic_index_in_dim(x, index, 0, keepdims=False)
-
-    def add(a, b):
-        return (a.astype(jnp.float32) + b.astype(jnp.float32)).astype(x.dtype)
-
-    down = up = None
-    for t in range(1, size):
-        low = part(position - size + t)
-        high = part(position + size - t)
-        if t > 1:
-            low, high = add(low, down), add(high, up)
-        down = lax.ppermute(low, "ctx", [(i, i - 1) for i in range(size - t, size)])
-        up = lax.ppermute(high, "ctx", [(i, i + 1) for i in range(0, t)])
-    return part(position).astype(jnp.float32) + down.astype(jnp.float32) + up.astype(jnp.float32)
-
-
 def turn_sum(x, size, position):
     total = lax.dynamic_index_in_dim(x, position, 0, keepdims=False).astype(jnp.float32)
     for k in range(1, size):
@@ -669,6 +766,32 @@
         got = lax.ppermute(block, "ctx", [(i, (i + k) % size) for i in range(size)])
         total = total + got.astype(jnp.float32)
     return total
+
+
+def far(x, k, shards_n, ctx_n):
+    pairs = []
+    for s in range(shards_n):
+        for z in range(ctx_n):
+            pairs.append((s * ctx_n + z, (s ^ k) * ctx_n + (z ^ 2)))
+    return lax.ppermute(x, ("shard", "ctx"), pairs)
+
+
+def three_parts(x):
+    one = x.astype(jnp.bfloat16)
+    rest = x - one.astype(jnp.float32)
+    two = rest.astype(jnp.bfloat16)
+    return jnp.stack([one, two, (rest - two.astype(jnp.float32)).astype(jnp.bfloat16)], axis=-2)
+
+
+def with_rows(slots, values, at):
+    extra = three_parts(values)
+    after = slots.shape[-2] - at - extra.shape[-2]
+    pads = ((0, 0), (at, after), (0, slots.shape[-1] - extra.shape[-1]))
+    return slots + jnp.pad(extra, pads)
+
+
+def row_values(slots, at):
+    return jnp.sum(slots[:, at : at + 3, : slots.shape[1]].astype(jnp.float32), axis=1)
 
 
 def by_core(
@@ -680,6 +803,7 @@
     shards_n, ctx_n = lax.axis_size("shard"), lax.axis_size("ctx")
     trees, rows, width = tokens.shape
     rows_d = w_qkv.shape[0]
+    part = width // 2
     seg = rows * ctx_n // parents.shape[1]
     own_segs = rows // seg
     edge = KEY_SEGS * seg - 2 * rows
@@ -687,78 +811,95 @@
     def own_tree(x):
         return lax.dynamic_index_in_dim(x, tp, 0, keepdims=False)
 
+    def in_order(x, other, axis=0):
+        return jnp.concatenate([jnp.where(tp == 0, x, other), jnp.where(tp == 0, other, x)], axis=axis)
+
     def both_trees(x, other):
-        ordered = jnp.stack([x, other])
-        return jnp.where(tp == 0, ordered, ordered[::-1])
+        return in_order(x[None], other[None])
 
     def swap(x):
         return flip(x, "tp", 1, 2)
+
+    def plus(x, y):
+        return (x.astype(full) + y.astype(full)).astype(low)
+
+    def my_half(x, which):
+        return lax.dynamic_slice_in_dim(x, which * part, part, x.ndim - 1)
 
     x_own = own_tree(tokens)
     ends = [(i, i + 1) for i in range(ctx_n - 1)]
     near_head = lax.ppermute(x_own[:edge], "ctx", ends)
     near_tail = lax.ppermute(x_own[edge:], "ctx", ends[:-1])
     near = jnp.concatenate([near_head, near_tail], axis=0)
-    mid = lax.ppermute(near, "ctx", ends[1:])
-    far = lax.ppermute(mid, "ctx", ends[2:])
-
-    mine = jnp.stack([w_qkv[:, 0], w_qkv[:, 1], w_qkv[:, 2], w_out])
+
+    mine = jnp.stack([w_qkv[:, 0], w_qkv[:, 1], w_qkv[:, 2], pin(w_out, x_own)])
     matrix = turn_gather(lax.dynamic_index_in_dim(mine, shard, 0, keepdims=False), ctx_n, ctx)
     matrix = matrix.reshape(width, -1)
-    plane = [matrix] + [flip(matrix, "shard", k, shards_n) for k in range(1, shards_n)]
-    plane = [jnp.concatenate([m, swap(m)], axis=1) for m in plane]
-    plane = jnp.stack(plane)
-    weight_q, weight_k, weight_v, weight_o = [
-        lax.dynamic_index_in_dim(plane, m ^ shard, 0, keepdims=False) for m in range(4)
-    ]
-    weight_kv = jnp.concatenate([weight_k, weight_v], axis=1)
-
-    small = jnp.concatenate(
-        [w_router.T, attn_gain[None], ffn_gain[None], const_vec.T], axis=0
-    )
-    small = turn_gather(small, ctx_n, ctx).transpose(1, 0, 2).reshape(small.shape[0], width)
+
+    small = jnp.concatenate([w_router.T, attn_gain[None], ffn_gain[None], const_vec.T], axis=0)
+    small = turn_gather(pin(small, matrix), ctx_n, ctx).transpose(1, 0, 2).reshape(small.shape[0], width)
     all_experts = w_router.shape[1]
     router_t = small[:all_experts]
     gain_a = small[all_experts].astype(full)
     gain_f = small[all_experts + 1].astype(full)
     const_t = small[all_experts + 2 :].astype(full)
 
-    units = w_down.shape[2]
-    pieces = units // PIECE
-
-    def packed(e):
-        gu = lax.dynamic_index_in_dim(w_gate_up, e, 1, keepdims=False)
-        dn = lax.dynamic_index_in_dim(w_down, e, 1, keepdims=False)
-        three = jnp.concatenate([gu, dn[:, None]], axis=1).reshape(rows_d, 3, pieces, PIECE)
-        return three.transpose(0, 2, 1, 3).reshape(rows_d, 3 * units)
-
-    half_near = packed(tp)
-    half_far = swap(packed(1 - tp))
-    expert_near = line_gather(half_near, ctx_n, ctx).reshape(width, 3 * units)
-    expert_far = line_gather(half_far, ctx_n, ctx).reshape(width, 3 * units)
+    mid = lax.ppermute(pin(near, matrix), "ctx", ends[1:])
+    plane = [matrix] + [flip(matrix, "shard", k, shards_n) for k in range(1, shards_n)]
+    plane = jnp.stack(plane)
+    farther = lax.ppermute(pin(mid, plane, small), "ctx", ends[2:])
+    plane = jnp.concatenate([plane, swap(plane)], axis=2)
+    weight_q, weight_k, weight_v, weight_o = [
+        lax.dynamic_index_in_dim(plane, m ^ shard, 0, keepdims=False) for m in range(4)
+    ]
+    weight_kv = jnp.concatenate([weight_k, weight_v], axis=1)
+
+    held, gu, dn = lax.optimization_barrier((farther, w_gate_up, w_down))
+    lower = ctx < 2
+    first = jnp.stack([gu[:, 0, 0], gu[:, 0, 1], dn[:, 0]])
+    second_e = jnp.stack([gu[:, 1, 0], gu[:, 1, 1], dn[:, 1]])
+    rows_own = jnp.where(lower, first, second_e)
+    rows_two = flip(jnp.where(lower, second_e, first), "ctx", 2, ctx_n)
+    rows_one = flip(rows_own, "ctx", 1, ctx_n)
 
     capacity = trees * rows * 2 // all_experts
     experts = shards_n * w_gate_up.shape[1]
-    padded = -(-capacity // 16) * 16
-    ids_block = expert_ids.reshape(trees * rows, 2)
-    flat = ids_block.reshape(-1)
-    order = (2 * priority[0, 0][:, None] + jnp.arange(2, dtype=jnp.int32)[None, :]).reshape(-1)
+    padded = -(-(capacity + 3) // 16) * 16
+    count = experts * padded
+    held, ids_in, order_in = lax.optimization_barrier((near_head, expert_ids, priority))
+    flat = ids_in.reshape(-1)
+    order = (2 * order_in[0, 0][:, None] + jnp.arange(2, dtype=jnp.int32)[None, :]).reshape(-1)
     earlier = (flat[:, None] == flat[None, :]) & (order[None, :] < order[:, None])
     ranks = jnp.sum(earlier.astype(jnp.int32), axis=1)
-    kept = (flat < experts) & (ranks < capacity) & (flat % 2 == tp)
-    place = jnp.where(kept, ((flat // 2) ^ shard) * padded + ranks, -1).reshape(trees, rows, 2)
-    place = jnp.where(tp == 0, place, place[::-1]).reshape(trees * rows, 2).T
-    slot = jnp.arange(shards_n * padded, dtype=jnp.int32)
-    table = slot[None, :, None] == place[:, None, :]
-    routed = (table[0] | table[1]).astype(low)
-
-    block0 = jnp.where(ctx == 0, x_own, jnp.where(ctx == 1, near, jnp.where(ctx == 2, mid, far)))
+    kept = (flat < experts) & (ranks < capacity)
+    piece = ((flat % 2) ^ (ctx // 2)) * shards_n + ((flat // 2) ^ shard)
+    place = jnp.where(kept, piece * padded + ranks, -1).reshape(trees, rows, 2)
+    place = jnp.where(tp == 0, place, place[::-1]).reshape(trees * rows, 2)
+    place_t = place.T
+
+    g_own = own_tree(cotangent)
+    g_other = lax.dynamic_index_in_dim(cotangent, 1 - tp, 0, keepdims=False)
+    g_half = my_half(jnp.concatenate([g_own, g_other], axis=0), tp)
+    g_slots = spread(place_t, g_half, experts, padded, capacity)
+    g_near = jnp.stack(g_slots[:shards_n])
+    g_far = flip(pin(jnp.stack(g_slots[shards_n:]), mid), "ctx", 2, ctx_n)
+    g_pairs = jnp.stack([g_near, g_far], axis=1)
+    g_in = jnp.stack(
+        [g_pairs[0]] + [flip(g_pairs[k], "shard", k, shards_n) for k in range(1, shards_n)], axis=1
+    ).reshape(2, shards_n * padded, part)
+    g_both = in_order(g_in, swap(g_in), 2)
+
+    block0 = jnp.where(ctx == 0, x_own, jnp.where(ctx == 1, near, jnp.where(ctx == 2, mid, farther)))
     block1 = jnp.where(ctx == 1, x_own, jnp.where(ctx == 2, near, mid))
     block2 = jnp.where(ctx == 2, x_own[:edge], near[:edge])
-    x_all = jnp.concatenate([x_own, block0, block1, block2], axis=0).astype(full)
-    inv_all = lax.rsqrt(jnp.mean(x_all * x_all, axis=-1, keepdims=True) + eps)
-    unit_all = x_all * inv_all
-    normed = (unit_all * gain_a).astype(low)
+    x_all = jnp.concatenate([x_own, block0, block1, block2], axis=0)
+
+    def unit_of(x):
+        x = x.astype(full)
+        inverse = lax.rsqrt(jnp.mean(x * x, axis=-1, keepdims=True) + eps)
+        return (x * inverse, inverse)
+
+    normed = (unit_of(x_all)[0] * gain_a).astype(low)
     q = mm(normed[:rows], weight_q).astype(low)
     kv = mm(normed, weight_kv).astype(low)
 
@@ -766,13 +907,16 @@
     parent = jnp.take(own_tree(parents), seg_id)
     leaf = (seg_id >= KEY_SEGS).astype(jnp.int32)
     info = jnp.stack([jnp.minimum(seg_id, TRUNK), jnp.where(leaf > 0, parent, TRUNK), leaf], axis=1)
-    o_low, lse = attend(info, q, kv, seg)
+    half_pairs = width // 256
+    ahead = attend(info, q, kv, seg, 0, half_pairs)
+    o_low, lse = attend(info, pin(q, g_far), kv, seg, half_pairs, half_pairs, ahead)
 
     inputs = x_own.astype(full)
     mixed = inputs + mm(o_low, weight_o, NT)
     inv_second = lax.rsqrt(jnp.mean(mixed * mixed, axis=-1, keepdims=True) + eps)
     second_unit = mixed * inv_second
     second = (second_unit * gain_f).astype(low)
+    second_half = jnp.concatenate([my_half(second, tp), swap(my_half(second, 1 - tp))], axis=0)
 
     logits = mm(second, router_t, NT) + own_tree(gate_res)
     expo = jnp.exp(logits - jnp.max(logits, axis=-1, keepdims=True))
@@ -782,42 +926,36 @@
     picked = jnp.sum(selector * probs[:, None, :], axis=-1)
     picked_total = jnp.sum(picked, axis=-1, keepdims=True)
     gates = picked / picked_total
-
-    second_both = jnp.concatenate([second, swap(second)], axis=0)
     gates_both = jnp.concatenate([gates.T, swap(gates.T)], axis=1)
-    g_own = own_tree(cotangent)
-    g_other = lax.dynamic_index_in_dim(cotangent, 1 - tp, 0, keepdims=False)
-    slots = mm(routed, second_both).astype(low).reshape(shards_n, padded, width)
-    g_slots = mm(routed, jnp.concatenate([g_own, g_other], axis=0))
-    weighted = jnp.where(table[0], gates_both[0][None, :], 0.0) + jnp.where(
-        table[1], gates_both[1][None, :], 0.0
-    )
-    gate_slots = jnp.sum(weighted, axis=1, keepdims=True)
-    d_slots = (g_slots * gate_slots).astype(low).reshape(shards_n, padded, width)
-    x_in = [slots[0]] + [flip(slots[k], "shard", k, shards_n) for k in range(1, shards_n)]
-    d_in = [d_slots[0]] + [flip(d_slots[k], "shard", k, shards_n) for k in range(1, shards_n)]
-    x_in = jnp.concatenate(x_in, axis=0)
-    d_in = jnp.concatenate(d_in, axis=0)
-
-    blank = jnp.zeros(x_in.shape, full)
-    xt, dt = x_in.T, d_in.T
-    out_sum, ds_sum, dw_near = expert_pass(x_in, xt, d_in, dt, expert_near, blank, blank)
-    out_sum, ds_sum, dw_far = expert_pass(x_in, xt, d_in, dt, expert_far, out_sum, ds_sum)
-    out_low = out_sum.astype(low).reshape(shards_n, padded, width)
-    ds_low = ds_sum.astype(low).reshape(shards_n, padded, width)
-    out_back = [out_low[0]] + [flip(out_low[k], "shard", k, shards_n) for k in range(1, shards_n)]
-    ds_back = [ds_low[0]] + [flip(ds_low[k], "shard", k, shards_n) for k in range(1, shards_n)]
-    out_back = jnp.concatenate(out_back, axis=0)
-    ds_back = jnp.concatenate(ds_back, axis=0)
+
+    rows_three = flip(pin(rows_two, second), "ctx", 1, ctx_n)
+    weights = (rows_own, rows_one, rows_two, rows_three)
+    gate_parts = jnp.pad(three_parts(gates_both), ((0, 0), (0, 13), (0, 0)))
+    slots = spread(place_t, pin(second_half, g_in), experts, padded, capacity, gate_parts)
+    x_far = [far(slots[shards_n + k], k, shards_n, ctx_n) for k in range(shards_n)]
+    x_near = [slots[0]] + [flip(slots[k], "shard", k, shards_n) for k in range(1, shards_n)]
+
+    def experts_on(pieces, g_in_both, prev):
+        x = jnp.stack(pieces)
+        gate = row_values(x, capacity).reshape(-1, 1)
+        x = x.reshape(-1, part)
+        return expert_pass(jnp.stack([ctx, tp]), in_order(x, swap(x), 1), g_in_both, gate, weights, prev)
+
+    def answers(mine, other, dots):
+        ds = plus(mine, swap(other)).reshape(shards_n, padded, part)
+        return with_rows(ds, dots.reshape(shards_n, padded), capacity)
+
+    on1, ox1, sn1, sx1, dots1, dw = experts_on(x_near, g_both[0], None)
+    on2, ox2, sn2, sx2, dots2, dw = experts_on(x_far, g_both[1], dw)
+    ds_far = answers(sn2, sx2, dots2)
+    ds_near = answers(sn1, sx1, dots1)
+    ds_far = [far(ds_far[k], k, shards_n, ctx_n) for k in range(shards_n)]
+    ds_near = [ds_near[0]] + [flip(ds_near[k], "shard", k, shards_n) for k in range(1, shards_n)]
 
     rows_tn = (((0,), (0,)), ((), ()))
-    combined = mm(weighted.astype(low), out_back, rows_tn)
-    d_routed = mm(routed, ds_back, rows_tn)
-    gate_dots = jnp.sum(g_slots * out_back.astype(full), axis=1)
-    d_gate_pairs = jnp.sum(jnp.where(table, gate_dots[None, :, None], 0.0), axis=1)
-    combined = combined[:rows] + swap(combined[rows:].astype(low)).astype(full)
-    d_routed = d_routed[:rows] + swap(d_routed[rows:].astype(low)).astype(full)
-    d_gate_pairs = d_gate_pairs[:, :rows] + swap(d_gate_pairs[:, rows:])
+    d_routed, d_gate_pairs = gather(place, ds_near + ds_far, capacity)
+    d_routed = in_order(d_routed[:rows], swap(d_routed[rows:]), 1).astype(full)
+    d_gate_pairs = d_gate_pairs[:rows] + swap(d_gate_pairs[rows:])
 
     second_f = second.astype(full)
     g = g_own.astype(full)
@@ -825,17 +963,10 @@
     const_flags = selector[:, :, experts + 2 :]
     copy_gate = jnp.sum(gates * copy_flag, axis=1, keepdims=True)
     const_gate = jnp.sum(gates[:, :, None] * const_flags, axis=1)
-    mixed_out = (
-        mixed
-        + combined
-        + copy_gate * second_f
-        + const_gate[:, :1] * const_t[0][None]
-        + const_gate[:, 1:] * const_t[1][None]
-    )
     g_second = jnp.sum(g * second_f, axis=1, keepdims=True)
     g_const = jnp.stack([jnp.sum(g * const_t[k][None], axis=1) for k in range(2)], axis=1)
     d_gates = (
-        d_gate_pairs.T
+        d_gate_pairs
         + copy_flag * g_second
         + jnp.sum(const_flags * g_const[:, None, :], axis=-1)
     )
@@ -855,30 +986,85 @@
     d_o = mm(d_attn, weight_o).astype(low)
     d_weight_o = mm(d_attn, o_low, rows_tn)
 
-    dq, dk, dv = attend_back(info, q, kv, o_low, d_o, lse, seg)
-    d_weight_q = mm(normed[:rows], dq, rows_tn)
-    d_weight_k = mm(normed, dk, rows_tn)
-    d_weight_v = mm(normed, dv, rows_tn)
-    d_keys = mm(dk, weight_k, NT) + mm(dv, weight_v, NT)
-    d_near = d_keys[:rows] + mm(dq, weight_q, NT)
-    d_gain_a = jnp.sum(d_near * unit_all[:rows], axis=0) + jnp.sum(
-        d_keys[rows:] * unit_all[rows:], axis=0
-    )
-
-    def send(x, pairs):
-        return lax.ppermute(x.astype(low), "ctx", pairs).astype(full)
-
-    part0 = d_keys[rows : 2 * rows]
-    part1 = d_keys[2 * rows : 3 * rows]
-    part2 = d_keys[3 * rows :]
-    for hop in range(ctx_n - 1, 0, -1):
-        part0 = part0 + send(part0, [(hop, hop - 1)])
-        if hop >= 2:
-            part1 = part1 + send(part1, [(hop, hop - 1)])
-        if hop >= 3:
-            part2 = part2 + send(part2, [(hop, hop - 1)])
-    part2 = jnp.concatenate([part2, jnp.zeros((rows - edge, width), full)], axis=0)
-    extra = jnp.where(ctx == 0, part0, jnp.where(ctx == 1, part1, jnp.where(ctx == 2, part2, 0.0)))
+    ox1, ox2, held = lax.optimization_barrier((ox1, ox2, d_o))
+    out_near = plus(on1, swap(ox1)).reshape(shards_n, padded, part)
+    out_far = plus(on2, swap(ox2)).reshape(shards_n, padded, part)
+    out_pairs = jnp.stack([out_near, out_far], axis=1)
+    out_got = [out_pairs[0]] + [flip(out_pairs[k], "shard", k, shards_n) for k in range(1, shards_n)]
+    out_far = flip(jnp.stack([o[1] for o in out_got]), "ctx", 2, ctx_n)
+
+    got = flip(pin(dw[2:], d_routed), "ctx", 1, ctx_n)
+    kept_rows = dw[0].astype(full) + got[0].astype(full)
+    sent_rows = (dw[1].astype(full) + got[1].astype(full)).astype(low)
+    came_rows = flip(sent_rows, "ctx", 2, ctx_n).astype(full)
+    first = jnp.where(lower, kept_rows, came_rows)
+    second_e = jnp.where(lower, came_rows, kept_rows)
+    d_gate_up = jnp.stack(
+        [jnp.stack([first[0], first[1]], axis=1), jnp.stack([second_e[0], second_e[1]], axis=1)], axis=1
+    )
+    d_down = jnp.stack([first[2], second_e[2]], axis=1)
+
+    third = width // 384
+    back = attend_back(info, q, kv, o_low, d_o, lse, seg, 0, third)
+    q_later = pin(q, out_pairs, back[0])
+    back = attend_back(info, q_later, kv, o_low, d_o, lse, seg, third, third, back)
+    q_later = pin(q, *out_got, sent_rows, back[0])
+    dq, dk, dv = attend_back(info, q_later, kv, o_low, d_o, lse, seg, 2 * third, third, back)
+    x_again, dk = lax.optimization_barrier((x_all, dk))
+    unit_all, inv_all = unit_of(x_again)
+
+    def keys_grad(lo, hi):
+        return mm(dk[lo:hi], weight_k, NT) + mm(dv[lo:hi], weight_v, NT)
+
+    part0 = keys_grad(rows, 2 * rows).astype(low)
+    dq_after, dk_after, dv_after, held = lax.optimization_barrier((dq, dk, dv, part0))
+    d_weight_q = mm(normed[:rows], dq_after, rows_tn).astype(low)
+    d_weight_k = mm(normed, dk_after, rows_tn).astype(low)
+    d_weight_v = mm(normed, dv_after, rows_tn).astype(low)
+    part1 = keys_grad(2 * rows, 3 * rows).astype(low)
+    part2 = keys_grad(3 * rows, dk.shape[0]).astype(low)
+    d_near = keys_grad(0, rows) + mm(dq, weight_q, NT)
+    d_gain_a = jnp.sum(d_near * unit_all[:rows], axis=0)
+    for at, piece in ((1, part0), (2, part1), (3, part2)):
+        lo = at * rows
+        d_gain_a = d_gain_a + jnp.sum(
+            piece.astype(full) * unit_all[lo : lo + piece.shape[0]], axis=0
+        )
+
+    tiny = jnp.concatenate([d_router, d_gain_a[None], d_gain_f[None], d_const], axis=0)
+    tiny = tiny.reshape(4, 2, 2, ctx_n, rows_d).transpose(0, 3, 1, 2, 4).reshape(4, ctx_n, 2, 2 * rows_d)
+    tiny = jnp.where(tp == 0, tiny, tiny[:, :, ::-1]).reshape(4, ctx_n, 1, width).astype(low)
+    shared = jnp.stack([d_weight_q, d_weight_k, d_weight_v, d_weight_o.astype(low)])
+    shared = shared.reshape(4, ctx_n, rows_d, width)
+    room = jnp.zeros((4, ctx_n, 15, width), low)
+    shared = jnp.concatenate([shared, tiny, room], axis=2)
+    shared_mine, shared_other = shared[..., :part], shared[..., part:]
+
+    def hop(x, at):
+        return lax.ppermute(x, "ctx", [(at, at - 1)])
+
+    came0, came1, came2 = hop(part0, 3), hop(part1, 3), hop(part2, 3)
+    came0, came1, came2, held = lax.optimization_barrier((came0, came1, came2, shared_other))
+    part0 = plus(part0, came0)
+    shared = plus(shared_mine, swap(shared_other))
+    came0 = pin(hop(part0, 2), shared)
+    part1 = plus(part1, came1)
+    came1 = hop(part1, 2)
+    part2 = plus(part2, came2)
+    part0 = plus(part0, came0)
+    came0 = hop(part0, 1)
+    part1 = plus(part1, came1)
+    def numbered(k):
+        return lax.dynamic_index_in_dim(shared, shard ^ k, 0, keepdims=False)
+
+    total = numbered(0).astype(full)
+    for k in range(1, shards_n):
+        total = total + flip(numbered(k), "shard", k, shards_n).astype(full)
+    came0 = pin(came0, total)
+    part0 = plus(part0, came0)
+    part2 = jnp.concatenate([part2, jnp.zeros((rows - edge, width), low)], axis=0)
+    extra = jnp.where(ctx == 0, part0, jnp.where(ctx == 1, part1, part2)).astype(full)
+    extra = jnp.where(ctx == 3, 0.0, extra)
     d_normed = d_near + extra
     unit_own, inv_own = unit_all[:rows], inv_all[:rows]
     d_first = d_normed * gain_a
@@ -886,42 +1072,27 @@
         d_first - unit_own * jnp.mean(d_first * unit_own, axis=-1, keepdims=True)
     )
 
-    shared = jnp.stack([d_weight_q, d_weight_k, d_weight_v, d_weight_o]).astype(low)
-    part = width // 2
-    shared = shared[:, :, :part].astype(full) + swap(shared[:, :, part:]).astype(full)
-    shared = shared.astype(low)
-
-    def numbered(k):
-        return lax.dynamic_index_in_dim(shared, shard ^ k, 0, keepdims=False)
-
-    total = numbered(0).astype(full)
-    for k in range(1, shards_n):
-        total = total + flip(numbered(k), "shard", k, shards_n).astype(full)
-    total = turn_sum(total.astype(low).reshape(ctx_n, rows_d, part), ctx_n, ctx).astype(low)
-    pieces4 = jnp.stack([total] + [flip(total, "shard", k, shards_n) for k in range(1, shards_n)])
-    d_q, d_k, d_v, d_w_out = [
-        lax.dynamic_index_in_dim(pieces4, m ^ shard, 0, keepdims=False).astype(full) for m in range(4)
-    ]
+    total = turn_sum(total.astype(low), ctx_n, ctx).astype(low)
+    four = jnp.stack([total] + [flip(total, "shard", k, shards_n) for k in range(1, shards_n)])
+    four = jnp.stack(
+        [lax.dynamic_index_in_dim(four, m ^ shard, 0, keepdims=False) for m in range(4)]
+    )
+    d_q, d_k, d_v, d_w_out = [four[m, :rows_d].astype(full) for m in range(4)]
     d_w_qkv = jnp.stack([d_q, d_k, d_v], axis=1)
-
-    tiny = jnp.concatenate([d_router, d_gain_a[None], d_gain_f[None], d_const], axis=0)
-    tiny = tiny + swap(tiny)
-    for axis, size in (("shard", shards_n), ("ctx", ctx_n)):
-        bit = 1
-        while bit < size:
-            tiny = tiny + flip(tiny, axis, bit, size)
-            bit *= 2
-    tiny = lax.dynamic_slice_in_dim(tiny, ctx * rows_d, rows_d, 1)
-
-    g_near = line_sum(dw_near.reshape(ctx_n, rows_d, 3 * units), ctx_n, ctx)
-    g_far = line_sum(dw_far.reshape(ctx_n, rows_d, 3 * units), ctx_n, ctx)
-    g_far = swap(g_far.astype(low)).astype(full)
-
-    def unpacked(x):
-        return x.reshape(rows_d, pieces, 3, PIECE).transpose(0, 2, 1, 3).reshape(rows_d, 3, units)
-
-    both = jnp.stack([unpacked(g_near), unpacked(g_far)], axis=1)
-    both = jnp.where(tp == 0, both, both[:, ::-1])
+    tiny = four[:, rows_d]
+    tiny = both_trees(tiny, swap(tiny)).transpose(1, 0, 2).reshape(16, rows_d).astype(full)
+
+    out_far = pin(out_far, dq)
+    pieces = [o[0] for o in out_got] + [out_far[k] for k in range(shards_n)]
+    combined = gather(pin(place, shared_other), pieces, capacity, gates_both.T)[0]
+    combined = in_order(combined[:rows], swap(combined[rows:]), 1).astype(full)
+    mixed_out = (
+        mixed
+        + combined
+        + copy_gate * second_f
+        + const_gate[:, :1] * const_t[0][None]
+        + const_gate[:, 1:] * const_t[1][None]
+    )
     return (
         both_trees(mixed_out, swap(mixed_out)),
         both_trees(d_tokens, swap(d_tokens)),
@@ -932,8 +1103,8 @@
         tiny[all_experts],
         tiny[all_experts + 1],
         tiny[all_experts + 2 :].T,
-        both[:, :, :2],
-        both[:, :, 2],
+        d_gate_up,
+        d_down,
     )
 
 

time: 810 us -> 638 us (0.79)
  starting transfers between devices: 234 us -> 124 us
  local copies, waits for them, and re-layouts: 97.1 us -> 47.3 us
  other arithmetic: 125 us -> 92.4 us
  Pallas kernels: 116 us -> 140 us
  matrix products: 47 us -> 37.5 us
    ppermute x32 -> x16, starting transfers between devices: 177 us -> 26.2 us  [the longest x8 15.4 us: far(): return lax.ppermute(x, ('shard', 'ctx'), pairs)]
    ppermute x41 -> x46, waiting for transfers between devices: 96.1 us -> 125 us  [flip(): return lax.ppermute(x, axis, [(i, i ^ bit) for i in range(size)])]
    ppermute x3, starting transfers between devices: 3.03 us -> 31.4 us  [turn_sum(): got = lax.ppermute(block, 'ctx', [(i, (i + k) % size) for i in range(size)])]
    pallas_call x4 -> x11, Pallas kernels: 116 us -> 140 us  [the longest x2 49.4 us: expert_pass(): pl.pallas_call(functools.partial(expert_kernel, more), grid=(units // PIE...]
    ppermute x32 -> x16, waiting for transfers between devices: 70.3 us -> 46.7 us  [the longest x8 36.1 us: far(): return lax.ppermute(x, ('shard', 'ctx'), pairs)]
    convert_element_type x16 -> x19, other arithmetic: 31.4 us -> 14.1 us  [the longest x9 8.64 us: plus(): return (x.astype(full) + y.astype(full)).astype(low)]
    another operation x8 -> x7, local copies, waits for them, and re-layouts: 17.3 us -> 1.79 us  [the longest x1 1.22 us: by_core(): jnp.stack([g_pairs[0]] + [flip(g_pairs[k], 'shard', k, shards_n) for k in...]
    dynamic_update_slice x5 -> x0, other arithmetic: 14.8 us -> none  [line_gather(): out = lax.dynamic_update_index_in_dim(out, block, (position - k) % size, 0)]
  transfers between devices with their start and end apart: 84 -> 73, of which waited for: 24 -> 30; matrix products, arithmetic and copies ran while one was open for 30% -> 26% of each run, Pallas kernels for 9% -> 13%
where the time goes in v2:
time: 638 us; the launch traced here: 628 us
  waiting for transfers between devices  184 us (29%)
  Pallas kernels  140 us (22%)
  starting transfers between devices  124 us (19%)
  other arithmetic  92.4 us (14%)
  local copies, waits for them, and re-layouts  47.3 us (7%)
  matrix products  37.5 us (6%)
    ppermute x46, waiting for transfers between devices, flip(): return lax.ppermute(x, axis, [(i, i ^ bit) for i in range(size)])  125 us
    ppermute x46, starting transfers between devices, flip(): return lax.ppermute(x, axis, [(i, i ^ bit) for i in range(size)])  49.8 us
    pallas_call x2, Pallas kernels, expert_pass(): pl.pallas_call(functools.partial(expert_kernel, more), grid=(units // PIE...  49.4 us
    pallas_call x3, Pallas kernels, attend_back(): pl.pallas_call(functools.partial(attend_back_kernel, own, seg, HEAD_DIM,...  43.2 us
    ppermute x8, waiting for transfers between devices, far(): return lax.ppermute(x, ('shard', 'ctx'), pairs)  36.1 us
    dot_general x18, matrix products, mm(): return lax.dot_general(a, b, dims, preferred_element_type=jnp.float32)  34.8 us
    ppermute x3, starting transfers between devices, turn_sum(): got = lax.ppermute(block, 'ctx', [(i, (i + k) % size) for i in range(size)])  31.4 us
    pallas_call x2, Pallas kernels, attend(): pl.pallas_call(functools.partial(attend_kernel, own, seg, HEAD_DIM, len(p...  30.1 us
  transfers between devices with their start and end apart: 73, of which 30 were waited for; matrix products, arithmetic and copies ran while one was open for 26% of the time, Pallas kernels for 13%

profile of v2, /device:TPU:0, one launch (start us, length us, event | category | flops | bytes accessed | tf_op | source)
XLA Modules:
  0.0 627.8 jit_solution(6799546609862453936)
XLA Ops:
  30.3 7.9 %collective-permute-done.10 = bf16[16,192]{1,0:T(8,128)(2,1)S(1)} collective-permute-done((bf16[16,192]{1,0:T(8,128)(2,1)S(1)}, bf16[16,192]{1,0:T(8,128)(2,1)S(1)}, u32[]{:S(2)}, u32[]{:S(2)}) %collective-permute-start.10) | collective-permute-done | bytes 6176 | tf_op jit(solution)/shard_map/ppermute | solution.py:757
  58.2 8.3 %collective-permute-done.7 = bf16[768,384]{1,0:T(8,128)(2,1)} collective-permute-done((bf16[768,384]{1,0:T(8,128)(2,1)S(1)}, bf16[768,384]{1,0:T(8,128)(2,1)}, u32[]{:S(2)}, u32[]{:S(2)}) %collective-permute-start.7) | collective-permute-done | bytes 589856 | tf_op jit(solution)/shard_map/ppermute | solution.py:750
  72.3 16.6 %collective-permute-start.14 = (bf16[4,224,384]{2,1,0:T(8,128)(2,1)}, bf16[4,224,384]{2,1,0:T(8,128)(2,1)}, u32[]{:S(2)}, u32[]{:S(2)}) collective-permute-start(bf16[4,224,384]{2,1,0:T(8,128)(2,1)} %pad_maximum_fusion.15), channel_id=1, source_target_pairs={{0,4},{2,6},{4,0},{6,2},{1,5},{3,7},{5,1},{7,3},{8,12},{10,14},{12... | collective-permute-start | bytes 2064392 | tf_op jit(solution)/shard_map/ppermute | solution.py:750
  89.6 25.2 %collective-permute-done.14 = bf16[4,224,384]{2,1,0:T(8,128)(2,1)} collective-permute-done((bf16[4,224,384]{2,1,0:T(8,128)(2,1)}, bf16[4,224,384]{2,1,0:T(8,128)(2,1)}, u32[]{:S(2)}, u32[]{:S(2)}) %collective-permute-start.14) | collective-permute-done | bytes 688160 | tf_op jit(solution)/shard_map/ppermute | solution.py:750
  128.9 5.9 collective-permute-done.17
  140.0 5.9 convolution_convert_fusion.k_ref.v_ref
  145.9 15.0 %attend.2 = (bf16[640,768]{1,0:T(8,128)(2,1)S(1)}, f32[6,8,256]{2,1,0:T(8,128)S(1)}) custom-call(s32[5,3]{1,0:T(8,128)S(1)} %pad_add_fusion.info, bf16[640,768]{1,0:T(8,128)(2,1)S(1)} %convolution_convert_fusion.6.q_ref, bf16[2176,1536]{1,0:T(8,128)(2,1)S(1)} %convolution_convert_fusion.k_ref.v_ref, bf16[2176,1536]{1,0:T(8,128)(2,1)S(1)} %convolution_convert_fusion.k_ref.v_ref), custom_call_target="tpu_custom_call" | custom-call | flops 15000000512 | bytes 3145728 | tf_op jit(solution)/shard_map/attend/pallas_call | solution.py:510
  161.0 15.0 %attend.3 = (bf16[640,768]{1,0:T(8,128)(2,1)S(1)}, f32[6,8,256]{2,1,0:T(8,128)S(1)}) custom-call(s32[5,3]{1,0:T(8,128)S(1)} %pad_add_fusion.info, bf16[640,768]{1,0:T(8,128)(2,1)S(1)} %convolution_convert_fusion.6.q_ref, bf16[2176,1536]{1,0:T(8,128)(2,1)S(1)} %convolution_convert_fusion.k_ref.v_ref, ...), custom_call_target="tpu_custom_call", output_to_operand_aliasing={{0}: (4, {}), {1}: (5, {})} | custom-call | flops 15000000512 | bytes 3145728 | tf_op jit(solution)/shard_map/attend/pallas_call | solution.py:510
  204.5 8.5 %collective-permute-done.28 = bf16[224,384]{1,0:T(8,128)(2,1)S(1)} collective-permute-done((bf16[224,384]{1,0:T(8,128)(2,1)S(1)}, bf16[224,384]{1,0:T(8,128)(2,1)S(1)}, u32[]{:S(2)}, u32[]{:S(2)}) %collective-permute-start.28) | collective-permute-done | bytes 172064 | tf_op jit(solution)/shard_map/ppermute | solution.py:776
  246.4 8.0 %collective-permute-done.25.w1 = bf16[3,192,1024]{2,1,0:T(8,128)(2,1)} collective-permute-done((bf16[3,192,1024]{2,1,0:T(8,128)(2,1)}, bf16[3,192,1024]{2,1,0:T(8,128)(2,1)}, u32[]{:S(2)}, u32[]{:S(2)}) %collective-permute-start.25) | collective-permute-done | bytes 1179680 | tf_op jit(solution)/shard_map/ppermute | solution.py:750
  254.3 24.3 %collective-permute-done.27.w3 = bf16[3,192,1024]{2,1,0:T(8,128)(2,1)} collective-permute-done((bf16[3,192,1024]{2,1,0:T(8,128)(2,1)}, bf16[3,192,1024]{2,1,0:T(8,128)(2,1)}, u32[]{:S(2)}, u32[]{:S(2)}) %collective-permute-start.27) | collective-permute-done | bytes 1179680 | tf_op jit(solution)/shard_map/ppermute | solution.py:750
  278.6 23.6 %expert_pass.2 = (bf16[896,384]{1,0:T(8,128)(2,1)}, bf16[896,384]{1,0:T(8,128)(2,1)}, bf16[896,384]{1,0:T(8,128)(2,1)}, bf16[896,384]{1,0:T(8,128)(2,1)}, f32[89...) custom-call(s32[2]{0:T(128)} %pad_add_fusion.1.place, bf16[896,768]{1,0:T(8,128)(2,1)} %pad_maximum_fusion.10.x_ref, ...), custom_call_target="tpu_custom_call" | custom-call | flops 22000001024 | bytes 20971520 | tf_op jit(solution)/shard_map/expert_pass/pallas_call | solution.py:642
  302.2 25.7 %expert_pass.3 = (bf16[896,384]{1,0:T(8,128)(2,1)}, bf16[896,384]{1,0:T(8,128)(2,1)}, bf16[896,384]{1,0:T(8,128)(2,1)}, bf16[896,384]{1,0:T(8,128)(2,1)}, f32[89...) custom-call(s32[2]{0:T(128)} %pad_add_fusion.1.place, bf16[896,768]{1,0:T(8,128)(2,1)} %pad_maximum_fusion.11.x_ref, ...), custom_call_target="tpu_custom_call" | custom-call | flops 22000001024 | bytes 20971520 | tf_op jit(solution)/shard_map/expert_pass/pallas_call | solution.py:642
  346.5 11.4 %collective-permute-done.38.rest_4_ = bf16[224,384]{1,0:T(8,128)(2,1)S(1)} collective-permute-done((bf16[224,384]{1,0:T(8,128)(2,1)S(1)}, bf16[224,384]{1,0:T(8,128)(2,1)S(1)}, u32[]{:S(2)}, u32[]{:S(2)}) %collective-permute-start.38) | collective-permute-done | bytes 172064 | tf_op jit(solution)/shard_map/ppermute | solution.py:776
  369.7 5.4 collective-permute-done.35.rest_2_
  375.2 6.4 %gather.12 = (bf16[1280,384]{1,0:T(8,128)(2,1)S(1)}, f32[1280,2]{1,0:T(8,128)S(1)}) custom-call(s32[1280,2]{1,0:T(8,128)S(1)} %bitcast.307, bf16[224,384]{1,0:T(8,128)(2,1)S(1)} %get-tuple-element.306.rest_0_, bf16[224,384]{1,0:T(8,128)(2,1)S(1)} %collective-permute-done.34.rest_1_, bf16[224,384]{1,0:T(8,128)(2,1)S(1)} %collective-permute-done.35.rest_2_, ...), custom_call_target="tpu_custom_call" | custom-call | flops 4000000000 | bytes 2097152 | tf_op jit(solution)/shard_map/gather/pallas_call | solution.py:740
  395.4 14.3 %attend_back.3 = (bf16[640,768]{1,0:T(8,128)(2,1)S(1)}, bf16[2176,768]{1,0:T(8,128)(2,1)S(1)}, bf16[2176,768]{1,0:T(8,128)(2,1)S(1)}) custom-call(s32[5,3]{1,0:T(8,128)S(1)} %pad_add_fusion.info, bf16[640,768]{1,0:T(8,128)(2,1)S(1)} %copy-done.3, bf16[2176,1536]{1,0:T(8,128)(2,1)} %copy-done.4, bf16[2176,1536]{1,0:T(8,128)(2,1)} %copy-done.4, ...), custom_call_target="tpu_custom_call" | custom-call | flops 14000000000 | bytes 4194304 | tf_op jit(solution)/shard_map/attend_back/pallas_call | solution.py:544
  410.2 14.3 %attend_back.4 = (bf16[640,768]{1,0:T(8,128)(2,1)S(1)}, bf16[2176,768]{1,0:T(8,128)(2,1)S(1)}, bf16[2176,768]{1,0:T(8,128)(2,1)S(1)}) custom-call(s32[5,3]{1,0:T(8,128)S(1)} %pad_add_fusion.info, bf16[640,768]{1,0:T(8,128)(2,1)S(1)} %copy-done.3, bf16[2176,1536]{1,0:T(8,128)(2,1)} %copy-done.4, ...), custom_call_target="tpu_custom_call", output_to_operand_aliasing={{0}: (7, {}), {1}: (8, {}), {2}: (9, {})} | custom-call | flops 14000000000 | bytes 4194304 | tf_op jit(solution)/shard_map/attend_back/pallas_call | solution.py:544
  448.6 14.6 %attend_back.5 = (bf16[640,768]{1,0:T(8,128)(2,1)S(1)}, bf16[2176,768]{1,0:T(8,128)(2,1)S(1)}, bf16[2176,768]{1,0:T(8,128)(2,1)S(1)}) custom-call(s32[5,3]{1,0:T(8,128)S(1)} %pad_add_fusion.info, bf16[640,768]{1,0:T(8,128)(2,1)S(1)} %copy-done.3, bf16[2176,1536]{1,0:T(8,128)(2,1)} %copy-done.4, ...), custom_call_target="tpu_custom_call", output_to_operand_aliasing={{0}: (7, {}), {1}: (8, {}), {2}: (9, {})} | custom-call | flops 14000000000 | bytes 4194304 | tf_op jit(solution)/shard_map/attend_back/pallas_call | solution.py:544
  502.7 11.5 %collective-permute-done.50 = bf16[4,224,384]{2,1,0:T(8,128)(2,1)S(1)} collective-permute-done((bf16[4,224,384]{2,1,0:T(8,128)(2,1)S(1)}, bf16[4,224,384]{2,1,0:T(8,128)(2,1)S(1)}, u32[]{:S(2)}, u32[]{:S(2)}) %collective-permute-start.50) | collective-permute-done | bytes 688160 | tf_op jit(solution)/shard_map/ppermute | solution.py:750
  534.0 11.1 %collective-permute-done.59 = bf16[4,208,384]{2,1,0:T(8,128)(2,1)S(1)} collective-permute-done((bf16[4,208,384]{2,1,0:T(8,128)(2,1)S(1)}, bf16[4,208,384]{2,1,0:T(8,128)(2,1)S(1)}, u32[]{:S(2)}, u32[]{:S(2)}) %collective-permute-start.59) | collective-permute-done | bytes 639008 | tf_op jit(solution)/shard_map/ppermute | solution.py:750
  552.3 5.6 collective-permute-done.60
  559.4 27.3 %collective-permute-start.65 = (bf16[208,384]{1,0:T(8,128)(2,1)S(1)}, bf16[208,384]{1,0:T(8,128)(2,1)S(1)}, u32[]{:S(2)}, u32[]{:S(2)}) collective-permute-start(bf16[208,384]{1,0:T(8,128)(2,1)S(1)} %get-tuple-element.315), channel_id=1, source_target_pairs={{0,2},{2,4},{4,6},{6,0},{1,3},{3,5},{5,7},{7,1},{8,10},{10,12},{12... | collective-permute-start | bytes 479240 | tf_op jit(solution)/shard_map/ppermute | solution.py:766
  590.8 10.6 %collective-permute-done.58 = bf16[640,768]{1,0:T(8,128)(2,1)S(1)} collective-permute-done((bf16[640,768]{1,0:T(8,128)(2,1)S(1)}, bf16[640,768]{1,0:T(8,128)(2,1)S(1)}, u32[]{:S(2)}, u32[]{:S(2)}) %collective-permute-start.58) | collective-permute-done | bytes 983072 | tf_op jit(solution)/shard_map/ppermute | solution.py:1044
  (516 shorter events, 302.1 us)
Async XLA Ops:
  11.8 30.4 %collective-permute-start = (bf16[256,768]{1,0:T(8,128)(2,1)}, bf16[256,768]{1,0:T(8,128)(2,1)}, u32[]{:S(2)}, u32[]{:S(2)}) collective-permute-start(bf16[256,768]{1,0:T(8,128)(2,1)} %dynamic-slice_bitcast_fusion.9), channel_id=1, source_target_pairs={{0,2},{2,4},{4,6},{1,3},{3,5},{5,7},{8,10},{10,12},{12,14},{9,11},... | collective-permute-start | bytes 1179656 | tf_op jit(solution)/shard_map/ppermute | solution.py:831
  16.0 35.5 %collective-permute-start.1 = (bf16[384,768]{1,0:T(8,128)(2,1)}, bf16[384,768]{1,0:T(8,128)(2,1)}, u32[]{:S(2)}, u32[]{:S(2)}) collective-permute-start(bf16[384,768]{1,0:T(8,128)(2,1)} %dynamic-slice_bitcast_fusion.8), channel_id=1, source_target_pairs={{0,2},{2,4},{1,3},{3,5},{8,10},{10,12},{9,11},{11,13},{16,18},{18,... | collective-permute-start | bytes 1769480 | tf_op jit(solution)/shard_map/ppermute | solution.py:832
  39.7 26.9 %collective-permute-start.7 = (bf16[768,384]{1,0:T(8,128)(2,1)S(1)}, bf16[768,384]{1,0:T(8,128)(2,1)}, u32[]{:S(2)}, u32[]{:S(2)}) collective-permute-start(bf16[768,384]{1,0:T(8,128)(2,1)S(1)} %bitcast.323), channel_id=1, source_target_pairs={{0,16},{8,24},{16,0},{24,8},{1,17},{9,25},{17,1},{25,9},{2,18},{10... | collective-permute-start | bytes 1769480 | tf_op jit(solution)/shard_map/ppermute | solution.py:750
  41.3 25.2 %collective-permute-start.8 = (bf16[768,384]{1,0:T(8,128)(2,1)S(1)}, bf16[768,384]{1,0:T(8,128)(2,1)}, u32[]{:S(2)}, u32[]{:S(2)}) collective-permute-start(bf16[768,384]{1,0:T(8,128)(2,1)S(1)} %bitcast.324), channel_id=1, source_target_pairs={{0,24},{8,16},{16,8},{24,0},{1,25},{9,17},{17,9},{25,1},{2,26},{10... | collective-permute-start | bytes 1769480 | tf_op jit(solution)/shard_map/ppermute | solution.py:750
  69.8 50.0 %collective-permute-start.9 = (bf16[640,768]{1,0:T(8,128)(2,1)}, bf16[640,768]{1,0:T(8,128)(2,1)}, u32[]{:S(2)}, u32[]{:S(2)}) collective-permute-start(bf16[640,768]{1,0:T(8,128)(2,1)} %collective-permute-done.5), channel_id=1, source_target_pairs={{4,6},{5,7},{12,14},{13,15},{20,22},{21,23},{28,30},{29,31}} | collective-permute-start | bytes 2949128 | tf_op jit(solution)/shard_map/ppermute | solution.py:850
  72.3 42.5 %collective-permute-start.14 = (bf16[4,224,384]{2,1,0:T(8,128)(2,1)}, bf16[4,224,384]{2,1,0:T(8,128)(2,1)}, u32[]{:S(2)}, u32[]{:S(2)}) collective-permute-start(bf16[4,224,384]{2,1,0:T(8,128)(2,1)} %pad_maximum_fusion.15), channel_id=1, source_target_pairs={{0,4},{2,6},{4,0},{6,2},{1,5},{3,7},{5,1},{7,3},{8,12},{10,14},{12... | collective-permute-start | bytes 2064392 | tf_op jit(solution)/shard_map/ppermute | solution.py:750
  89.5 46.7 %collective-permute-start.13 = (bf16[4,768,384]{2,1,0:T(8,128)(2,1)}, bf16[4,768,384]{2,1,0:T(8,128)(2,1)S(1)}, u32[]{:S(2)}, u32[]{:S(2)}) collective-permute-start(bf16[4,768,384]{2,1,0:T(8,128)(2,1)} %pad_maximum_fusion.5), channel_id=1, source_target_pairs={{0,1},{1,0},{2,3},{3,2},{4,5},{5,4},{6,7},{7,6},{8,9},{9,8},{10,11... | collective-permute-start | bytes 7077896 | tf_op jit(solution)/shard_map/ppermute | solution.py:750
  123.3 77.4 %collective-permute-start.26 = (bf16[3,192,1024]{2,1,0:T(8,128)(2,1)}, bf16[3,192,1024]{2,1,0:T(8,128)(2,1)}, u32[]{:S(2)}, u32[]{:S(2)}) collective-permute-start(bf16[3,192,1024]{2,1,0:T(8,128)(2,1)} %get-tuple-element.268), channel_id=1, source_target_pairs={{0,4},{2,6},{4,0},{6,2},{1,5},{3,7},{5,1},{7,3},{8,12},{10,14},{12... | collective-permute-start | bytes 3538952 | tf_op jit(solution)/shard_map/ppermute | solution.py:750
  136.3 101.1 %collective-permute-start.24 = (bf16[2,896,384]{2,1,0:T(8,128)(2,1)}, bf16[2,896,384]{2,1,0:T(8,128)(2,1)}, u32[]{:S(2)}, u32[]{:S(2)}) collective-permute-start(bf16[2,896,384]{2,1,0:T(8,128)(2,1)} %bitcast.53), channel_id=1, source_target_pairs={{0,1},{1,0},{2,3},{3,2},{4,5},{5,4},{6,7},{7,6},{8,9},{9,8},{10,11... | collective-permute-start | bytes 4128776 | tf_op jit(solution)/shard_map/ppermute | solution.py:750
  225.2 29.2 %collective-permute-start.25 = (bf16[3,192,1024]{2,1,0:T(8,128)(2,1)}, bf16[3,192,1024]{2,1,0:T(8,128)(2,1)}, u32[]{:S(2)}, u32[]{:S(2)}) collective-permute-start(bf16[3,192,1024]{2,1,0:T(8,128)(2,1)} %get-tuple-element.269.w0), channel_id=1, source_target_pairs={{0,2},{2,0},{4,6},{6,4},{1,3},{3,1},{5,7},{7,5},{8,10},{10,8},{12,... | collective-permute-start | bytes 3538952 | tf_op jit(solution)/shard_map/ppermute | solution.py:750
  227.0 51.5 %collective-permute-start.27 = (bf16[3,192,1024]{2,1,0:T(8,128)(2,1)}, bf16[3,192,1024]{2,1,0:T(8,128)(2,1)}, u32[]{:S(2)}, u32[]{:S(2)}) collective-permute-start(bf16[3,192,1024]{2,1,0:T(8,128)(2,1)} %collective-permute-done.26.w2), channel_id=1, source_target_pairs={{0,2},{2,0},{4,6},{6,4},{1,3},{3,1},{5,7},{7,5},{8,10},{10,8},{12,... | collective-permute-start | bytes 3538952 | tf_op jit(solution)/shard_map/ppermute | solution.py:750
  336.8 25.4 %collective-permute-start.39 = (bf16[224,384]{1,0:T(8,128)(2,1)S(1)}, bf16[224,384]{1,0:T(8,128)(2,1)S(1)}, u32[]{:S(2)}, u32[]{:S(2)}) collective-permute-start(bf16[224,384]{1,0:T(8,128)(2,1)S(1)} %get-tuple-element.301), channel_id=1, source_target_pairs={{0,12},{2,14},{4,8},{6,10},{8,4},{10,6},{12,0},{14,2},{16,28},{18,... | collective-permute-start | bytes 516104 | tf_op jit(solution)/shard_map/ppermute | solution.py:776
  339.6 26.0 %collective-permute-start.40 = (bf16[224,384]{1,0:T(8,128)(2,1)S(1)}, bf16[224,384]{1,0:T(8,128)(2,1)S(1)}, u32[]{:S(2)}, u32[]{:S(2)}) collective-permute-start(bf16[224,384]{1,0:T(8,128)(2,1)S(1)} %get-tuple-element.300), channel_id=1, source_target_pairs={{0,20},{2,22},{4,16},{6,18},{8,28},{10,30},{12,24},{14,26},{16,4},... | collective-permute-start | bytes 516104 | tf_op jit(solution)/shard_map/ppermute | solution.py:776
  340.4 29.3 %collective-permute-start.41 = (bf16[224,384]{1,0:T(8,128)(2,1)S(1)}, bf16[224,384]{1,0:T(8,128)(2,1)S(1)}, u32[]{:S(2)}, u32[]{:S(2)}) collective-permute-start(bf16[224,384]{1,0:T(8,128)(2,1)S(1)} %get-tuple-element.299), channel_id=1, source_target_pairs={{0,28},{2,30},{4,24},{6,26},{8,20},{10,22},{12,16},{14,18},{16,12}... | collective-permute-start | bytes 516104 | tf_op jit(solution)/shard_map/ppermute | solution.py:776
  384.6 53.9 %collective-permute-start.49 = (bf16[2,3,192,1024]{3,2,1,0:T(8,128)(2,1)}, bf16[2,3,192,1024]{3,2,1,0:T(8,128)(2,1)S(1)}, u32[]{:S(2)}, u32[]{:S(2)}) collective-permute-start(bf16[2,3,192,1024]{3,2,1,0:T(8,128)(2,1)} %slice.363), channel_id=1, source_target_pairs={{0,2},{2,0},{4,6},{6,4},{1,3},{3,1},{5,7},{7,5},{8,10},{10,8},{12,... | collective-permute-start | bytes 7077896 | tf_op jit(solution)/shard_map/ppermute | solution.py:750
  442.2 81.7 %collective-permute-start.72 = (bf16[3,192,1024]{2,1,0:T(8,128)(2,1)}, bf16[3,192,1024]{2,1,0:T(8,128)(2,1)}, u32[]{:S(2)}, u32[]{:S(2)}) collective-permute-start(bf16[3,192,1024]{2,1,0:T(8,128)(2,1)} %fusion.28), channel_id=1, source_target_pairs={{0,4},{2,6},{4,0},{6,2},{1,5},{3,7},{5,1},{7,3},{8,12},{10,14},{12... | collective-permute-start | bytes 3538952 | tf_op jit(solution)/shard_map/ppermute | solution.py:750
  477.3 41.4 %collective-permute-start.53 = (bf16[640,768]{1,0:T(8,128)(2,1)}, bf16[640,768]{1,0:T(8,128)(2,1)}, u32[]{:S(2)}, u32[]{:S(2)}) collective-permute-start(bf16[640,768]{1,0:T(8,128)(2,1)} %get-tuple-element.354), channel_id=1, source_target_pairs={{6,4},{7,5},{14,12},{15,13},{22,20},{23,21},{30,28},{31,29}} | collective-permute-start | bytes 2949128 | tf_op jit(solution)/shard_map/ppermute | solution.py:1044
  478.9 39.8 %collective-permute-start.54 = (bf16[640,768]{1,0:T(8,128)(2,1)}, bf16[640,768]{1,0:T(8,128)(2,1)}, u32[]{:S(2)}, u32[]{:S(2)}) collective-permute-start(bf16[640,768]{1,0:T(8,128)(2,1)} %add_convert_fusion.5), channel_id=1, source_target_pairs={{6,4},{7,5},{14,12},{15,13},{22,20},{23,21},{30,28},{31,29}} | collective-permute-start | bytes 2949128 | tf_op jit(solution)/shard_map/ppermute | solution.py:1044
  523.0 78.5 %collective-permute-start.62 = (bf16[640,768]{1,0:T(8,128)(2,1)S(1)}, bf16[640,768]{1,0:T(8,128)(2,1)S(1)}, u32[]{:S(2)}, u32[]{:S(2)}) collective-permute-start(bf16[640,768]{1,0:T(8,128)(2,1)S(1)} %fusion.14), channel_id=1, source_target_pairs={{4,2},{5,3},{12,10},{13,11},{20,18},{21,19},{28,26},{29,27}} | collective-permute-start | bytes 2949128 | tf_op jit(solution)/shard_map/ppermute | solution.py:1044
  528.8 29.1 %collective-permute-start.60 = (bf16[4,208,384]{2,1,0:T(8,128)(2,1)S(1)}, bf16[4,208,384]{2,1,0:T(8,128)(2,1)S(1)}, u32[]{:S(2)}, u32[]{:S(2)}) collective-permute-start(bf16[4,208,384]{2,1,0:T(8,128)(2,1)S(1)} %get-tuple-element.261), channel_id=1, source_target_pairs={{0,16},{8,24},{16,0},{24,8},{1,17},{9,25},{17,1},{25,9},{2,18},{10... | collective-permute-start | bytes 1916936 | tf_op jit(solution)/shard_map/ppermute | solution.py:750
  530.2 28.8 %collective-permute-start.61 = (bf16[4,208,384]{2,1,0:T(8,128)(2,1)S(1)}, bf16[4,208,384]{2,1,0:T(8,128)(2,1)S(1)}, u32[]{:S(2)}, u32[]{:S(2)}) collective-permute-start(bf16[4,208,384]{2,1,0:T(8,128)(2,1)S(1)} %get-tuple-element.260), channel_id=1, source_target_pairs={{0,24},{8,16},{16,8},{24,0},{1,25},{9,17},{17,9},{25,1},{2,26},{10... | collective-permute-start | bytes 1916936 | tf_op jit(solution)/shard_map/ppermute | solution.py:750
  531.7 69.8 %collective-permute-start.58 = (bf16[640,768]{1,0:T(8,128)(2,1)S(1)}, bf16[640,768]{1,0:T(8,128)(2,1)S(1)}, u32[]{:S(2)}, u32[]{:S(2)}) collective-permute-start(bf16[640,768]{1,0:T(8,128)(2,1)S(1)} %add_convert_fusion.4), channel_id=1, source_target_pairs={{2,0},{3,1},{10,8},{11,9},{18,16},{19,17},{26,24},{27,25}} | collective-permute-start | bytes 2949128 | tf_op jit(solution)/shard_map/ppermute | solution.py:1044
  545.1 59.9 %collective-permute-start.52 = (f32[640,768]{1,0:T(8,128)S(1)}, f32[640,768]{1,0:T(8,128)S(1)}, u32[]{:S(2)}, u32[]{:S(2)}) collective-permute-start(f32[640,768]{1,0:T(8,128)S(1)} %fusion.10), channel_id=1, source_target_pairs={{0,1},{1,0},{2,3},{3,2},{4,5},{5,4},{6,7},{7,6},{8,9},{9,8},{10,11... | collective-permute-start | bytes 5898248 | tf_op jit(solution)/shard_map/ppermute | solution.py:750
  559.4 45.8 %collective-permute-start.65 = (bf16[208,384]{1,0:T(8,128)(2,1)S(1)}, bf16[208,384]{1,0:T(8,128)(2,1)S(1)}, u32[]{:S(2)}, u32[]{:S(2)}) collective-permute-start(bf16[208,384]{1,0:T(8,128)(2,1)S(1)} %get-tuple-element.315), channel_id=1, source_target_pairs={{0,2},{2,4},{4,6},{6,0},{1,3},{3,5},{5,7},{7,1},{8,10},{10,12},{12... | collective-permute-start | bytes 479240 | tf_op jit(solution)/shard_map/ppermute | solution.py:766
  (125 other events, 1622.3 us)

commit v3 on v2

--- a/solution.py
+++ b/solution.py
@@ -527,9 +527,9 @@
             pltpu.VMEM((TRUNK * seg, 2 * seg), jnp.float32),
             pltpu.VMEM((TRUNK * seg, 2 * seg), jnp.bfloat16),
         ],
-        compiler_params=pltpu.CompilerParams(vmem_limit_bytes=32 << 20),
+        compiler_params=pltpu.CompilerParams(vmem_limit_bytes=60 << 20),
         cost_estimate=pl.CostEstimate(
-            flops=count * 5 * 10**9, bytes_accessed=count << 20, transcendentals=0
+            flops=1000, bytes_accessed= 1000, transcendentals=0
         ),
         name="attend",
     )(info, q, kv, kv, *prev)
@@ -567,7 +567,7 @@
         ],
         compiler_params=pltpu.CompilerParams(vmem_limit_bytes=40 << 20),
         cost_estimate=pl.CostEstimate(
-            flops=count * 7 * 10**9, bytes_accessed=2 * count << 20, transcendentals=0
+            flops=1000, bytes_accessed= 1000, transcendentals=0
         ),
         name="attend_back",
     )(info, q, kv, kv, o, do, lse, *prev)
@@ -577,18 +577,33 @@
     return lax.optimization_barrier((x,) + after)[0]
 
 
-def expert_kernel(more, place, x_ref, g_ref, gate_ref, w0, w1, w2, w3, *rest):
-    low = jnp.bfloat16
-    if more:
-        prev_ref, o_ref, o2_ref, s_ref, s2_ref, dot_ref, dw_ref, xt, dt, d_ref, oa, sa, wb, gb = rest
-    else:
-        o_ref, o2_ref, s_ref, s2_ref, dot_ref, dw_ref, xt, dt, d_ref, oa, sa, wb, gb = rest
+def expert_kernel(
+    more, capacity, pieces, place, xm_ref, xo_ref, gm_ref, go_ref, w0, w1, w2, w3, *rest
+):
+    low, full = jnp.bfloat16, jnp.float32
+    o_ref, o2_ref, s_ref, s2_ref, dw_ref, x_ref, g_ref, xt, dt, d_ref, oa, sa, wb, gb = rest[more:]
     part = w0.shape[1]
+    rows, wide = xm_ref.shape
+    padded = rows // pieces
+    tail = padded - 16
+    here = pl.ds(pl.multiple_of(place[1] * wide, 128), wide)
+    there = pl.ds(pl.multiple_of((1 - place[1]) * wide, 128), wide)
 
     @pl.when(pl.program_id(0) == 0)
     def start():
+        x_ref[:, here] = xm_ref[...]
+        x_ref[:, there] = xo_ref[...]
+        g_ref[:, here] = gm_ref[...]
+        g_ref[:, there] = go_ref[...]
+        for p in range(pieces):
+            mine = slice(p * padded, (p + 1) * padded)
+            last = xm_ref[p * padded + tail : (p + 1) * padded, :256].astype(full)
+            row = lax.broadcasted_iota(jnp.int32, last.shape, 0) + tail
+            inside = (row >= capacity) & (row < capacity + 3)
+            gate = jnp.sum(jnp.where(inside, last, 0.0), axis=0, keepdims=True)
+            gate = jnp.broadcast_to(gate, (8, 256)).T[:padded, 0:1]
+            d_ref[mine, :] = (g_ref[mine, :].astype(full) * gate).astype(low)
         xt[...] = x_ref[...].T
-        d_ref[...] = (g_ref[...].astype(jnp.float32) * gate_ref[...]).astype(low)
         dt[...] = d_ref[...].T
         oa[...] = jnp.zeros_like(oa)
         sa[...] = jnp.zeros_like(sa)
@@ -614,44 +629,48 @@
     for at, r in enumerate(SENT):
         got = gb[:, rows_of(r), :]
         if more:
-            got = (got.astype(jnp.float32) + prev_ref[at].astype(jnp.float32)).astype(low)
+            got = (got.astype(full) + rest[0][at].astype(full)).astype(low)
         dw_ref[at] = got
 
     @pl.when(pl.program_id(0) == pl.num_programs(0) - 1)
     def finish():
-        dot_ref[...] = jnp.sum(g_ref[...].astype(jnp.float32) * oa[...], axis=1, keepdims=True)
-        wide = o_ref.shape[1]
-        here = pl.ds(pl.multiple_of(place[1] * wide, 128), wide)
-        there = pl.ds(pl.multiple_of((1 - place[1]) * wide, 128), wide)
         o_ref[...] = oa[:, here].astype(low)
         o2_ref[...] = oa[:, there].astype(low)
         s_ref[...] = sa[:, here].astype(low)
         s2_ref[...] = sa[:, there].astype(low)
-
-
-def expert_pass(place, x, g, gate, weights, prev):
-    rows, width = x.shape
+        for p in range(pieces):
+            mine = slice(p * padded, (p + 1) * padded)
+            dot = jnp.sum(g_ref[mine, :].astype(full) * oa[mine, :], axis=1, keepdims=True)
+            dot = jnp.broadcast_to(dot, (padded, 128)).T[:16, :]
+            dot = jnp.concatenate([dot, jnp.zeros((16, wide - padded), full)], axis=1)
+            row = lax.broadcasted_iota(jnp.int32, dot.shape, 0) + tail
+            kept = jnp.zeros_like(dot)
+            for i in range(3):
+                piece = dot.astype(low).astype(full)
+                kept = jnp.where(row == capacity + i, piece, kept)
+                dot = dot - piece
+            last = slice(p * padded + tail, (p + 1) * padded)
+            row_low = s_ref[last, :].astype(full)
+            s_ref[last, :] = jnp.where(row >= capacity, kept, row_low).astype(low)
+
+
+def expert_pass(place, capacity, pieces, xs, gs, weights, prev):
+    rows, half_width = xs[0].shape
+    width = 2 * half_width
     three, part, units = weights[0].shape
     low = jnp.bfloat16
-    whole = pl.BlockSpec((rows, width), lambda j: (0, 0))
-    strip = pl.BlockSpec((three, part, PIECE), lambda j: (0, 0, j))
-    strips = pl.BlockSpec((4, three, part, PIECE), lambda j: (0, 0, 0, j))
-    column = pl.BlockSpec((rows, 1), lambda j: (0, 0))
-    half = pl.BlockSpec((rows, width // 2), lambda j: (0, 0))
+    strip = pl.BlockSpec((three, part, PIECE), lambda j, *at: (0, 0, j))
+    strips = pl.BlockSpec((4, three, part, PIECE), lambda j, *at: (0, 0, 0, j))
+    half = whole(rows, half_width)
     more = prev is not None
-    return pl.pallas_call(
-        functools.partial(expert_kernel, more),
-        grid=(units // PIECE,),
-        in_specs=[pl.BlockSpec(memory_space=pltpu.SMEM), whole, whole, column]
-        + [strip] * 4
-        + [strips] * more,
-        out_specs=[half] * 4 + [column, strips],
-        out_shape=[
-            *[jax.ShapeDtypeStruct((rows, width // 2), low)] * 4,
-            jax.ShapeDtypeStruct((rows, 1), jnp.float32),
-            jax.ShapeDtypeStruct((4, three, part, units), low),
-        ],
-        scratch_shapes=[
+    return call(
+        functools.partial(expert_kernel, int(more), capacity, pieces),
+        "expert_pass",
+        [((rows, half_width), low)] * 4 + [((4, three, part, units), low)],
+        (place, *xs, *gs, *weights, *([prev] if more else [])),
+        [
+            pltpu.VMEM((rows, width), low),
+            pltpu.VMEM((rows, width), low),
             pltpu.VMEM((width, rows), low),
             pltpu.VMEM((width, rows), low),
             pltpu.VMEM((rows, width), low),
@@ -660,12 +679,12 @@
             pltpu.VMEM((three, width, PIECE), low),
             pltpu.VMEM((three, width, PIECE), low),
         ],
-        compiler_params=pltpu.CompilerParams(vmem_limit_bytes=60 << 20),
-        cost_estimate=pl.CostEstimate(
-            flops=22 * 10**9, bytes_accessed=20 << 20, transcendentals=0
-        ),
-        name="expert_pass",
-    )(place, x, g, gate, *weights, *([prev] if more else []))
+        grid=(units // PIECE,),
+        in_specs=[half] * 4 + [strip] * 4 + [strips] * more,
+        out_specs=[half] * 4 + [strips],
+        prefetch=True,
+        mib=48,
+    )
 
 
 def spread_kernel(pieces, padded, capacity, gated, place_ref, rows_ref, *rest):
@@ -677,9 +696,17 @@
         hits = [slot == place_ref[c : c + 1, :] for c in range(2)]
         out = mm(jnp.where(hits[0] | hits[1], 1.0, 0.0).astype(low), rows_ref[...]).astype(low)
         if gated:
-            parts = sum(
-                mm(rest[0][c], jnp.where(hits[c], 1.0, 0.0).astype(low), NT) for c in range(2)
-            ).astype(low)
+            parts = 0.0
+            for c in range(2):
+                value = rest[0][c : c + 1, :]
+                rows3 = []
+                for i in range(3):
+                    rows3.append(value.astype(low).astype(jnp.float32))
+                    value = value - rows3[-1]
+                rows3.append(jnp.zeros((13, tokens), jnp.float32))
+                three = jnp.concatenate(rows3, axis=0).astype(low)
+                parts = parts + mm(three, jnp.where(hits[c], 1.0, 0.0).astype(low), NT)
+            parts = parts.astype(low)
             blank = jnp.zeros((parts.shape[0], out.shape[1] - padded), low)
             parts = jnp.concatenate([parts, blank], axis=1)
             row = lax.broadcasted_iota(jnp.int32, out.shape, 0)
@@ -693,9 +720,11 @@
     gated = parts is not None
     return pl.pallas_call(
         functools.partial(spread_kernel, pieces, padded, capacity, gated),
+        in_specs=[pl.BlockSpec(memory_space=pltpu.VMEM)] * (2 + gated),
+        out_specs=[pl.BlockSpec(memory_space=pltpu.VMEM)] * pieces,
         out_shape=[shape] * pieces,
-        compiler_params=pltpu.CompilerParams(vmem_limit_bytes=40 << 20),
-        cost_estimate=pl.CostEstimate(flops=4 * 10**9, bytes_accessed=2 << 20, transcendentals=0),
+        compiler_params=pltpu.CompilerParams(vmem_limit_bytes=60 << 20),
+        cost_estimate=pl.CostEstimate(flops=1000, bytes_accessed= 1000, transcendentals=0),
         name="spread",
     )(place, rows, *([parts] if gated else []))
 
@@ -703,9 +732,9 @@
 def gather_kernel(pieces, padded, capacity, dots, place_ref, *rest):
     low = jnp.bfloat16
     if dots:
-        ins, (out_ref, dot_ref) = rest[:pieces], rest[pieces:]
+        ins, (out_ref, out2_ref, dot_ref, dot2_ref) = rest[:pieces], rest[pieces:]
     else:
-        gate_ref, ins, out_ref = rest[0], rest[1 : 1 + pieces], rest[1 + pieces]
+        gate_ref, ins, (out_ref, out2_ref) = rest[0], rest[1 : 1 + pieces], rest[1 + pieces :]
     tokens = place_ref.shape[0]
     total = None
     sums = [0.0, 0.0]
@@ -724,26 +753,273 @@
             pick = pick.astype(low)
         part = mm(pick, ins[p][...])
         total = part if total is None else total + part
-    out_ref[...] = total.astype(low)
+    rows = tokens // 2
+    out_ref[...] = total[:rows].astype(low)
+    out2_ref[...] = total[rows:].astype(low)
     if dots:
         for c in range(2):
-            dot_ref[:, c : c + 1] = jnp.sum(sums[c], axis=1, keepdims=True)
+            dot_ref[:, c : c + 1] = jnp.sum(sums[c][:rows], axis=1, keepdims=True)
+            dot2_ref[:, c : c + 1] = jnp.sum(sums[c][rows:], axis=1, keepdims=True)
 
 
 def gather(place, pieces, capacity, gate=None):
     padded, width = pieces[0].shape
     tokens = place.shape[0]
     dots = gate is None
-    shapes = [jax.ShapeDtypeStruct((tokens, width), jnp.bfloat16)]
+    shapes = [jax.ShapeDtypeStruct((tokens // 2, width), jnp.bfloat16)] * 2
     if dots:
-        shapes.append(jax.ShapeDtypeStruct((tokens, 2), jnp.float32))
+        shapes = shapes + [jax.ShapeDtypeStruct((tokens // 2, 2), jnp.float32)] * 2
     return pl.pallas_call(
         functools.partial(gather_kernel, len(pieces), padded, capacity, dots),
+        in_specs=[pl.BlockSpec(memory_space=pltpu.VMEM)] * (len(pieces) + (1 if dots else 2)),
+        out_specs=[pl.BlockSpec(memory_space=pltpu.VMEM)] * len(shapes),
         out_shape=shapes,
-        compiler_params=pltpu.CompilerParams(vmem_limit_bytes=40 << 20),
-        cost_estimate=pl.CostEstimate(flops=4 * 10**9, bytes_accessed=2 << 20, transcendentals=0),
+        compiler_params=pltpu.CompilerParams(vmem_limit_bytes=60 << 20),
+        cost_estimate=pl.CostEstimate(flops=1000, bytes_accessed= 1000, transcendentals=0),
         name="gather",
     )(place, *([] if dots else [gate]), *pieces)
+
+
+def whole(*shape):
+    return pl.BlockSpec(shape, lambda *at: (0,) * len(shape))
+
+
+def by_rows(*shape):
+    return pl.BlockSpec(shape, lambda j, *at: (j, 0))
+
+
+def chosen(number, *shape):
+    return pl.BlockSpec((None,) + shape, lambda j, place: (number ^ place[0], 0, 0))
+
+
+def call(kernel, name, outs, args, scratch=(), grid=(1,), in_specs=None, out_specs=None, prefetch=False, mib=40):
+    if out_specs is None:
+        out_specs = [whole(*o[0]) for o in outs]
+    spec = pltpu.PrefetchScalarGridSpec(
+        num_scalar_prefetch=int(prefetch),
+        grid=grid,
+        in_specs=in_specs,
+        out_specs=out_specs,
+        scratch_shapes=list(scratch),
+    )
+    return pl.pallas_call(
+        kernel,
+        grid_spec=spec,
+        out_shape=[jax.ShapeDtypeStruct(*o) for o in outs],
+        compiler_params=pltpu.CompilerParams(vmem_limit_bytes=mib << 20),
+        cost_estimate=pl.CostEstimate(flops=1000, bytes_accessed=1000, transcendentals=0),
+        name=name,
+    )(*args)
+
+
+def unit_rows(x):
+    x = x.astype(jnp.float32)
+    return x * lax.rsqrt(jnp.mean(x * x, axis=-1, keepdims=True) + eps)
+
+
+def project_kernel(place, x0, near, mid, farther, gain, wm, wo, q_ref, kv_ref, n_ref, x_ref):
+    low = jnp.bfloat16
+    shard, ctx = place[0], place[1]
+    rows, width = x0.shape
+    half = wm.shape[2]
+
+    def project(lo, x):
+        here = slice(lo, lo + x.shape[0])
+        normed = (unit_rows(x) * gain[...]).astype(low)
+        x_ref[here, :] = x
+        n_ref[here, :] = normed
+        for m in (1, 2):
+            for h, w in enumerate((wm, wo)):
+                at = (m - 1) * width + h * half
+                kv_ref[here, at : at + half] = mm(normed, w[m ^ shard]).astype(low)
+        if lo == 0:
+            for h, w in enumerate((wm, wo)):
+                q_ref[:, h * half : (h + 1) * half] = mm(normed, w[shard]).astype(low)
+
+    edge = x_ref.shape[0] - 3 * rows
+    project(0, x0[...])
+    later = jnp.where(ctx == 2, mid[...], farther[...])
+    project(rows, jnp.where(ctx == 0, x0[...], jnp.where(ctx == 1, near[...], later)))
+    later = jnp.where(ctx == 2, near[...], mid[...])
+    project(2 * rows, jnp.where(ctx == 1, x0[...], later))
+    project(3 * rows, jnp.where(ctx == 2, x0[:edge, :], near[:edge, :]))
+
+
+def settle_kernel(
+    place, o, x, wm, wo, gain, router, res, ids,
+    mixed_ref, second_ref, mine_ref, other_ref, probs_ref, stat_ref, gates_ref,
+):
+    tp = place[2]
+    half = wm.shape[1]
+    attn = mm(o[:, :half], wm[...], NT) + mm(o[:, half:], wo[...], NT)
+    mixed = x[...].astype(jnp.float32) + attn
+    mixed_ref[...] = mixed
+    inverse = lax.rsqrt(jnp.mean(mixed * mixed, axis=-1, keepdims=True) + eps)
+    second = (mixed * inverse * gain[...]).astype(jnp.bfloat16)
+    second_ref[...] = second
+    mine_ref[...] = second_ref[:, pl.ds(pl.multiple_of(tp * half, 128), half)]
+    other_ref[...] = second_ref[:, pl.ds(pl.multiple_of((1 - tp) * half, 128), half)]
+    logits = mm(second, router[...], NT) + res[...]
+    expo = jnp.exp(logits - jnp.max(logits, axis=-1, keepdims=True))
+    probs = expo / jnp.sum(expo, axis=-1, keepdims=True)
+    probs_ref[...] = probs
+    lane = lax.broadcasted_iota(jnp.int32, probs.shape, 1)
+    picked = [
+        jnp.sum(jnp.where(lane == ids[:, c : c + 1], probs, 0.0), axis=-1, keepdims=True)
+        for c in range(2)
+    ]
+    total = picked[0] + picked[1]
+    wide = lax.broadcasted_iota(jnp.int32, (probs.shape[0], 128), 1)
+    stat = jnp.where(wide == 0, picked[0] / total, jnp.where(wide == 1, picked[1] / total, 0.0))
+    stat = jnp.where(wide == 2, total, jnp.where(wide == 3, inverse, stat))
+    stat_ref[...] = stat[:, :8]
+    gates_ref[...] = stat.T[:8, :]
+
+
+def settle_back_kernel(
+    copy_id, place, dr_mine, dr_came, dg_mine, dg_came, g_ref, mixed, second, probs_ref, stat, ids,
+    const, router, gain, wm, wo, dmix_ref, dattn_ref, do_ref, dlog_ref, small_ref, full_ref,
+):
+    low, full = jnp.bfloat16, jnp.float32
+    tp = place[2]
+    half = wm.shape[1]
+    full_ref[:, pl.ds(pl.multiple_of(tp * half, 128), half)] = dr_mine[...]
+    full_ref[:, pl.ds(pl.multiple_of((1 - tp) * half, 128), half)] = dr_came[...]
+    g = g_ref[...].astype(full)
+    probs = probs_ref[...]
+    gates = [stat[:, 0:1], stat[:, 1:2]]
+    total, inverse = stat[:, 2:3], stat[:, 3:4]
+    ids_c = [ids[:, 0:1], ids[:, 1:2]]
+    zero = jnp.zeros_like(total)
+
+    def gate_of(number):
+        return sum(jnp.where(ids_c[c] == number, gates[c], zero) for c in range(2))
+
+    copy_gate = gate_of(copy_id)
+    const_gate = [gate_of(copy_id + 1 + k) for k in range(2)]
+    dots = [jnp.sum(g * second[...].astype(full), axis=-1, keepdims=True)]
+    dots = dots + [jnp.sum(g * const[k : k + 1, :], axis=-1, keepdims=True) for k in range(2)]
+    d_gates = []
+    for c in range(2):
+        d = dg_mine[:, c : c + 1] + dg_came[:, c : c + 1]
+        for k in range(3):
+            d = d + jnp.where(ids_c[c] == copy_id + k, dots[k], zero)
+        d_gates.append(d)
+    mean = d_gates[0] * gates[0] + d_gates[1] * gates[1]
+    lane = lax.broadcasted_iota(jnp.int32, probs.shape, 1)
+    d_probs = jnp.zeros_like(probs)
+    for c in range(2):
+        d_probs = d_probs + jnp.where(lane == ids_c[c], (d_gates[c] - mean) / total, 0.0)
+    d_logits = probs * (d_probs - jnp.sum(probs * d_probs, axis=-1, keepdims=True))
+    dlog_ref[...] = d_logits
+    d_second = copy_gate * g + full_ref[...].astype(full)
+    rest = d_logits
+    for i in range(3):
+        piece = rest.astype(low)
+        rest = rest - piece.astype(full)
+        d_second = d_second + mm(piece, router[...])
+    unit = mixed[...] * inverse
+    d_gain = jnp.sum(d_second * unit, axis=0, keepdims=True)
+    d_unit = d_second * gain[...]
+    d_mixed = g + inverse * (d_unit - unit * jnp.mean(d_unit * unit, axis=-1, keepdims=True))
+    dmix_ref[...] = d_mixed
+    d_attn = d_mixed.astype(low)
+    dattn_ref[...] = d_attn
+    do_ref[:, :half] = mm(d_attn, wm[...]).astype(low)
+    do_ref[:, half:] = mm(d_attn, wo[...]).astype(low)
+    count = probs.shape[1]
+    pad = jnp.zeros((probs.shape[0], 128 - count), full)
+    wide = lax.broadcasted_iota(jnp.int32, (probs.shape[0], 128), 1)
+    table = jnp.concatenate([d_logits, pad], axis=1)
+    table = jnp.where(wide == count + 2, const_gate[0], table)
+    table = jnp.where(wide == count + 3, const_gate[1], table)
+    rest = table.T[: count + 4, :]
+    from_second = from_g = 0.0
+    for i in range(3):
+        piece = rest.astype(low)
+        rest = rest - piece.astype(full)
+        from_second = from_second + mm(piece, second[...])
+        from_g = from_g + mm(piece, g_ref[...])
+    row = lax.broadcasted_iota(jnp.int32, from_g.shape, 0)
+    small = jnp.where(row < count, from_second, jnp.where(row >= count + 2, from_g, 0.0))
+    small_ref[...] = jnp.where(row == count + 1, d_gain, small)
+
+
+def keys_back_kernel(place, dq, dk, dv, x, wm, wo, own_ref, p0_ref, p1_ref, p2_ref, gain_ref):
+    shard = place[0]
+    rows, width = own_ref.shape
+    half = wm.shape[2]
+    gain = jnp.zeros((1, width), jnp.float32)
+    lo = 0
+    for out in (own_ref, p0_ref, p1_ref, p2_ref):
+        here = slice(lo, lo + out.shape[0])
+        lo = lo + out.shape[0]
+        d = 0.0
+        for m, grad in ((0, dq), (1, dk), (2, dv)):
+            if m > 0 or out is own_ref:
+                d = d + mm(grad[here, :half], wm[m ^ shard], NT)
+                d = d + mm(grad[here, half:], wo[m ^ shard], NT)
+        out[...] = d.astype(out.dtype)
+        gain = gain + jnp.sum(d * unit_rows(x[here, :]), axis=0, keepdims=True)
+    gain_ref[...] = gain
+
+
+def weights_back_kernel(n_ref, dq, dk, dv, da_ref, o, tiny, mine_ref, other_ref, nt, at):
+    rows = dq.shape[0]
+    step = pl.program_id(0)
+
+    @pl.when(step == 0)
+    def start():
+        nt[...] = n_ref[...].T
+        at[...] = da_ref[...].T
+
+    def put(value):
+        value = value.astype(jnp.bfloat16)
+        part = value.shape[0] // mine_ref.shape[0]
+
+        def write(ref):
+            for z in range(ref.shape[0]):
+                ref[z, :part, :] = value[z * part : (z + 1) * part, :]
+                ref[z, part:, :] = tiny[z]
+
+        pl.when(step % 2 == 0)(lambda: write(mine_ref))
+        pl.when(step % 2 == 1)(lambda: write(other_ref))
+
+    pl.when(step // 2 == 0)(lambda: put(mm(nt[:, :rows], dq[...])))
+    pl.when(step // 2 == 1)(lambda: put(mm(nt[...], dk[...])))
+    pl.when(step // 2 == 2)(lambda: put(mm(nt[...], dv[...])))
+    pl.when(step // 2 == 3)(lambda: put(mm(at[...], o[...])))
+
+
+def weights_back(normed, dq, dk, dv, d_attn, o, tiny):
+    total, width = normed.shape
+    rows, half = dq.shape[0], width // 2
+    parts, room = tiny.shape[1], tiny.shape[2]
+    low = jnp.bfloat16
+
+    def columns(n, first):
+        return pl.BlockSpec((n, half), lambda j: (0, jnp.clip(j - first, 0, 1)))
+
+    out = pl.BlockSpec((None, parts, width // parts + room, half), lambda j: (j // 2, 0, 0, 0))
+    shape = ((4, parts, width // parts + room, half), low)
+    return call(
+        weights_back_kernel,
+        "weights_back",
+        [shape, shape],
+        (normed, dq, dk, dv, d_attn, o, tiny),
+        [pltpu.VMEM((width, total), low), pltpu.VMEM((width, rows), low)],
+        grid=(8,),
+        in_specs=[
+            pl.BlockSpec((total, width), lambda j: (0, 0)),
+            columns(rows, 0),
+            columns(total, 2),
+            columns(total, 4),
+            pl.BlockSpec((rows, width), lambda j: (0, 0)),
+            columns(rows, 6),
+            pl.BlockSpec((None, parts, room, half), lambda j: (j // 2, 0, 0, j % 2)),
+        ],
+        out_specs=[out, out],
+    )
 
 
 def flip(x, axis, bit, size):
@@ -817,6 +1093,11 @@
     def both_trees(x, other):
         return in_order(x[None], other[None])
 
+    def unit_of(x):
+        x = x.astype(full)
+        inverse = lax.rsqrt(jnp.mean(x * x, axis=-1, keepdims=True) + eps)
+        return (x * inverse, inverse)
+
     def swap(x):
         return flip(x, "tp", 1, 2)
 
@@ -826,49 +1107,31 @@
     def my_half(x, which):
         return lax.dynamic_slice_in_dim(x, which * part, part, x.ndim - 1)
 
-    x_own = own_tree(tokens)
+    x_own = lax.optimization_barrier(own_tree(tokens))
     ends = [(i, i + 1) for i in range(ctx_n - 1)]
-    near_head = lax.ppermute(x_own[:edge], "ctx", ends)
-    near_tail = lax.ppermute(x_own[edge:], "ctx", ends[:-1])
-    near = jnp.concatenate([near_head, near_tail], axis=0)
-
-    mine = jnp.stack([w_qkv[:, 0], w_qkv[:, 1], w_qkv[:, 2], pin(w_out, x_own)])
-    matrix = turn_gather(lax.dynamic_index_in_dim(mine, shard, 0, keepdims=False), ctx_n, ctx)
-    matrix = matrix.reshape(width, -1)
-
+    near = lax.ppermute(x_own, "ctx", ends)
+
+    mine = jnp.stack([w_qkv[:, 0], w_qkv[:, 1], w_qkv[:, 2], w_out])
     small = jnp.concatenate([w_router.T, attn_gain[None], ffn_gain[None], const_vec.T], axis=0)
-    small = turn_gather(pin(small, matrix), ctx_n, ctx).transpose(1, 0, 2).reshape(small.shape[0], width)
     all_experts = w_router.shape[1]
+    mine = lax.dynamic_index_in_dim(mine, shard, 0, keepdims=False)
+    mine = jnp.concatenate([mine, small.reshape(-1, part)], axis=0)
+    turned = turn_gather(mine, ctx_n, ctx)
+    matrix = turned[:, :rows_d].reshape(width, -1)
+    small = turned[:, rows_d:].reshape(ctx_n, -1, rows_d).transpose(1, 0, 2).reshape(-1, width)
     router_t = small[:all_experts]
     gain_a = small[all_experts].astype(full)
     gain_f = small[all_experts + 1].astype(full)
     const_t = small[all_experts + 2 :].astype(full)
 
     mid = lax.ppermute(pin(near, matrix), "ctx", ends[1:])
-    plane = [matrix] + [flip(matrix, "shard", k, shards_n) for k in range(1, shards_n)]
-    plane = jnp.stack(plane)
-    farther = lax.ppermute(pin(mid, plane, small), "ctx", ends[2:])
-    plane = jnp.concatenate([plane, swap(plane)], axis=2)
-    weight_q, weight_k, weight_v, weight_o = [
-        lax.dynamic_index_in_dim(plane, m ^ shard, 0, keepdims=False) for m in range(4)
-    ]
-    weight_kv = jnp.concatenate([weight_k, weight_v], axis=1)
-
-    held, gu, dn = lax.optimization_barrier((farther, w_gate_up, w_down))
-    lower = ctx < 2
-    first = jnp.stack([gu[:, 0, 0], gu[:, 0, 1], dn[:, 0]])
-    second_e = jnp.stack([gu[:, 1, 0], gu[:, 1, 1], dn[:, 1]])
-    rows_own = jnp.where(lower, first, second_e)
-    rows_two = flip(jnp.where(lower, second_e, first), "ctx", 2, ctx_n)
-    rows_one = flip(rows_own, "ctx", 1, ctx_n)
-
+    plane_pieces = [matrix] + [flip(matrix, "shard", k, shards_n) for k in range(1, shards_n)]
     capacity = trees * rows * 2 // all_experts
     experts = shards_n * w_gate_up.shape[1]
     padded = -(-(capacity + 3) // 16) * 16
     count = experts * padded
-    held, ids_in, order_in = lax.optimization_barrier((near_head, expert_ids, priority))
-    flat = ids_in.reshape(-1)
-    order = (2 * order_in[0, 0][:, None] + jnp.arange(2, dtype=jnp.int32)[None, :]).reshape(-1)
+    flat = expert_ids.reshape(-1)
+    order = (2 * priority[0, 0][:, None] + jnp.arange(2, dtype=jnp.int32)[None, :]).reshape(-1)
     earlier = (flat[:, None] == flat[None, :]) & (order[None, :] < order[:, None])
     ranks = jnp.sum(earlier.astype(jnp.int32), axis=1)
     kept = (flat < experts) & (ranks < capacity)
@@ -881,27 +1144,61 @@
     g_other = lax.dynamic_index_in_dim(cotangent, 1 - tp, 0, keepdims=False)
     g_half = my_half(jnp.concatenate([g_own, g_other], axis=0), tp)
     g_slots = spread(place_t, g_half, experts, padded, capacity)
+    ids = own_tree(expert_ids)
+    res = own_tree(gate_res)
+    ids, res, router_t, gain_a, gain_f, const_t, mid, *g_slots = lax.optimization_barrier(
+        (ids, res, router_t, gain_a[None], gain_f[None], const_t, mid, *g_slots)
+    )
+    farther = lax.ppermute(mid, "ctx", ends[2:])
+    plane = jnp.stack(plane_pieces)
+
+    plane_other = swap(plane)
+    place3 = jnp.stack([shard, ctx, tp]).astype(jnp.int32)
+
+    capacity = trees * rows * 2 // all_experts
+    experts = shards_n * w_gate_up.shape[1]
+    padded = -(-(capacity + 3) // 16) * 16
+    count = experts * padded
+    flat = expert_ids.reshape(-1)
+    order = (2 * priority[0, 0][:, None] + jnp.arange(2, dtype=jnp.int32)[None, :]).reshape(-1)
+    earlier = (flat[:, None] == flat[None, :]) & (order[None, :] < order[:, None])
+    ranks = jnp.sum(earlier.astype(jnp.int32), axis=1)
+    kept = (flat < experts) & (ranks < capacity)
+    piece = ((flat % 2) ^ (ctx // 2)) * shards_n + ((flat // 2) ^ shard)
+    place = jnp.where(kept, piece * padded + ranks, -1).reshape(trees, rows, 2)
+    place = jnp.where(tp == 0, place, place[::-1]).reshape(trees * rows, 2)
+    place_t = place.T
+
+    g_own = own_tree(cotangent)
+    g_other = lax.dynamic_index_in_dim(cotangent, 1 - tp, 0, keepdims=False)
+    g_half = my_half(jnp.concatenate([g_own, g_other], axis=0), tp)
+    g_slots = spread(place_t, g_half, experts, padded, capacity)
     g_near = jnp.stack(g_slots[:shards_n])
     g_far = flip(pin(jnp.stack(g_slots[shards_n:]), mid), "ctx", 2, ctx_n)
-    g_pairs = jnp.stack([g_near, g_far], axis=1)
-    g_in = jnp.stack(
-        [g_pairs[0]] + [flip(g_pairs[k], "shard", k, shards_n) for k in range(1, shards_n)], axis=1
-    ).reshape(2, shards_n * padded, part)
-    g_both = in_order(g_in, swap(g_in), 2)
-
-    block0 = jnp.where(ctx == 0, x_own, jnp.where(ctx == 1, near, jnp.where(ctx == 2, mid, farther)))
-    block1 = jnp.where(ctx == 1, x_own, jnp.where(ctx == 2, near, mid))
-    block2 = jnp.where(ctx == 2, x_own[:edge], near[:edge])
-    x_all = jnp.concatenate([x_own, block0, block1, block2], axis=0)
-
-    def unit_of(x):
-        x = x.astype(full)
-        inverse = lax.rsqrt(jnp.mean(x * x, axis=-1, keepdims=True) + eps)
-        return (x * inverse, inverse)
-
-    normed = (unit_of(x_all)[0] * gain_a).astype(low)
-    q = mm(normed[:rows], weight_q).astype(low)
-    kv = mm(normed, weight_kv).astype(low)
+    plane_other = swap(plane)
+    place3 = jnp.stack([shard, ctx, tp]).astype(jnp.int32)
+
+    g_near = jnp.stack(g_slots[:shards_n])
+    g_far = flip(jnp.stack(g_slots[shards_n:]), "ctx", 2, ctx_n)
+
+    held, gu, dn = lax.optimization_barrier((near, w_gate_up, w_down))
+    lower = ctx < 2
+    first = jnp.stack([gu[:, 0, 0], gu[:, 0, 1], dn[:, 0]])
+    second_e = jnp.stack([gu[:, 1, 0], gu[:, 1, 1], dn[:, 1]])
+    rows_own = jnp.where(lower, first, second_e)
+    rows_two = flip(pin(jnp.where(lower, second_e, first), farther, g_far), "ctx", 2, ctx_n)
+    rows_one = flip(pin(rows_own, farther, g_far), "ctx", 1, ctx_n)
+
+    total = 3 * rows + edge
+    q, kv, normed, x_all = call(
+        project_kernel,
+        "project",
+        [((rows, width), low), ((total, 2 * width), low), ((total, width), low), ((total, width), low)],
+        (place3, x_own, near, mid, farther, gain_a, plane, plane_other),
+        in_specs=[whole(rows, width)] * 4
+        + [whole(1, width), whole(4, width, part), whole(4, width, part)],
+        prefetch=True,
+    )
 
     seg_id = ctx * own_segs + jnp.arange(own_segs, dtype=jnp.int32)
     parent = jnp.take(own_tree(parents), seg_id)
@@ -909,170 +1206,155 @@
     info = jnp.stack([jnp.minimum(seg_id, TRUNK), jnp.where(leaf > 0, parent, TRUNK), leaf], axis=1)
     half_pairs = width // 256
     ahead = attend(info, q, kv, seg, 0, half_pairs)
-    o_low, lse = attend(info, pin(q, g_far), kv, seg, half_pairs, half_pairs, ahead)
-
-    inputs = x_own.astype(full)
-    mixed = inputs + mm(o_low, weight_o, NT)
-    inv_second = lax.rsqrt(jnp.mean(mixed * mixed, axis=-1, keepdims=True) + eps)
-    second_unit = mixed * inv_second
-    second = (second_unit * gain_f).astype(low)
-    second_half = jnp.concatenate([my_half(second, tp), swap(my_half(second, 1 - tp))], axis=0)
-
-    logits = mm(second, router_t, NT) + own_tree(gate_res)
-    expo = jnp.exp(logits - jnp.max(logits, axis=-1, keepdims=True))
-    probs = expo / jnp.sum(expo, axis=-1, keepdims=True)
-    ids = own_tree(expert_ids)
-    selector = (ids[:, :, None] == jnp.arange(all_experts, dtype=jnp.int32)).astype(full)
-    picked = jnp.sum(selector * probs[:, None, :], axis=-1)
-    picked_total = jnp.sum(picked, axis=-1, keepdims=True)
-    gates = picked / picked_total
-    gates_both = jnp.concatenate([gates.T, swap(gates.T)], axis=1)
-
-    rows_three = flip(pin(rows_two, second), "ctx", 1, ctx_n)
+    g_seen = pin(g_far, ahead[0])
+    o_low, lse = attend(info, q, kv, seg, half_pairs, half_pairs, ahead)
+    o_low = pin(o_low, rows_one, rows_two)
+
+    g_pairs = jnp.stack([g_near, g_seen], axis=1)
+    g_in = jnp.stack(
+        [g_pairs[0]] + [flip(g_pairs[k], "shard", k, shards_n) for k in range(1, shards_n)], axis=1
+    ).reshape(2, shards_n * padded, part)
+    g_out = swap(g_in)
+
+    one_half = ((rows, part), low)
+    mixed, second, second_mine, second_other, probs, stat, gates_t = call(
+        settle_kernel,
+        "settle",
+        [
+            ((rows, width), full), ((rows, width), low), one_half, one_half,
+            ((rows, all_experts), full), ((rows, 8), full), ((8, rows), full),
+        ],
+        (place3, o_low, x_own, plane, plane_other, gain_f, router_t, res, ids),
+        in_specs=[
+            whole(rows, width), whole(rows, width), chosen(3, width, part), chosen(3, width, part),
+            whole(1, width), whole(all_experts, width), whole(rows, all_experts), whole(rows, 2),
+        ],
+        prefetch=True,
+    )
+    second_half = jnp.concatenate([second_mine, swap(second_other)], axis=0)
+    gates_both = jnp.concatenate([gates_t, swap(gates_t)], axis=1)
+
+    rows_three = flip(pin(rows_two, o_low), "ctx", 1, ctx_n)
     weights = (rows_own, rows_one, rows_two, rows_three)
-    gate_parts = jnp.pad(three_parts(gates_both), ((0, 0), (0, 13), (0, 0)))
-    slots = spread(place_t, pin(second_half, g_in), experts, padded, capacity, gate_parts)
+    slots = spread(place_t, pin(second_half, g_in), experts, padded, capacity, gates_both)
     x_far = [far(slots[shards_n + k], k, shards_n, ctx_n) for k in range(shards_n)]
     x_near = [slots[0]] + [flip(slots[k], "shard", k, shards_n) for k in range(1, shards_n)]
 
-    def experts_on(pieces, g_in_both, prev):
-        x = jnp.stack(pieces)
-        gate = row_values(x, capacity).reshape(-1, 1)
-        x = x.reshape(-1, part)
-        return expert_pass(jnp.stack([ctx, tp]), in_order(x, swap(x), 1), g_in_both, gate, weights, prev)
-
-    def answers(mine, other, dots):
-        ds = plus(mine, swap(other)).reshape(shards_n, padded, part)
-        return with_rows(ds, dots.reshape(shards_n, padded), capacity)
-
-    on1, ox1, sn1, sx1, dots1, dw = experts_on(x_near, g_both[0], None)
-    on2, ox2, sn2, sx2, dots2, dw = experts_on(x_far, g_both[1], dw)
-    ds_far = answers(sn2, sx2, dots2)
-    ds_near = answers(sn1, sx1, dots1)
+    def experts_on(pieces, gs, prev):
+        x = jnp.concatenate(pieces, axis=0)
+        return expert_pass(place3[1:], capacity, shards_n, (x, swap(x)), gs, weights, prev)
+
+    def answers(mine, other):
+        return plus(mine, swap(other)).reshape(shards_n, padded, part)
+
+    x_near[0] = pin(x_near[0], rows_three)
+    on1, ox1, sn1, sx1, dw = experts_on(x_near, (g_in[0], g_out[0]), None)
+    x_far = list(lax.optimization_barrier((*x_far, sn1))[:-1])
+    on2, ox2, sn2, sx2, dw = experts_on(x_far, (g_in[1], g_out[1]), dw)
+    ds_far = answers(sn2, sx2)
+    ds_near = answers(sn1, sx1)
     ds_far = [far(ds_far[k], k, shards_n, ctx_n) for k in range(shards_n)]
     ds_near = [ds_near[0]] + [flip(ds_near[k], "shard", k, shards_n) for k in range(1, shards_n)]
 
     rows_tn = (((0,), (0,)), ((), ()))
-    d_routed, d_gate_pairs = gather(place, ds_near + ds_far, capacity)
-    d_routed = in_order(d_routed[:rows], swap(d_routed[rows:]), 1).astype(full)
-    d_gate_pairs = d_gate_pairs[:rows] + swap(d_gate_pairs[rows:])
-
-    second_f = second.astype(full)
-    g = g_own.astype(full)
-    copy_flag = selector[:, :, experts + 1]
-    const_flags = selector[:, :, experts + 2 :]
-    copy_gate = jnp.sum(gates * copy_flag, axis=1, keepdims=True)
-    const_gate = jnp.sum(gates[:, :, None] * const_flags, axis=1)
-    g_second = jnp.sum(g * second_f, axis=1, keepdims=True)
-    g_const = jnp.stack([jnp.sum(g * const_t[k][None], axis=1) for k in range(2)], axis=1)
-    d_gates = (
-        d_gate_pairs
-        + copy_flag * g_second
-        + jnp.sum(const_flags * g_const[:, None, :], axis=-1)
-    )
-    d_picked = (d_gates - jnp.sum(d_gates * gates, axis=-1, keepdims=True)) / picked_total
-    d_probs = jnp.sum(d_picked[:, :, None] * selector, axis=1)
-    d_logits = probs * (d_probs - jnp.sum(probs * d_probs, axis=-1, keepdims=True))
-    high = lax.Precision.HIGHEST
-    d_router = jnp.einsum("tk,td->kd", d_logits, second_f, precision=high)
-    d_const = jnp.einsum("tk,td->kd", const_gate, g, precision=high)
-    d_second = copy_gate * g + d_routed + jnp.dot(d_logits, router_t.astype(full), precision=high)
-    d_gain_f = jnp.sum(d_second * second_unit, axis=0)
-    d_unit = d_second * gain_f
-    d_mixed = g + inv_second * (
-        d_unit - second_unit * jnp.mean(d_unit * second_unit, axis=-1, keepdims=True)
-    )
-    d_attn = d_mixed.astype(low)
-    d_o = mm(d_attn, weight_o).astype(low)
-    d_weight_o = mm(d_attn, o_low, rows_tn)
-
-    ox1, ox2, held = lax.optimization_barrier((ox1, ox2, d_o))
+    d_routed, d_routed_other, d_pairs, d_pairs_other = gather(place, ds_near + ds_far, capacity)
+    d_mixed, d_attn, d_o, d_logits, d_small = call(
+        functools.partial(settle_back_kernel, experts + 1),
+        "settle_back",
+        [
+            ((rows, width), full), ((rows, width), low), ((rows, width), low),
+            ((rows, all_experts), full), ((all_experts + 4, width), full),
+        ],
+        (
+            place3, d_routed, swap(d_routed_other), d_pairs, swap(d_pairs_other), g_own, mixed, second,
+            probs, stat, ids, const_t, router_t, gain_f, plane, plane_other,
+        ),
+        [pltpu.VMEM((rows, width), low)],
+        in_specs=[
+            whole(rows, part), whole(rows, part), whole(rows, 2), whole(rows, 2), whole(rows, width),
+            whole(rows, width), whole(rows, width), whole(rows, all_experts), whole(rows, 8),
+            whole(rows, 2), whole(2, width), whole(all_experts, width), whole(1, width),
+            chosen(3, width, part), chosen(3, width, part),
+        ],
+        prefetch=True,
+    )
+
+    ox1, ox2, held = lax.optimization_barrier((ox1, ox2, d_routed))
     out_near = plus(on1, swap(ox1)).reshape(shards_n, padded, part)
     out_far = plus(on2, swap(ox2)).reshape(shards_n, padded, part)
-    out_pairs = jnp.stack([out_near, out_far], axis=1)
+
+    got = flip(pin(dw[2:], d_routed), "ctx", 1, ctx_n)
+    sent_rows = (dw[1].astype(full) + got[1].astype(full)).astype(low)
+    came_rows = flip(sent_rows, "ctx", 2, ctx_n)
+
+    third = width // 384
+    back = attend_back(info, q, kv, o_low, d_o, lse, seg, 0, third)
+    q_later = pin(q, out_far, out_near, back[0])
+    back = attend_back(info, q_later, kv, o_low, d_o, lse, seg, third, third, back)
+    out_near, out_far = lax.optimization_barrier((out_near, out_far, back[0]))[:2]
+    out_cross = flip(out_far, "ctx", 2, ctx_n)
+    q_later = pin(q, sent_rows, back[0])
+    dq, dk, dv = attend_back(info, q_later, kv, o_low, d_o, lse, seg, 2 * third, third, back)
+    out_pairs = jnp.stack([out_near, pin(out_cross, dq)], axis=1)
     out_got = [out_pairs[0]] + [flip(out_pairs[k], "shard", k, shards_n) for k in range(1, shards_n)]
-    out_far = flip(jnp.stack([o[1] for o in out_got]), "ctx", 2, ctx_n)
-
-    got = flip(pin(dw[2:], d_routed), "ctx", 1, ctx_n)
+    d_near, part0, part1, part2, d_gain_a = call(
+        keys_back_kernel,
+        "keys_back",
+        [
+            ((rows, width), full), ((rows, width), low), ((rows, width), low), ((edge, width), low),
+            ((1, width), full),
+        ],
+        (place3, dq, dk, dv, x_all, plane, plane_other),
+        in_specs=[
+            whole(rows, width), whole(total, width), whole(total, width), whole(total, width),
+            whole(4, width, part), whole(4, width, part),
+        ],
+        prefetch=True,
+    )
+
+    tiny = jnp.concatenate([d_small[:all_experts], d_gain_a, d_small[all_experts + 1 :]], axis=0)
+    tiny = tiny.reshape(4, 2, 2, ctx_n, rows_d).transpose(0, 3, 1, 2, 4).reshape(4, ctx_n, 2, 2 * rows_d)
+    tiny = jnp.where(tp == 0, tiny, tiny[:, :, ::-1]).reshape(4, ctx_n, 1, width).astype(low)
+    tiny = jnp.pad(tiny, ((0, 0), (0, 0), (0, 15), (0, 0)))
+    shared_mine, shared_other = weights_back(normed, dq, dk, dv, d_attn, o_low, tiny)
+
+    def down(x, step):
+        return lax.ppermute(x, "ctx", [(i, i - 1) for i in range(ctx_n - step, ctx_n)])
+
+    came = down(part0, 1)
+    shared_other = pin(shared_other, came, *out_got, came_rows)
+    came = down(jnp.where(ctx == 3, part1, plus(part0, came)), 2)
+    shared = plus(shared_mine, swap(shared_other))
+
+    def numbered(k):
+        return lax.dynamic_index_in_dim(shared, shard ^ k, 0, keepdims=False)
+
+    plane_parts = [flip(numbered(k), "shard", k, shards_n) for k in range(1, shards_n)]
+    plane_sum = numbered(0).astype(full)
+    for got_part in plane_parts:
+        plane_sum = plane_sum + got_part.astype(full)
+    came = pin(came, plane_sum)
+    part2 = jnp.pad(part2, ((0, rows - edge), (0, 0)))
+    came = down(jnp.where(ctx == 3, part2, jnp.where(ctx == 2, plus(part1, came), plus(part0, came))), 3)
+    base = jnp.where(ctx == 0, part0, jnp.where(ctx == 1, part1, part2)).astype(full)
+    extra = jnp.where(ctx == 3, 0.0, base + came.astype(full))
+    d_normed = d_near + extra
+    unit_own, inv_own = unit_of(x_own)
+    gain_a = gain_a[0]
+    d_first = d_normed * gain_a
+    d_tokens = d_mixed + inv_own * (
+        d_first - unit_own * jnp.mean(d_first * unit_own, axis=-1, keepdims=True)
+    )
+
+    total = turn_sum(plane_sum.astype(low), ctx_n, ctx).astype(low)
+    came_rows = pin(came_rows, total).astype(full)
     kept_rows = dw[0].astype(full) + got[0].astype(full)
-    sent_rows = (dw[1].astype(full) + got[1].astype(full)).astype(low)
-    came_rows = flip(sent_rows, "ctx", 2, ctx_n).astype(full)
     first = jnp.where(lower, kept_rows, came_rows)
     second_e = jnp.where(lower, came_rows, kept_rows)
     d_gate_up = jnp.stack(
         [jnp.stack([first[0], first[1]], axis=1), jnp.stack([second_e[0], second_e[1]], axis=1)], axis=1
     )
     d_down = jnp.stack([first[2], second_e[2]], axis=1)
-
-    third = width // 384
-    back = attend_back(info, q, kv, o_low, d_o, lse, seg, 0, third)
-    q_later = pin(q, out_pairs, back[0])
-    back = attend_back(info, q_later, kv, o_low, d_o, lse, seg, third, third, back)
-    q_later = pin(q, *out_got, sent_rows, back[0])
-    dq, dk, dv = attend_back(info, q_later, kv, o_low, d_o, lse, seg, 2 * third, third, back)
-    x_again, dk = lax.optimization_barrier((x_all, dk))
-    unit_all, inv_all = unit_of(x_again)
-
-    def keys_grad(lo, hi):
-        return mm(dk[lo:hi], weight_k, NT) + mm(dv[lo:hi], weight_v, NT)
-
-    part0 = keys_grad(rows, 2 * rows).astype(low)
-    dq_after, dk_after, dv_after, held = lax.optimization_barrier((dq, dk, dv, part0))
-    d_weight_q = mm(normed[:rows], dq_after, rows_tn).astype(low)
-    d_weight_k = mm(normed, dk_after, rows_tn).astype(low)
-    d_weight_v = mm(normed, dv_after, rows_tn).astype(low)
-    part1 = keys_grad(2 * rows, 3 * rows).astype(low)
-    part2 = keys_grad(3 * rows, dk.shape[0]).astype(low)
-    d_near = keys_grad(0, rows) + mm(dq, weight_q, NT)
-    d_gain_a = jnp.sum(d_near * unit_all[:rows], axis=0)
-    for at, piece in ((1, part0), (2, part1), (3, part2)):
-        lo = at * rows
-        d_gain_a = d_gain_a + jnp.sum(
-            piece.astype(full) * unit_all[lo : lo + piece.shape[0]], axis=0
-        )
-
-    tiny = jnp.concatenate([d_router, d_gain_a[None], d_gain_f[None], d_const], axis=0)
-    tiny = tiny.reshape(4, 2, 2, ctx_n, rows_d).transpose(0, 3, 1, 2, 4).reshape(4, ctx_n, 2, 2 * rows_d)
-    tiny = jnp.where(tp == 0, tiny, tiny[:, :, ::-1]).reshape(4, ctx_n, 1, width).astype(low)
-    shared = jnp.stack([d_weight_q, d_weight_k, d_weight_v, d_weight_o.astype(low)])
-    shared = shared.reshape(4, ctx_n, rows_d, width)
-    room = jnp.zeros((4, ctx_n, 15, width), low)
-    shared = jnp.concatenate([shared, tiny, room], axis=2)
-    shared_mine, shared_other = shared[..., :part], shared[..., part:]
-
-    def hop(x, at):
-        return lax.ppermute(x, "ctx", [(at, at - 1)])
-
-    came0, came1, came2 = hop(part0, 3), hop(part1, 3), hop(part2, 3)
-    came0, came1, came2, held = lax.optimization_barrier((came0, came1, came2, shared_other))
-    part0 = plus(part0, came0)
-    shared = plus(shared_mine, swap(shared_other))
-    came0 = pin(hop(part0, 2), shared)
-    part1 = plus(part1, came1)
-    came1 = hop(part1, 2)
-    part2 = plus(part2, came2)
-    part0 = plus(part0, came0)
-    came0 = hop(part0, 1)
-    part1 = plus(part1, came1)
-    def numbered(k):
-        return lax.dynamic_index_in_dim(shared, shard ^ k, 0, keepdims=False)
-
-    total = numbered(0).astype(full)
-    for k in range(1, shards_n):
-        total = total + flip(numbered(k), "shard", k, shards_n).astype(full)
-    came0 = pin(came0, total)
-    part0 = plus(part0, came0)
-    part2 = jnp.concatenate([part2, jnp.zeros((rows - edge, width), low)], axis=0)
-    extra = jnp.where(ctx == 0, part0, jnp.where(ctx == 1, part1, part2)).astype(full)
-    extra = jnp.where(ctx == 3, 0.0, extra)
-    d_normed = d_near + extra
-    unit_own, inv_own = unit_all[:rows], inv_all[:rows]
-    d_first = d_normed * gain_a
-    d_tokens = d_mixed + inv_own * (
-        d_first - unit_own * jnp.mean(d_first * unit_own, axis=-1, keepdims=True)
-    )
-
-    total = turn_sum(total.astype(low), ctx_n, ctx).astype(low)
     four = jnp.stack([total] + [flip(total, "shard", k, shards_n) for k in range(1, shards_n)])
     four = jnp.stack(
         [lax.dynamic_index_in_dim(four, m ^ shard, 0, keepdims=False) for m in range(4)]
@@ -1082,10 +1364,18 @@
     tiny = four[:, rows_d]
     tiny = both_trees(tiny, swap(tiny)).transpose(1, 0, 2).reshape(16, rows_d).astype(full)
 
-    out_far = pin(out_far, dq)
-    pieces = [o[0] for o in out_got] + [out_far[k] for k in range(shards_n)]
-    combined = gather(pin(place, shared_other), pieces, capacity, gates_both.T)[0]
-    combined = in_order(combined[:rows], swap(combined[rows:]), 1).astype(full)
+    out_got = [pin(o, plane_parts[0]) for o in out_got]
+    pieces = [o[0] for o in out_got] + [o[1] for o in out_got]
+    gate_columns = jnp.stack([gates_both[0], gates_both[1]], axis=1)
+    combined, combined_other = gather(place, pieces, capacity, gate_columns)
+    combined = in_order(combined, swap(combined_other), 1).astype(full)
+    second_f = second.astype(full)
+
+    def gate_of(number):
+        return jnp.sum(jnp.where(ids == number, stat[:, :2], 0.0), axis=1, keepdims=True)
+
+    copy_gate = gate_of(experts + 1)
+    const_gate = jnp.concatenate([gate_of(experts + 2), gate_of(experts + 3)], axis=1)
     mixed_out = (
         mixed
         + combined

time: 638 us -> 568 us (0.89)
  Pallas kernels: 140 us -> 212 us
  waiting for transfers between devices: 184 us -> 133 us
  starting transfers between devices: 124 us -> 84.9 us
  matrix products: 37.5 us -> 0 us
  other arithmetic: 92.4 us -> 63.7 us
  local copies, waits for them, and re-layouts: 47.3 us -> 64.2 us
    pallas_call x2 -> x7, Pallas kernels: 49.4 us -> 109 us  [call(): pl.pallas_call(kernel, grid_spec=spec, out_shape=[jax.ShapeDtypeStruct(*o...]
    dot_general x21 -> x0, matrix products: 37.5 us -> none  [the longest x18 34.8 us: mm(): return lax.dot_general(a, b, dims, preferred_element_type=jnp.float32)]
    ppermute x3, starting transfers between devices: 31.4 us -> 3.83 us  [turn_sum(): got = lax.ppermute(block, 'ctx', [(i, (i + k) % size) for i in range(size)])]
    ppermute x46, waiting for transfers between devices: 125 us -> 99.9 us  [flip(): return lax.ppermute(x, axis, [(i, i ^ bit) for i in range(size)])]
    unnamed x154 -> x169, local copies, waits for them, and re-layouts: 14.7 us -> 30.3 us
    ppermute x8, waiting for transfers between devices: 36.1 us -> 26 us  [far(): return lax.ppermute(x, ('shard', 'ctx'), pairs)]
    reduce_sum x9 -> x1, other arithmetic: 9.29 us -> 1.32 us  [gate_of(): jnp.sum(jnp.where(ids == number, stat[:, :2], 0.0), axis=1, keepdims=True)]
    ppermute x6 -> x3, waiting for transfers between devices: 7.94 us -> 0.01 us  [turn_gather(): block = lax.ppermute(x, 'ctx', [(i, (i + k) % size) for i in range(size)])]
  transfers between devices with their start and end apart: 73 -> 66, of which waited for: 30 -> 24; matrix products, arithmetic and copies ran while one was open for 26% -> 17% of each run, Pallas kernels for 13% -> 36%
where the time goes in v3:
time: 568 us; the launch traced here: 560 us
  Pallas kernels  212 us (37%)
  waiting for transfers between devices  133 us (23%)
  starting transfers between devices  84.9 us (15%)
  local copies, waits for them, and re-layouts  64.2 us (11%)
  other arithmetic  63.7 us (11%)
    pallas_call x7, Pallas kernels, call(): pl.pallas_call(kernel, grid_spec=spec, out_shape=[jax.ShapeDtypeStruct(*o...  109 us
    ppermute x46, waiting for transfers between devices, flip(): return lax.ppermute(x, axis, [(i, i ^ bit) for i in range(size)])  99.9 us
    ppermute x46, starting transfers between devices, flip(): return lax.ppermute(x, axis, [(i, i ^ bit) for i in range(size)])  50.2 us
    pallas_call x3, Pallas kernels, attend_back(): pl.pallas_call(functools.partial(attend_back_kernel, own, seg, HEAD_DIM,...  44.3 us
    pallas_call x2, Pallas kernels, attend(): pl.pallas_call(functools.partial(attend_kernel, own, seg, HEAD_DIM, len(p...  32.2 us
    unnamed x169, local copies, waits for them, and re-layouts  30.3 us
    ppermute x8, waiting for transfers between devices, far(): return lax.ppermute(x, ('shard', 'ctx'), pairs)  26 us
    pallas_call x2, Pallas kernels, gather(): pl.pallas_call(functools.partial(gather_kernel, len(pieces), padded, capa...  14.7 us
  transfers between devices with their start and end apart: 66, of which 24 were waited for; matrix products, arithmetic and copies ran while one was open for 17% of the time, Pallas kernels for 36%

profile of v3, /device:TPU:0, one launch (start us, length us, event | category | flops | bytes accessed | tf_op | source)
XLA Modules:
  0.0 560.3 jit_solution(923246405729813471)
XLA Ops:
  16.0 5.2 convert_reduce_fusion
  31.1 7.1 %collective-permute-done.near = bf16[640,768]{1,0:T(8,128)(2,1)} collective-permute-done((bf16[640,768]{1,0:T(8,128)(2,1)S(1)}, bf16[640,768]{1,0:T(8,128)(2,1)}, u32[]{:S(2)}, u32[]{:S(2)}) %collective-permute-start) | collective-permute-done | bytes 983072 | tf_op jit(solution)/shard_map/ppermute | solution.py:1112
  47.7 8.2 %collective-permute-done.7 = bf16[768,384]{1,0:T(8,128)(2,1)} collective-permute-done((bf16[768,384]{1,0:T(8,128)(2,1)S(1)}, bf16[768,384]{1,0:T(8,128)(2,1)}, u32[]{:S(2)}, u32[]{:S(2)}) %collective-permute-start.7) | collective-permute-done | bytes 589856 | tf_op jit(solution)/shard_map/ppermute | solution.py:1026
  64.0 11.4 %collective-permute-start.10 = (bf16[4,224,384]{2,1,0:T(8,128)(2,1)}, bf16[4,224,384]{2,1,0:T(8,128)(2,1)}, u32[]{:S(2)}, u32[]{:S(2)}) collective-permute-start(bf16[4,224,384]{2,1,0:T(8,128)(2,1)} %pad_maximum_fusion.9), channel_id=1, source_target_pairs={{0,4},{2,6},{4,0},{6,2},{1,5},{3,7},{5,1},{7,3},{8,12},{10,14},{12... | collective-permute-start | bytes 2064392 | tf_op jit(solution)/shard_map/ppermute | solution.py:1026
  79.4 23.3 %collective-permute-done.10 = bf16[4,224,384]{2,1,0:T(8,128)(2,1)} collective-permute-done((bf16[4,224,384]{2,1,0:T(8,128)(2,1)}, bf16[4,224,384]{2,1,0:T(8,128)(2,1)}, u32[]{:S(2)}, u32[]{:S(2)}) %collective-permute-start.10) | collective-permute-done | bytes 688160 | tf_op jit(solution)/shard_map/ppermute | solution.py:1026
  110.8 15.0 %project.1 = (bf16[640,768]{1,0:T(8,128)(2,1)S(1)}, bf16[2176,1536]{1,0:T(8,128)(2,1)}, bf16[2176,768]{1,0:T(8,128)(2,1)S(1)}, bf16[2176,768]{1,0:T(8,128)(2,1)}) custom-call(s32[3]{0:T(128)S(1)} %pad_add_fusion.1.place, bf16[640,768]{1,0:T(8,128)(2,1)S(1)} %dynamic-slice_bitcast_fusion.2.x0.x, bf16[640,768]{1,0:T(8,128)(2,1)} %collective-permute-done.near, ...), custom_call_target="tpu_custom_call" | custom-call | flops 1000 | bytes 1000 | tf_op jit(solution)/shard_map/project/pallas_call | solution.py:805
  128.5 16.3 %attend.2 = (bf16[640,768]{1,0:T(8,128)(2,1)}, f32[6,8,256]{2,1,0:T(8,128)}) custom-call(s32[5,3]{1,0:T(8,128)} %pad_add_fusion.info, bf16[640,768]{1,0:T(8,128)(2,1)} %copy-done.7, bf16[2176,1536]{1,0:T(8,128)(2,1)} %get-tuple-element.127.k_ref.v_ref, bf16[2176,1536]{1,0:T(8,128)(2,1)} %get-tuple-element.127.k_ref.v_ref), custom_call_target="tpu_custom_call" | custom-call | flops 1000 | bytes 1000 | tf_op jit(solution)/shard_map/attend/pallas_call | solution.py:510
  144.8 15.9 %attend.3 = (bf16[640,768]{1,0:T(8,128)(2,1)}, f32[6,8,256]{2,1,0:T(8,128)}) custom-call(s32[5,3]{1,0:T(8,128)} %pad_add_fusion.info, bf16[640,768]{1,0:T(8,128)(2,1)} %copy-done.7, bf16[2176,1536]{1,0:T(8,128)(2,1)} %get-tuple-element.127.k_ref.v_ref, ...), custom_call_target="tpu_custom_call", output_to_operand_aliasing={{0}: (4, {}), {1}: (5, {})} | custom-call | flops 1000 | bytes 1000 | tf_op jit(solution)/shard_map/attend/pallas_call | solution.py:510
  174.1 5.6 collective-permute-done.16
  185.2 7.1 %spread.3 = (bf16[224,384]{1,0:T(8,128)(2,1)}, bf16[224,384]{1,0:T(8,128)(2,1)}, bf16[224,384]{1,0:T(8,128)(2,1)}, bf16[224,384]{1,0:T(8,128)(2,1)}, bf16[224,38...) custom-call(s32[2,1280]{1,0:T(2,128)} %copy.167.place_ref, ...), custom_call_target="tpu_custom_call" | custom-call | flops 1000 | bytes 1000 | tf_op jit(solution)/shard_map/spread/pallas_call | solution.py:721
  213.6 22.5 %expert_pass.2 = (bf16[896,384]{1,0:T(8,128)(2,1)S(1)}, bf16[896,384]{1,0:T(8,128)(2,1)S(1)}, bf16[896,384]{1,0:T(8,128)(2,1)S(1)}, bf16[896,384]{1,0:T(8,128)(2,1)S(1)}, bf16[4,3,192,1024]{3,2,1,0:T(8,128)(2,1)}) custom-call(s32[2]{0:T(128)S(1)} %pad_add_fusion.2.place, bf16[896,384]{1,0:T(8,128)(2,1)S(1)} %constant_dynamic-update-slice_fusion.2.xm_ref, ...), custom_call_target="tpu_custom_call" | custom-call | flops 1000 | bytes 1000 | tf_op jit(solution)/shard_map/expert_pass/pallas_call | solution.py:805
  241.6 24.4 %expert_pass.3 = (bf16[896,384]{1,0:T(8,128)(2,1)S(1)}, bf16[896,384]{1,0:T(8,128)(2,1)S(1)}, bf16[896,384]{1,0:T(8,128)(2,1)S(1)}, bf16[896,384]{1,0:T(8,128)(2,1)S(1)}, bf16[4,3,192,1024]{3,2,1,0:T(8,128)(2,1)}) custom-call(s32[2]{0:T(128)S(1)} %pad_add_fusion.2.place, bf16[896,384]{1,0:T(8,128)(2,1)S(1)} %constant_dynamic-update-slice_fusion.6.xm_ref, ...), custom_call_target="tpu_custom_call" | custom-call | flops 1000 | bytes 1000 | tf_op jit(solution)/shard_map/expert_pass/pallas_call | solution.py:805
  280.3 11.4 %collective-permute-done.34.rest_4_ = bf16[224,384]{1,0:T(8,128)(2,1)S(1)} collective-permute-done((bf16[224,384]{1,0:T(8,128)(2,1)S(1)}, bf16[224,384]{1,0:T(8,128)(2,1)S(1)}, u32[]{:S(2)}, u32[]{:S(2)}) %collective-permute-start.34) | collective-permute-done | bytes 172064 | tf_op jit(solution)/shard_map/ppermute | solution.py:1052
  303.9 8.9 %gather.12 = (bf16[640,384]{1,0:T(8,128)(2,1)}, bf16[640,384]{1,0:T(8,128)(2,1)}, f32[640,2]{1,0:T(8,128)}, f32[640,2]{1,0:T(8,128)}) custom-call(s32[1280,2]{1,0:T(8,128)} %bitcast.217, bf16[224,384]{1,0:T(8,128)(2,1)} %get-tuple-element.325.rest_0_, bf16[224,384]{1,0:T(8,128)(2,1)} %copy-done.62, bf16[224,384]{1,0:T(8,128)(2,1)} %copy-done.63, ...), custom_call_target="tpu_custom_call" | custom-call | flops 1000 | bytes 1000 | tf_op jit(solution)/shard_map/gather/pallas_call | solution.py:772
  325.3 13.0 %settle_back.1 = (f32[640,768]{1,0:T(8,128)S(1)}, bf16[640,768]{1,0:T(8,128)(2,1)S(1)}, bf16[640,768]{1,0:T(8,128)(2,1)S(1)}, f32[640,12]{1,0:T(8,128)S(1)}, f32[16,768]{1,0:T(8,128)S(1)}) custom-call(s32[3]{0:T(128)S(1)} %pad_add_fusion.1.place, bf16[640,384]{1,0:T(8,128)(2,1)S(1)} %copy-done.42, bf16[640,384]{1,0:T(8,128)(2,1)S(1)} %collective-permute-done.40.dr_came, ...), custom_call_target="tpu_custom_call" | custom-call | flops 1000 | bytes 1000 | tf_op jit(solution)/shard_map/settle_back/pallas_call | solution.py:805
  338.4 15.5 %attend_back.3 = (bf16[640,768]{1,0:T(8,128)(2,1)S(1)}, bf16[2176,768]{1,0:T(8,128)(2,1)S(1)}, bf16[2176,768]{1,0:T(8,128)(2,1)S(1)}) custom-call(s32[5,3]{1,0:T(8,128)S(1)} %copy-done.48, bf16[640,768]{1,0:T(8,128)(2,1)S(1)} %copy-done.8, bf16[2176,1536]{1,0:T(8,128)(2,1)} %get-tuple-element.127.k_ref.v_ref, ...), custom_call_target="tpu_custom_call" | custom-call | flops 1000 | bytes 1000 | tf_op jit(solution)/shard_map/attend_back/pallas_call | solution.py:544
  356.7 14.3 %attend_back.4 = (bf16[640,768]{1,0:T(8,128)(2,1)S(1)}, bf16[2176,768]{1,0:T(8,128)(2,1)S(1)}, bf16[2176,768]{1,0:T(8,128)(2,1)S(1)}) custom-call(s32[5,3]{1,0:T(8,128)S(1)} %copy-done.48, bf16[640,768]{1,0:T(8,128)(2,1)S(1)} %copy-done.8, ...), custom_call_target="tpu_custom_call", output_to_operand_aliasing={{0}: (7, {}), {1}: (8, {}), {2}: (9, {})} | custom-call | flops 1000 | bytes 1000 | tf_op jit(solution)/shard_map/attend_back/pallas_call | solution.py:544
  377.1 14.5 %attend_back.5 = (bf16[640,768]{1,0:T(8,128)(2,1)S(1)}, bf16[2176,768]{1,0:T(8,128)(2,1)S(1)}, bf16[2176,768]{1,0:T(8,128)(2,1)S(1)}) custom-call(s32[5,3]{1,0:T(8,128)S(1)} %copy-done.48, bf16[640,768]{1,0:T(8,128)(2,1)S(1)} %copy-done.8, ...), custom_call_target="tpu_custom_call", output_to_operand_aliasing={{0}: (7, {}), {1}: (8, {}), {2}: (9, {})} | custom-call | flops 1000 | bytes 1000 | tf_op jit(solution)/shard_map/attend_back/pallas_call | solution.py:544
  393.3 13.7 %keys_back.1 = (f32[640,768]{1,0:T(8,128)S(1)}, bf16[640,768]{1,0:T(8,128)(2,1)}, bf16[640,768]{1,0:T(8,128)(2,1)S(1)}, bf16[256,768]{1,0:T(8,128)(2,1)S(1)}, f32[1,768]{1,0:T(1,128)S(1)}) custom-call(s32[3]{0:T(128)S(1)} %pad_add_fusion.1.place, bf16[640,768]{1,0:T(8,128)(2,1)S(1)} %get-tuple-element.193.dq, bf16[2176,768]{1,0:T(8,128)(2,1)S(1)} %get-tuple-element.196.dk, ...), custom_call_target="tpu_custom_call" | custom-call | flops 1000 | bytes 1000 | tf_op jit(solution)/shard_map/keys_back/pallas_call | solution.py:805
  411.9 18.3 %collective-permute-done.42 = bf16[4,224,384]{2,1,0:T(8,128)(2,1)S(1)} collective-permute-done((bf16[4,224,384]{2,1,0:T(8,128)(2,1)S(1)}, bf16[4,224,384]{2,1,0:T(8,128)(2,1)S(1)}, u32[]{:S(2)}, u32[]{:S(2)}) %collective-permute-start.42) | collective-permute-done | bytes 688160 | tf_op jit(solution)/shard_map/ppermute | solution.py:1026
  438.9 16.1 %weights_back.1 = (bf16[4,4,208,384]{3,2,1,0:T(8,128)(2,1)S(1)}, bf16[4,4,208,384]{3,2,1,0:T(8,128)(2,1)}) custom-call(bf16[2176,768]{1,0:T(8,128)(2,1)S(1)} %copy-done.28, bf16[640,768]{1,0:T(8,128)(2,1)S(1)} %copy-done.12, bf16[2176,768]{1,0:T(8,128)(2,1)} %copy-done.2, bf16[2176,768]{1,0:T(8,128)(2,1)} %copy-done.3, bf16[640,768]{1,0:T(8,128)(2,1)S(1)} %copy-done.36, ...), custom_call_target="tpu_custom_call" | custom-call | flops 1000 | bytes 1000 | tf_op jit(solution)/shard_map/weights_back/pallas_call | solution.py:805
  476.3 7.4 %collective-permute-done.50 = bf16[4,208,384]{2,1,0:T(8,128)(2,1)} collective-permute-done((bf16[4,208,384]{2,1,0:T(8,128)(2,1)}, bf16[4,208,384]{2,1,0:T(8,128)(2,1)}, u32[]{:S(2)}, u32[]{:S(2)}) %collective-permute-start.50) | collective-permute-done | bytes 639008 | tf_op jit(solution)/shard_map/ppermute | solution.py:1026
  483.7 12.5 %collective-permute-done.54 = bf16[4,208,384]{2,1,0:T(8,128)(2,1)} collective-permute-done((bf16[4,208,384]{2,1,0:T(8,128)(2,1)}, bf16[4,208,384]{2,1,0:T(8,128)(2,1)}, u32[]{:S(2)}, u32[]{:S(2)}) %collective-permute-start.54) | collective-permute-done | bytes 639008 | tf_op jit(solution)/shard_map/ppermute | solution.py:1026
  514.2 5.8 %gather.13 = (bf16[640,384]{1,0:T(8,128)(2,1)}, bf16[640,384]{1,0:T(8,128)(2,1)}) custom-call(s32[1280,2]{1,0:T(8,128)} %bitcast.218, f32[1280,2]{1,0:T(8,128)} %copy.181.rest_0_, bf16[224,384]{1,0:T(8,128)(2,1)} %get-tuple-element.349.rest_1_, bf16[224,384]{1,0:T(8,128)(2,1)} %get-tuple-element.347.rest_2_, bf16[224,384]{1,0:T(8,128)(2,1)} %get-tuple-element.345.rest_3_, ...), custom_call_target="tpu_custom_call" | custom-call | flops 1000 | bytes 1000 | tf_op jit(solution)/shard_map/gather/pallas_call | solution.py:772
  (432 shorter events, 244.3 us)
Async XLA Ops:
  11.3 26.9 %collective-permute-start = (bf16[640,768]{1,0:T(8,128)(2,1)S(1)}, bf16[640,768]{1,0:T(8,128)(2,1)}, u32[]{:S(2)}, u32[]{:S(2)}) collective-permute-start(bf16[640,768]{1,0:T(8,128)(2,1)S(1)} %dynamic-slice_bitcast_fusion.2.x0.x), channel_id=1, source_target_pairs={{0,2},{2,4},{4,6},{1,3},{3,5},{5,7},{8,10},{10,12},{12,14},{9,11},... | collective-permute-start | bytes 2949128 | tf_op jit(solution)/shard_map/ppermute | solution.py:1112
  28.7 27.1 %collective-permute-start.7 = (bf16[768,384]{1,0:T(8,128)(2,1)S(1)}, bf16[768,384]{1,0:T(8,128)(2,1)}, u32[]{:S(2)}, u32[]{:S(2)}) collective-permute-start(bf16[768,384]{1,0:T(8,128)(2,1)S(1)} %bitcast.221), channel_id=1, source_target_pairs={{0,16},{8,24},{16,0},{24,8},{1,17},{9,25},{17,1},{25,9},{2,18},{10... | collective-permute-start | bytes 1769480 | tf_op jit(solution)/shard_map/ppermute | solution.py:1026
  57.9 53.0 %collective-permute-start.9 = (bf16[4,768,384]{2,1,0:T(8,128)(2,1)S(1)}, bf16[4,768,384]{2,1,0:T(8,128)(2,1)}, u32[]{:S(2)}, u32[]{:S(2)}) collective-permute-start(bf16[4,768,384]{2,1,0:T(8,128)(2,1)S(1)} %pad_maximum_fusion.3.wm), channel_id=1, source_target_pairs={{0,1},{1,0},{2,3},{3,2},{4,5},{5,4},{6,7},{7,6},{8,9},{9,8},{10,11... | collective-permute-start | bytes 7077896 | tf_op jit(solution)/shard_map/ppermute | solution.py:1026
  60.1 42.6 %collective-permute-start.5 = (bf16[640,768]{1,0:T(8,128)(2,1)}, bf16[640,768]{1,0:T(8,128)(2,1)}, u32[]{:S(2)}, u32[]{:S(2)}) collective-permute-start(bf16[640,768]{1,0:T(8,128)(2,1)} %collective-permute-done.4.mid), channel_id=1, source_target_pairs={{4,6},{5,7},{12,14},{13,15},{20,22},{21,23},{28,30},{29,31}} | collective-permute-start | bytes 2949128 | tf_op jit(solution)/shard_map/ppermute | solution.py:1152
  64.0 38.7 %collective-permute-start.10 = (bf16[4,224,384]{2,1,0:T(8,128)(2,1)}, bf16[4,224,384]{2,1,0:T(8,128)(2,1)}, u32[]{:S(2)}, u32[]{:S(2)}) collective-permute-start(bf16[4,224,384]{2,1,0:T(8,128)(2,1)} %pad_maximum_fusion.9), channel_id=1, source_target_pairs={{0,4},{2,6},{4,0},{6,2},{1,5},{3,7},{5,1},{7,3},{8,12},{10,14},{12... | collective-permute-start | bytes 2064392 | tf_op jit(solution)/shard_map/ppermute | solution.py:1026
  102.7 58.0 %collective-permute-start.12 = (bf16[3,192,1024]{2,1,0:T(8,128)(2,1)}, bf16[3,192,1024]{2,1,0:T(8,128)(2,1)}, u32[]{:S(2)}, u32[]{:S(2)}) collective-permute-start(bf16[3,192,1024]{2,1,0:T(8,128)(2,1)} %get-tuple-element.134), channel_id=1, source_target_pairs={{0,4},{2,6},{4,0},{6,2},{1,5},{3,7},{5,1},{7,3},{8,12},{10,14},{12... | collective-permute-start | bytes 3538952 | tf_op jit(solution)/shard_map/ppermute | solution.py:1026
  106.7 54.0 %collective-permute-start.11 = (bf16[3,192,1024]{2,1,0:T(8,128)(2,1)}, bf16[3,192,1024]{2,1,0:T(8,128)(2,1)}, u32[]{:S(2)}, u32[]{:S(2)}) collective-permute-start(bf16[3,192,1024]{2,1,0:T(8,128)(2,1)} %get-tuple-element.133.w0), channel_id=1, source_target_pairs={{0,2},{2,0},{4,6},{6,4},{1,3},{3,1},{5,7},{7,5},{8,10},{10,8},{12,... | collective-permute-start | bytes 3538952 | tf_op jit(solution)/shard_map/ppermute | solution.py:1026
  160.7 35.1 %collective-permute-start.18 = (bf16[3,192,1024]{2,1,0:T(8,128)(2,1)}, bf16[3,192,1024]{2,1,0:T(8,128)(2,1)}, u32[]{:S(2)}, u32[]{:S(2)}) collective-permute-start(bf16[3,192,1024]{2,1,0:T(8,128)(2,1)} %collective-permute-done.12.w2), channel_id=1, source_target_pairs={{0,2},{2,0},{4,6},{6,4},{1,3},{3,1},{5,7},{7,5},{8,10},{10,8},{12,... | collective-permute-start | bytes 3538952 | tf_op jit(solution)/shard_map/ppermute | solution.py:1026
  181.2 29.5 %collective-permute-start.23 = (bf16[2,896,384]{2,1,0:T(8,128)(2,1)}, bf16[2,896,384]{2,1,0:T(8,128)(2,1)}, u32[]{:S(2)}, u32[]{:S(2)}) collective-permute-start(bf16[2,896,384]{2,1,0:T(8,128)(2,1)} %bitcast.54), channel_id=1, source_target_pairs={{0,1},{1,0},{2,3},{3,2},{4,5},{5,4},{6,7},{7,6},{8,9},{9,8},{10,11... | collective-permute-start | bytes 4128776 | tf_op jit(solution)/shard_map/ppermute | solution.py:1026
  204.4 31.7 %collective-permute-start.24 = (bf16[224,384]{1,0:T(8,128)(2,1)S(1)}, bf16[224,384]{1,0:T(8,128)(2,1)S(1)}, u32[]{:S(2)}, u32[]{:S(2)}) collective-permute-start(bf16[224,384]{1,0:T(8,128)(2,1)S(1)} %copy-done.77), channel_id=1, source_target_pairs={{0,4},{2,6},{4,0},{6,2},{8,12},{10,14},{12,8},{14,10},{16,20},{18,... | collective-permute-start | bytes 516104 | tf_op jit(solution)/shard_map/ppermute | solution.py:1052
  206.6 29.6 %collective-permute-start.25 = (bf16[224,384]{1,0:T(8,128)(2,1)S(1)}, bf16[224,384]{1,0:T(8,128)(2,1)S(1)}, u32[]{:S(2)}, u32[]{:S(2)}) collective-permute-start(bf16[224,384]{1,0:T(8,128)(2,1)S(1)} %copy-done.76), channel_id=1, source_target_pairs={{0,12},{2,14},{4,8},{6,10},{8,4},{10,6},{12,0},{14,2},{16,28},{18,... | collective-permute-start | bytes 516104 | tf_op jit(solution)/shard_map/ppermute | solution.py:1052
  207.5 28.6 %collective-permute-start.26 = (bf16[224,384]{1,0:T(8,128)(2,1)S(1)}, bf16[224,384]{1,0:T(8,128)(2,1)S(1)}, u32[]{:S(2)}, u32[]{:S(2)}) collective-permute-start(bf16[224,384]{1,0:T(8,128)(2,1)S(1)} %copy-done.75), channel_id=1, source_target_pairs={{0,20},{2,22},{4,16},{6,18},{8,28},{10,30},{12,24},{14,26},{16,4},... | collective-permute-start | bytes 516104 | tf_op jit(solution)/shard_map/ppermute | solution.py:1052
  210.7 28.5 %collective-permute-start.27 = (bf16[224,384]{1,0:T(8,128)(2,1)S(1)}, bf16[224,384]{1,0:T(8,128)(2,1)S(1)}, u32[]{:S(2)}, u32[]{:S(2)}) collective-permute-start(bf16[224,384]{1,0:T(8,128)(2,1)S(1)} %copy-done.74), channel_id=1, source_target_pairs={{0,28},{2,30},{4,24},{6,26},{8,20},{10,22},{12,16},{14,18},{16,12}... | collective-permute-start | bytes 516104 | tf_op jit(solution)/shard_map/ppermute | solution.py:1052
  239.4 26.8 %collective-permute-start.29 = (bf16[896,384]{1,0:T(8,128)(2,1)S(1)}, bf16[896,384]{1,0:T(8,128)(2,1)S(1)}, u32[]{:S(2)}, u32[]{:S(2)}) collective-permute-start(bf16[896,384]{1,0:T(8,128)(2,1)S(1)} %get-tuple-element.165), channel_id=1, source_target_pairs={{0,1},{1,0},{2,3},{3,2},{4,5},{5,4},{6,7},{7,6},{8,9},{9,8},{10,11... | collective-permute-start | bytes 2064392 | tf_op jit(solution)/shard_map/ppermute | solution.py:1026
  312.8 60.5 %collective-permute-start.43 = (bf16[2,3,192,1024]{3,2,1,0:T(8,128)(2,1)}, bf16[2,3,192,1024]{3,2,1,0:T(8,128)(2,1)}, u32[]{:S(2)}, u32[]{:S(2)}) collective-permute-start(bf16[2,3,192,1024]{3,2,1,0:T(8,128)(2,1)} %slice.269), channel_id=1, source_target_pairs={{0,2},{2,0},{4,6},{6,4},{1,3},{3,1},{5,7},{7,5},{8,10},{10,8},{12,... | collective-permute-start | bytes 7077896 | tf_op jit(solution)/shard_map/ppermute | solution.py:1026
  312.8 41.2 %collective-permute-start.39 = (bf16[896,384]{1,0:T(8,128)(2,1)}, bf16[896,384]{1,0:T(8,128)(2,1)}, u32[]{:S(2)}, u32[]{:S(2)}) collective-permute-start(bf16[896,384]{1,0:T(8,128)(2,1)} %copy-done.50), channel_id=1, source_target_pairs={{0,1},{1,0},{2,3},{3,2},{4,5},{5,4},{6,7},{7,6},{8,9},{9,8},{10,11... | collective-permute-start | bytes 2064392 | tf_op jit(solution)/shard_map/ppermute | solution.py:1026
  313.3 42.0 %collective-permute-start.38 = (bf16[896,384]{1,0:T(8,128)(2,1)}, bf16[896,384]{1,0:T(8,128)(2,1)}, u32[]{:S(2)}, u32[]{:S(2)}) collective-permute-start(bf16[896,384]{1,0:T(8,128)(2,1)} %copy-done.49), channel_id=1, source_target_pairs={{0,1},{1,0},{2,3},{3,2},{4,5},{5,4},{6,7},{7,6},{8,9},{9,8},{10,11... | collective-permute-start | bytes 2064392 | tf_op jit(solution)/shard_map/ppermute | solution.py:1026
  371.0 59.3 %collective-permute-start.42 = (bf16[4,224,384]{2,1,0:T(8,128)(2,1)S(1)}, bf16[4,224,384]{2,1,0:T(8,128)(2,1)S(1)}, u32[]{:S(2)}, u32[]{:S(2)}) collective-permute-start(bf16[4,224,384]{2,1,0:T(8,128)(2,1)S(1)} %bitcast.224), channel_id=1, source_target_pairs={{0,4},{2,6},{4,0},{6,2},{1,5},{3,7},{5,1},{7,3},{8,12},{10,14},{12... | collective-permute-start | bytes 2064392 | tf_op jit(solution)/shard_map/ppermute | solution.py:1026
  376.4 80.1 %collective-permute-start.48 = (bf16[3,192,1024]{2,1,0:T(8,128)(2,1)}, bf16[3,192,1024]{2,1,0:T(8,128)(2,1)}, u32[]{:S(2)}, u32[]{:S(2)}) collective-permute-start(bf16[3,192,1024]{2,1,0:T(8,128)(2,1)} %fusion.12), channel_id=1, source_target_pairs={{0,4},{2,6},{4,0},{6,2},{1,5},{3,7},{5,1},{7,3},{8,12},{10,14},{12... | collective-permute-start | bytes 3538952 | tf_op jit(solution)/shard_map/ppermute | solution.py:1026
  410.2 46.3 %collective-permute-start.44 = (bf16[640,768]{1,0:T(8,128)(2,1)}, bf16[640,768]{1,0:T(8,128)(2,1)}, u32[]{:S(2)}, u32[]{:S(2)}) collective-permute-start(bf16[640,768]{1,0:T(8,128)(2,1)} %get-tuple-element.204), channel_id=1, source_target_pairs={{6,4},{7,5},{14,12},{15,13},{22,20},{23,21},{30,28},{31,29}} | collective-permute-start | bytes 2949128 | tf_op jit(solution)/shard_map/ppermute | solution.py:1322
  466.8 29.4 %collective-permute-start.54 = (bf16[4,208,384]{2,1,0:T(8,128)(2,1)}, bf16[4,208,384]{2,1,0:T(8,128)(2,1)}, u32[]{:S(2)}, u32[]{:S(2)}) collective-permute-start(bf16[4,208,384]{2,1,0:T(8,128)(2,1)} %get-tuple-element.285), channel_id=1, source_target_pairs={{0,16},{8,24},{16,0},{24,8},{1,17},{9,25},{17,1},{25,9},{2,18},{10... | collective-permute-start | bytes 1916936 | tf_op jit(solution)/shard_map/ppermute | solution.py:1026
  468.5 28.4 %collective-permute-start.55 = (bf16[4,208,384]{2,1,0:T(8,128)(2,1)}, bf16[4,208,384]{2,1,0:T(8,128)(2,1)}, u32[]{:S(2)}, u32[]{:S(2)}) collective-permute-start(bf16[4,208,384]{2,1,0:T(8,128)(2,1)} %get-tuple-element.286), channel_id=1, source_target_pairs={{0,24},{8,16},{16,8},{24,0},{1,25},{9,17},{17,9},{25,1},{2,26},{10... | collective-permute-start | bytes 1916936 | tf_op jit(solution)/shard_map/ppermute | solution.py:1026
  472.5 31.0 %collective-permute-start.53 = (bf16[640,768]{1,0:T(8,128)(2,1)}, bf16[640,768]{1,0:T(8,128)(2,1)}, u32[]{:S(2)}, u32[]{:S(2)}) collective-permute-start(bf16[640,768]{1,0:T(8,128)(2,1)} %fusion.16), channel_id=1, source_target_pairs={{4,2},{6,4},{5,3},{7,5},{12,10},{14,12},{13,11},{15,13},{20,18},{2... | collective-permute-start | bytes 2949128 | tf_op jit(solution)/shard_map/ppermute | solution.py:1322
  506.4 32.0 %collective-permute-start.56 = (bf16[640,768]{1,0:T(8,128)(2,1)}, bf16[640,768]{1,0:T(8,128)(2,1)}, u32[]{:S(2)}, u32[]{:S(2)}) collective-permute-start(bf16[640,768]{1,0:T(8,128)(2,1)} %pad_select_fusion), channel_id=1, source_target_pairs={{2,0},{4,2},{6,4},{3,1},{5,3},{7,5},{10,8},{12,10},{14,12},{11,9},... | collective-permute-start | bytes 2949128 | tf_op jit(solution)/shard_map/ppermute | solution.py:1322
  (121 other events, 1351.8 us)

commit v4 on v3

--- a/solution.py
+++ b/solution.py
@@ -435,7 +435,7 @@
         lse_ref[pl.ds(i, 1), :] = top + jnp.log(total)
         return 0
 
-    lax.fori_loop(0, own // seg, one, 0)
+    lax.fori_loop(0, own // seg, one, 0, unroll=True)
 
 
 def attend_back_kernel(
@@ -497,7 +497,7 @@
         dq_ref[here, :] = (unstack(dq, half, seg) * 0.125).T.astype(low)
         return 0
 
-    lax.fori_loop(0, own // seg, one, 0)
+    lax.fori_loop(0, own // seg, one, 0, unroll=True)
     dk_ref[...] = ak[...].astype(low)
     dv_ref[...] = av[...].astype(low)
 
@@ -734,7 +734,7 @@
     if dots:
         ins, (out_ref, out2_ref, dot_ref, dot2_ref) = rest[:pieces], rest[pieces:]
     else:
-        gate_ref, ins, (out_ref, out2_ref) = rest[0], rest[1 : 1 + pieces], rest[1 + pieces :]
+        gate_ref, ins, (out_ref, out2_ref) = rest[0], rest[1 : 1 + pieces // 2], rest[1 + pieces // 2 :]
     tokens = place_ref.shape[0]
     total = None
     sums = [0.0, 0.0]
@@ -751,7 +751,7 @@
         else:
             pick = jnp.where(hits[0], gate_ref[:, 0:1], jnp.where(hits[1], gate_ref[:, 1:2], 0.0))
             pick = pick.astype(low)
-        part = mm(pick, ins[p][...])
+        part = mm(pick, ins[p][...] if dots else ins[p % 4][p // 4])
         total = part if total is None else total + part
     rows = tokens // 2
     out_ref[...] = total[:rows].astype(low)
@@ -763,14 +763,15 @@
 
 
 def gather(place, pieces, capacity, gate=None):
-    padded, width = pieces[0].shape
+    padded, width = pieces[0].shape[-2:]
+    number = sum(p.size // (padded * width) for p in pieces)
     tokens = place.shape[0]
     dots = gate is None
     shapes = [jax.ShapeDtypeStruct((tokens // 2, width), jnp.bfloat16)] * 2
     if dots:
         shapes = shapes + [jax.ShapeDtypeStruct((tokens // 2, 2), jnp.float32)] * 2
     return pl.pallas_call(
-        functools.partial(gather_kernel, len(pieces), padded, capacity, dots),
+        functools.partial(gather_kernel, number, padded, capacity, dots),
         in_specs=[pl.BlockSpec(memory_space=pltpu.VMEM)] * (len(pieces) + (1 if dots else 2)),
         out_specs=[pl.BlockSpec(memory_space=pltpu.VMEM)] * len(shapes),
         out_shape=shapes,
@@ -1206,14 +1207,11 @@
     info = jnp.stack([jnp.minimum(seg_id, TRUNK), jnp.where(leaf > 0, parent, TRUNK), leaf], axis=1)
     half_pairs = width // 256
     ahead = attend(info, q, kv, seg, 0, half_pairs)
-    g_seen = pin(g_far, ahead[0])
     o_low, lse = attend(info, q, kv, seg, half_pairs, half_pairs, ahead)
-    o_low = pin(o_low, rows_one, rows_two)
-
-    g_pairs = jnp.stack([g_near, g_seen], axis=1)
-    g_in = jnp.stack(
-        [g_pairs[0]] + [flip(g_pairs[k], "shard", k, shards_n) for k in range(1, shards_n)], axis=1
-    ).reshape(2, shards_n * padded, part)
+    g_pairs = jnp.stack([g_near, pin(g_far, ahead[0])], axis=1)
+    g_got = [g_pairs[0]] + [flip(g_pairs[k], "shard", k, shards_n) for k in range(1, shards_n)]
+    o_low = pin(o_low, rows_one, rows_two, *g_got)
+    g_in = jnp.stack(g_got, axis=1).reshape(2, shards_n * padded, part)
     g_out = swap(g_in)
 
     one_half = ((rows, part), low)
@@ -1236,7 +1234,7 @@
 
     rows_three = flip(pin(rows_two, o_low), "ctx", 1, ctx_n)
     weights = (rows_own, rows_one, rows_two, rows_three)
-    slots = spread(place_t, pin(second_half, g_in), experts, padded, capacity, gates_both)
+    slots = spread(place_t, second_half, experts, padded, capacity, gates_both)
     x_far = [far(slots[shards_n + k], k, shards_n, ctx_n) for k in range(shards_n)]
     x_near = [slots[0]] + [flip(slots[k], "shard", k, shards_n) for k in range(1, shards_n)]
 
@@ -1284,17 +1282,18 @@
     out_far = plus(on2, swap(ox2)).reshape(shards_n, padded, part)
 
     got = flip(pin(dw[2:], d_routed), "ctx", 1, ctx_n)
-    sent_rows = (dw[1].astype(full) + got[1].astype(full)).astype(low)
-    came_rows = flip(sent_rows, "ctx", 2, ctx_n)
 
     third = width // 384
     back = attend_back(info, q, kv, o_low, d_o, lse, seg, 0, third)
-    q_later = pin(q, out_far, out_near, back[0])
+    out_near, out_far, q_later, held = lax.optimization_barrier((out_near, out_far, q, back[0]))
     back = attend_back(info, q_later, kv, o_low, d_o, lse, seg, third, third, back)
-    out_near, out_far = lax.optimization_barrier((out_near, out_far, back[0]))[:2]
+    out_near, out_far = (out_near, out_far)
     out_cross = flip(out_far, "ctx", 2, ctx_n)
-    q_later = pin(q, sent_rows, back[0])
+    q_later = pin(q, back[0])
     dq, dk, dv = attend_back(info, q_later, kv, o_low, d_o, lse, seg, 2 * third, third, back)
+    got = pin(got, dq)
+    sent_rows = plus(dw[1], got[1])
+    came_rows = flip(sent_rows, "ctx", 2, ctx_n)
     out_pairs = jnp.stack([out_near, pin(out_cross, dq)], axis=1)
     out_got = [out_pairs[0]] + [flip(out_pairs[k], "shard", k, shards_n) for k in range(1, shards_n)]
     d_near, part0, part1, part2, d_gain_a = call(
@@ -1304,7 +1303,7 @@
             ((rows, width), full), ((rows, width), low), ((rows, width), low), ((edge, width), low),
             ((1, width), full),
         ],
-        (place3, dq, dk, dv, x_all, plane, plane_other),
+        (pin(place3, sent_rows), dq, dk, dv, x_all, plane, plane_other),
         in_specs=[
             whole(rows, width), whole(total, width), whole(total, width), whole(total, width),
             whole(4, width, part), whole(4, width, part),
@@ -1323,8 +1322,9 @@
 
     came = down(part0, 1)
     shared_other = pin(shared_other, came, *out_got, came_rows)
-    came = down(jnp.where(ctx == 3, part1, plus(part0, came)), 2)
-    shared = plus(shared_mine, swap(shared_other))
+    payload = jnp.where(ctx == 3, part1, plus(part0, came))
+    came = down(payload, 2)
+    shared = plus(pin(shared_mine, payload), swap(shared_other))
 
     def numbered(k):
         return lax.dynamic_index_in_dim(shared, shard ^ k, 0, keepdims=False)
@@ -1333,11 +1333,19 @@
     plane_sum = numbered(0).astype(full)
     for got_part in plane_parts:
         plane_sum = plane_sum + got_part.astype(full)
-    came = pin(came, plane_sum)
+    came = pin(came, plane_parts[0])
     part2 = jnp.pad(part2, ((0, rows - edge), (0, 0)))
     came = down(jnp.where(ctx == 3, part2, jnp.where(ctx == 2, plus(part1, came), plus(part0, came))), 3)
     base = jnp.where(ctx == 0, part0, jnp.where(ctx == 1, part1, part2)).astype(full)
     extra = jnp.where(ctx == 3, 0.0, base + came.astype(full))
+    came_rows = pin(came_rows, plane_parts[0]).astype(full)
+    kept_rows = dw[0].astype(full) + got[0].astype(full)
+    first = jnp.where(lower, kept_rows, came_rows)
+    second_e = jnp.where(lower, came_rows, kept_rows)
+    d_gate_up = jnp.stack(
+        [jnp.stack([first[0], first[1]], axis=1), jnp.stack([second_e[0], second_e[1]], axis=1)], axis=1
+    )
+    d_down = jnp.stack([first[2], second_e[2]], axis=1)
     d_normed = d_near + extra
     unit_own, inv_own = unit_of(x_own)
     gain_a = gain_a[0]
@@ -1347,27 +1355,9 @@
     )
 
     total = turn_sum(plane_sum.astype(low), ctx_n, ctx).astype(low)
-    came_rows = pin(came_rows, total).astype(full)
-    kept_rows = dw[0].astype(full) + got[0].astype(full)
-    first = jnp.where(lower, kept_rows, came_rows)
-    second_e = jnp.where(lower, came_rows, kept_rows)
-    d_gate_up = jnp.stack(
-        [jnp.stack([first[0], first[1]], axis=1), jnp.stack([second_e[0], second_e[1]], axis=1)], axis=1
-    )
-    d_down = jnp.stack([first[2], second_e[2]], axis=1)
-    four = jnp.stack([total] + [flip(total, "shard", k, shards_n) for k in range(1, shards_n)])
-    four = jnp.stack(
-        [lax.dynamic_index_in_dim(four, m ^ shard, 0, keepdims=False) for m in range(4)]
-    )
-    d_q, d_k, d_v, d_w_out = [four[m, :rows_d].astype(full) for m in range(4)]
-    d_w_qkv = jnp.stack([d_q, d_k, d_v], axis=1)
-    tiny = four[:, rows_d]
-    tiny = both_trees(tiny, swap(tiny)).transpose(1, 0, 2).reshape(16, rows_d).astype(full)
-
     out_got = [pin(o, plane_parts[0]) for o in out_got]
-    pieces = [o[0] for o in out_got] + [o[1] for o in out_got]
     gate_columns = jnp.stack([gates_both[0], gates_both[1]], axis=1)
-    combined, combined_other = gather(place, pieces, capacity, gate_columns)
+    combined, combined_other = gather(place, out_got, capacity, gate_columns)
     combined = in_order(combined, swap(combined_other), 1).astype(full)
     second_f = second.astype(full)
 
@@ -1383,6 +1373,16 @@
         + const_gate[:, :1] * const_t[0][None]
         + const_gate[:, 1:] * const_t[1][None]
     )
+    total = pin(total, mixed_out, d_tokens)
+    four = jnp.stack([total] + [flip(total, "shard", k, shards_n) for k in range(1, shards_n)])
+    four = jnp.stack(
+        [lax.dynamic_index_in_dim(four, m ^ shard, 0, keepdims=False) for m in range(4)]
+    )
+    d_q, d_k, d_v, d_w_out = [four[m, :rows_d].astype(full) for m in range(4)]
+    d_w_qkv = jnp.stack([d_q, d_k, d_v], axis=1)
+    tiny = four[:, rows_d]
+    tiny = both_trees(tiny, swap(tiny)).transpose(1, 0, 2).reshape(16, rows_d).astype(full)
+
     return (
         both_trees(mixed_out, swap(mixed_out)),
         both_trees(d_tokens, swap(d_tokens)),

time: 568 us -> 547 us (0.963)
  Pallas kernels: 212 us -> 193 us
  local copies, waits for them, and re-layouts: 64.2 us -> 56.9 us
  waiting for transfers between devices: 133 us -> 140 us
    ppermute x3, waiting for transfers between devices: 0.01 us -> 20 us  [turn_sum(): got = lax.ppermute(block, 'ctx', [(i, (i + k) % size) for i in range(size)])]
    ppermute x46, waiting for transfers between devices: 99.9 us -> 85.7 us  [flip(): return lax.ppermute(x, axis, [(i, i ^ bit) for i in range(size)])]
    pallas_call x2, Pallas kernels: 32.2 us -> 21.3 us  [attend(): pl.pallas_call(functools.partial(attend_kernel, own, seg, HEAD_DIM, len(p...]
    pallas_call x3, Pallas kernels: 44.3 us -> 37.6 us  [attend_back(): pl.pallas_call(functools.partial(attend_back_kernel, own, seg, HEAD_DIM,...]
    squeeze x4 -> x0, local copies, waits for them, and re-layouts: 6.06 us -> none  [by_core(): pieces = [o[0] for o in out_got] + [o[1] for o in out_got]]
    unnamed x169 -> x171, local copies, waits for them, and re-layouts: 30.3 us -> 31.1 us
  transfers between devices with their start and end apart: 66 -> 66, of which waited for: 24 -> 26; matrix products, arithmetic and copies ran while one was open for 17% -> 17% of each run, Pallas kernels for 36% -> 34%
where the time goes in v4:
time: 547 us; the launch traced here: 539 us
  Pallas kernels  193 us (35%)
  waiting for transfers between devices  140 us (26%)
  starting transfers between devices  81.5 us (15%)
  other arithmetic  64.8 us (12%)
  local copies, waits for them, and re-layouts  56.9 us (10%)
    pallas_call x7, Pallas kernels, call(): pl.pallas_call(kernel, grid_spec=spec, out_shape=[jax.ShapeDtypeStruct(*o...  108 us
    ppermute x46, waiting for transfers between devices, flip(): return lax.ppermute(x, axis, [(i, i ^ bit) for i in range(size)])  85.7 us
    ppermute x46, starting transfers between devices, flip(): return lax.ppermute(x, axis, [(i, i ^ bit) for i in range(size)])  46.9 us
    pallas_call x3, Pallas kernels, attend_back(): pl.pallas_call(functools.partial(attend_back_kernel, own, seg, HEAD_DIM,...  37.6 us
    unnamed x171, local copies, waits for them, and re-layouts  31.1 us
    ppermute x8, waiting for transfers between devices, far(): return lax.ppermute(x, ('shard', 'ctx'), pairs)  25.6 us
    pallas_call x2, Pallas kernels, attend(): pl.pallas_call(functools.partial(attend_kernel, own, seg, HEAD_DIM, len(p...  21.3 us
    ppermute x3, waiting for transfers between devices, turn_sum(): got = lax.ppermute(block, 'ctx', [(i, (i + k) % size) for i in range(size)])  20 us
  transfers between devices with their start and end apart: 66, of which 26 were waited for; matrix products, arithmetic and copies ran while one was open for 17% of the time, Pallas kernels for 34%

profile of v4, /device:TPU:0, one launch (start us, length us, event | category | flops | bytes accessed | tf_op | source)
XLA Modules:
  0.0 538.7 jit_solution(15467210829730689669)
XLA Ops:
  29.9 8.4 %collective-permute-done.near = bf16[640,768]{1,0:T(8,128)(2,1)} collective-permute-done((bf16[640,768]{1,0:T(8,128)(2,1)S(1)}, bf16[640,768]{1,0:T(8,128)(2,1)}, u32[]{:S(2)}, u32[]{:S(2)}) %collective-permute-start) | collective-permute-done | bytes 983072 | tf_op jit(solution)/shard_map/ppermute | solution.py:1113
  42.2 10.7 %collective-permute-done.7 = bf16[768,384]{1,0:T(8,128)(2,1)} collective-permute-done((bf16[768,384]{1,0:T(8,128)(2,1)S(1)}, bf16[768,384]{1,0:T(8,128)(2,1)}, u32[]{:S(2)}, u32[]{:S(2)}) %collective-permute-start.7) | collective-permute-done | bytes 589856 | tf_op jit(solution)/shard_map/ppermute | solution.py:1027
  66.9 8.9 %collective-permute-start.10 = (bf16[4,224,384]{2,1,0:T(8,128)(2,1)}, bf16[4,224,384]{2,1,0:T(8,128)(2,1)}, u32[]{:S(2)}, u32[]{:S(2)}) collective-permute-start(bf16[4,224,384]{2,1,0:T(8,128)(2,1)} %pad_maximum_fusion.9), channel_id=1, source_target_pairs={{0,4},{2,6},{4,0},{6,2},{1,5},{3,7},{5,1},{7,3},{8,12},{10,14},{12... | collective-permute-start | bytes 2064392 | tf_op jit(solution)/shard_map/ppermute | solution.py:1027
  79.8 23.3 %collective-permute-done.10 = bf16[4,224,384]{2,1,0:T(8,128)(2,1)} collective-permute-done((bf16[4,224,384]{2,1,0:T(8,128)(2,1)}, bf16[4,224,384]{2,1,0:T(8,128)(2,1)}, u32[]{:S(2)}, u32[]{:S(2)}) %collective-permute-start.10) | collective-permute-done | bytes 688160 | tf_op jit(solution)/shard_map/ppermute | solution.py:1027
  103.1 6.1 %collective-permute-start.12 = (bf16[3,192,1024]{2,1,0:T(8,128)(2,1)}, bf16[3,192,1024]{2,1,0:T(8,128)(2,1)}, u32[]{:S(2)}, u32[]{:S(2)}) collective-permute-start(bf16[3,192,1024]{2,1,0:T(8,128)(2,1)} %get-tuple-element.137), channel_id=1, source_target_pairs={{0,4},{2,6},{4,0},{6,2},{1,5},{3,7},{5,1},{7,3},{8,12},{10,14},{12... | collective-permute-start | bytes 3538952 | tf_op jit(solution)/shard_map/ppermute | solution.py:1027
  112.8 15.0 %project.1 = (bf16[640,768]{1,0:T(8,128)(2,1)S(1)}, bf16[2176,1536]{1,0:T(8,128)(2,1)}, bf16[2176,768]{1,0:T(8,128)(2,1)S(1)}, bf16[2176,768]{1,0:T(8,128)(2,1)}) custom-call(s32[3]{0:T(128)S(1)} %pad_add_fusion.1.place, bf16[640,768]{1,0:T(8,128)(2,1)S(1)} %dynamic-slice_bitcast_fusion.2.x0.x, bf16[640,768]{1,0:T(8,128)(2,1)} %collective-permute-done.near, ...), custom_call_target="tpu_custom_call" | custom-call | flops 1000 | bytes 1000 | tf_op jit(solution)/shard_map/project/pallas_call | solution.py:806
  130.4 10.6 %attend.2 = (bf16[640,768]{1,0:T(8,128)(2,1)}, f32[6,8,256]{2,1,0:T(8,128)}) custom-call(s32[5,3]{1,0:T(8,128)} %pad_add_fusion.info, bf16[640,768]{1,0:T(8,128)(2,1)} %copy-done.7, bf16[2176,1536]{1,0:T(8,128)(2,1)} %get-tuple-element.130.k_ref.v_ref, bf16[2176,1536]{1,0:T(8,128)(2,1)} %get-tuple-element.130.k_ref.v_ref), custom_call_target="tpu_custom_call" | custom-call | flops 1000 | bytes 1000 | tf_op jit(solution)/shard_map/attend/pallas_call | solution.py:510
  147.5 10.7 %attend.3 = (bf16[640,768]{1,0:T(8,128)(2,1)}, f32[6,8,256]{2,1,0:T(8,128)}) custom-call(s32[5,3]{1,0:T(8,128)} %pad_add_fusion.info, bf16[640,768]{1,0:T(8,128)(2,1)} %copy-done.7, bf16[2176,1536]{1,0:T(8,128)(2,1)} %get-tuple-element.130.k_ref.v_ref, ...), custom_call_target="tpu_custom_call", output_to_operand_aliasing={{0}: (4, {}), {1}: (5, {})} | custom-call | flops 1000 | bytes 1000 | tf_op jit(solution)/shard_map/attend/pallas_call | solution.py:510
  174.4 7.1 %spread.3 = (bf16[224,384]{1,0:T(8,128)(2,1)}, bf16[224,384]{1,0:T(8,128)(2,1)}, bf16[224,384]{1,0:T(8,128)(2,1)}, bf16[224,384]{1,0:T(8,128)(2,1)}, bf16[224,38...) custom-call(s32[2,1280]{1,0:T(2,128)} %copy.167.place_ref, ...), custom_call_target="tpu_custom_call" | custom-call | flops 1000 | bytes 1000 | tf_op jit(solution)/shard_map/spread/pallas_call | solution.py:721
  202.8 22.7 %expert_pass.2 = (bf16[896,384]{1,0:T(8,128)(2,1)S(1)}, bf16[896,384]{1,0:T(8,128)(2,1)S(1)}, bf16[896,384]{1,0:T(8,128)(2,1)S(1)}, bf16[896,384]{1,0:T(8,128)(2,1)S(1)}, bf16[4,3,192,1024]{3,2,1,0:T(8,128)(2,1)}) custom-call(s32[2]{0:T(128)S(1)} %pad_add_fusion.2.place, bf16[896,384]{1,0:T(8,128)(2,1)S(1)} %constant_dynamic-update-slice_fusion.2.xm_ref, ...), custom_call_target="tpu_custom_call" | custom-call | flops 1000 | bytes 1000 | tf_op jit(solution)/shard_map/expert_pass/pallas_call | solution.py:806
  230.7 24.4 %expert_pass.3 = (bf16[896,384]{1,0:T(8,128)(2,1)S(1)}, bf16[896,384]{1,0:T(8,128)(2,1)S(1)}, bf16[896,384]{1,0:T(8,128)(2,1)S(1)}, bf16[896,384]{1,0:T(8,128)(2,1)S(1)}, bf16[4,3,192,1024]{3,2,1,0:T(8,128)(2,1)}) custom-call(s32[2]{0:T(128)S(1)} %pad_add_fusion.2.place, bf16[896,384]{1,0:T(8,128)(2,1)S(1)} %constant_dynamic-update-slice_fusion.6.xm_ref, ...), custom_call_target="tpu_custom_call" | custom-call | flops 1000 | bytes 1000 | tf_op jit(solution)/shard_map/expert_pass/pallas_call | solution.py:806
  269.5 11.1 %collective-permute-done.34.rest_4_ = bf16[224,384]{1,0:T(8,128)(2,1)S(1)} collective-permute-done((bf16[224,384]{1,0:T(8,128)(2,1)S(1)}, bf16[224,384]{1,0:T(8,128)(2,1)S(1)}, u32[]{:S(2)}, u32[]{:S(2)}) %collective-permute-start.34) | collective-permute-done | bytes 172064 | tf_op jit(solution)/shard_map/ppermute | solution.py:1053
  292.9 8.9 %gather.12 = (bf16[640,384]{1,0:T(8,128)(2,1)}, bf16[640,384]{1,0:T(8,128)(2,1)}, f32[640,2]{1,0:T(8,128)}, f32[640,2]{1,0:T(8,128)}) custom-call(s32[1280,2]{1,0:T(8,128)} %bitcast.201, bf16[224,384]{1,0:T(8,128)(2,1)} %get-tuple-element.331.rest_0_, bf16[224,384]{1,0:T(8,128)(2,1)} %copy-done.64, bf16[224,384]{1,0:T(8,128)(2,1)} %copy-done.65, ...), custom_call_target="tpu_custom_call" | custom-call | flops 1000 | bytes 1000 | tf_op jit(solution)/shard_map/gather/pallas_call | solution.py:773
  314.3 12.8 %settle_back.1 = (f32[640,768]{1,0:T(8,128)S(1)}, bf16[640,768]{1,0:T(8,128)(2,1)S(1)}, bf16[640,768]{1,0:T(8,128)(2,1)S(1)}, f32[640,12]{1,0:T(8,128)S(1)}, f32[16,768]{1,0:T(8,128)S(1)}) custom-call(s32[3]{0:T(128)S(1)} %pad_add_fusion.1.place, bf16[640,384]{1,0:T(8,128)(2,1)S(1)} %copy-done.43, bf16[640,384]{1,0:T(8,128)(2,1)S(1)} %collective-permute-done.40.dr_came, ...), custom_call_target="tpu_custom_call" | custom-call | flops 1000 | bytes 1000 | tf_op jit(solution)/shard_map/settle_back/pallas_call | solution.py:806
  327.2 13.2 %attend_back.3 = (bf16[640,768]{1,0:T(8,128)(2,1)S(1)}, bf16[2176,768]{1,0:T(8,128)(2,1)S(1)}, bf16[2176,768]{1,0:T(8,128)(2,1)S(1)}) custom-call(s32[5,3]{1,0:T(8,128)S(1)} %copy-done.49, bf16[640,768]{1,0:T(8,128)(2,1)S(1)} %copy-done.8, bf16[2176,1536]{1,0:T(8,128)(2,1)} %get-tuple-element.130.k_ref.v_ref, ...), custom_call_target="tpu_custom_call" | custom-call | flops 1000 | bytes 1000 | tf_op jit(solution)/shard_map/attend_back/pallas_call | solution.py:544
  345.6 12.3 %attend_back.4 = (bf16[640,768]{1,0:T(8,128)(2,1)S(1)}, bf16[2176,768]{1,0:T(8,128)(2,1)S(1)}, bf16[2176,768]{1,0:T(8,128)(2,1)S(1)}) custom-call(s32[5,3]{1,0:T(8,128)S(1)} %copy-done.49, bf16[640,768]{1,0:T(8,128)(2,1)S(1)} %copy-done.8, ...), custom_call_target="tpu_custom_call", output_to_operand_aliasing={{0}: (7, {}), {1}: (8, {}), {2}: (9, {})} | custom-call | flops 1000 | bytes 1000 | tf_op jit(solution)/shard_map/attend_back/pallas_call | solution.py:544
  357.9 12.1 %attend_back.5 = (bf16[640,768]{1,0:T(8,128)(2,1)S(1)}, bf16[2176,768]{1,0:T(8,128)(2,1)S(1)}, bf16[2176,768]{1,0:T(8,128)(2,1)S(1)}) custom-call(s32[5,3]{1,0:T(8,128)S(1)} %copy-done.49, bf16[640,768]{1,0:T(8,128)(2,1)S(1)} %copy-done.8, ...), custom_call_target="tpu_custom_call", output_to_operand_aliasing={{0}: (7, {}), {1}: (8, {}), {2}: (9, {})} | custom-call | flops 1000 | bytes 1000 | tf_op jit(solution)/shard_map/attend_back/pallas_call | solution.py:544
  377.0 12.7 %keys_back.1 = (f32[640,768]{1,0:T(8,128)S(1)}, bf16[640,768]{1,0:T(8,128)(2,1)}, bf16[640,768]{1,0:T(8,128)(2,1)S(1)}, bf16[256,768]{1,0:T(8,128)(2,1)S(1)}, f32[1,768]{1,0:T(1,128)S(1)}) custom-call(s32[3]{0:T(128)S(1)} %pad_add_fusion.1.place, bf16[640,768]{1,0:T(8,128)(2,1)S(1)} %get-tuple-element.193.dq, bf16[2176,768]{1,0:T(8,128)(2,1)S(1)} %get-tuple-element.196.dk, ...), custom_call_target="tpu_custom_call" | custom-call | flops 1000 | bytes 1000 | tf_op jit(solution)/shard_map/keys_back/pallas_call | solution.py:806
  403.3 16.1 %weights_back.1 = (bf16[4,4,208,384]{3,2,1,0:T(8,128)(2,1)S(1)}, bf16[4,4,208,384]{3,2,1,0:T(8,128)(2,1)}) custom-call(bf16[2176,768]{1,0:T(8,128)(2,1)S(1)} %copy-done.28, bf16[640,768]{1,0:T(8,128)(2,1)S(1)} %copy-done.12, bf16[2176,768]{1,0:T(8,128)(2,1)} %copy-done.2, bf16[2176,768]{1,0:T(8,128)(2,1)} %copy-done.3, bf16[640,768]{1,0:T(8,128)(2,1)S(1)} %copy-done.37, ...), custom_call_target="tpu_custom_call" | custom-call | flops 1000 | bytes 1000 | tf_op jit(solution)/shard_map/weights_back/pallas_call | solution.py:806
  420.9 9.7 %collective-permute-done.48 = bf16[3,192,1024]{2,1,0:T(8,128)(2,1)} collective-permute-done((bf16[3,192,1024]{2,1,0:T(8,128)(2,1)}, bf16[3,192,1024]{2,1,0:T(8,128)(2,1)}, u32[]{:S(2)}, u32[]{:S(2)}) %collective-permute-start.48) | collective-permute-done | bytes 1179680 | tf_op jit(solution)/shard_map/ppermute | solution.py:1027
  447.7 10.7 %collective-permute-done.50 = bf16[4,208,384]{2,1,0:T(8,128)(2,1)} collective-permute-done((bf16[4,208,384]{2,1,0:T(8,128)(2,1)}, bf16[4,208,384]{2,1,0:T(8,128)(2,1)}, u32[]{:S(2)}, u32[]{:S(2)}) %collective-permute-start.50) | collective-permute-done | bytes 639008 | tf_op jit(solution)/shard_map/ppermute | solution.py:1027
  458.4 5.8 %gather.13 = (bf16[640,384]{1,0:T(8,128)(2,1)}, bf16[640,384]{1,0:T(8,128)(2,1)}) custom-call(s32[1280,2]{1,0:T(8,128)} %bitcast.202, f32[1280,2]{1,0:T(8,128)} %copy.181.rest_0_, bf16[2,224,384]{2,1,0:T(8,128)(2,1)} %get-tuple-element.212.rest_1_, bf16[2,224,384]{2,1,0:T(8,128)(2,1)} %collective-permute-done.45.rest_2_, ...), custom_call_target="tpu_custom_call" | custom-call | flops 1000 | bytes 1000 | tf_op jit(solution)/shard_map/gather/pallas_call | solution.py:773
  484.8 12.2 %collective-permute-done.61 = bf16[208,384]{1,0:T(8,128)(2,1)S(1)} collective-permute-done((bf16[208,384]{1,0:T(8,128)(2,1)S(1)}, bf16[208,384]{1,0:T(8,128)(2,1)S(1)}, u32[]{:S(2)}, u32[]{:S(2)}) %collective-permute-start.61) | collective-permute-done | bytes 159776 | tf_op jit(solution)/shard_map/ppermute | solution.py:1043
  497.0 7.8 %collective-permute-done.60 = bf16[208,384]{1,0:T(8,128)(2,1)S(1)} collective-permute-done((bf16[208,384]{1,0:T(8,128)(2,1)S(1)}, bf16[208,384]{1,0:T(8,128)(2,1)S(1)}, u32[]{:S(2)}, u32[]{:S(2)}) %collective-permute-start.60) | collective-permute-done | bytes 159776 | tf_op jit(solution)/shard_map/ppermute | solution.py:1043
  (430 shorter events, 242.9 us)
Async XLA Ops:
  11.3 26.9 %collective-permute-start = (bf16[640,768]{1,0:T(8,128)(2,1)S(1)}, bf16[640,768]{1,0:T(8,128)(2,1)}, u32[]{:S(2)}, u32[]{:S(2)}) collective-permute-start(bf16[640,768]{1,0:T(8,128)(2,1)S(1)} %dynamic-slice_bitcast_fusion.2.x0.x), channel_id=1, source_target_pairs={{0,2},{2,4},{4,6},{1,3},{3,5},{5,7},{8,10},{10,12},{12,14},{9,11},... | collective-permute-start | bytes 2949128 | tf_op jit(solution)/shard_map/ppermute | solution.py:1113
  54.9 57.9 %collective-permute-start.9 = (bf16[4,768,384]{2,1,0:T(8,128)(2,1)S(1)}, bf16[4,768,384]{2,1,0:T(8,128)(2,1)}, u32[]{:S(2)}, u32[]{:S(2)}) collective-permute-start(bf16[4,768,384]{2,1,0:T(8,128)(2,1)S(1)} %pad_maximum_fusion.3.wm), channel_id=1, source_target_pairs={{0,1},{1,0},{2,3},{3,2},{4,5},{5,4},{6,7},{7,6},{8,9},{9,8},{10,11... | collective-permute-start | bytes 7077896 | tf_op jit(solution)/shard_map/ppermute | solution.py:1027
  62.6 40.5 %collective-permute-start.5 = (bf16[640,768]{1,0:T(8,128)(2,1)}, bf16[640,768]{1,0:T(8,128)(2,1)}, u32[]{:S(2)}, u32[]{:S(2)}) collective-permute-start(bf16[640,768]{1,0:T(8,128)(2,1)} %collective-permute-done.4.mid), channel_id=1, source_target_pairs={{4,6},{5,7},{12,14},{13,15},{20,22},{21,23},{28,30},{29,31}} | collective-permute-start | bytes 2949128 | tf_op jit(solution)/shard_map/ppermute | solution.py:1153
  66.9 36.2 %collective-permute-start.10 = (bf16[4,224,384]{2,1,0:T(8,128)(2,1)}, bf16[4,224,384]{2,1,0:T(8,128)(2,1)}, u32[]{:S(2)}, u32[]{:S(2)}) collective-permute-start(bf16[4,224,384]{2,1,0:T(8,128)(2,1)} %pad_maximum_fusion.9), channel_id=1, source_target_pairs={{0,4},{2,6},{4,0},{6,2},{1,5},{3,7},{5,1},{7,3},{8,12},{10,14},{12... | collective-permute-start | bytes 2064392 | tf_op jit(solution)/shard_map/ppermute | solution.py:1027
  103.1 56.9 %collective-permute-start.11 = (bf16[3,192,1024]{2,1,0:T(8,128)(2,1)}, bf16[3,192,1024]{2,1,0:T(8,128)(2,1)}, u32[]{:S(2)}, u32[]{:S(2)}) collective-permute-start(bf16[3,192,1024]{2,1,0:T(8,128)(2,1)} %get-tuple-element.136.w0), channel_id=1, source_target_pairs={{0,2},{2,0},{4,6},{6,4},{1,3},{3,1},{5,7},{7,5},{8,10},{10,8},{12,... | collective-permute-start | bytes 3538952 | tf_op jit(solution)/shard_map/ppermute | solution.py:1027
  103.1 56.9 %collective-permute-start.12 = (bf16[3,192,1024]{2,1,0:T(8,128)(2,1)}, bf16[3,192,1024]{2,1,0:T(8,128)(2,1)}, u32[]{:S(2)}, u32[]{:S(2)}) collective-permute-start(bf16[3,192,1024]{2,1,0:T(8,128)(2,1)} %get-tuple-element.137), channel_id=1, source_target_pairs={{0,4},{2,6},{4,0},{6,2},{1,5},{3,7},{5,1},{7,3},{8,12},{10,14},{12... | collective-permute-start | bytes 3538952 | tf_op jit(solution)/shard_map/ppermute | solution.py:1027
  170.5 28.6 %collective-permute-start.23 = (bf16[2,896,384]{2,1,0:T(8,128)(2,1)}, bf16[2,896,384]{2,1,0:T(8,128)(2,1)}, u32[]{:S(2)}, u32[]{:S(2)}) collective-permute-start(bf16[2,896,384]{2,1,0:T(8,128)(2,1)} %bitcast.55), channel_id=1, source_target_pairs={{0,1},{1,0},{2,3},{3,2},{4,5},{5,4},{6,7},{7,6},{8,9},{9,8},{10,11... | collective-permute-start | bytes 4128776 | tf_op jit(solution)/shard_map/ppermute | solution.py:1027
  193.6 31.9 %collective-permute-start.24 = (bf16[224,384]{1,0:T(8,128)(2,1)S(1)}, bf16[224,384]{1,0:T(8,128)(2,1)S(1)}, u32[]{:S(2)}, u32[]{:S(2)}) collective-permute-start(bf16[224,384]{1,0:T(8,128)(2,1)S(1)} %copy-done.78), channel_id=1, source_target_pairs={{0,4},{2,6},{4,0},{6,2},{8,12},{10,14},{12,8},{14,10},{16,20},{18,... | collective-permute-start | bytes 516104 | tf_op jit(solution)/shard_map/ppermute | solution.py:1053
  195.2 30.3 %collective-permute-start.25 = (bf16[224,384]{1,0:T(8,128)(2,1)S(1)}, bf16[224,384]{1,0:T(8,128)(2,1)S(1)}, u32[]{:S(2)}, u32[]{:S(2)}) collective-permute-start(bf16[224,384]{1,0:T(8,128)(2,1)S(1)} %copy-done.77), channel_id=1, source_target_pairs={{0,12},{2,14},{4,8},{6,10},{8,4},{10,6},{12,0},{14,2},{16,28},{18,... | collective-permute-start | bytes 516104 | tf_op jit(solution)/shard_map/ppermute | solution.py:1053
  196.7 28.8 %collective-permute-start.26 = (bf16[224,384]{1,0:T(8,128)(2,1)S(1)}, bf16[224,384]{1,0:T(8,128)(2,1)S(1)}, u32[]{:S(2)}, u32[]{:S(2)}) collective-permute-start(bf16[224,384]{1,0:T(8,128)(2,1)S(1)} %copy-done.76), channel_id=1, source_target_pairs={{0,20},{2,22},{4,16},{6,18},{8,28},{10,30},{12,24},{14,26},{16,4},... | collective-permute-start | bytes 516104 | tf_op jit(solution)/shard_map/ppermute | solution.py:1053
  199.1 29.3 %collective-permute-start.27 = (bf16[224,384]{1,0:T(8,128)(2,1)S(1)}, bf16[224,384]{1,0:T(8,128)(2,1)S(1)}, u32[]{:S(2)}, u32[]{:S(2)}) collective-permute-start(bf16[224,384]{1,0:T(8,128)(2,1)S(1)} %copy-done.75), channel_id=1, source_target_pairs={{0,28},{2,30},{4,24},{6,26},{8,20},{10,22},{12,16},{14,18},{16,12}... | collective-permute-start | bytes 516104 | tf_op jit(solution)/shard_map/ppermute | solution.py:1053
  228.6 26.8 %collective-permute-start.29 = (bf16[896,384]{1,0:T(8,128)(2,1)S(1)}, bf16[896,384]{1,0:T(8,128)(2,1)S(1)}, u32[]{:S(2)}, u32[]{:S(2)}) collective-permute-start(bf16[896,384]{1,0:T(8,128)(2,1)S(1)} %get-tuple-element.167), channel_id=1, source_target_pairs={{0,1},{1,0},{2,3},{3,2},{4,5},{5,4},{6,7},{7,6},{8,9},{9,8},{10,11... | collective-permute-start | bytes 2064392 | tf_op jit(solution)/shard_map/ppermute | solution.py:1027
  266.9 25.3 %collective-permute-start.37 = (bf16[224,384]{1,0:T(8,128)(2,1)S(1)}, bf16[224,384]{1,0:T(8,128)(2,1)S(1)}, u32[]{:S(2)}, u32[]{:S(2)}) collective-permute-start(bf16[224,384]{1,0:T(8,128)(2,1)S(1)} %get-tuple-element.324), channel_id=1, source_target_pairs={{0,28},{2,30},{4,24},{6,26},{8,20},{10,22},{12,16},{14,18},{16,12}... | collective-permute-start | bytes 516104 | tf_op jit(solution)/shard_map/ppermute | solution.py:1053
  301.8 70.0 %collective-permute-start.43 = (bf16[2,3,192,1024]{3,2,1,0:T(8,128)(2,1)}, bf16[2,3,192,1024]{3,2,1,0:T(8,128)(2,1)}, u32[]{:S(2)}, u32[]{:S(2)}) collective-permute-start(bf16[2,3,192,1024]{3,2,1,0:T(8,128)(2,1)} %slice.247), channel_id=1, source_target_pairs={{0,2},{2,0},{4,6},{6,4},{1,3},{3,1},{5,7},{7,5},{8,10},{10,8},{12,... | collective-permute-start | bytes 7077896 | tf_op jit(solution)/shard_map/ppermute | solution.py:1027
  301.8 38.7 %collective-permute-start.38 = (bf16[896,384]{1,0:T(8,128)(2,1)}, bf16[896,384]{1,0:T(8,128)(2,1)}, u32[]{:S(2)}, u32[]{:S(2)}) collective-permute-start(bf16[896,384]{1,0:T(8,128)(2,1)} %copy-done.50), channel_id=1, source_target_pairs={{0,1},{1,0},{2,3},{3,2},{4,5},{5,4},{6,7},{7,6},{8,9},{9,8},{10,11... | collective-permute-start | bytes 2064392 | tf_op jit(solution)/shard_map/ppermute | solution.py:1027
  302.4 39.5 %collective-permute-start.39 = (bf16[896,384]{1,0:T(8,128)(2,1)}, bf16[896,384]{1,0:T(8,128)(2,1)}, u32[]{:S(2)}, u32[]{:S(2)}) collective-permute-start(bf16[896,384]{1,0:T(8,128)(2,1)} %copy-done.51), channel_id=1, source_target_pairs={{0,1},{1,0},{2,3},{3,2},{4,5},{5,4},{6,7},{7,6},{8,9},{9,8},{10,11... | collective-permute-start | bytes 2064392 | tf_op jit(solution)/shard_map/ppermute | solution.py:1027
  343.1 51.6 %collective-permute-start.42 = (bf16[4,224,384]{2,1,0:T(8,128)(2,1)S(1)}, bf16[4,224,384]{2,1,0:T(8,128)(2,1)S(1)}, u32[]{:S(2)}, u32[]{:S(2)}) collective-permute-start(bf16[4,224,384]{2,1,0:T(8,128)(2,1)S(1)} %bitcast.209), channel_id=1, source_target_pairs={{0,4},{2,6},{4,0},{6,2},{1,5},{3,7},{5,1},{7,3},{8,12},{10,14},{12... | collective-permute-start | bytes 2064392 | tf_op jit(solution)/shard_map/ppermute | solution.py:1027
  376.5 54.1 %collective-permute-start.48 = (bf16[3,192,1024]{2,1,0:T(8,128)(2,1)}, bf16[3,192,1024]{2,1,0:T(8,128)(2,1)}, u32[]{:S(2)}, u32[]{:S(2)}) collective-permute-start(bf16[3,192,1024]{2,1,0:T(8,128)(2,1)} %fusion.13), channel_id=1, source_target_pairs={{0,4},{2,6},{4,0},{6,2},{1,5},{3,7},{5,1},{7,3},{8,12},{10,14},{12... | collective-permute-start | bytes 3538952 | tf_op jit(solution)/shard_map/ppermute | solution.py:1027
  392.9 28.0 %collective-permute-start.44 = (bf16[640,768]{1,0:T(8,128)(2,1)}, bf16[640,768]{1,0:T(8,128)(2,1)}, u32[]{:S(2)}, u32[]{:S(2)}) collective-permute-start(bf16[640,768]{1,0:T(8,128)(2,1)} %get-tuple-element.208), channel_id=1, source_target_pairs={{6,4},{7,5},{14,12},{15,13},{22,20},{23,21},{30,28},{31,29}} | collective-permute-start | bytes 2949128 | tf_op jit(solution)/shard_map/ppermute | solution.py:1321
  435.2 29.1 %collective-permute-start.53 = (bf16[640,768]{1,0:T(8,128)(2,1)}, bf16[640,768]{1,0:T(8,128)(2,1)}, u32[]{:S(2)}, u32[]{:S(2)}) collective-permute-start(bf16[640,768]{1,0:T(8,128)(2,1)} %fusion.17), channel_id=1, source_target_pairs={{4,2},{6,4},{5,3},{7,5},{12,10},{14,12},{13,11},{15,13},{20,18},{2... | collective-permute-start | bytes 2949128 | tf_op jit(solution)/shard_map/ppermute | solution.py:1321
  443.8 28.3 %collective-permute-start.58 = (bf16[4,208,384]{2,1,0:T(8,128)(2,1)}, bf16[4,208,384]{2,1,0:T(8,128)(2,1)}, u32[]{:S(2)}, u32[]{:S(2)}) collective-permute-start(bf16[4,208,384]{2,1,0:T(8,128)(2,1)} %get-tuple-element.292), channel_id=1, source_target_pairs={{0,24},{8,16},{16,8},{24,0},{1,25},{9,17},{17,9},{25,1},{2,26},{10... | collective-permute-start | bytes 1916936 | tf_op jit(solution)/shard_map/ppermute | solution.py:1027
  445.5 30.3 %collective-permute-start.57 = (bf16[4,208,384]{2,1,0:T(8,128)(2,1)}, bf16[4,208,384]{2,1,0:T(8,128)(2,1)}, u32[]{:S(2)}, u32[]{:S(2)}) collective-permute-start(bf16[4,208,384]{2,1,0:T(8,128)(2,1)} %get-tuple-element.291), channel_id=1, source_target_pairs={{0,16},{8,24},{16,0},{24,8},{1,17},{9,25},{17,1},{25,9},{2,18},{10... | collective-permute-start | bytes 1916936 | tf_op jit(solution)/shard_map/ppermute | solution.py:1027
  464.3 40.6 %collective-permute-start.51 = (bf16[640,384]{1,0:T(8,128)(2,1)}, bf16[640,384]{1,0:T(8,128)(2,1)S(1)}, u32[]{:S(2)}, u32[]{:S(2)}) collective-permute-start(bf16[640,384]{1,0:T(8,128)(2,1)} %get-tuple-element.217), channel_id=1, source_target_pairs={{0,1},{1,0},{2,3},{3,2},{4,5},{5,4},{6,7},{7,6},{8,9},{9,8},{10,11... | collective-permute-start | bytes 1474568 | tf_op jit(solution)/shard_map/ppermute | solution.py:1027
  466.3 40.8 %collective-permute-start.54 = (bf16[640,768]{1,0:T(8,128)(2,1)S(1)}, bf16[640,768]{1,0:T(8,128)(2,1)S(1)}, u32[]{:S(2)}, u32[]{:S(2)}) collective-permute-start(bf16[640,768]{1,0:T(8,128)(2,1)S(1)} %pad_select_fusion), channel_id=1, source_target_pairs={{2,0},{4,2},{6,4},{3,1},{5,3},{7,5},{10,8},{12,10},{14,12},{11,9},... | collective-permute-start | bytes 2949128 | tf_op jit(solution)/shard_map/ppermute | solution.py:1321
  (122 other events, 1259.5 us)

commit v5 on v4

--- a/solution.py
+++ b/solution.py
@@ -729,12 +729,67 @@
     )(place, rows, *([parts] if gated else []))
 
 
-def gather_kernel(pieces, padded, capacity, dots, place_ref, *rest):
-    low = jnp.bfloat16
+def expert_of(where_ref, piece):
+    upper = jnp.where(where_ref[1] >= 2, 1, 0)
+    return (2 * ((piece % 4) ^ where_ref[0]) + ((piece // 4) ^ upper)).astype(jnp.float32)
+
+
+def spread_gated_kernel(pieces, padded, capacity, gated, where_ref, place_ref, rows_ref, *rest):
+    low, full = jnp.bfloat16, jnp.float32
+    tokens, width = rows_ref.shape
+    if gated:
+        gates_ref, outs, wide_ref = rest[0], rest[1:-1], rest[-1]
+        lines = []
+        for c in range(2):
+            value = gates_ref[c : c + 1, :]
+            for i in range(3):
+                lines.append(value.astype(low).astype(full))
+                value = value - lines[-1]
+        lines = lines + [gates_ref[4:5, :], jnp.zeros((121, tokens), full)]
+        wide_ref[:, :width] = rows_ref[...]
+        wide_ref[:, width:] = jnp.concatenate(lines, axis=0).T.astype(low)
+    else:
+        outs, wide_ref = rest, rows_ref
+    for p in range(pieces):
+        slot = lax.broadcasted_iota(jnp.int32, (padded, tokens), 0) + p * padded
+        hit = (slot == place_ref[0:1, :]) | (slot == place_ref[1:2, :])
+        out = mm(jnp.where(hit, 1.0, 0.0).astype(low), wide_ref[...])
+        if gated:
+            extra = out[:, width:].T
+            out = out[:, :width].astype(low)
+            row = lax.broadcasted_iota(jnp.int32, out.shape, 0)
+            blank = jnp.zeros((1, width - padded), full)
+            for i in range(3):
+                picked = jnp.where(
+                    extra[6:7, :] == expert_of(where_ref, p), extra[i : i + 1, :], extra[3 + i : 4 + i, :]
+                )
+                picked = jnp.concatenate([picked, blank], axis=1).astype(low)
+                out = jnp.where(row == capacity + i, picked, out)
+        outs[p][...] = out.astype(low)
+
+
+def spread_gated(where, place, rows, pieces, padded, capacity, gates=None):
+    shape = jax.ShapeDtypeStruct((padded, rows.shape[1]), jnp.bfloat16)
+    gated = gates is not None
+    return pl.pallas_call(
+        functools.partial(spread_gated_kernel, pieces, padded, capacity, gated),
+        in_specs=[pl.BlockSpec(memory_space=pltpu.SMEM)]
+        + [pl.BlockSpec(memory_space=pltpu.VMEM)] * (2 + gated),
+        out_specs=[pl.BlockSpec(memory_space=pltpu.VMEM)] * pieces,
+        out_shape=[shape] * pieces,
+        scratch_shapes=[pltpu.VMEM((rows.shape[0], rows.shape[1] + 128), jnp.bfloat16)] * gated,
+        compiler_params=pltpu.CompilerParams(vmem_limit_bytes=40 << 20),
+        cost_estimate=pl.CostEstimate(flops=1000, bytes_accessed=1000, transcendentals=0),
+        name="spread",
+    )(where, place, rows, *([gates] if gated else []))
+
+
+def gather_kernel(pieces, padded, capacity, dots, where_ref, place_ref, pair_ref, *rest):
+    low, full = jnp.bfloat16, jnp.float32
     if dots:
         ins, (out_ref, out2_ref, dot_ref, dot2_ref) = rest[:pieces], rest[pieces:]
     else:
-        gate_ref, ins, (out_ref, out2_ref) = rest[0], rest[1 : 1 + pieces // 2], rest[1 + pieces // 2 :]
+        ins, (out_ref, out2_ref) = rest[: pieces // 2], rest[pieces // 2 :]
     tokens = place_ref.shape[0]
     total = None
     sums = [0.0, 0.0]
@@ -742,16 +797,22 @@
         slot = lax.broadcasted_iota(jnp.int32, (tokens, padded), 1) + p * padded
         hits = [slot == place_ref[:, c : c + 1] for c in range(2)]
         if dots:
-            picks = [jnp.where(h, 1.0, 0.0).astype(low) for h in hits]
-            values = ins[p][capacity : capacity + 3, :padded]
-            values = jnp.concatenate([values, jnp.zeros((13, padded), low)], axis=0)
-            for c in range(2):
-                sums[c] = sums[c] + mm(picks[c], values, NT)
-            pick = picks[0] + picks[1]
+            source = ins[p][...]
+            width = source.shape[1]
+            values = ins[p][padded - 16 :, :padded].astype(full)
+            values = jnp.concatenate([values, jnp.zeros((112, padded), full)], axis=0).T
+            source = jnp.concatenate([source, values.astype(low)], axis=1)
+            part = mm(jnp.where(hits[0] | hits[1], 1.0, 0.0).astype(low), source)
+            lane = lax.broadcasted_iota(jnp.int32, (tokens, 128), 1)
+            lane = lane + (padded - 16 - capacity)
+            dot = jnp.where((lane >= 0) & (lane < 3), part[:, width:], 0.0)
+            mine = pair_ref[:, 0:1] == expert_of(where_ref, p)
+            sums[0] = sums[0] + jnp.where(mine, dot, 0.0)
+            sums[1] = sums[1] + jnp.where(mine, 0.0, dot)
+            part = part[:, :width]
         else:
-            pick = jnp.where(hits[0], gate_ref[:, 0:1], jnp.where(hits[1], gate_ref[:, 1:2], 0.0))
-            pick = pick.astype(low)
-        part = mm(pick, ins[p][...] if dots else ins[p % 4][p // 4])
+            pick = jnp.where(hits[0], pair_ref[:, 0:1], jnp.where(hits[1], pair_ref[:, 1:2], 0.0))
+            part = mm(pick.astype(low), ins[p % 4][p // 4])
         total = part if total is None else total + part
     rows = tokens // 2
     out_ref[...] = total[:rows].astype(low)
@@ -762,23 +823,23 @@
             dot2_ref[:, c : c + 1] = jnp.sum(sums[c][rows:], axis=1, keepdims=True)
 
 
-def gather(place, pieces, capacity, gate=None):
+def gather(where, place, pair, pieces, capacity, dots):
     padded, width = pieces[0].shape[-2:]
     number = sum(p.size // (padded * width) for p in pieces)
     tokens = place.shape[0]
-    dots = gate is None
     shapes = [jax.ShapeDtypeStruct((tokens // 2, width), jnp.bfloat16)] * 2
     if dots:
         shapes = shapes + [jax.ShapeDtypeStruct((tokens // 2, 2), jnp.float32)] * 2
     return pl.pallas_call(
         functools.partial(gather_kernel, number, padded, capacity, dots),
-        in_specs=[pl.BlockSpec(memory_space=pltpu.VMEM)] * (len(pieces) + (1 if dots else 2)),
+        in_specs=[pl.BlockSpec(memory_space=pltpu.SMEM)]
+        + [pl.BlockSpec(memory_space=pltpu.VMEM)] * (len(pieces) + 2),
         out_specs=[pl.BlockSpec(memory_space=pltpu.VMEM)] * len(shapes),
         out_shape=shapes,
         compiler_params=pltpu.CompilerParams(vmem_limit_bytes=60 << 20),
         cost_estimate=pl.CostEstimate(flops=1000, bytes_accessed= 1000, transcendentals=0),
         name="gather",
-    )(place, *([] if dots else [gate]), *pieces)
+    )(where, place, pair, *pieces)
 
 
 def whole(*shape):
@@ -873,6 +934,7 @@
     wide = lax.broadcasted_iota(jnp.int32, (probs.shape[0], 128), 1)
     stat = jnp.where(wide == 0, picked[0] / total, jnp.where(wide == 1, picked[1] / total, 0.0))
     stat = jnp.where(wide == 2, total, jnp.where(wide == 3, inverse, stat))
+    stat = jnp.where(wide == 4, ids[:, 0:1].astype(jnp.float32), stat)
     stat_ref[...] = stat[:, :8]
     gates_ref[...] = stat.T[:8, :]
 
@@ -976,20 +1038,18 @@
 
     def put(value):
         value = value.astype(jnp.bfloat16)
-        part = value.shape[0] // mine_ref.shape[0]
-
-        def write(ref):
-            for z in range(ref.shape[0]):
-                ref[z, :part, :] = value[z * part : (z + 1) * part, :]
-                ref[z, part:, :] = tiny[z]
-
-        pl.when(step % 2 == 0)(lambda: write(mine_ref))
-        pl.when(step % 2 == 1)(lambda: write(other_ref))
-
-    pl.when(step // 2 == 0)(lambda: put(mm(nt[:, :rows], dq[...])))
-    pl.when(step // 2 == 1)(lambda: put(mm(nt[...], dk[...])))
-    pl.when(step // 2 == 2)(lambda: put(mm(nt[...], dv[...])))
-    pl.when(step // 2 == 3)(lambda: put(mm(at[...], o[...])))
+        parts, half = mine_ref.shape[0], mine_ref.shape[2]
+        part = value.shape[0] // parts
+        for z in range(parts):
+            mine_ref[z, :part, :] = value[z * part : (z + 1) * part, :half]
+            other_ref[z, :part, :] = value[z * part : (z + 1) * part, half:]
+            mine_ref[z, part:, :] = tiny[z, :, :half]
+            other_ref[z, part:, :] = tiny[z, :, half:]
+
+    pl.when(step == 0)(lambda: put(mm(nt[:, :rows], dq[...])))
+    pl.when(step == 1)(lambda: put(mm(nt[...], dk[...])))
+    pl.when(step == 2)(lambda: put(mm(nt[...], dv[...])))
+    pl.when(step == 3)(lambda: put(mm(at[...], o[...])))
 
 
 def weights_back(normed, dq, dk, dv, d_attn, o, tiny):
@@ -997,11 +1057,7 @@
     rows, half = dq.shape[0], width // 2
     parts, room = tiny.shape[1], tiny.shape[2]
     low = jnp.bfloat16
-
-    def columns(n, first):
-        return pl.BlockSpec((n, half), lambda j: (0, jnp.clip(j - first, 0, 1)))
-
-    out = pl.BlockSpec((None, parts, width // parts + room, half), lambda j: (j // 2, 0, 0, 0))
+    out = pl.BlockSpec((None, parts, width // parts + room, half), lambda j: (j, 0, 0, 0))
     shape = ((4, parts, width // parts + room, half), low)
     return call(
         weights_back_kernel,
@@ -1009,16 +1065,10 @@
         [shape, shape],
         (normed, dq, dk, dv, d_attn, o, tiny),
         [pltpu.VMEM((width, total), low), pltpu.VMEM((width, rows), low)],
-        grid=(8,),
-        in_specs=[
-            pl.BlockSpec((total, width), lambda j: (0, 0)),
-            columns(rows, 0),
-            columns(total, 2),
-            columns(total, 4),
-            pl.BlockSpec((rows, width), lambda j: (0, 0)),
-            columns(rows, 6),
-            pl.BlockSpec((None, parts, room, half), lambda j: (j // 2, 0, 0, j % 2)),
-        ],
+        grid=(4,),
+        in_specs=[whole(total, width), whole(rows, width), whole(total, width), whole(total, width)]
+        + [whole(rows, width), whole(rows, width)]
+        + [pl.BlockSpec((None, parts, room, width), lambda j: (j, 0, 0, 0))],
         out_specs=[out, out],
     )
 
@@ -1234,7 +1284,7 @@
 
     rows_three = flip(pin(rows_two, o_low), "ctx", 1, ctx_n)
     weights = (rows_own, rows_one, rows_two, rows_three)
-    slots = spread(place_t, second_half, experts, padded, capacity, gates_both)
+    slots = spread_gated(place3, place_t, second_half, experts, padded, capacity, gates_both)
     x_far = [far(slots[shards_n + k], k, shards_n, ctx_n) for k in range(shards_n)]
     x_near = [slots[0]] + [flip(slots[k], "shard", k, shards_n) for k in range(1, shards_n)]
 
@@ -1255,7 +1305,9 @@
     ds_near = [ds_near[0]] + [flip(ds_near[k], "shard", k, shards_n) for k in range(1, shards_n)]
 
     rows_tn = (((0,), (0,)), ((), ()))
-    d_routed, d_routed_other, d_pairs, d_pairs_other = gather(place, ds_near + ds_far, capacity)
+    d_routed, d_routed_other, d_pairs, d_pairs_other = gather(
+        place3, place, gates_both[4][:, None], ds_near + ds_far, capacity, True
+    )
     d_mixed, d_attn, d_o, d_logits, d_small = call(
         functools.partial(settle_back_kernel, experts + 1),
         "settle_back",
@@ -1357,7 +1409,7 @@
     total = turn_sum(plane_sum.astype(low), ctx_n, ctx).astype(low)
     out_got = [pin(o, plane_parts[0]) for o in out_got]
     gate_columns = jnp.stack([gates_both[0], gates_both[1]], axis=1)
-    combined, combined_other = gather(place, out_got, capacity, gate_columns)
+    combined, combined_other = gather(place3, place, gate_columns, out_got, capacity, False)
     combined = in_order(combined, swap(combined_other), 1).astype(full)
     second_f = second.astype(full)
 

time: 547 us -> 537 us (0.982)
  Pallas kernels: 193 us -> 183 us
    pallas_call x2 -> x1, Pallas kernels: 11.6 us -> 4.48 us  [spread(): pl.pallas_call(functools.partial(spread_kernel, pieces, padded, capacity,...]
    unnamed x171 -> x157, local copies, waits for them, and re-layouts: 31.1 us -> 30.6 us
  transfers between devices with their start and end apart: 66 -> 66, of which waited for: 26 -> 25; matrix products, arithmetic and copies ran while one was open for 17% -> 17% of each run, Pallas kernels for 34% -> 33%
where the time goes in v5:
time: 537 us; the launch traced here: 530 us
  Pallas kernels  183 us (34%)
  waiting for transfers between devices  141 us (26%)
  starting transfers between devices  82.6 us (15%)
  other arithmetic  62.9 us (12%)
  local copies, waits for them, and re-layouts  56.9 us (11%)
    pallas_call x7, Pallas kernels, call(): pl.pallas_call(kernel, grid_spec=spec, out_shape=[jax.ShapeDtypeStruct(*o...  104 us
    ppermute x46, waiting for transfers between devices, flip(): return lax.ppermute(x, axis, [(i, i ^ bit) for i in range(size)])  88.3 us
    ppermute x46, starting transfers between devices, flip(): return lax.ppermute(x, axis, [(i, i ^ bit) for i in range(size)])  47 us
    pallas_call x3, Pallas kernels, attend_back(): pl.pallas_call(functools.partial(attend_back_kernel, own, seg, HEAD_DIM,...  37.2 us
    unnamed x157, local copies, waits for them, and re-layouts  30.6 us
    ppermute x8, waiting for transfers between devices, far(): return lax.ppermute(x, ('shard', 'ctx'), pairs)  24.1 us
    pallas_call x2, Pallas kernels, attend(): pl.pallas_call(functools.partial(attend_kernel, own, seg, HEAD_DIM, len(p...  21.3 us
    ppermute x3, waiting for transfers between devices, turn_sum(): got = lax.ppermute(block, 'ctx', [(i, (i + k) % size) for i in range(size)])  20.6 us
  transfers between devices with their start and end apart: 66, of which 25 were waited for; matrix products, arithmetic and copies ran while one was open for 17% of the time, Pallas kernels for 33%

profile of v5, /device:TPU:0, one launch (start us, length us, event | category | flops | bytes accessed | tf_op | source)
XLA Modules:
  0.0 529.5 jit_solution(15651335394203307030)
XLA Ops:
  16.1 5.2 convert_reduce_fusion
  29.9 8.4 %collective-permute-done.near = bf16[640,768]{1,0:T(8,128)(2,1)} collective-permute-done((bf16[640,768]{1,0:T(8,128)(2,1)S(1)}, bf16[640,768]{1,0:T(8,128)(2,1)}, u32[]{:S(2)}, u32[]{:S(2)}) %collective-permute-start) | collective-permute-done | bytes 983072 | tf_op jit(solution)/shard_map/ppermute | solution.py:1163
  42.2 10.7 %collective-permute-done.7 = bf16[768,384]{1,0:T(8,128)(2,1)} collective-permute-done((bf16[768,384]{1,0:T(8,128)(2,1)S(1)}, bf16[768,384]{1,0:T(8,128)(2,1)}, u32[]{:S(2)}, u32[]{:S(2)}) %collective-permute-start.7) | collective-permute-done | bytes 589856 | tf_op jit(solution)/shard_map/ppermute | solution.py:1077
  66.9 8.9 %collective-permute-start.10 = (bf16[4,224,384]{2,1,0:T(8,128)(2,1)}, bf16[4,224,384]{2,1,0:T(8,128)(2,1)}, u32[]{:S(2)}, u32[]{:S(2)}) collective-permute-start(bf16[4,224,384]{2,1,0:T(8,128)(2,1)} %pad_maximum_fusion.9), channel_id=1, source_target_pairs={{0,4},{2,6},{4,0},{6,2},{1,5},{3,7},{5,1},{7,3},{8,12},{10,14},{12... | collective-permute-start | bytes 2064392 | tf_op jit(solution)/shard_map/ppermute | solution.py:1077
  79.8 23.3 %collective-permute-done.10 = bf16[4,224,384]{2,1,0:T(8,128)(2,1)} collective-permute-done((bf16[4,224,384]{2,1,0:T(8,128)(2,1)}, bf16[4,224,384]{2,1,0:T(8,128)(2,1)}, u32[]{:S(2)}, u32[]{:S(2)}) %collective-permute-start.10) | collective-permute-done | bytes 688160 | tf_op jit(solution)/shard_map/ppermute | solution.py:1077
  103.1 6.1 %collective-permute-start.12 = (bf16[3,192,1024]{2,1,0:T(8,128)(2,1)}, bf16[3,192,1024]{2,1,0:T(8,128)(2,1)}, u32[]{:S(2)}, u32[]{:S(2)}) collective-permute-start(bf16[3,192,1024]{2,1,0:T(8,128)(2,1)} %get-tuple-element.137), channel_id=1, source_target_pairs={{0,4},{2,6},{4,0},{6,2},{1,5},{3,7},{5,1},{7,3},{8,12},{10,14},{12... | collective-permute-start | bytes 3538952 | tf_op jit(solution)/shard_map/ppermute | solution.py:1077
  112.8 15.0 %project.1 = (bf16[640,768]{1,0:T(8,128)(2,1)S(1)}, bf16[2176,1536]{1,0:T(8,128)(2,1)}, bf16[2176,768]{1,0:T(8,128)(2,1)S(1)}, bf16[2176,768]{1,0:T(8,128)(2,1)}) custom-call(s32[3]{0:T(128)S(1)} %pad_add_fusion.1.place.where_ref, bf16[640,768]{1,0:T(8,128)(2,1)S(1)} %dynamic-slice_bitcast_fusion.2.x0.x, bf16[640,768]{1,0:T(8,128)(2,1)} %collective-permute-done.near, ...), custom_call_target="tpu_custom_call" | custom-call | flops 1000 | bytes 1000 | tf_op jit(solution)/shard_map/project/pallas_call | solution.py:867
  130.4 10.6 %attend.2 = (bf16[640,768]{1,0:T(8,128)(2,1)}, f32[6,8,256]{2,1,0:T(8,128)}) custom-call(s32[5,3]{1,0:T(8,128)} %pad_add_fusion.info, bf16[640,768]{1,0:T(8,128)(2,1)} %copy-done.7, bf16[2176,1536]{1,0:T(8,128)(2,1)} %get-tuple-element.130.k_ref.v_ref, bf16[2176,1536]{1,0:T(8,128)(2,1)} %get-tuple-element.130.k_ref.v_ref), custom_call_target="tpu_custom_call" | custom-call | flops 1000 | bytes 1000 | tf_op jit(solution)/shard_map/attend/pallas_call | solution.py:510
  147.5 10.7 %attend.3 = (bf16[640,768]{1,0:T(8,128)(2,1)}, f32[6,8,256]{2,1,0:T(8,128)}) custom-call(s32[5,3]{1,0:T(8,128)} %pad_add_fusion.info, bf16[640,768]{1,0:T(8,128)(2,1)} %copy-done.7, bf16[2176,1536]{1,0:T(8,128)(2,1)} %get-tuple-element.130.k_ref.v_ref, ...), custom_call_target="tpu_custom_call", output_to_operand_aliasing={{0}: (4, {}), {1}: (5, {})} | custom-call | flops 1000 | bytes 1000 | tf_op jit(solution)/shard_map/attend/pallas_call | solution.py:510
  195.8 22.7 %expert_pass.2 = (bf16[896,384]{1,0:T(8,128)(2,1)S(1)}, bf16[896,384]{1,0:T(8,128)(2,1)S(1)}, bf16[896,384]{1,0:T(8,128)(2,1)S(1)}, bf16[896,384]{1,0:T(8,128)(2,1)S(1)}, bf16[4,3,192,1024]{3,2,1,0:T(8,128)(2,1)}) custom-call(s32[2]{0:T(128)S(1)} %pad_add_fusion.2.place, bf16[896,384]{1,0:T(8,128)(2,1)S(1)} %constant_dynamic-update-slice_fusion.2.xm_ref, ...), custom_call_target="tpu_custom_call" | custom-call | flops 1000 | bytes 1000 | tf_op jit(solution)/shard_map/expert_pass/pallas_call | solution.py:867
  225.0 24.3 %expert_pass.3 = (bf16[896,384]{1,0:T(8,128)(2,1)S(1)}, bf16[896,384]{1,0:T(8,128)(2,1)S(1)}, bf16[896,384]{1,0:T(8,128)(2,1)S(1)}, bf16[896,384]{1,0:T(8,128)(2,1)S(1)}, bf16[4,3,192,1024]{3,2,1,0:T(8,128)(2,1)}) custom-call(s32[2]{0:T(128)S(1)} %pad_add_fusion.2.place, bf16[896,384]{1,0:T(8,128)(2,1)S(1)} %constant_dynamic-update-slice_fusion.6.xm_ref, ...), custom_call_target="tpu_custom_call" | custom-call | flops 1000 | bytes 1000 | tf_op jit(solution)/shard_map/expert_pass/pallas_call | solution.py:867
  267.4 8.4 %collective-permute-done.34.rest_4_ = bf16[224,384]{1,0:T(8,128)(2,1)} collective-permute-done((bf16[224,384]{1,0:T(8,128)(2,1)}, bf16[224,384]{1,0:T(8,128)(2,1)}, u32[]{:S(2)}, u32[]{:S(2)}) %collective-permute-start.34) | collective-permute-done | bytes 172064 | tf_op jit(solution)/shard_map/ppermute | solution.py:1103
  287.3 6.8 %gather.12 = (bf16[640,384]{1,0:T(8,128)(2,1)}, bf16[640,384]{1,0:T(8,128)(2,1)}, f32[640,2]{1,0:T(8,128)}, f32[640,2]{1,0:T(8,128)}) custom-call(s32[3]{0:T(128)} %copy-done.53, s32[1280,2]{1,0:T(8,128)} %bitcast.203, f32[1280,1]{1,0:T(8,128)} %copy.182.pair_ref, bf16[224,384]{1,0:T(8,128)(2,1)} %get-tuple-element.331.rest_0_, bf16[224,384]{1,0:T(8,128)(2,1)} %copy-done.67, ...), custom_call_target="tpu_custom_call" | custom-call | flops 1000 | bytes 1000 | tf_op jit(solution)/shard_map/gather/pallas_call | solution.py:833
  306.7 13.0 %settle_back.1 = (f32[640,768]{1,0:T(8,128)S(1)}, bf16[640,768]{1,0:T(8,128)(2,1)S(1)}, bf16[640,768]{1,0:T(8,128)(2,1)S(1)}, f32[640,12]{1,0:T(8,128)S(1)}, f32[16,768]{1,0:T(8,128)S(1)}) custom-call(s32[3]{0:T(128)S(1)} %copy-done.54, bf16[640,384]{1,0:T(8,128)(2,1)S(1)} %copy-done.45, bf16[640,384]{1,0:T(8,128)(2,1)S(1)} %collective-permute-done.40.dr_came, ...), custom_call_target="tpu_custom_call" | custom-call | flops 1000 | bytes 1000 | tf_op jit(solution)/shard_map/settle_back/pallas_call | solution.py:867
  319.9 13.2 %attend_back.3 = (bf16[640,768]{1,0:T(8,128)(2,1)S(1)}, bf16[2176,768]{1,0:T(8,128)(2,1)S(1)}, bf16[2176,768]{1,0:T(8,128)(2,1)S(1)}) custom-call(s32[5,3]{1,0:T(8,128)S(1)} %copy-done.51, bf16[640,768]{1,0:T(8,128)(2,1)S(1)} %copy-done.8, bf16[2176,1536]{1,0:T(8,128)(2,1)} %get-tuple-element.130.k_ref.v_ref, ...), custom_call_target="tpu_custom_call" | custom-call | flops 1000 | bytes 1000 | tf_op jit(solution)/shard_map/attend_back/pallas_call | solution.py:544
  338.3 11.9 %attend_back.4 = (bf16[640,768]{1,0:T(8,128)(2,1)S(1)}, bf16[2176,768]{1,0:T(8,128)(2,1)S(1)}, bf16[2176,768]{1,0:T(8,128)(2,1)S(1)}) custom-call(s32[5,3]{1,0:T(8,128)S(1)} %copy-done.51, bf16[640,768]{1,0:T(8,128)(2,1)S(1)} %copy-done.8, ...), custom_call_target="tpu_custom_call", output_to_operand_aliasing={{0}: (7, {}), {1}: (8, {}), {2}: (9, {})} | custom-call | flops 1000 | bytes 1000 | tf_op jit(solution)/shard_map/attend_back/pallas_call | solution.py:544
  350.3 12.1 %attend_back.5 = (bf16[640,768]{1,0:T(8,128)(2,1)S(1)}, bf16[2176,768]{1,0:T(8,128)(2,1)S(1)}, bf16[2176,768]{1,0:T(8,128)(2,1)S(1)}) custom-call(s32[5,3]{1,0:T(8,128)S(1)} %copy-done.51, bf16[640,768]{1,0:T(8,128)(2,1)S(1)} %copy-done.8, ...), custom_call_target="tpu_custom_call", output_to_operand_aliasing={{0}: (7, {}), {1}: (8, {}), {2}: (9, {})} | custom-call | flops 1000 | bytes 1000 | tf_op jit(solution)/shard_map/attend_back/pallas_call | solution.py:544
  369.3 12.7 %keys_back.1 = (f32[640,768]{1,0:T(8,128)S(1)}, bf16[640,768]{1,0:T(8,128)(2,1)}, bf16[640,768]{1,0:T(8,128)(2,1)S(1)}, bf16[256,768]{1,0:T(8,128)(2,1)S(1)}, f32[1,768]{1,0:T(1,128)S(1)}) custom-call(s32[3]{0:T(128)S(1)} %copy-done.54, bf16[640,768]{1,0:T(8,128)(2,1)S(1)} %get-tuple-element.193.dq, bf16[2176,768]{1,0:T(8,128)(2,1)S(1)} %get-tuple-element.196.dk, ...), custom_call_target="tpu_custom_call" | custom-call | flops 1000 | bytes 1000 | tf_op jit(solution)/shard_map/keys_back/pallas_call | solution.py:867
  396.7 12.1 %weights_back.1 = (bf16[4,4,208,384]{3,2,1,0:T(8,128)(2,1)S(1)}, bf16[4,4,208,384]{3,2,1,0:T(8,128)(2,1)}) custom-call(bf16[2176,768]{1,0:T(8,128)(2,1)S(1)} %copy-done.29, bf16[640,768]{1,0:T(8,128)(2,1)S(1)} %copy-done.12, bf16[2176,768]{1,0:T(8,128)(2,1)} %copy-done.2, bf16[2176,768]{1,0:T(8,128)(2,1)} %copy-done.3, bf16[640,768]{1,0:T(8,128)(2,1)S(1)} %copy-done.39, ...), custom_call_target="tpu_custom_call" | custom-call | flops 1000 | bytes 1000 | tf_op jit(solution)/shard_map/weights_back/pallas_call | solution.py:867
  410.3 12.6 %collective-permute-done.48 = bf16[3,192,1024]{2,1,0:T(8,128)(2,1)} collective-permute-done((bf16[3,192,1024]{2,1,0:T(8,128)(2,1)}, bf16[3,192,1024]{2,1,0:T(8,128)(2,1)}, u32[]{:S(2)}, u32[]{:S(2)}) %collective-permute-start.48) | collective-permute-done | bytes 1179680 | tf_op jit(solution)/shard_map/ppermute | solution.py:1077
  438.3 11.2 %collective-permute-done.50 = bf16[4,208,384]{2,1,0:T(8,128)(2,1)} collective-permute-done((bf16[4,208,384]{2,1,0:T(8,128)(2,1)}, bf16[4,208,384]{2,1,0:T(8,128)(2,1)}, u32[]{:S(2)}, u32[]{:S(2)}) %collective-permute-start.50) | collective-permute-done | bytes 639008 | tf_op jit(solution)/shard_map/ppermute | solution.py:1077
  449.5 5.8 %gather.13 = (bf16[640,384]{1,0:T(8,128)(2,1)}, bf16[640,384]{1,0:T(8,128)(2,1)}) custom-call(s32[3]{0:T(128)} %copy-done.53, s32[1280,2]{1,0:T(8,128)} %bitcast.204, f32[1280,2]{1,0:T(8,128)} %copy.185.pair_ref, bf16[2,224,384]{2,1,0:T(8,128)(2,1)} %get-tuple-element.212.rest_0_, bf16[2,224,384]{2,1,0:T(8,128)(2,1)} %collective-permute-done.45.rest_1_, ...), custom_call_target="tpu_custom_call" | custom-call | flops 1000 | bytes 1000 | tf_op jit(solution)/shard_map/gather/pallas_call | solution.py:833
  475.4 12.7 %collective-permute-done.61 = bf16[208,384]{1,0:T(8,128)(2,1)S(1)} collective-permute-done((bf16[208,384]{1,0:T(8,128)(2,1)S(1)}, bf16[208,384]{1,0:T(8,128)(2,1)S(1)}, u32[]{:S(2)}, u32[]{:S(2)}) %collective-permute-start.61) | collective-permute-done | bytes 159776 | tf_op jit(solution)/shard_map/ppermute | solution.py:1093
  488.1 7.9 %collective-permute-done.60 = bf16[208,384]{1,0:T(8,128)(2,1)S(1)} collective-permute-done((bf16[208,384]{1,0:T(8,128)(2,1)S(1)}, bf16[208,384]{1,0:T(8,128)(2,1)S(1)}, u32[]{:S(2)}, u32[]{:S(2)}) %collective-permute-start.60) | collective-permute-done | bytes 159776 | tf_op jit(solution)/shard_map/ppermute | solution.py:1093
  (417 shorter events, 240.9 us)
Async XLA Ops:
  11.3 26.9 %collective-permute-start = (bf16[640,768]{1,0:T(8,128)(2,1)S(1)}, bf16[640,768]{1,0:T(8,128)(2,1)}, u32[]{:S(2)}, u32[]{:S(2)}) collective-permute-start(bf16[640,768]{1,0:T(8,128)(2,1)S(1)} %dynamic-slice_bitcast_fusion.2.x0.x), channel_id=1, source_target_pairs={{0,2},{2,4},{4,6},{1,3},{3,5},{5,7},{8,10},{10,12},{12,14},{9,11},... | collective-permute-start | bytes 2949128 | tf_op jit(solution)/shard_map/ppermute | solution.py:1163
  54.9 57.9 %collective-permute-start.9 = (bf16[4,768,384]{2,1,0:T(8,128)(2,1)S(1)}, bf16[4,768,384]{2,1,0:T(8,128)(2,1)}, u32[]{:S(2)}, u32[]{:S(2)}) collective-permute-start(bf16[4,768,384]{2,1,0:T(8,128)(2,1)S(1)} %pad_maximum_fusion.3.wm), channel_id=1, source_target_pairs={{0,1},{1,0},{2,3},{3,2},{4,5},{5,4},{6,7},{7,6},{8,9},{9,8},{10,11... | collective-permute-start | bytes 7077896 | tf_op jit(solution)/shard_map/ppermute | solution.py:1077
  62.6 40.5 %collective-permute-start.5 = (bf16[640,768]{1,0:T(8,128)(2,1)}, bf16[640,768]{1,0:T(8,128)(2,1)}, u32[]{:S(2)}, u32[]{:S(2)}) collective-permute-start(bf16[640,768]{1,0:T(8,128)(2,1)} %collective-permute-done.4.mid), channel_id=1, source_target_pairs={{4,6},{5,7},{12,14},{13,15},{20,22},{21,23},{28,30},{29,31}} | collective-permute-start | bytes 2949128 | tf_op jit(solution)/shard_map/ppermute | solution.py:1203
  66.9 36.2 %collective-permute-start.10 = (bf16[4,224,384]{2,1,0:T(8,128)(2,1)}, bf16[4,224,384]{2,1,0:T(8,128)(2,1)}, u32[]{:S(2)}, u32[]{:S(2)}) collective-permute-start(bf16[4,224,384]{2,1,0:T(8,128)(2,1)} %pad_maximum_fusion.9), channel_id=1, source_target_pairs={{0,4},{2,6},{4,0},{6,2},{1,5},{3,7},{5,1},{7,3},{8,12},{10,14},{12... | collective-permute-start | bytes 2064392 | tf_op jit(solution)/shard_map/ppermute | solution.py:1077
  103.1 56.9 %collective-permute-start.11 = (bf16[3,192,1024]{2,1,0:T(8,128)(2,1)}, bf16[3,192,1024]{2,1,0:T(8,128)(2,1)}, u32[]{:S(2)}, u32[]{:S(2)}) collective-permute-start(bf16[3,192,1024]{2,1,0:T(8,128)(2,1)} %get-tuple-element.136.w0), channel_id=1, source_target_pairs={{0,2},{2,0},{4,6},{6,4},{1,3},{3,1},{5,7},{7,5},{8,10},{10,8},{12,... | collective-permute-start | bytes 3538952 | tf_op jit(solution)/shard_map/ppermute | solution.py:1077
  103.1 56.9 %collective-permute-start.12 = (bf16[3,192,1024]{2,1,0:T(8,128)(2,1)}, bf16[3,192,1024]{2,1,0:T(8,128)(2,1)}, u32[]{:S(2)}, u32[]{:S(2)}) collective-permute-start(bf16[3,192,1024]{2,1,0:T(8,128)(2,1)} %get-tuple-element.137), channel_id=1, source_target_pairs={{0,4},{2,6},{4,0},{6,2},{1,5},{3,7},{5,1},{7,3},{8,12},{10,14},{12... | collective-permute-start | bytes 3538952 | tf_op jit(solution)/shard_map/ppermute | solution.py:1077
  187.9 30.6 %collective-permute-start.24 = (bf16[224,384]{1,0:T(8,128)(2,1)S(1)}, bf16[224,384]{1,0:T(8,128)(2,1)S(1)}, u32[]{:S(2)}, u32[]{:S(2)}) collective-permute-start(bf16[224,384]{1,0:T(8,128)(2,1)S(1)} %get-tuple-element.156), channel_id=1, source_target_pairs={{0,4},{2,6},{4,0},{6,2},{8,12},{10,14},{12,8},{14,10},{16,20},{18,... | collective-permute-start | bytes 516104 | tf_op jit(solution)/shard_map/ppermute | solution.py:1103
  189.5 29.0 %collective-permute-start.25 = (bf16[224,384]{1,0:T(8,128)(2,1)S(1)}, bf16[224,384]{1,0:T(8,128)(2,1)S(1)}, u32[]{:S(2)}, u32[]{:S(2)}) collective-permute-start(bf16[224,384]{1,0:T(8,128)(2,1)S(1)} %get-tuple-element.157), channel_id=1, source_target_pairs={{0,12},{2,14},{4,8},{6,10},{8,4},{10,6},{12,0},{14,2},{16,28},{18,... | collective-permute-start | bytes 516104 | tf_op jit(solution)/shard_map/ppermute | solution.py:1103
  190.9 27.5 %collective-permute-start.26 = (bf16[224,384]{1,0:T(8,128)(2,1)S(1)}, bf16[224,384]{1,0:T(8,128)(2,1)S(1)}, u32[]{:S(2)}, u32[]{:S(2)}) collective-permute-start(bf16[224,384]{1,0:T(8,128)(2,1)S(1)} %get-tuple-element.158), channel_id=1, source_target_pairs={{0,20},{2,22},{4,16},{6,18},{8,28},{10,30},{12,24},{14,26},{16,4},... | collective-permute-start | bytes 516104 | tf_op jit(solution)/shard_map/ppermute | solution.py:1103
  193.4 29.3 %collective-permute-start.27 = (bf16[224,384]{1,0:T(8,128)(2,1)S(1)}, bf16[224,384]{1,0:T(8,128)(2,1)S(1)}, u32[]{:S(2)}, u32[]{:S(2)}) collective-permute-start(bf16[224,384]{1,0:T(8,128)(2,1)S(1)} %get-tuple-element.159), channel_id=1, source_target_pairs={{0,28},{2,30},{4,24},{6,26},{8,20},{10,22},{12,16},{14,18},{16,12}... | collective-permute-start | bytes 516104 | tf_op jit(solution)/shard_map/ppermute | solution.py:1103
  222.9 26.7 %collective-permute-start.29 = (bf16[896,384]{1,0:T(8,128)(2,1)S(1)}, bf16[896,384]{1,0:T(8,128)(2,1)S(1)}, u32[]{:S(2)}, u32[]{:S(2)}) collective-permute-start(bf16[896,384]{1,0:T(8,128)(2,1)S(1)} %get-tuple-element.167), channel_id=1, source_target_pairs={{0,1},{1,0},{2,3},{3,2},{4,5},{5,4},{6,7},{7,6},{8,9},{9,8},{10,11... | collective-permute-start | bytes 2064392 | tf_op jit(solution)/shard_map/ppermute | solution.py:1077
  258.1 25.1 %collective-permute-start.36 = (bf16[224,384]{1,0:T(8,128)(2,1)}, bf16[224,384]{1,0:T(8,128)(2,1)}, u32[]{:S(2)}, u32[]{:S(2)}) collective-permute-start(bf16[224,384]{1,0:T(8,128)(2,1)} %get-tuple-element.325), channel_id=1, source_target_pairs={{0,20},{2,22},{4,16},{6,18},{8,28},{10,30},{12,24},{14,26},{16,4},... | collective-permute-start | bytes 516104 | tf_op jit(solution)/shard_map/ppermute | solution.py:1103
  261.2 26.2 %collective-permute-start.37 = (bf16[224,384]{1,0:T(8,128)(2,1)}, bf16[224,384]{1,0:T(8,128)(2,1)}, u32[]{:S(2)}, u32[]{:S(2)}) collective-permute-start(bf16[224,384]{1,0:T(8,128)(2,1)} %get-tuple-element.324), channel_id=1, source_target_pairs={{0,28},{2,30},{4,24},{6,26},{8,20},{10,22},{12,16},{14,18},{16,12}... | collective-permute-start | bytes 516104 | tf_op jit(solution)/shard_map/ppermute | solution.py:1103
  294.2 70.0 %collective-permute-start.43 = (bf16[2,3,192,1024]{3,2,1,0:T(8,128)(2,1)}, bf16[2,3,192,1024]{3,2,1,0:T(8,128)(2,1)}, u32[]{:S(2)}, u32[]{:S(2)}) collective-permute-start(bf16[2,3,192,1024]{3,2,1,0:T(8,128)(2,1)} %slice.251), channel_id=1, source_target_pairs={{0,2},{2,0},{4,6},{6,4},{1,3},{3,1},{5,7},{7,5},{8,10},{10,8},{12,... | collective-permute-start | bytes 7077896 | tf_op jit(solution)/shard_map/ppermute | solution.py:1077
  294.2 38.9 %collective-permute-start.38 = (bf16[896,384]{1,0:T(8,128)(2,1)}, bf16[896,384]{1,0:T(8,128)(2,1)}, u32[]{:S(2)}, u32[]{:S(2)}) collective-permute-start(bf16[896,384]{1,0:T(8,128)(2,1)} %copy-done.55), channel_id=1, source_target_pairs={{0,1},{1,0},{2,3},{3,2},{4,5},{5,4},{6,7},{7,6},{8,9},{9,8},{10,11... | collective-permute-start | bytes 2064392 | tf_op jit(solution)/shard_map/ppermute | solution.py:1077
  294.8 39.7 %collective-permute-start.39 = (bf16[896,384]{1,0:T(8,128)(2,1)}, bf16[896,384]{1,0:T(8,128)(2,1)}, u32[]{:S(2)}, u32[]{:S(2)}) collective-permute-start(bf16[896,384]{1,0:T(8,128)(2,1)} %copy-done.56), channel_id=1, source_target_pairs={{0,1},{1,0},{2,3},{3,2},{4,5},{5,4},{6,7},{7,6},{8,9},{9,8},{10,11... | collective-permute-start | bytes 2064392 | tf_op jit(solution)/shard_map/ppermute | solution.py:1077
  335.7 51.2 %collective-permute-start.42 = (bf16[4,224,384]{2,1,0:T(8,128)(2,1)S(1)}, bf16[4,224,384]{2,1,0:T(8,128)(2,1)S(1)}, u32[]{:S(2)}, u32[]{:S(2)}) collective-permute-start(bf16[4,224,384]{2,1,0:T(8,128)(2,1)S(1)} %bitcast.212), channel_id=1, source_target_pairs={{0,4},{2,6},{4,0},{6,2},{1,5},{3,7},{5,1},{7,3},{8,12},{10,14},{12... | collective-permute-start | bytes 2064392 | tf_op jit(solution)/shard_map/ppermute | solution.py:1077
  368.8 54.1 %collective-permute-start.48 = (bf16[3,192,1024]{2,1,0:T(8,128)(2,1)}, bf16[3,192,1024]{2,1,0:T(8,128)(2,1)}, u32[]{:S(2)}, u32[]{:S(2)}) collective-permute-start(bf16[3,192,1024]{2,1,0:T(8,128)(2,1)} %fusion.13), channel_id=1, source_target_pairs={{0,4},{2,6},{4,0},{6,2},{1,5},{3,7},{5,1},{7,3},{8,12},{10,14},{12... | collective-permute-start | bytes 3538952 | tf_op jit(solution)/shard_map/ppermute | solution.py:1077
  385.1 25.2 %collective-permute-start.44 = (bf16[640,768]{1,0:T(8,128)(2,1)}, bf16[640,768]{1,0:T(8,128)(2,1)}, u32[]{:S(2)}, u32[]{:S(2)}) collective-permute-start(bf16[640,768]{1,0:T(8,128)(2,1)} %get-tuple-element.208), channel_id=1, source_target_pairs={{6,4},{7,5},{14,12},{15,13},{22,20},{23,21},{30,28},{31,29}} | collective-permute-start | bytes 2949128 | tf_op jit(solution)/shard_map/ppermute | solution.py:1373
  426.2 29.1 %collective-permute-start.53 = (bf16[640,768]{1,0:T(8,128)(2,1)}, bf16[640,768]{1,0:T(8,128)(2,1)}, u32[]{:S(2)}, u32[]{:S(2)}) collective-permute-start(bf16[640,768]{1,0:T(8,128)(2,1)} %fusion.17), channel_id=1, source_target_pairs={{4,2},{6,4},{5,3},{7,5},{12,10},{14,12},{13,11},{15,13},{20,18},{2... | collective-permute-start | bytes 2949128 | tf_op jit(solution)/shard_map/ppermute | solution.py:1373
  434.4 28.8 %collective-permute-start.58 = (bf16[4,208,384]{2,1,0:T(8,128)(2,1)}, bf16[4,208,384]{2,1,0:T(8,128)(2,1)}, u32[]{:S(2)}, u32[]{:S(2)}) collective-permute-start(bf16[4,208,384]{2,1,0:T(8,128)(2,1)} %get-tuple-element.292), channel_id=1, source_target_pairs={{0,24},{8,16},{16,8},{24,0},{1,25},{9,17},{17,9},{25,1},{2,26},{10... | collective-permute-start | bytes 1916936 | tf_op jit(solution)/shard_map/ppermute | solution.py:1077
  436.2 30.3 %collective-permute-start.57 = (bf16[4,208,384]{2,1,0:T(8,128)(2,1)}, bf16[4,208,384]{2,1,0:T(8,128)(2,1)}, u32[]{:S(2)}, u32[]{:S(2)}) collective-permute-start(bf16[4,208,384]{2,1,0:T(8,128)(2,1)} %get-tuple-element.291), channel_id=1, source_target_pairs={{0,16},{8,24},{16,0},{24,8},{1,17},{9,25},{17,1},{25,9},{2,18},{10... | collective-permute-start | bytes 1916936 | tf_op jit(solution)/shard_map/ppermute | solution.py:1077
  455.4 40.7 %collective-permute-start.51 = (bf16[640,384]{1,0:T(8,128)(2,1)}, bf16[640,384]{1,0:T(8,128)(2,1)S(1)}, u32[]{:S(2)}, u32[]{:S(2)}) collective-permute-start(bf16[640,384]{1,0:T(8,128)(2,1)} %get-tuple-element.217), channel_id=1, source_target_pairs={{0,1},{1,0},{2,3},{3,2},{4,5},{5,4},{6,7},{7,6},{8,9},{9,8},{10,11... | collective-permute-start | bytes 1474568 | tf_op jit(solution)/shard_map/ppermute | solution.py:1077
  457.4 40.8 %collective-permute-start.54 = (bf16[640,768]{1,0:T(8,128)(2,1)S(1)}, bf16[640,768]{1,0:T(8,128)(2,1)S(1)}, u32[]{:S(2)}, u32[]{:S(2)}) collective-permute-start(bf16[640,768]{1,0:T(8,128)(2,1)S(1)} %pad_select_fusion), channel_id=1, source_target_pairs={{2,0},{4,2},{6,4},{3,1},{5,3},{7,5},{10,8},{12,10},{14,12},{11,9},... | collective-permute-start | bytes 2949128 | tf_op jit(solution)/shard_map/ppermute | solution.py:1373
  (115 other events, 1234.9 us)

commit v6 on v5

--- a/solution.py
+++ b/solution.py
@@ -1070,6 +1070,7 @@
         + [whole(rows, width), whole(rows, width)]
         + [pl.BlockSpec((None, parts, room, width), lambda j: (j, 0, 0, 0))],
         out_specs=[out, out],
+        mib=60,
     )
 
 
@@ -1142,7 +1143,8 @@
         return jnp.concatenate([jnp.where(tp == 0, x, other), jnp.where(tp == 0, other, x)], axis=axis)
 
     def both_trees(x, other):
-        return in_order(x[None], other[None])
+        both = jnp.broadcast_to(x[None], (2,) + x.shape)
+        return lax.dynamic_update_index_in_dim(both, other, 1 - tp, 0)
 
     def unit_of(x):
         x = x.astype(full)
@@ -1327,6 +1329,7 @@
             chosen(3, width, part), chosen(3, width, part),
         ],
         prefetch=True,
+        mib=60,
     )
 
     ox1, ox2, held = lax.optimization_barrier((ox1, ox2, d_routed))
@@ -1361,6 +1364,7 @@
             whole(4, width, part), whole(4, width, part),
         ],
         prefetch=True,
+        mib=60,
     )
 
     tiny = jnp.concatenate([d_small[:all_experts], d_gain_a, d_small[all_experts + 1 :]], axis=0)
@@ -1426,7 +1430,9 @@
         + const_gate[:, 1:] * const_t[1][None]
     )
     total = pin(total, mixed_out, d_tokens)
-    four = jnp.stack([total] + [flip(total, "shard", k, shards_n) for k in range(1, shards_n)])
+    d_tokens_other = swap(d_tokens)
+    four = [total] + [flip(total, "shard", k, shards_n) for k in range(1, shards_n)]
+    four = jnp.stack([pin(f, d_tokens_other) for f in four])
     four = jnp.stack(
         [lax.dynamic_index_in_dim(four, m ^ shard, 0, keepdims=False) for m in range(4)]
     )
@@ -1437,7 +1443,7 @@
 
     return (
         both_trees(mixed_out, swap(mixed_out)),
-        both_trees(d_tokens, swap(d_tokens)),
+        both_trees(d_tokens, d_tokens_other),
         both_trees(d_logits, swap(d_logits)),
         d_w_qkv,
         d_w_out,

time: 537 us -> 527 us (0.981)
  other arithmetic: 62.9 us -> 50.8 us
  Pallas kernels: 183 us -> 191 us
    ppermute x3, waiting for transfers between devices: 20.6 us -> 0.01 us  [turn_sum(): got = lax.ppermute(block, 'ctx', [(i, (i + k) % size) for i in range(size)])]
    ppermute x3, waiting for transfers between devices: 0.01 us -> 13.7 us  [down(): lax.ppermute(x, 'ctx', [(i, i - 1) for i in range(ctx_n - step, ctx_n)])]
    unnamed x157, local copies, waits for them, and re-layouts: 30.6 us -> 21.8 us
    pallas_call x7, Pallas kernels: 104 us -> 112 us  [call(): pl.pallas_call(kernel, grid_spec=spec, out_shape=[jax.ShapeDtypeStruct(*o...]
  transfers between devices with their start and end apart: 66 -> 66, of which waited for: 25 -> 26; matrix products, arithmetic and copies ran while one was open for 17% -> 16% of each run, Pallas kernels for 33% -> 36%
where the time goes in v6:
time: 527 us; the launch traced here: 519 us
  Pallas kernels  191 us (36%)
  waiting for transfers between devices  139 us (26%)
  starting transfers between devices  79.6 us (15%)
  local copies, waits for them, and re-layouts  55.8 us (11%)
  other arithmetic  50.8 us (10%)
    pallas_call x7, Pallas kernels, call(): pl.pallas_call(kernel, grid_spec=spec, out_shape=[jax.ShapeDtypeStruct(*o...  112 us
    ppermute x46, waiting for transfers between devices, flip(): return lax.ppermute(x, axis, [(i, i ^ bit) for i in range(size)])  92.9 us
    ppermute x46, starting transfers between devices, flip(): return lax.ppermute(x, axis, [(i, i ^ bit) for i in range(size)])  45.9 us
    pallas_call x3, Pallas kernels, attend_back(): pl.pallas_call(functools.partial(attend_back_kernel, own, seg, HEAD_DIM,...  36.1 us
    ppermute x8, waiting for transfers between devices, far(): return lax.ppermute(x, ('shard', 'ctx'), pairs)  23.7 us
    unnamed x157, local copies, waits for them, and re-layouts  21.8 us
    pallas_call x2, Pallas kernels, attend(): pl.pallas_call(functools.partial(attend_kernel, own, seg, HEAD_DIM, len(p...  21.4 us
    ppermute x3, waiting for transfers between devices, down(): lax.ppermute(x, 'ctx', [(i, i - 1) for i in range(ctx_n - step, ctx_n)])  13.7 us
  transfers between devices with their start and end apart: 66, of which 26 were waited for; matrix products, arithmetic and copies ran while one was open for 16% of the time, Pallas kernels for 36%

profile of v6, /device:TPU:0, one launch (start us, length us, event | category | flops | bytes accessed | tf_op | source)
XLA Modules:
  0.0 518.6 jit_solution(9955388909833090482)
XLA Ops:
  16.1 5.2 %convert_reduce_fusion = s32[2560]{0:T(1024)S(1)} fusion(s32[2560]{0:T(1024)S(1)} %add.303, s32[2560]{0:T(1024)S(1)} %eq.72), kind=kLoop, calls=%fused_computation.1 | loop fusion | flops 32765440 | bytes 30720 | tf_op jit(solution)/shard_map/reduce_sum | solution.py:1189
  29.9 8.4 %collective-permute-done.near = bf16[640,768]{1,0:T(8,128)(2,1)} collective-permute-done((bf16[640,768]{1,0:T(8,128)(2,1)S(1)}, bf16[640,768]{1,0:T(8,128)(2,1)}, u32[]{:S(2)}, u32[]{:S(2)}) %collective-permute-start) | collective-permute-done | bytes 983072 | tf_op jit(solution)/shard_map/ppermute | solution.py:1165
  42.2 10.7 %collective-permute-done.7 = bf16[768,384]{1,0:T(8,128)(2,1)} collective-permute-done((bf16[768,384]{1,0:T(8,128)(2,1)S(1)}, bf16[768,384]{1,0:T(8,128)(2,1)}, u32[]{:S(2)}, u32[]{:S(2)}) %collective-permute-start.7) | collective-permute-done | bytes 589856 | tf_op jit(solution)/shard_map/ppermute | solution.py:1078
  55.0 5.2 %spread.2 = (bf16[224,384]{1,0:T(8,128)(2,1)}, bf16[224,384]{1,0:T(8,128)(2,1)}, bf16[224,384]{1,0:T(8,128)(2,1)}, bf16[224,384]{1,0:T(8,128)(2,1)}, bf16[224,38...) custom-call(s32[2,1280]{1,0:T(2,128)} %copy.170.place_ref, ...), custom_call_target="tpu_custom_call" | custom-call | flops 1000 | bytes 1000 | tf_op jit(solution)/shard_map/spread/pallas_call | solution.py:721
  67.8 7.6 %collective-permute-start.10 = (bf16[4,224,384]{2,1,0:T(8,128)(2,1)}, bf16[4,224,384]{2,1,0:T(8,128)(2,1)}, u32[]{:S(2)}, u32[]{:S(2)}) collective-permute-start(bf16[4,224,384]{2,1,0:T(8,128)(2,1)} %pad_maximum_fusion.7), channel_id=1, source_target_pairs={{0,4},{2,6},{4,0},{6,2},{1,5},{3,7},{5,1},{7,3},{8,12},{10,14},{12... | collective-permute-start | bytes 2064392 | tf_op jit(solution)/shard_map/ppermute | solution.py:1078
  79.4 23.3 %collective-permute-done.10 = bf16[4,224,384]{2,1,0:T(8,128)(2,1)} collective-permute-done((bf16[4,224,384]{2,1,0:T(8,128)(2,1)}, bf16[4,224,384]{2,1,0:T(8,128)(2,1)}, u32[]{:S(2)}, u32[]{:S(2)}) %collective-permute-start.10) | collective-permute-done | bytes 688160 | tf_op jit(solution)/shard_map/ppermute | solution.py:1078
  102.7 6.5 %collective-permute-start.12 = (bf16[3,192,1024]{2,1,0:T(8,128)(2,1)}, bf16[3,192,1024]{2,1,0:T(8,128)(2,1)}, u32[]{:S(2)}, u32[]{:S(2)}) collective-permute-start(bf16[3,192,1024]{2,1,0:T(8,128)(2,1)} %get-tuple-element.141), channel_id=1, source_target_pairs={{0,4},{2,6},{4,0},{6,2},{1,5},{3,7},{5,1},{7,3},{8,12},{10,14},{12... | collective-permute-start | bytes 3538952 | tf_op jit(solution)/shard_map/ppermute | solution.py:1078
  113.9 14.9 %project.1 = (bf16[640,768]{1,0:T(8,128)(2,1)S(1)}, bf16[2176,1536]{1,0:T(8,128)(2,1)}, bf16[2176,768]{1,0:T(8,128)(2,1)S(1)}, bf16[2176,768]{1,0:T(8,128)(2,1)}) custom-call(s32[3]{0:T(128)S(1)} %pad_add_fusion.1.place.where_ref, bf16[640,768]{1,0:T(8,128)(2,1)S(1)} %dynamic-slice_bitcast_fusion.2.x0.x, bf16[640,768]{1,0:T(8,128)(2,1)} %collective-permute-done.near, ...), custom_call_target="tpu_custom_call" | custom-call | flops 1000 | bytes 1000 | tf_op jit(solution)/shard_map/project/pallas_call | solution.py:867
  131.5 10.7 %attend.2 = (bf16[640,768]{1,0:T(8,128)(2,1)}, f32[6,8,256]{2,1,0:T(8,128)}) custom-call(s32[5,3]{1,0:T(8,128)} %pad_add_fusion.info, bf16[640,768]{1,0:T(8,128)(2,1)} %copy-done.9, bf16[2176,1536]{1,0:T(8,128)(2,1)} %get-tuple-element.134.k_ref.v_ref, bf16[2176,1536]{1,0:T(8,128)(2,1)} %get-tuple-element.134.k_ref.v_ref), custom_call_target="tpu_custom_call" | custom-call | flops 1000 | bytes 1000 | tf_op jit(solution)/shard_map/attend/pallas_call | solution.py:510
  148.6 10.7 %attend.3 = (bf16[640,768]{1,0:T(8,128)(2,1)}, f32[6,8,256]{2,1,0:T(8,128)}) custom-call(s32[5,3]{1,0:T(8,128)} %pad_add_fusion.info, bf16[640,768]{1,0:T(8,128)(2,1)} %copy-done.9, bf16[2176,1536]{1,0:T(8,128)(2,1)} %get-tuple-element.134.k_ref.v_ref, ...), custom_call_target="tpu_custom_call", output_to_operand_aliasing={{0}: (4, {}), {1}: (5, {})} | custom-call | flops 1000 | bytes 1000 | tf_op jit(solution)/shard_map/attend/pallas_call | solution.py:510
  197.0 22.9 %expert_pass.2 = (bf16[896,384]{1,0:T(8,128)(2,1)S(1)}, bf16[896,384]{1,0:T(8,128)(2,1)}, bf16[896,384]{1,0:T(8,128)(2,1)S(1)}, bf16[896,384]{1,0:T(8,128)(2,1)S(1)}, bf16[4,3,192,1024]{3,2,1,0:T(8,128)(2,1)}) custom-call(s32[2]{0:T(128)S(1)} %pad_add_fusion.2.place, bf16[896,384]{1,0:T(8,128)(2,1)S(1)} %constant_dynamic-update-slice_fusion.2.xm_ref, ...), custom_call_target="tpu_custom_call" | custom-call | flops 1000 | bytes 1000 | tf_op jit(solution)/shard_map/expert_pass/pallas_call | solution.py:867
  226.2 24.5 %expert_pass.3 = (bf16[896,384]{1,0:T(8,128)(2,1)S(1)}, bf16[896,384]{1,0:T(8,128)(2,1)}, bf16[896,384]{1,0:T(8,128)(2,1)S(1)}, bf16[896,384]{1,0:T(8,128)(2,1)S(1)}, bf16[4,3,192,1024]{3,2,1,0:T(8,128)(2,1)}) custom-call(s32[2]{0:T(128)S(1)} %pad_add_fusion.2.place, bf16[896,384]{1,0:T(8,128)(2,1)S(1)} %constant_dynamic-update-slice_fusion.6.xm_ref, ...), custom_call_target="tpu_custom_call" | custom-call | flops 1000 | bytes 1000 | tf_op jit(solution)/shard_map/expert_pass/pallas_call | solution.py:867
  268.0 8.1 %collective-permute-done.34.rest_4_ = bf16[224,384]{1,0:T(8,128)(2,1)S(1)} collective-permute-done((bf16[224,384]{1,0:T(8,128)(2,1)S(1)}, bf16[224,384]{1,0:T(8,128)(2,1)S(1)}, u32[]{:S(2)}, u32[]{:S(2)}) %collective-permute-start.34) | collective-permute-done | bytes 172064 | tf_op jit(solution)/shard_map/ppermute | solution.py:1104
  288.3 6.8 %gather.12 = (bf16[640,384]{1,0:T(8,128)(2,1)}, bf16[640,384]{1,0:T(8,128)(2,1)}, f32[640,2]{1,0:T(8,128)}, f32[640,2]{1,0:T(8,128)}) custom-call(s32[3]{0:T(128)} %copy-done.32, s32[1280,2]{1,0:T(8,128)} %bitcast.190, f32[1280,1]{1,0:T(8,128)} %copy.182.pair_ref, bf16[224,384]{1,0:T(8,128)(2,1)} %get-tuple-element.335.rest_0_, bf16[224,384]{1,0:T(8,128)(2,1)} %copy-done.58, ...), custom_call_target="tpu_custom_call" | custom-call | flops 1000 | bytes 1000 | tf_op jit(solution)/shard_map/gather/pallas_call | solution.py:833
  300.7 16.0 %settle_back.1 = (f32[640,768]{1,0:T(8,128)}, bf16[640,768]{1,0:T(8,128)(2,1)}, bf16[640,768]{1,0:T(8,128)(2,1)}, f32[640,12]{1,0:T(8,128)}, f32[16,768]{1,0:T(8,128)}) custom-call(s32[3]{0:T(128)} %copy-done.32, bf16[640,384]{1,0:T(8,128)(2,1)} %get-tuple-element.174.dr_mine, bf16[640,384]{1,0:T(8,128)(2,1)} %copy-done.52, ...), custom_call_target="tpu_custom_call" | custom-call | flops 1000 | bytes 1000 | tf_op jit(solution)/shard_map/settle_back/pallas_call | solution.py:867
  320.3 12.0 %attend_back.3 = (bf16[640,768]{1,0:T(8,128)(2,1)S(1)}, bf16[2176,768]{1,0:T(8,128)(2,1)S(1)}, bf16[2176,768]{1,0:T(8,128)(2,1)S(1)}) custom-call(s32[5,3]{1,0:T(8,128)S(1)} %copy-done.30, bf16[640,768]{1,0:T(8,128)(2,1)S(1)} %copy-done.10, bf16[2176,1536]{1,0:T(8,128)(2,1)} %get-tuple-element.134.k_ref.v_ref, ...), custom_call_target="tpu_custom_call" | custom-call | flops 1000 | bytes 1000 | tf_op jit(solution)/shard_map/attend_back/pallas_call | solution.py:544
  339.2 11.9 %attend_back.4 = (bf16[640,768]{1,0:T(8,128)(2,1)S(1)}, bf16[2176,768]{1,0:T(8,128)(2,1)S(1)}, bf16[2176,768]{1,0:T(8,128)(2,1)S(1)}) custom-call(s32[5,3]{1,0:T(8,128)S(1)} %copy-done.30, bf16[640,768]{1,0:T(8,128)(2,1)S(1)} %copy-done.10, ...), custom_call_target="tpu_custom_call", output_to_operand_aliasing={{0}: (7, {}), {1}: (8, {}), {2}: (9, {})} | custom-call | flops 1000 | bytes 1000 | tf_op jit(solution)/shard_map/attend_back/pallas_call | solution.py:544
  351.2 12.1 %attend_back.5 = (bf16[640,768]{1,0:T(8,128)(2,1)S(1)}, bf16[2176,768]{1,0:T(8,128)(2,1)S(1)}, bf16[2176,768]{1,0:T(8,128)(2,1)S(1)}) custom-call(s32[5,3]{1,0:T(8,128)S(1)} %copy-done.30, bf16[640,768]{1,0:T(8,128)(2,1)S(1)} %copy-done.10, ...), custom_call_target="tpu_custom_call", output_to_operand_aliasing={{0}: (7, {}), {1}: (8, {}), {2}: (9, {})} | custom-call | flops 1000 | bytes 1000 | tf_op jit(solution)/shard_map/attend_back/pallas_call | solution.py:544
  370.7 15.6 %keys_back.1 = (f32[640,768]{1,0:T(8,128)}, bf16[640,768]{1,0:T(8,128)(2,1)}, bf16[640,768]{1,0:T(8,128)(2,1)}, bf16[256,768]{1,0:T(8,128)(2,1)}, f32[1,768]{1,0:T(1,128)}) custom-call(s32[3]{0:T(128)} %copy-done.32, bf16[640,768]{1,0:T(8,128)(2,1)} %copy-done.11, bf16[2176,768]{1,0:T(8,128)(2,1)} %copy-done.3, bf16[2176,768]{1,0:T(8,128)(2,1)} %copy-done.4, ...), custom_call_target="tpu_custom_call" | custom-call | flops 1000 | bytes 1000 | tf_op jit(solution)/shard_map/keys_back/pallas_call | solution.py:867
  396.0 14.2 %weights_back.1 = (bf16[4,4,208,384]{3,2,1,0:T(8,128)(2,1)}, bf16[4,4,208,384]{3,2,1,0:T(8,128)(2,1)}) custom-call(bf16[2176,768]{1,0:T(8,128)(2,1)} %copy-done.19, bf16[640,768]{1,0:T(8,128)(2,1)} %copy-done.11, bf16[2176,768]{1,0:T(8,128)(2,1)} %copy-done.3, bf16[2176,768]{1,0:T(8,128)(2,1)} %copy-done.4, bf16[640,768]{1,0:T(8,128)(2,1)} %get-tuple-element.202.da_ref, ...), custom_call_target="tpu_custom_call" | custom-call | flops 1000 | bytes 1000 | tf_op jit(solution)/shard_map/weights_back/pallas_call | solution.py:867
  410.2 14.2 %collective-permute-done.48 = bf16[3,192,1024]{2,1,0:T(8,128)(2,1)} collective-permute-done((bf16[3,192,1024]{2,1,0:T(8,128)(2,1)}, bf16[3,192,1024]{2,1,0:T(8,128)(2,1)}, u32[]{:S(2)}, u32[]{:S(2)}) %collective-permute-start.48) | collective-permute-done | bytes 1179680 | tf_op jit(solution)/shard_map/ppermute | solution.py:1078
  442.3 9.9 %collective-permute-done.50 = bf16[4,208,384]{2,1,0:T(8,128)(2,1)} collective-permute-done((bf16[4,208,384]{2,1,0:T(8,128)(2,1)}, bf16[4,208,384]{2,1,0:T(8,128)(2,1)}, u32[]{:S(2)}, u32[]{:S(2)}) %collective-permute-start.50) | collective-permute-done | bytes 639008 | tf_op jit(solution)/shard_map/ppermute | solution.py:1078
  452.2 5.8 %gather.13 = (bf16[640,384]{1,0:T(8,128)(2,1)}, bf16[640,384]{1,0:T(8,128)(2,1)}) custom-call(s32[3]{0:T(128)} %copy-done.32, s32[1280,2]{1,0:T(8,128)} %bitcast.191, f32[1280,2]{1,0:T(8,128)} %copy.185.pair_ref, bf16[2,224,384]{2,1,0:T(8,128)(2,1)} %get-tuple-element.216.rest_0_, bf16[2,224,384]{2,1,0:T(8,128)(2,1)} %copy-done.53, ...), custom_call_target="tpu_custom_call" | custom-call | flops 1000 | bytes 1000 | tf_op jit(solution)/shard_map/gather/pallas_call | solution.py:833
  472.9 13.7 %collective-permute-done.54 = bf16[640,768]{1,0:T(8,128)(2,1)S(1)} collective-permute-done((bf16[640,768]{1,0:T(8,128)(2,1)S(1)}, bf16[640,768]{1,0:T(8,128)(2,1)S(1)}, u32[]{:S(2)}, u32[]{:S(2)}) %collective-permute-start.54) | collective-permute-done | bytes 983072 | tf_op jit(solution)/shard_map/ppermute | solution.py:1377
  (418 shorter events, 225.4 us)
Async XLA Ops:
  11.3 26.9 %collective-permute-start = (bf16[640,768]{1,0:T(8,128)(2,1)S(1)}, bf16[640,768]{1,0:T(8,128)(2,1)}, u32[]{:S(2)}, u32[]{:S(2)}) collective-permute-start(bf16[640,768]{1,0:T(8,128)(2,1)S(1)} %dynamic-slice_bitcast_fusion.2.x0.x), channel_id=1, source_target_pairs={{0,2},{2,4},{4,6},{1,3},{3,5},{5,7},{8,10},{10,12},{12,14},{9,11},... | collective-permute-start | bytes 2949128 | tf_op jit(solution)/shard_map/ppermute | solution.py:1165
  54.9 59.0 %collective-permute-start.9 = (bf16[4,768,384]{2,1,0:T(8,128)(2,1)S(1)}, bf16[4,768,384]{2,1,0:T(8,128)(2,1)}, u32[]{:S(2)}, u32[]{:S(2)}) collective-permute-start(bf16[4,768,384]{2,1,0:T(8,128)(2,1)S(1)} %pad_maximum_fusion.1.wm), channel_id=1, source_target_pairs={{0,1},{1,0},{2,3},{3,2},{4,5},{5,4},{6,7},{7,6},{8,9},{9,8},{10,11... | collective-permute-start | bytes 7077896 | tf_op jit(solution)/shard_map/ppermute | solution.py:1078
  63.9 38.8 %collective-permute-start.5 = (bf16[640,768]{1,0:T(8,128)(2,1)}, bf16[640,768]{1,0:T(8,128)(2,1)}, u32[]{:S(2)}, u32[]{:S(2)}) collective-permute-start(bf16[640,768]{1,0:T(8,128)(2,1)} %collective-permute-done.4.mid), channel_id=1, source_target_pairs={{4,6},{5,7},{12,14},{13,15},{20,22},{21,23},{28,30},{29,31}} | collective-permute-start | bytes 2949128 | tf_op jit(solution)/shard_map/ppermute | solution.py:1205
  67.8 34.9 %collective-permute-start.10 = (bf16[4,224,384]{2,1,0:T(8,128)(2,1)}, bf16[4,224,384]{2,1,0:T(8,128)(2,1)}, u32[]{:S(2)}, u32[]{:S(2)}) collective-permute-start(bf16[4,224,384]{2,1,0:T(8,128)(2,1)} %pad_maximum_fusion.7), channel_id=1, source_target_pairs={{0,4},{2,6},{4,0},{6,2},{1,5},{3,7},{5,1},{7,3},{8,12},{10,14},{12... | collective-permute-start | bytes 2064392 | tf_op jit(solution)/shard_map/ppermute | solution.py:1078
  102.7 58.4 %collective-permute-start.11 = (bf16[3,192,1024]{2,1,0:T(8,128)(2,1)}, bf16[3,192,1024]{2,1,0:T(8,128)(2,1)}, u32[]{:S(2)}, u32[]{:S(2)}) collective-permute-start(bf16[3,192,1024]{2,1,0:T(8,128)(2,1)} %get-tuple-element.140.w0), channel_id=1, source_target_pairs={{0,2},{2,0},{4,6},{6,4},{1,3},{3,1},{5,7},{7,5},{8,10},{10,8},{12,... | collective-permute-start | bytes 3538952 | tf_op jit(solution)/shard_map/ppermute | solution.py:1078
  102.7 58.4 %collective-permute-start.12 = (bf16[3,192,1024]{2,1,0:T(8,128)(2,1)}, bf16[3,192,1024]{2,1,0:T(8,128)(2,1)}, u32[]{:S(2)}, u32[]{:S(2)}) collective-permute-start(bf16[3,192,1024]{2,1,0:T(8,128)(2,1)} %get-tuple-element.141), channel_id=1, source_target_pairs={{0,4},{2,6},{4,0},{6,2},{1,5},{3,7},{5,1},{7,3},{8,12},{10,14},{12... | collective-permute-start | bytes 3538952 | tf_op jit(solution)/shard_map/ppermute | solution.py:1078
  189.1 30.7 %collective-permute-start.24 = (bf16[224,384]{1,0:T(8,128)(2,1)S(1)}, bf16[224,384]{1,0:T(8,128)(2,1)S(1)}, u32[]{:S(2)}, u32[]{:S(2)}) collective-permute-start(bf16[224,384]{1,0:T(8,128)(2,1)S(1)} %get-tuple-element.160), channel_id=1, source_target_pairs={{0,4},{2,6},{4,0},{6,2},{8,12},{10,14},{12,8},{14,10},{16,20},{18,... | collective-permute-start | bytes 516104 | tf_op jit(solution)/shard_map/ppermute | solution.py:1104
  190.0 29.9 %collective-permute-start.25 = (bf16[224,384]{1,0:T(8,128)(2,1)S(1)}, bf16[224,384]{1,0:T(8,128)(2,1)S(1)}, u32[]{:S(2)}, u32[]{:S(2)}) collective-permute-start(bf16[224,384]{1,0:T(8,128)(2,1)S(1)} %get-tuple-element.161), channel_id=1, source_target_pairs={{0,12},{2,14},{4,8},{6,10},{8,4},{10,6},{12,0},{14,2},{16,28},{18,... | collective-permute-start | bytes 516104 | tf_op jit(solution)/shard_map/ppermute | solution.py:1104
  192.1 27.7 %collective-permute-start.26 = (bf16[224,384]{1,0:T(8,128)(2,1)S(1)}, bf16[224,384]{1,0:T(8,128)(2,1)S(1)}, u32[]{:S(2)}, u32[]{:S(2)}) collective-permute-start(bf16[224,384]{1,0:T(8,128)(2,1)S(1)} %get-tuple-element.162), channel_id=1, source_target_pairs={{0,20},{2,22},{4,16},{6,18},{8,28},{10,30},{12,24},{14,26},{16,4},... | collective-permute-start | bytes 516104 | tf_op jit(solution)/shard_map/ppermute | solution.py:1104
  194.1 29.7 %collective-permute-start.27 = (bf16[224,384]{1,0:T(8,128)(2,1)S(1)}, bf16[224,384]{1,0:T(8,128)(2,1)S(1)}, u32[]{:S(2)}, u32[]{:S(2)}) collective-permute-start(bf16[224,384]{1,0:T(8,128)(2,1)S(1)} %get-tuple-element.163), channel_id=1, source_target_pairs={{0,28},{2,30},{4,24},{6,26},{8,20},{10,22},{12,16},{14,18},{16,12}... | collective-permute-start | bytes 516104 | tf_op jit(solution)/shard_map/ppermute | solution.py:1104
  224.1 26.9 %collective-permute-start.29 = (bf16[896,384]{1,0:T(8,128)(2,1)S(1)}, bf16[896,384]{1,0:T(8,128)(2,1)S(1)}, u32[]{:S(2)}, u32[]{:S(2)}) collective-permute-start(bf16[896,384]{1,0:T(8,128)(2,1)S(1)} %get-tuple-element.171), channel_id=1, source_target_pairs={{0,1},{1,0},{2,3},{3,2},{4,5},{5,4},{6,7},{7,6},{8,9},{9,8},{10,11... | collective-permute-start | bytes 2064392 | tf_op jit(solution)/shard_map/ppermute | solution.py:1078
  295.2 70.8 %collective-permute-start.43 = (bf16[2,3,192,1024]{3,2,1,0:T(8,128)(2,1)}, bf16[2,3,192,1024]{3,2,1,0:T(8,128)(2,1)}, u32[]{:S(2)}, u32[]{:S(2)}) collective-permute-start(bf16[2,3,192,1024]{3,2,1,0:T(8,128)(2,1)} %slice.251), channel_id=1, source_target_pairs={{0,2},{2,0},{4,6},{6,4},{1,3},{3,1},{5,7},{7,5},{8,10},{10,8},{12,... | collective-permute-start | bytes 7077896 | tf_op jit(solution)/shard_map/ppermute | solution.py:1078
  295.2 37.2 %collective-permute-start.38 = (bf16[896,384]{1,0:T(8,128)(2,1)}, bf16[896,384]{1,0:T(8,128)(2,1)}, u32[]{:S(2)}, u32[]{:S(2)}) collective-permute-start(bf16[896,384]{1,0:T(8,128)(2,1)} %get-tuple-element.175), channel_id=1, source_target_pairs={{0,1},{1,0},{2,3},{3,2},{4,5},{5,4},{6,7},{7,6},{8,9},{9,8},{10,11... | collective-permute-start | bytes 2064392 | tf_op jit(solution)/shard_map/ppermute | solution.py:1078
  295.7 38.9 %collective-permute-start.39 = (bf16[896,384]{1,0:T(8,128)(2,1)}, bf16[896,384]{1,0:T(8,128)(2,1)}, u32[]{:S(2)}, u32[]{:S(2)}) collective-permute-start(bf16[896,384]{1,0:T(8,128)(2,1)} %get-tuple-element.177), channel_id=1, source_target_pairs={{0,1},{1,0},{2,3},{3,2},{4,5},{5,4},{6,7},{7,6},{8,9},{9,8},{10,11... | collective-permute-start | bytes 2064392 | tf_op jit(solution)/shard_map/ppermute | solution.py:1078
  336.7 51.4 %collective-permute-start.42 = (bf16[4,224,384]{2,1,0:T(8,128)(2,1)}, bf16[4,224,384]{2,1,0:T(8,128)(2,1)}, u32[]{:S(2)}, u32[]{:S(2)}) collective-permute-start(bf16[4,224,384]{2,1,0:T(8,128)(2,1)} %bitcast.61), channel_id=1, source_target_pairs={{0,4},{2,6},{4,0},{6,2},{1,5},{3,7},{5,1},{7,3},{8,12},{10,14},{12... | collective-permute-start | bytes 2064392 | tf_op jit(solution)/shard_map/ppermute | solution.py:1078
  370.3 54.1 %collective-permute-start.48 = (bf16[3,192,1024]{2,1,0:T(8,128)(2,1)}, bf16[3,192,1024]{2,1,0:T(8,128)(2,1)}, u32[]{:S(2)}, u32[]{:S(2)}) collective-permute-start(bf16[3,192,1024]{2,1,0:T(8,128)(2,1)} %fusion.13), channel_id=1, source_target_pairs={{0,4},{2,6},{4,0},{6,2},{1,5},{3,7},{5,1},{7,3},{8,12},{10,14},{12... | collective-permute-start | bytes 3538952 | tf_op jit(solution)/shard_map/ppermute | solution.py:1078
  427.4 30.6 %collective-permute-start.53 = (bf16[640,768]{1,0:T(8,128)(2,1)}, bf16[640,768]{1,0:T(8,128)(2,1)}, u32[]{:S(2)}, u32[]{:S(2)}) collective-permute-start(bf16[640,768]{1,0:T(8,128)(2,1)} %fusion.17), channel_id=1, source_target_pairs={{4,2},{6,4},{5,3},{7,5},{12,10},{14,12},{13,11},{15,13},{20,18},{2... | collective-permute-start | bytes 2949128 | tf_op jit(solution)/shard_map/ppermute | solution.py:1377
  435.3 30.2 %collective-permute-start.58 = (bf16[4,208,384]{2,1,0:T(8,128)(2,1)}, bf16[4,208,384]{2,1,0:T(8,128)(2,1)}, u32[]{:S(2)}, u32[]{:S(2)}) collective-permute-start(bf16[4,208,384]{2,1,0:T(8,128)(2,1)} %get-tuple-element.296), channel_id=1, source_target_pairs={{0,24},{8,16},{16,8},{24,0},{1,25},{9,17},{17,9},{25,1},{2,26},{10... | collective-permute-start | bytes 1916936 | tf_op jit(solution)/shard_map/ppermute | solution.py:1078
  437.1 29.7 %collective-permute-start.57 = (bf16[4,208,384]{2,1,0:T(8,128)(2,1)S(1)}, bf16[4,208,384]{2,1,0:T(8,128)(2,1)}, u32[]{:S(2)}, u32[]{:S(2)}) collective-permute-start(bf16[4,208,384]{2,1,0:T(8,128)(2,1)S(1)} %get-tuple-element.295), channel_id=1, source_target_pairs={{0,16},{8,24},{16,0},{24,8},{1,17},{9,25},{17,1},{25,9},{2,18},{10... | collective-permute-start | bytes 1916936 | tf_op jit(solution)/shard_map/ppermute | solution.py:1078
  460.0 26.6 %collective-permute-start.54 = (bf16[640,768]{1,0:T(8,128)(2,1)S(1)}, bf16[640,768]{1,0:T(8,128)(2,1)S(1)}, u32[]{:S(2)}, u32[]{:S(2)}) collective-permute-start(bf16[640,768]{1,0:T(8,128)(2,1)S(1)} %pad_select_fusion), channel_id=1, source_target_pairs={{2,0},{4,2},{6,4},{3,1},{5,3},{7,5},{10,8},{12,10},{14,12},{11,9},... | collective-permute-start | bytes 2949128 | tf_op jit(solution)/shard_map/ppermute | solution.py:1377
  468.9 30.7 %collective-permute-start.61 = (bf16[208,384]{1,0:T(8,128)(2,1)S(1)}, bf16[208,384]{1,0:T(8,128)(2,1)S(1)}, u32[]{:S(2)}, u32[]{:S(2)}) collective-permute-start(bf16[208,384]{1,0:T(8,128)(2,1)S(1)} %get-tuple-element.345), channel_id=1, source_target_pairs={{0,6},{2,0},{4,2},{6,4},{1,7},{3,1},{5,3},{7,5},{8,14},{10,8},{12,... | collective-permute-start | bytes 479240 | tf_op jit(solution)/shard_map/ppermute | solution.py:1094
  471.2 28.4 %collective-permute-start.60 = (bf16[208,384]{1,0:T(8,128)(2,1)S(1)}, bf16[208,384]{1,0:T(8,128)(2,1)S(1)}, u32[]{:S(2)}, u32[]{:S(2)}) collective-permute-start(bf16[208,384]{1,0:T(8,128)(2,1)S(1)} %get-tuple-element.346), channel_id=1, source_target_pairs={{0,4},{2,6},{4,0},{6,2},{1,5},{3,7},{5,1},{7,3},{8,12},{10,14},{12... | collective-permute-start | bytes 479240 | tf_op jit(solution)/shard_map/ppermute | solution.py:1094
  471.2 28.4 %collective-permute-start.59 = (bf16[208,384]{1,0:T(8,128)(2,1)S(1)}, bf16[208,384]{1,0:T(8,128)(2,1)S(1)}, u32[]{:S(2)}, u32[]{:S(2)}) collective-permute-start(bf16[208,384]{1,0:T(8,128)(2,1)S(1)} %get-tuple-element.344), channel_id=1, source_target_pairs={{0,2},{2,4},{4,6},{6,0},{1,3},{3,5},{5,7},{7,1},{8,10},{10,12},{12... | collective-permute-start | bytes 479240 | tf_op jit(solution)/shard_map/ppermute | solution.py:1094
  472.9 30.5 %collective-permute-start.52 = (f32[640,768]{1,0:T(8,128)S(1)}, f32[640,768]{1,0:T(8,128)S(1)}, u32[]{:S(2)}, u32[]{:S(2)}) collective-permute-start(f32[640,768]{1,0:T(8,128)S(1)} %multiply_add_fusion), channel_id=1, source_target_pairs={{0,1},{1,0},{2,3},{3,2},{4,5},{5,4},{6,7},{7,6},{8,9},{9,8},{10,11... | collective-permute-start | bytes 5898248 | tf_op jit(solution)/shard_map/ppermute | solution.py:1078
  (115 other events, 1693.4 us)

commit v7 on v6

--- a/solution.py
+++ b/solution.py
@@ -1392,8 +1392,6 @@
     came = pin(came, plane_parts[0])
     part2 = jnp.pad(part2, ((0, rows - edge), (0, 0)))
     came = down(jnp.where(ctx == 3, part2, jnp.where(ctx == 2, plus(part1, came), plus(part0, came))), 3)
-    base = jnp.where(ctx == 0, part0, jnp.where(ctx == 1, part1, part2)).astype(full)
-    extra = jnp.where(ctx == 3, 0.0, base + came.astype(full))
     came_rows = pin(came_rows, plane_parts[0]).astype(full)
     kept_rows = dw[0].astype(full) + got[0].astype(full)
     first = jnp.where(lower, kept_rows, came_rows)
@@ -1402,6 +1400,9 @@
         [jnp.stack([first[0], first[1]], axis=1), jnp.stack([second_e[0], second_e[1]], axis=1)], axis=1
     )
     d_down = jnp.stack([first[2], second_e[2]], axis=1)
+    came = pin(came, d_gate_up, d_down)
+    base = jnp.where(ctx == 0, part0, jnp.where(ctx == 1, part1, part2)).astype(full)
+    extra = jnp.where(ctx == 3, 0.0, base + came.astype(full))
     d_normed = d_near + extra
     unit_own, inv_own = unit_of(x_own)
     gain_a = gain_a[0]

time: 527 us -> 572 us (1.085)
  waiting for transfers between devices: 139 us -> 168 us
  local copies, waits for them, and re-layouts: 55.8 us -> 65 us
  other arithmetic: 50.8 us -> 58.9 us
    ppermute x46, waiting for transfers between devices: 92.9 us -> 118 us  [flip(): return lax.ppermute(x, axis, [(i, i ^ bit) for i in range(size)])]
    unnamed x157 -> x165, local copies, waits for them, and re-layouts: 21.8 us -> 23.3 us
  transfers between devices with their start and end apart: 66 -> 66, of which waited for: 26 -> 27; matrix products, arithmetic and copies ran while one was open for 16% -> 18% of each run, Pallas kernels for 36% -> 33%
where the time goes in v7:
time: 572 us; the launch traced here: 564 us
  Pallas kernels  192 us (34%)
  waiting for transfers between devices  168 us (29%)
  starting transfers between devices  78.2 us (14%)
  local copies, waits for them, and re-layouts  65 us (11%)
  other arithmetic  58.9 us (10%)
    ppermute x46, waiting for transfers between devices, flip(): return lax.ppermute(x, axis, [(i, i ^ bit) for i in range(size)])  118 us
    pallas_call x7, Pallas kernels, call(): pl.pallas_call(kernel, grid_spec=spec, out_shape=[jax.ShapeDtypeStruct(*o...  113 us
    ppermute x46, starting transfers between devices, flip(): return lax.ppermute(x, axis, [(i, i ^ bit) for i in range(size)])  45.2 us
    pallas_call x3, Pallas kernels, attend_back(): pl.pallas_call(functools.partial(attend_back_kernel, own, seg, HEAD_DIM,...  36.1 us
    ppermute x8, waiting for transfers between devices, far(): return lax.ppermute(x, ('shard', 'ctx'), pairs)  23.7 us
    unnamed x165, local copies, waits for them, and re-layouts  23.3 us
    pallas_call x2, Pallas kernels, attend(): pl.pallas_call(functools.partial(attend_kernel, own, seg, HEAD_DIM, len(p...  21.4 us
    ppermute x3, waiting for transfers between devices, down(): lax.ppermute(x, 'ctx', [(i, i - 1) for i in range(ctx_n - step, ctx_n)])  13.8 us
  transfers between devices with their start and end apart: 66, of which 27 were waited for; matrix products, arithmetic and copies ran while one was open for 18% of the time, Pallas kernels for 33%

profile of v7, /device:TPU:0, one launch (start us, length us, event | category | flops | bytes accessed | tf_op | source)
XLA Modules:
  0.0 563.9 jit_solution(218595646461555294)
XLA Ops:
  29.9 8.3 %collective-permute-done.near = bf16[640,768]{1,0:T(8,128)(2,1)} collective-permute-done((bf16[640,768]{1,0:T(8,128)(2,1)S(1)}, bf16[640,768]{1,0:T(8,128)(2,1)}, u32[]{:S(2)}, u32[]{:S(2)}) %collective-permute-start) | collective-permute-done | bytes 983072 | tf_op jit(solution)/shard_map/ppermute | solution.py:1165
  42.3 10.7 %collective-permute-done.7 = bf16[768,384]{1,0:T(8,128)(2,1)} collective-permute-done((bf16[768,384]{1,0:T(8,128)(2,1)S(1)}, bf16[768,384]{1,0:T(8,128)(2,1)}, u32[]{:S(2)}, u32[]{:S(2)}) %collective-permute-start.7) | collective-permute-done | bytes 589856 | tf_op jit(solution)/shard_map/ppermute | solution.py:1078
  67.8 7.6 %collective-permute-start.10 = (bf16[4,224,384]{2,1,0:T(8,128)(2,1)}, bf16[4,224,384]{2,1,0:T(8,128)(2,1)}, u32[]{:S(2)}, u32[]{:S(2)}) collective-permute-start(bf16[4,224,384]{2,1,0:T(8,128)(2,1)} %pad_maximum_fusion.7), channel_id=1, source_target_pairs={{0,4},{2,6},{4,0},{6,2},{1,5},{3,7},{5,1},{7,3},{8,12},{10,14},{12... | collective-permute-start | bytes 2064392 | tf_op jit(solution)/shard_map/ppermute | solution.py:1078
  79.4 23.3 %collective-permute-done.10 = bf16[4,224,384]{2,1,0:T(8,128)(2,1)} collective-permute-done((bf16[4,224,384]{2,1,0:T(8,128)(2,1)}, bf16[4,224,384]{2,1,0:T(8,128)(2,1)}, u32[]{:S(2)}, u32[]{:S(2)}) %collective-permute-start.10) | collective-permute-done | bytes 688160 | tf_op jit(solution)/shard_map/ppermute | solution.py:1078
  102.7 6.5 %collective-permute-start.12 = (bf16[3,192,1024]{2,1,0:T(8,128)(2,1)}, bf16[3,192,1024]{2,1,0:T(8,128)(2,1)}, u32[]{:S(2)}, u32[]{:S(2)}) collective-permute-start(bf16[3,192,1024]{2,1,0:T(8,128)(2,1)} %get-tuple-element.142), channel_id=1, source_target_pairs={{0,4},{2,6},{4,0},{6,2},{1,5},{3,7},{5,1},{7,3},{8,12},{10,14},{12... | collective-permute-start | bytes 3538952 | tf_op jit(solution)/shard_map/ppermute | solution.py:1078
  113.9 15.0 %project.1 = (bf16[640,768]{1,0:T(8,128)(2,1)S(1)}, bf16[2176,1536]{1,0:T(8,128)(2,1)}, bf16[2176,768]{1,0:T(8,128)(2,1)S(1)}, bf16[2176,768]{1,0:T(8,128)(2,1)}) custom-call(s32[3]{0:T(128)S(1)} %pad_add_fusion.1.place.where_ref, bf16[640,768]{1,0:T(8,128)(2,1)S(1)} %dynamic-slice_bitcast_fusion.2.x0.x, bf16[640,768]{1,0:T(8,128)(2,1)} %collective-permute-done.near, ...), custom_call_target="tpu_custom_call" | custom-call | flops 1000 | bytes 1000 | tf_op jit(solution)/shard_map/project/pallas_call | solution.py:867
  131.5 10.7 %attend.2 = (bf16[640,768]{1,0:T(8,128)(2,1)}, f32[6,8,256]{2,1,0:T(8,128)}) custom-call(s32[5,3]{1,0:T(8,128)} %pad_add_fusion.info, bf16[640,768]{1,0:T(8,128)(2,1)} %copy-done.9, bf16[2176,1536]{1,0:T(8,128)(2,1)} %get-tuple-element.135.k_ref.v_ref, bf16[2176,1536]{1,0:T(8,128)(2,1)} %get-tuple-element.135.k_ref.v_ref), custom_call_target="tpu_custom_call" | custom-call | flops 1000 | bytes 1000 | tf_op jit(solution)/shard_map/attend/pallas_call | solution.py:510
  148.7 10.7 %attend.3 = (bf16[640,768]{1,0:T(8,128)(2,1)}, f32[6,8,256]{2,1,0:T(8,128)}) custom-call(s32[5,3]{1,0:T(8,128)} %pad_add_fusion.info, bf16[640,768]{1,0:T(8,128)(2,1)} %copy-done.9, bf16[2176,1536]{1,0:T(8,128)(2,1)} %get-tuple-element.135.k_ref.v_ref, ...), custom_call_target="tpu_custom_call", output_to_operand_aliasing={{0}: (4, {}), {1}: (5, {})} | custom-call | flops 1000 | bytes 1000 | tf_op jit(solution)/shard_map/attend/pallas_call | solution.py:510
  197.0 22.9 %expert_pass.2 = (bf16[896,384]{1,0:T(8,128)(2,1)S(1)}, bf16[896,384]{1,0:T(8,128)(2,1)}, bf16[896,384]{1,0:T(8,128)(2,1)S(1)}, bf16[896,384]{1,0:T(8,128)(2,1)S(1)}, bf16[4,3,192,1024]{3,2,1,0:T(8,128)(2,1)}) custom-call(s32[2]{0:T(128)S(1)} %pad_add_fusion.2.place, bf16[896,384]{1,0:T(8,128)(2,1)S(1)} %constant_dynamic-update-slice_fusion.2.xm_ref, ...), custom_call_target="tpu_custom_call" | custom-call | flops 1000 | bytes 1000 | tf_op jit(solution)/shard_map/expert_pass/pallas_call | solution.py:867
  226.2 24.5 %expert_pass.3 = (bf16[896,384]{1,0:T(8,128)(2,1)S(1)}, bf16[896,384]{1,0:T(8,128)(2,1)}, bf16[896,384]{1,0:T(8,128)(2,1)S(1)}, bf16[896,384]{1,0:T(8,128)(2,1)S(1)}, bf16[4,3,192,1024]{3,2,1,0:T(8,128)(2,1)}) custom-call(s32[2]{0:T(128)S(1)} %pad_add_fusion.2.place, bf16[896,384]{1,0:T(8,128)(2,1)S(1)} %constant_dynamic-update-slice_fusion.6.xm_ref, ...), custom_call_target="tpu_custom_call" | custom-call | flops 1000 | bytes 1000 | tf_op jit(solution)/shard_map/expert_pass/pallas_call | solution.py:867
  268.0 8.1 %collective-permute-done.34.rest_4_ = bf16[224,384]{1,0:T(8,128)(2,1)S(1)} collective-permute-done((bf16[224,384]{1,0:T(8,128)(2,1)S(1)}, bf16[224,384]{1,0:T(8,128)(2,1)S(1)}, u32[]{:S(2)}, u32[]{:S(2)}) %collective-permute-start.34) | collective-permute-done | bytes 172064 | tf_op jit(solution)/shard_map/ppermute | solution.py:1104
  288.4 6.9 %gather.12 = (bf16[640,384]{1,0:T(8,128)(2,1)}, bf16[640,384]{1,0:T(8,128)(2,1)}, f32[640,2]{1,0:T(8,128)}, f32[640,2]{1,0:T(8,128)}) custom-call(s32[3]{0:T(128)} %copy-done.32, s32[1280,2]{1,0:T(8,128)} %bitcast.190, f32[1280,1]{1,0:T(8,128)} %copy.182.pair_ref, bf16[224,384]{1,0:T(8,128)(2,1)} %get-tuple-element.337.rest_0_, bf16[224,384]{1,0:T(8,128)(2,1)} %copy-done.62, ...), custom_call_target="tpu_custom_call" | custom-call | flops 1000 | bytes 1000 | tf_op jit(solution)/shard_map/gather/pallas_call | solution.py:833
  300.8 16.2 %settle_back.1 = (f32[640,768]{1,0:T(8,128)}, bf16[640,768]{1,0:T(8,128)(2,1)}, bf16[640,768]{1,0:T(8,128)(2,1)}, f32[640,12]{1,0:T(8,128)}, f32[16,768]{1,0:T(8,128)}) custom-call(s32[3]{0:T(128)} %copy-done.32, bf16[640,384]{1,0:T(8,128)(2,1)} %get-tuple-element.175.dr_mine, bf16[640,384]{1,0:T(8,128)(2,1)} %copy-done.54, ...), custom_call_target="tpu_custom_call" | custom-call | flops 1000 | bytes 1000 | tf_op jit(solution)/shard_map/settle_back/pallas_call | solution.py:867
  320.5 12.0 %attend_back.3 = (bf16[640,768]{1,0:T(8,128)(2,1)S(1)}, bf16[2176,768]{1,0:T(8,128)(2,1)S(1)}, bf16[2176,768]{1,0:T(8,128)(2,1)S(1)}) custom-call(s32[5,3]{1,0:T(8,128)S(1)} %copy-done.30, bf16[640,768]{1,0:T(8,128)(2,1)S(1)} %copy-done.10, bf16[2176,1536]{1,0:T(8,128)(2,1)} %get-tuple-element.135.k_ref.v_ref, ...), custom_call_target="tpu_custom_call" | custom-call | flops 1000 | bytes 1000 | tf_op jit(solution)/shard_map/attend_back/pallas_call | solution.py:544
  339.4 11.9 %attend_back.4 = (bf16[640,768]{1,0:T(8,128)(2,1)S(1)}, bf16[2176,768]{1,0:T(8,128)(2,1)S(1)}, bf16[2176,768]{1,0:T(8,128)(2,1)S(1)}) custom-call(s32[5,3]{1,0:T(8,128)S(1)} %copy-done.30, bf16[640,768]{1,0:T(8,128)(2,1)S(1)} %copy-done.10, ...), custom_call_target="tpu_custom_call", output_to_operand_aliasing={{0}: (7, {}), {1}: (8, {}), {2}: (9, {})} | custom-call | flops 1000 | bytes 1000 | tf_op jit(solution)/shard_map/attend_back/pallas_call | solution.py:544
  351.4 12.1 %attend_back.5 = (bf16[640,768]{1,0:T(8,128)(2,1)S(1)}, bf16[2176,768]{1,0:T(8,128)(2,1)S(1)}, bf16[2176,768]{1,0:T(8,128)(2,1)S(1)}) custom-call(s32[5,3]{1,0:T(8,128)S(1)} %copy-done.30, bf16[640,768]{1,0:T(8,128)(2,1)S(1)} %copy-done.10, ...), custom_call_target="tpu_custom_call", output_to_operand_aliasing={{0}: (7, {}), {1}: (8, {}), {2}: (9, {})} | custom-call | flops 1000 | bytes 1000 | tf_op jit(solution)/shard_map/attend_back/pallas_call | solution.py:544
  370.9 15.6 %keys_back.1 = (f32[640,768]{1,0:T(8,128)}, bf16[640,768]{1,0:T(8,128)(2,1)}, bf16[640,768]{1,0:T(8,128)(2,1)}, bf16[256,768]{1,0:T(8,128)(2,1)}, f32[1,768]{1,0:T(1,128)}) custom-call(s32[3]{0:T(128)} %copy-done.32, bf16[640,768]{1,0:T(8,128)(2,1)} %copy-done.11, bf16[2176,768]{1,0:T(8,128)(2,1)} %copy-done.3, bf16[2176,768]{1,0:T(8,128)(2,1)} %copy-done.4, ...), custom_call_target="tpu_custom_call" | custom-call | flops 1000 | bytes 1000 | tf_op jit(solution)/shard_map/keys_back/pallas_call | solution.py:867
  396.2 14.2 %weights_back.1 = (bf16[4,4,208,384]{3,2,1,0:T(8,128)(2,1)}, bf16[4,4,208,384]{3,2,1,0:T(8,128)(2,1)}) custom-call(bf16[2176,768]{1,0:T(8,128)(2,1)} %copy-done.19, bf16[640,768]{1,0:T(8,128)(2,1)} %copy-done.11, bf16[2176,768]{1,0:T(8,128)(2,1)} %copy-done.3, bf16[2176,768]{1,0:T(8,128)(2,1)} %copy-done.4, bf16[640,768]{1,0:T(8,128)(2,1)} %get-tuple-element.203.da_ref, ...), custom_call_target="tpu_custom_call" | custom-call | flops 1000 | bytes 1000 | tf_op jit(solution)/shard_map/weights_back/pallas_call | solution.py:867
  410.5 14.1 %collective-permute-done.48 = bf16[3,192,1024]{2,1,0:T(8,128)(2,1)} collective-permute-done((bf16[3,192,1024]{2,1,0:T(8,128)(2,1)}, bf16[3,192,1024]{2,1,0:T(8,128)(2,1)}, u32[]{:S(2)}, u32[]{:S(2)}) %collective-permute-start.48) | collective-permute-done | bytes 1179680 | tf_op jit(solution)/shard_map/ppermute | solution.py:1078
  438.5 14.7 %collective-permute-done.50 = bf16[4,208,384]{2,1,0:T(8,128)(2,1)} collective-permute-done((bf16[4,208,384]{2,1,0:T(8,128)(2,1)}, bf16[4,208,384]{2,1,0:T(8,128)(2,1)}, u32[]{:S(2)}, u32[]{:S(2)}) %collective-permute-start.50) | collective-permute-done | bytes 639008 | tf_op jit(solution)/shard_map/ppermute | solution.py:1078
  453.2 5.8 %gather.13 = (bf16[640,384]{1,0:T(8,128)(2,1)}, bf16[640,384]{1,0:T(8,128)(2,1)}) custom-call(s32[3]{0:T(128)} %copy-done.32, s32[1280,2]{1,0:T(8,128)} %bitcast.191, f32[1280,2]{1,0:T(8,128)} %copy.185.pair_ref, bf16[2,224,384]{2,1,0:T(8,128)(2,1)} %get-tuple-element.217.rest_0_, bf16[2,224,384]{2,1,0:T(8,128)(2,1)} %copy-done.55, ...), custom_call_target="tpu_custom_call" | custom-call | flops 1000 | bytes 1000 | tf_op jit(solution)/shard_map/gather/pallas_call | solution.py:833
  473.2 13.8 %collective-permute-done.54 = bf16[640,768]{1,0:T(8,128)(2,1)S(1)} collective-permute-done((bf16[640,768]{1,0:T(8,128)(2,1)S(1)}, bf16[640,768]{1,0:T(8,128)(2,1)S(1)}, u32[]{:S(2)}, u32[]{:S(2)}) %collective-permute-start.54) | collective-permute-done | bytes 983072 | tf_op jit(solution)/shard_map/ppermute | solution.py:1377
  493.0 16.1 %collective-permute-done.58 = bf16[4,208,384]{2,1,0:T(8,128)(2,1)} collective-permute-done((bf16[4,208,384]{2,1,0:T(8,128)(2,1)}, bf16[4,208,384]{2,1,0:T(8,128)(2,1)}, u32[]{:S(2)}, u32[]{:S(2)}) %collective-permute-start.58) | collective-permute-done | bytes 639008 | tf_op jit(solution)/shard_map/ppermute | solution.py:1078
  509.1 13.6 %collective-permute-done.57 = bf16[4,208,384]{2,1,0:T(8,128)(2,1)} collective-permute-done((bf16[4,208,384]{2,1,0:T(8,128)(2,1)}, bf16[4,208,384]{2,1,0:T(8,128)(2,1)}, u32[]{:S(2)}, u32[]{:S(2)}) %collective-permute-start.57) | collective-permute-done | bytes 639008 | tf_op jit(solution)/shard_map/ppermute | solution.py:1078
  (426 shorter events, 246.5 us)
Async XLA Ops:
  11.3 26.9 %collective-permute-start = (bf16[640,768]{1,0:T(8,128)(2,1)S(1)}, bf16[640,768]{1,0:T(8,128)(2,1)}, u32[]{:S(2)}, u32[]{:S(2)}) collective-permute-start(bf16[640,768]{1,0:T(8,128)(2,1)S(1)} %dynamic-slice_bitcast_fusion.2.x0.x), channel_id=1, source_target_pairs={{0,2},{2,4},{4,6},{1,3},{3,5},{5,7},{8,10},{10,12},{12,14},{9,11},... | collective-permute-start | bytes 2949128 | tf_op jit(solution)/shard_map/ppermute | solution.py:1165
  38.3 25.7 %collective-permute-start.4 = (bf16[640,768]{1,0:T(8,128)(2,1)}, bf16[640,768]{1,0:T(8,128)(2,1)}, u32[]{:S(2)}, u32[]{:S(2)}) collective-permute-start(bf16[640,768]{1,0:T(8,128)(2,1)} %collective-permute-done.near), channel_id=1, source_target_pairs={{2,4},{4,6},{3,5},{5,7},{10,12},{12,14},{11,13},{13,15},{18,20},{2... | collective-permute-start | bytes 2949128 | tf_op jit(solution)/shard_map/ppermute | solution.py:1180
  54.9 59.0 %collective-permute-start.9 = (bf16[4,768,384]{2,1,0:T(8,128)(2,1)S(1)}, bf16[4,768,384]{2,1,0:T(8,128)(2,1)}, u32[]{:S(2)}, u32[]{:S(2)}) collective-permute-start(bf16[4,768,384]{2,1,0:T(8,128)(2,1)S(1)} %pad_maximum_fusion.1.wm), channel_id=1, source_target_pairs={{0,1},{1,0},{2,3},{3,2},{4,5},{5,4},{6,7},{7,6},{8,9},{9,8},{10,11... | collective-permute-start | bytes 7077896 | tf_op jit(solution)/shard_map/ppermute | solution.py:1078
  63.9 38.8 %collective-permute-start.5 = (bf16[640,768]{1,0:T(8,128)(2,1)}, bf16[640,768]{1,0:T(8,128)(2,1)}, u32[]{:S(2)}, u32[]{:S(2)}) collective-permute-start(bf16[640,768]{1,0:T(8,128)(2,1)} %collective-permute-done.4.mid), channel_id=1, source_target_pairs={{4,6},{5,7},{12,14},{13,15},{20,22},{21,23},{28,30},{29,31}} | collective-permute-start | bytes 2949128 | tf_op jit(solution)/shard_map/ppermute | solution.py:1205
  67.8 34.9 %collective-permute-start.10 = (bf16[4,224,384]{2,1,0:T(8,128)(2,1)}, bf16[4,224,384]{2,1,0:T(8,128)(2,1)}, u32[]{:S(2)}, u32[]{:S(2)}) collective-permute-start(bf16[4,224,384]{2,1,0:T(8,128)(2,1)} %pad_maximum_fusion.7), channel_id=1, source_target_pairs={{0,4},{2,6},{4,0},{6,2},{1,5},{3,7},{5,1},{7,3},{8,12},{10,14},{12... | collective-permute-start | bytes 2064392 | tf_op jit(solution)/shard_map/ppermute | solution.py:1078
  102.7 58.4 %collective-permute-start.11 = (bf16[3,192,1024]{2,1,0:T(8,128)(2,1)}, bf16[3,192,1024]{2,1,0:T(8,128)(2,1)}, u32[]{:S(2)}, u32[]{:S(2)}) collective-permute-start(bf16[3,192,1024]{2,1,0:T(8,128)(2,1)} %get-tuple-element.141.w0), channel_id=1, source_target_pairs={{0,2},{2,0},{4,6},{6,4},{1,3},{3,1},{5,7},{7,5},{8,10},{10,8},{12,... | collective-permute-start | bytes 3538952 | tf_op jit(solution)/shard_map/ppermute | solution.py:1078
  102.7 58.4 %collective-permute-start.12 = (bf16[3,192,1024]{2,1,0:T(8,128)(2,1)}, bf16[3,192,1024]{2,1,0:T(8,128)(2,1)}, u32[]{:S(2)}, u32[]{:S(2)}) collective-permute-start(bf16[3,192,1024]{2,1,0:T(8,128)(2,1)} %get-tuple-element.142), channel_id=1, source_target_pairs={{0,4},{2,6},{4,0},{6,2},{1,5},{3,7},{5,1},{7,3},{8,12},{10,14},{12... | collective-permute-start | bytes 3538952 | tf_op jit(solution)/shard_map/ppermute | solution.py:1078
  189.1 30.7 %collective-permute-start.24 = (bf16[224,384]{1,0:T(8,128)(2,1)S(1)}, bf16[224,384]{1,0:T(8,128)(2,1)S(1)}, u32[]{:S(2)}, u32[]{:S(2)}) collective-permute-start(bf16[224,384]{1,0:T(8,128)(2,1)S(1)} %get-tuple-element.161), channel_id=1, source_target_pairs={{0,4},{2,6},{4,0},{6,2},{8,12},{10,14},{12,8},{14,10},{16,20},{18,... | collective-permute-start | bytes 516104 | tf_op jit(solution)/shard_map/ppermute | solution.py:1104
  190.0 29.9 %collective-permute-start.25 = (bf16[224,384]{1,0:T(8,128)(2,1)S(1)}, bf16[224,384]{1,0:T(8,128)(2,1)S(1)}, u32[]{:S(2)}, u32[]{:S(2)}) collective-permute-start(bf16[224,384]{1,0:T(8,128)(2,1)S(1)} %get-tuple-element.162), channel_id=1, source_target_pairs={{0,12},{2,14},{4,8},{6,10},{8,4},{10,6},{12,0},{14,2},{16,28},{18,... | collective-permute-start | bytes 516104 | tf_op jit(solution)/shard_map/ppermute | solution.py:1104
  192.2 27.7 %collective-permute-start.26 = (bf16[224,384]{1,0:T(8,128)(2,1)S(1)}, bf16[224,384]{1,0:T(8,128)(2,1)S(1)}, u32[]{:S(2)}, u32[]{:S(2)}) collective-permute-start(bf16[224,384]{1,0:T(8,128)(2,1)S(1)} %get-tuple-element.163), channel_id=1, source_target_pairs={{0,20},{2,22},{4,16},{6,18},{8,28},{10,30},{12,24},{14,26},{16,4},... | collective-permute-start | bytes 516104 | tf_op jit(solution)/shard_map/ppermute | solution.py:1104
  194.2 29.7 %collective-permute-start.27 = (bf16[224,384]{1,0:T(8,128)(2,1)S(1)}, bf16[224,384]{1,0:T(8,128)(2,1)S(1)}, u32[]{:S(2)}, u32[]{:S(2)}) collective-permute-start(bf16[224,384]{1,0:T(8,128)(2,1)S(1)} %get-tuple-element.164), channel_id=1, source_target_pairs={{0,28},{2,30},{4,24},{6,26},{8,20},{10,22},{12,16},{14,18},{16,12}... | collective-permute-start | bytes 516104 | tf_op jit(solution)/shard_map/ppermute | solution.py:1104
  224.1 26.9 %collective-permute-start.29 = (bf16[896,384]{1,0:T(8,128)(2,1)S(1)}, bf16[896,384]{1,0:T(8,128)(2,1)S(1)}, u32[]{:S(2)}, u32[]{:S(2)}) collective-permute-start(bf16[896,384]{1,0:T(8,128)(2,1)S(1)} %get-tuple-element.172), channel_id=1, source_target_pairs={{0,1},{1,0},{2,3},{3,2},{4,5},{5,4},{6,7},{7,6},{8,9},{9,8},{10,11... | collective-permute-start | bytes 2064392 | tf_op jit(solution)/shard_map/ppermute | solution.py:1078
  262.6 25.1 %collective-permute-start.37 = (bf16[224,384]{1,0:T(8,128)(2,1)S(1)}, bf16[224,384]{1,0:T(8,128)(2,1)S(1)}, u32[]{:S(2)}, u32[]{:S(2)}) collective-permute-start(bf16[224,384]{1,0:T(8,128)(2,1)S(1)} %get-tuple-element.330), channel_id=1, source_target_pairs={{0,28},{2,30},{4,24},{6,26},{8,20},{10,22},{12,16},{14,18},{16,12}... | collective-permute-start | bytes 516104 | tf_op jit(solution)/shard_map/ppermute | solution.py:1104
  295.2 70.9 %collective-permute-start.43 = (bf16[2,3,192,1024]{3,2,1,0:T(8,128)(2,1)}, bf16[2,3,192,1024]{3,2,1,0:T(8,128)(2,1)}, u32[]{:S(2)}, u32[]{:S(2)}) collective-permute-start(bf16[2,3,192,1024]{3,2,1,0:T(8,128)(2,1)} %slice.251), channel_id=1, source_target_pairs={{0,2},{2,0},{4,6},{6,4},{1,3},{3,1},{5,7},{7,5},{8,10},{10,8},{12,... | collective-permute-start | bytes 7077896 | tf_op jit(solution)/shard_map/ppermute | solution.py:1078
  295.2 37.3 %collective-permute-start.38 = (bf16[896,384]{1,0:T(8,128)(2,1)}, bf16[896,384]{1,0:T(8,128)(2,1)}, u32[]{:S(2)}, u32[]{:S(2)}) collective-permute-start(bf16[896,384]{1,0:T(8,128)(2,1)} %get-tuple-element.176), channel_id=1, source_target_pairs={{0,1},{1,0},{2,3},{3,2},{4,5},{5,4},{6,7},{7,6},{8,9},{9,8},{10,11... | collective-permute-start | bytes 2064392 | tf_op jit(solution)/shard_map/ppermute | solution.py:1078
  295.8 39.0 %collective-permute-start.39 = (bf16[896,384]{1,0:T(8,128)(2,1)}, bf16[896,384]{1,0:T(8,128)(2,1)}, u32[]{:S(2)}, u32[]{:S(2)}) collective-permute-start(bf16[896,384]{1,0:T(8,128)(2,1)} %get-tuple-element.178), channel_id=1, source_target_pairs={{0,1},{1,0},{2,3},{3,2},{4,5},{5,4},{6,7},{7,6},{8,9},{9,8},{10,11... | collective-permute-start | bytes 2064392 | tf_op jit(solution)/shard_map/ppermute | solution.py:1078
  336.9 51.4 %collective-permute-start.42 = (bf16[4,224,384]{2,1,0:T(8,128)(2,1)}, bf16[4,224,384]{2,1,0:T(8,128)(2,1)}, u32[]{:S(2)}, u32[]{:S(2)}) collective-permute-start(bf16[4,224,384]{2,1,0:T(8,128)(2,1)} %bitcast.61), channel_id=1, source_target_pairs={{0,4},{2,6},{4,0},{6,2},{1,5},{3,7},{5,1},{7,3},{8,12},{10,14},{12... | collective-permute-start | bytes 2064392 | tf_op jit(solution)/shard_map/ppermute | solution.py:1078
  370.5 54.1 %collective-permute-start.48 = (bf16[3,192,1024]{2,1,0:T(8,128)(2,1)}, bf16[3,192,1024]{2,1,0:T(8,128)(2,1)}, u32[]{:S(2)}, u32[]{:S(2)}) collective-permute-start(bf16[3,192,1024]{2,1,0:T(8,128)(2,1)} %fusion.13), channel_id=1, source_target_pairs={{0,4},{2,6},{4,0},{6,2},{1,5},{3,7},{5,1},{7,3},{8,12},{10,14},{12... | collective-permute-start | bytes 3538952 | tf_op jit(solution)/shard_map/ppermute | solution.py:1078
  427.5 31.5 %collective-permute-start.53 = (bf16[640,768]{1,0:T(8,128)(2,1)}, bf16[640,768]{1,0:T(8,128)(2,1)}, u32[]{:S(2)}, u32[]{:S(2)}) collective-permute-start(bf16[640,768]{1,0:T(8,128)(2,1)} %fusion.17), channel_id=1, source_target_pairs={{4,2},{6,4},{5,3},{7,5},{12,10},{14,12},{13,11},{15,13},{20,18},{2... | collective-permute-start | bytes 2949128 | tf_op jit(solution)/shard_map/ppermute | solution.py:1377
  461.0 26.0 %collective-permute-start.54 = (bf16[640,768]{1,0:T(8,128)(2,1)S(1)}, bf16[640,768]{1,0:T(8,128)(2,1)S(1)}, u32[]{:S(2)}, u32[]{:S(2)}) collective-permute-start(bf16[640,768]{1,0:T(8,128)(2,1)S(1)} %pad_select_fusion), channel_id=1, source_target_pairs={{2,0},{4,2},{6,4},{3,1},{5,3},{7,5},{10,8},{12,10},{14,12},{11,9},... | collective-permute-start | bytes 2949128 | tf_op jit(solution)/shard_map/ppermute | solution.py:1377
  472.7 74.0 %collective-permute-start.52 = (f32[640,768]{1,0:T(8,128)}, f32[640,768]{1,0:T(8,128)}, u32[]{:S(2)}, u32[]{:S(2)}) collective-permute-start(f32[640,768]{1,0:T(8,128)} %multiply_add_fusion), channel_id=1, source_target_pairs={{0,1},{1,0},{2,3},{3,2},{4,5},{5,4},{6,7},{7,6},{8,9},{9,8},{10,11... | collective-permute-start | bytes 5898248 | tf_op jit(solution)/shard_map/ppermute | solution.py:1078
  491.0 60.1 %collective-permute-start.55 = (f32[640,768]{1,0:T(8,128)}, f32[640,768]{1,0:T(8,128)}, u32[]{:S(2)}, u32[]{:S(2)}) collective-permute-start(f32[640,768]{1,0:T(8,128)} %fusion.5), channel_id=1, source_target_pairs={{0,1},{1,0},{2,3},{3,2},{4,5},{5,4},{6,7},{7,6},{8,9},{9,8},{10,11... | collective-permute-start | bytes 5898248 | tf_op jit(solution)/shard_map/ppermute | solution.py:1078
  492.7 30.0 %collective-permute-start.57 = (bf16[4,208,384]{2,1,0:T(8,128)(2,1)}, bf16[4,208,384]{2,1,0:T(8,128)(2,1)}, u32[]{:S(2)}, u32[]{:S(2)}) collective-permute-start(bf16[4,208,384]{2,1,0:T(8,128)(2,1)} %get-tuple-element.297), channel_id=1, source_target_pairs={{0,16},{8,24},{16,0},{24,8},{1,17},{9,25},{17,1},{25,9},{2,18},{10... | collective-permute-start | bytes 1916936 | tf_op jit(solution)/shard_map/ppermute | solution.py:1078
  493.0 34.3 %collective-permute-start.56 = (f32[640,12]{1,0:T(8,128)S(1)}, f32[640,12]{1,0:T(8,128)S(1)}, u32[]{:S(2)}, u32[]{:S(2)}) collective-permute-start(f32[640,12]{1,0:T(8,128)S(1)} %copy-done.59), channel_id=1, source_target_pairs={{0,1},{1,0},{2,3},{3,2},{4,5},{5,4},{6,7},{7,6},{8,9},{9,8},{10,11... | collective-permute-start | bytes 92168 | tf_op jit(solution)/shard_map/ppermute | solution.py:1078
  (119 other events, 1699.0 us)

commit v8 on v6

--- a/solution.py
+++ b/solution.py
@@ -612,25 +612,27 @@
         return pl.ds(pl.multiple_of((place[0] ^ r) * part, 64), part)
 
     for r, w in enumerate((w0, w1, w2, w3)):
-        wb[:, rows_of(r), :] = w[...]
-    u = mm(x_ref[...], wb[0])
-    up = mm(x_ref[...], wb[1])
+        for k in range(3):
+            wb[rows_of(r), k * PIECE : (k + 1) * PIECE] = w[k]
+    pair = mm(x_ref[...], wb[:, : 2 * PIECE])
+    u, up = pair[:, :PIECE], pair[:, PIECE:]
     sigma = 1.0 / (1.0 + jnp.exp(-u))
     silu = u * sigma
     hidden = (silu * up).astype(low)
-    oa[...] += mm(hidden, wb[2], NT)
-    dh = mm(d_ref[...], wb[2])
+    oa[...] += mm(hidden, wb[:, 2 * PIECE :], NT)
+    dh = mm(d_ref[...], wb[:, 2 * PIECE :])
     du = (dh * up * sigma * (1.0 + u * (1.0 - sigma))).astype(low)
     dup = (dh * silu).astype(low)
-    sa[...] += mm(du, wb[0], NT) + mm(dup, wb[1], NT)
-    gb[0] = mm(xt[...], du).astype(low)
-    gb[1] = mm(xt[...], dup).astype(low)
-    gb[2] = mm(dt[...], hidden).astype(low)
+    d_pair = jnp.concatenate([du, dup], axis=1)
+    sa[...] += mm(d_pair, wb[:, : 2 * PIECE], NT)
+    gb[:, : 2 * PIECE] = mm(xt[...], d_pair).astype(low)
+    gb[:, 2 * PIECE :] = mm(dt[...], hidden).astype(low)
     for at, r in enumerate(SENT):
-        got = gb[:, rows_of(r), :]
-        if more:
-            got = (got.astype(full) + rest[0][at].astype(full)).astype(low)
-        dw_ref[at] = got
+        for k in range(3):
+            got = gb[rows_of(r), k * PIECE : (k + 1) * PIECE]
+            if more:
+                got = (got.astype(full) + rest[0][at, k].astype(full)).astype(low)
+            dw_ref[at, k] = got
 
     @pl.when(pl.program_id(0) == pl.num_programs(0) - 1)
     def finish():
@@ -676,8 +678,8 @@
             pltpu.VMEM((rows, width), low),
             pltpu.VMEM((rows, width), jnp.float32),
             pltpu.VMEM((rows, width), jnp.float32),
-            pltpu.VMEM((three, width, PIECE), low),
-            pltpu.VMEM((three, width, PIECE), low),
+            pltpu.VMEM((width, three * PIECE), low),
+            pltpu.VMEM((width, three * PIECE), low),
         ],
         grid=(units // PIECE,),
         in_specs=[half] * 4 + [strip] * 4 + [strips] * more,

time: 527 us -> 529 us (level)
  no operation moved by 1% of the time
where the time goes in v8:
time: 529 us; the launch traced here: 521 us
  Pallas kernels  196 us (37%)
  waiting for transfers between devices  135 us (26%)
  starting transfers between devices  80.6 us (15%)
  local copies, waits for them, and re-layouts  55.8 us (11%)
  other arithmetic  50.8 us (10%)
    pallas_call x7, Pallas kernels, call(): pl.pallas_call(kernel, grid_spec=spec, out_shape=[jax.ShapeDtypeStruct(*o...  117 us
    ppermute x46, waiting for transfers between devices, flip(): return lax.ppermute(x, axis, [(i, i ^ bit) for i in range(size)])  91.9 us
    ppermute x46, starting transfers between devices, flip(): return lax.ppermute(x, axis, [(i, i ^ bit) for i in range(size)])  45.9 us
    pallas_call x3, Pallas kernels, attend_back(): pl.pallas_call(functools.partial(attend_back_kernel, own, seg, HEAD_DIM,...  36.1 us
    ppermute x8, waiting for transfers between devices, far(): return lax.ppermute(x, ('shard', 'ctx'), pairs)  22 us
    unnamed x157, local copies, waits for them, and re-layouts  21.8 us
    pallas_call x2, Pallas kernels, attend(): pl.pallas_call(functools.partial(attend_kernel, own, seg, HEAD_DIM, len(p...  21.4 us
    ppermute x3, waiting for transfers between devices, down(): lax.ppermute(x, 'ctx', [(i, i - 1) for i in range(ctx_n - step, ctx_n)])  13.1 us
  transfers between devices with their start and end apart: 66, of which 26 were waited for; matrix products, arithmetic and copies ran while one was open for 16% of the time, Pallas kernels for 36%

profile of v8, /device:TPU:0, one launch (start us, length us, event | category | flops | bytes accessed | tf_op | source)
XLA Modules:
  0.0 521.0 jit_solution(5658086564399385608)
XLA Ops:
  16.1 5.2 convert_reduce_fusion
  29.9 8.4 %collective-permute-done.near = bf16[640,768]{1,0:T(8,128)(2,1)} collective-permute-done((bf16[640,768]{1,0:T(8,128)(2,1)S(1)}, bf16[640,768]{1,0:T(8,128)(2,1)}, u32[]{:S(2)}, u32[]{:S(2)}) %collective-permute-start) | collective-permute-done | bytes 983072 | tf_op jit(solution)/shard_map/ppermute | solution.py:1167
  42.2 10.7 %collective-permute-done.7 = bf16[768,384]{1,0:T(8,128)(2,1)} collective-permute-done((bf16[768,384]{1,0:T(8,128)(2,1)S(1)}, bf16[768,384]{1,0:T(8,128)(2,1)}, u32[]{:S(2)}, u32[]{:S(2)}) %collective-permute-start.7) | collective-permute-done | bytes 589856 | tf_op jit(solution)/shard_map/ppermute | solution.py:1080
  55.0 5.2 %spread.2 = (bf16[224,384]{1,0:T(8,128)(2,1)}, bf16[224,384]{1,0:T(8,128)(2,1)}, bf16[224,384]{1,0:T(8,128)(2,1)}, bf16[224,384]{1,0:T(8,128)(2,1)}, bf16[224,38...) custom-call(s32[2,1280]{1,0:T(2,128)} %copy.170.place_ref, ...), custom_call_target="tpu_custom_call" | custom-call | flops 1000 | bytes 1000 | tf_op jit(solution)/shard_map/spread/pallas_call | solution.py:723
  67.8 7.6 %collective-permute-start.10 = (bf16[4,224,384]{2,1,0:T(8,128)(2,1)}, bf16[4,224,384]{2,1,0:T(8,128)(2,1)}, u32[]{:S(2)}, u32[]{:S(2)}) collective-permute-start(bf16[4,224,384]{2,1,0:T(8,128)(2,1)} %pad_maximum_fusion.7), channel_id=1, source_target_pairs={{0,4},{2,6},{4,0},{6,2},{1,5},{3,7},{5,1},{7,3},{8,12},{10,14},{12... | collective-permute-start | bytes 2064392 | tf_op jit(solution)/shard_map/ppermute | solution.py:1080
  79.4 23.3 %collective-permute-done.10 = bf16[4,224,384]{2,1,0:T(8,128)(2,1)} collective-permute-done((bf16[4,224,384]{2,1,0:T(8,128)(2,1)}, bf16[4,224,384]{2,1,0:T(8,128)(2,1)}, u32[]{:S(2)}, u32[]{:S(2)}) %collective-permute-start.10) | collective-permute-done | bytes 688160 | tf_op jit(solution)/shard_map/ppermute | solution.py:1080
  102.7 6.5 %collective-permute-start.12 = (bf16[3,192,1024]{2,1,0:T(8,128)(2,1)}, bf16[3,192,1024]{2,1,0:T(8,128)(2,1)}, u32[]{:S(2)}, u32[]{:S(2)}) collective-permute-start(bf16[3,192,1024]{2,1,0:T(8,128)(2,1)} %get-tuple-element.141), channel_id=1, source_target_pairs={{0,4},{2,6},{4,0},{6,2},{1,5},{3,7},{5,1},{7,3},{8,12},{10,14},{12... | collective-permute-start | bytes 3538952 | tf_op jit(solution)/shard_map/ppermute | solution.py:1080
  113.9 14.9 %project.1 = (bf16[640,768]{1,0:T(8,128)(2,1)S(1)}, bf16[2176,1536]{1,0:T(8,128)(2,1)}, bf16[2176,768]{1,0:T(8,128)(2,1)S(1)}, bf16[2176,768]{1,0:T(8,128)(2,1)}) custom-call(s32[3]{0:T(128)S(1)} %pad_add_fusion.1.place.where_ref, bf16[640,768]{1,0:T(8,128)(2,1)S(1)} %dynamic-slice_bitcast_fusion.2.x0.x, bf16[640,768]{1,0:T(8,128)(2,1)} %collective-permute-done.near, ...), custom_call_target="tpu_custom_call" | custom-call | flops 1000 | bytes 1000 | tf_op jit(solution)/shard_map/project/pallas_call | solution.py:869
  131.5 10.7 %attend.2 = (bf16[640,768]{1,0:T(8,128)(2,1)}, f32[6,8,256]{2,1,0:T(8,128)}) custom-call(s32[5,3]{1,0:T(8,128)} %pad_add_fusion.info, bf16[640,768]{1,0:T(8,128)(2,1)} %copy-done.9, bf16[2176,1536]{1,0:T(8,128)(2,1)} %get-tuple-element.134.k_ref.v_ref, bf16[2176,1536]{1,0:T(8,128)(2,1)} %get-tuple-element.134.k_ref.v_ref), custom_call_target="tpu_custom_call" | custom-call | flops 1000 | bytes 1000 | tf_op jit(solution)/shard_map/attend/pallas_call | solution.py:510
  148.6 10.7 %attend.3 = (bf16[640,768]{1,0:T(8,128)(2,1)}, f32[6,8,256]{2,1,0:T(8,128)}) custom-call(s32[5,3]{1,0:T(8,128)} %pad_add_fusion.info, bf16[640,768]{1,0:T(8,128)(2,1)} %copy-done.9, bf16[2176,1536]{1,0:T(8,128)(2,1)} %get-tuple-element.134.k_ref.v_ref, ...), custom_call_target="tpu_custom_call", output_to_operand_aliasing={{0}: (4, {}), {1}: (5, {})} | custom-call | flops 1000 | bytes 1000 | tf_op jit(solution)/shard_map/attend/pallas_call | solution.py:510
  197.0 25.5 %expert_pass.2 = (bf16[896,384]{1,0:T(8,128)(2,1)S(1)}, bf16[896,384]{1,0:T(8,128)(2,1)}, bf16[896,384]{1,0:T(8,128)(2,1)S(1)}, bf16[896,384]{1,0:T(8,128)(2,1)S(1)}, bf16[4,3,192,1024]{3,2,1,0:T(8,128)(2,1)}) custom-call(s32[2]{0:T(128)S(1)} %pad_add_fusion.2.place, bf16[896,384]{1,0:T(8,128)(2,1)S(1)} %constant_dynamic-update-slice_fusion.2.xm_ref, ...), custom_call_target="tpu_custom_call" | custom-call | flops 1000 | bytes 1000 | tf_op jit(solution)/shard_map/expert_pass/pallas_call | solution.py:869
  226.2 26.5 %expert_pass.3 = (bf16[896,384]{1,0:T(8,128)(2,1)S(1)}, bf16[896,384]{1,0:T(8,128)(2,1)}, bf16[896,384]{1,0:T(8,128)(2,1)S(1)}, bf16[896,384]{1,0:T(8,128)(2,1)S(1)}, bf16[4,3,192,1024]{3,2,1,0:T(8,128)(2,1)}) custom-call(s32[2]{0:T(128)S(1)} %pad_add_fusion.2.place, bf16[896,384]{1,0:T(8,128)(2,1)S(1)} %constant_dynamic-update-slice_fusion.6.xm_ref, ...), custom_call_target="tpu_custom_call" | custom-call | flops 1000 | bytes 1000 | tf_op jit(solution)/shard_map/expert_pass/pallas_call | solution.py:869
  270.2 8.9 %collective-permute-done.34.rest_4_ = bf16[224,384]{1,0:T(8,128)(2,1)S(1)} collective-permute-done((bf16[224,384]{1,0:T(8,128)(2,1)S(1)}, bf16[224,384]{1,0:T(8,128)(2,1)S(1)}, u32[]{:S(2)}, u32[]{:S(2)}) %collective-permute-start.34) | collective-permute-done | bytes 172064 | tf_op jit(solution)/shard_map/ppermute | solution.py:1106
  291.5 6.9 %gather.12 = (bf16[640,384]{1,0:T(8,128)(2,1)}, bf16[640,384]{1,0:T(8,128)(2,1)}, f32[640,2]{1,0:T(8,128)}, f32[640,2]{1,0:T(8,128)}) custom-call(s32[3]{0:T(128)} %copy-done.32, s32[1280,2]{1,0:T(8,128)} %bitcast.190, f32[1280,1]{1,0:T(8,128)} %copy.182.pair_ref, bf16[224,384]{1,0:T(8,128)(2,1)} %get-tuple-element.335.rest_0_, bf16[224,384]{1,0:T(8,128)(2,1)} %copy-done.58, ...), custom_call_target="tpu_custom_call" | custom-call | flops 1000 | bytes 1000 | tf_op jit(solution)/shard_map/gather/pallas_call | solution.py:835
  303.9 16.0 %settle_back.1 = (f32[640,768]{1,0:T(8,128)}, bf16[640,768]{1,0:T(8,128)(2,1)}, bf16[640,768]{1,0:T(8,128)(2,1)}, f32[640,12]{1,0:T(8,128)}, f32[16,768]{1,0:T(8,128)}) custom-call(s32[3]{0:T(128)} %copy-done.32, bf16[640,384]{1,0:T(8,128)(2,1)} %get-tuple-element.174.dr_mine, bf16[640,384]{1,0:T(8,128)(2,1)} %copy-done.52, ...), custom_call_target="tpu_custom_call" | custom-call | flops 1000 | bytes 1000 | tf_op jit(solution)/shard_map/settle_back/pallas_call | solution.py:869
  323.5 12.0 %attend_back.3 = (bf16[640,768]{1,0:T(8,128)(2,1)S(1)}, bf16[2176,768]{1,0:T(8,128)(2,1)S(1)}, bf16[2176,768]{1,0:T(8,128)(2,1)S(1)}) custom-call(s32[5,3]{1,0:T(8,128)S(1)} %copy-done.30, bf16[640,768]{1,0:T(8,128)(2,1)S(1)} %copy-done.10, bf16[2176,1536]{1,0:T(8,128)(2,1)} %get-tuple-element.134.k_ref.v_ref, ...), custom_call_target="tpu_custom_call" | custom-call | flops 1000 | bytes 1000 | tf_op jit(solution)/shard_map/attend_back/pallas_call | solution.py:544
  341.3 11.9 %attend_back.4 = (bf16[640,768]{1,0:T(8,128)(2,1)S(1)}, bf16[2176,768]{1,0:T(8,128)(2,1)S(1)}, bf16[2176,768]{1,0:T(8,128)(2,1)S(1)}) custom-call(s32[5,3]{1,0:T(8,128)S(1)} %copy-done.30, bf16[640,768]{1,0:T(8,128)(2,1)S(1)} %copy-done.10, ...), custom_call_target="tpu_custom_call", output_to_operand_aliasing={{0}: (7, {}), {1}: (8, {}), {2}: (9, {})} | custom-call | flops 1000 | bytes 1000 | tf_op jit(solution)/shard_map/attend_back/pallas_call | solution.py:544
  353.2 12.1 %attend_back.5 = (bf16[640,768]{1,0:T(8,128)(2,1)S(1)}, bf16[2176,768]{1,0:T(8,128)(2,1)S(1)}, bf16[2176,768]{1,0:T(8,128)(2,1)S(1)}) custom-call(s32[5,3]{1,0:T(8,128)S(1)} %copy-done.30, bf16[640,768]{1,0:T(8,128)(2,1)S(1)} %copy-done.10, ...), custom_call_target="tpu_custom_call", output_to_operand_aliasing={{0}: (7, {}), {1}: (8, {}), {2}: (9, {})} | custom-call | flops 1000 | bytes 1000 | tf_op jit(solution)/shard_map/attend_back/pallas_call | solution.py:544
  373.9 15.6 %keys_back.1 = (f32[640,768]{1,0:T(8,128)}, bf16[640,768]{1,0:T(8,128)(2,1)}, bf16[640,768]{1,0:T(8,128)(2,1)}, bf16[256,768]{1,0:T(8,128)(2,1)}, f32[1,768]{1,0:T(1,128)}) custom-call(s32[3]{0:T(128)} %copy-done.32, bf16[640,768]{1,0:T(8,128)(2,1)} %copy-done.11, bf16[2176,768]{1,0:T(8,128)(2,1)} %copy-done.3, bf16[2176,768]{1,0:T(8,128)(2,1)} %copy-done.4, ...), custom_call_target="tpu_custom_call" | custom-call | flops 1000 | bytes 1000 | tf_op jit(solution)/shard_map/keys_back/pallas_call | solution.py:869
  399.1 14.2 %weights_back.1 = (bf16[4,4,208,384]{3,2,1,0:T(8,128)(2,1)}, bf16[4,4,208,384]{3,2,1,0:T(8,128)(2,1)}) custom-call(bf16[2176,768]{1,0:T(8,128)(2,1)} %copy-done.19, bf16[640,768]{1,0:T(8,128)(2,1)} %copy-done.11, bf16[2176,768]{1,0:T(8,128)(2,1)} %copy-done.3, bf16[2176,768]{1,0:T(8,128)(2,1)} %copy-done.4, bf16[640,768]{1,0:T(8,128)(2,1)} %get-tuple-element.202.da_ref, ...), custom_call_target="tpu_custom_call" | custom-call | flops 1000 | bytes 1000 | tf_op jit(solution)/shard_map/weights_back/pallas_call | solution.py:869
  413.4 13.4 %collective-permute-done.48 = bf16[3,192,1024]{2,1,0:T(8,128)(2,1)} collective-permute-done((bf16[3,192,1024]{2,1,0:T(8,128)(2,1)}, bf16[3,192,1024]{2,1,0:T(8,128)(2,1)}, u32[]{:S(2)}, u32[]{:S(2)}) %collective-permute-start.48) | collective-permute-done | bytes 1179680 | tf_op jit(solution)/shard_map/ppermute | solution.py:1080
  444.7 9.9 %collective-permute-done.50 = bf16[4,208,384]{2,1,0:T(8,128)(2,1)} collective-permute-done((bf16[4,208,384]{2,1,0:T(8,128)(2,1)}, bf16[4,208,384]{2,1,0:T(8,128)(2,1)}, u32[]{:S(2)}, u32[]{:S(2)}) %collective-permute-start.50) | collective-permute-done | bytes 639008 | tf_op jit(solution)/shard_map/ppermute | solution.py:1080
  454.6 5.8 %gather.13 = (bf16[640,384]{1,0:T(8,128)(2,1)}, bf16[640,384]{1,0:T(8,128)(2,1)}) custom-call(s32[3]{0:T(128)} %copy-done.32, s32[1280,2]{1,0:T(8,128)} %bitcast.191, f32[1280,2]{1,0:T(8,128)} %copy.185.pair_ref, bf16[2,224,384]{2,1,0:T(8,128)(2,1)} %get-tuple-element.216.rest_0_, bf16[2,224,384]{2,1,0:T(8,128)(2,1)} %copy-done.53, ...), custom_call_target="tpu_custom_call" | custom-call | flops 1000 | bytes 1000 | tf_op jit(solution)/shard_map/gather/pallas_call | solution.py:835
  475.9 13.1 %collective-permute-done.54 = bf16[640,768]{1,0:T(8,128)(2,1)S(1)} collective-permute-done((bf16[640,768]{1,0:T(8,128)(2,1)S(1)}, bf16[640,768]{1,0:T(8,128)(2,1)S(1)}, u32[]{:S(2)}, u32[]{:S(2)}) %collective-permute-start.54) | collective-permute-done | bytes 983072 | tf_op jit(solution)/shard_map/ppermute | solution.py:1379
  (418 shorter events, 223.7 us)
Async XLA Ops:
  11.3 26.9 %collective-permute-start = (bf16[640,768]{1,0:T(8,128)(2,1)S(1)}, bf16[640,768]{1,0:T(8,128)(2,1)}, u32[]{:S(2)}, u32[]{:S(2)}) collective-permute-start(bf16[640,768]{1,0:T(8,128)(2,1)S(1)} %dynamic-slice_bitcast_fusion.2.x0.x), channel_id=1, source_target_pairs={{0,2},{2,4},{4,6},{1,3},{3,5},{5,7},{8,10},{10,12},{12,14},{9,11},... | collective-permute-start | bytes 2949128 | tf_op jit(solution)/shard_map/ppermute | solution.py:1167
  54.9 59.0 %collective-permute-start.9 = (bf16[4,768,384]{2,1,0:T(8,128)(2,1)S(1)}, bf16[4,768,384]{2,1,0:T(8,128)(2,1)}, u32[]{:S(2)}, u32[]{:S(2)}) collective-permute-start(bf16[4,768,384]{2,1,0:T(8,128)(2,1)S(1)} %pad_maximum_fusion.1.wm), channel_id=1, source_target_pairs={{0,1},{1,0},{2,3},{3,2},{4,5},{5,4},{6,7},{7,6},{8,9},{9,8},{10,11... | collective-permute-start | bytes 7077896 | tf_op jit(solution)/shard_map/ppermute | solution.py:1080
  63.9 38.8 %collective-permute-start.5 = (bf16[640,768]{1,0:T(8,128)(2,1)}, bf16[640,768]{1,0:T(8,128)(2,1)}, u32[]{:S(2)}, u32[]{:S(2)}) collective-permute-start(bf16[640,768]{1,0:T(8,128)(2,1)} %collective-permute-done.4.mid), channel_id=1, source_target_pairs={{4,6},{5,7},{12,14},{13,15},{20,22},{21,23},{28,30},{29,31}} | collective-permute-start | bytes 2949128 | tf_op jit(solution)/shard_map/ppermute | solution.py:1207
  67.8 34.9 %collective-permute-start.10 = (bf16[4,224,384]{2,1,0:T(8,128)(2,1)}, bf16[4,224,384]{2,1,0:T(8,128)(2,1)}, u32[]{:S(2)}, u32[]{:S(2)}) collective-permute-start(bf16[4,224,384]{2,1,0:T(8,128)(2,1)} %pad_maximum_fusion.7), channel_id=1, source_target_pairs={{0,4},{2,6},{4,0},{6,2},{1,5},{3,7},{5,1},{7,3},{8,12},{10,14},{12... | collective-permute-start | bytes 2064392 | tf_op jit(solution)/shard_map/ppermute | solution.py:1080
  102.7 58.4 %collective-permute-start.11 = (bf16[3,192,1024]{2,1,0:T(8,128)(2,1)}, bf16[3,192,1024]{2,1,0:T(8,128)(2,1)}, u32[]{:S(2)}, u32[]{:S(2)}) collective-permute-start(bf16[3,192,1024]{2,1,0:T(8,128)(2,1)} %get-tuple-element.140.w0), channel_id=1, source_target_pairs={{0,2},{2,0},{4,6},{6,4},{1,3},{3,1},{5,7},{7,5},{8,10},{10,8},{12,... | collective-permute-start | bytes 3538952 | tf_op jit(solution)/shard_map/ppermute | solution.py:1080
  102.7 58.4 %collective-permute-start.12 = (bf16[3,192,1024]{2,1,0:T(8,128)(2,1)}, bf16[3,192,1024]{2,1,0:T(8,128)(2,1)}, u32[]{:S(2)}, u32[]{:S(2)}) collective-permute-start(bf16[3,192,1024]{2,1,0:T(8,128)(2,1)} %get-tuple-element.141), channel_id=1, source_target_pairs={{0,4},{2,6},{4,0},{6,2},{1,5},{3,7},{5,1},{7,3},{8,12},{10,14},{12... | collective-permute-start | bytes 3538952 | tf_op jit(solution)/shard_map/ppermute | solution.py:1080
  189.1 33.4 %collective-permute-start.24 = (bf16[224,384]{1,0:T(8,128)(2,1)S(1)}, bf16[224,384]{1,0:T(8,128)(2,1)S(1)}, u32[]{:S(2)}, u32[]{:S(2)}) collective-permute-start(bf16[224,384]{1,0:T(8,128)(2,1)S(1)} %get-tuple-element.160), channel_id=1, source_target_pairs={{0,4},{2,6},{4,0},{6,2},{8,12},{10,14},{12,8},{14,10},{16,20},{18,... | collective-permute-start | bytes 516104 | tf_op jit(solution)/shard_map/ppermute | solution.py:1106
  190.0 32.5 %collective-permute-start.25 = (bf16[224,384]{1,0:T(8,128)(2,1)S(1)}, bf16[224,384]{1,0:T(8,128)(2,1)S(1)}, u32[]{:S(2)}, u32[]{:S(2)}) collective-permute-start(bf16[224,384]{1,0:T(8,128)(2,1)S(1)} %get-tuple-element.161), channel_id=1, source_target_pairs={{0,12},{2,14},{4,8},{6,10},{8,4},{10,6},{12,0},{14,2},{16,28},{18,... | collective-permute-start | bytes 516104 | tf_op jit(solution)/shard_map/ppermute | solution.py:1106
  192.1 30.3 %collective-permute-start.26 = (bf16[224,384]{1,0:T(8,128)(2,1)S(1)}, bf16[224,384]{1,0:T(8,128)(2,1)S(1)}, u32[]{:S(2)}, u32[]{:S(2)}) collective-permute-start(bf16[224,384]{1,0:T(8,128)(2,1)S(1)} %get-tuple-element.162), channel_id=1, source_target_pairs={{0,20},{2,22},{4,16},{6,18},{8,28},{10,30},{12,24},{14,26},{16,4},... | collective-permute-start | bytes 516104 | tf_op jit(solution)/shard_map/ppermute | solution.py:1106
  194.1 29.7 %collective-permute-start.27 = (bf16[224,384]{1,0:T(8,128)(2,1)S(1)}, bf16[224,384]{1,0:T(8,128)(2,1)S(1)}, u32[]{:S(2)}, u32[]{:S(2)}) collective-permute-start(bf16[224,384]{1,0:T(8,128)(2,1)S(1)} %get-tuple-element.163), channel_id=1, source_target_pairs={{0,28},{2,30},{4,24},{6,26},{8,20},{10,22},{12,16},{14,18},{16,12}... | collective-permute-start | bytes 516104 | tf_op jit(solution)/shard_map/ppermute | solution.py:1106
  224.1 28.9 %collective-permute-start.29 = (bf16[896,384]{1,0:T(8,128)(2,1)S(1)}, bf16[896,384]{1,0:T(8,128)(2,1)S(1)}, u32[]{:S(2)}, u32[]{:S(2)}) collective-permute-start(bf16[896,384]{1,0:T(8,128)(2,1)S(1)} %get-tuple-element.171), channel_id=1, source_target_pairs={{0,1},{1,0},{2,3},{3,2},{4,5},{5,4},{6,7},{7,6},{8,9},{9,8},{10,11... | collective-permute-start | bytes 2064392 | tf_op jit(solution)/shard_map/ppermute | solution.py:1080
  298.3 69.6 %collective-permute-start.43 = (bf16[2,3,192,1024]{3,2,1,0:T(8,128)(2,1)}, bf16[2,3,192,1024]{3,2,1,0:T(8,128)(2,1)}, u32[]{:S(2)}, u32[]{:S(2)}) collective-permute-start(bf16[2,3,192,1024]{3,2,1,0:T(8,128)(2,1)} %slice.251), channel_id=1, source_target_pairs={{0,2},{2,0},{4,6},{6,4},{1,3},{3,1},{5,7},{7,5},{8,10},{10,8},{12,... | collective-permute-start | bytes 7077896 | tf_op jit(solution)/shard_map/ppermute | solution.py:1080
  298.4 37.2 %collective-permute-start.38 = (bf16[896,384]{1,0:T(8,128)(2,1)}, bf16[896,384]{1,0:T(8,128)(2,1)}, u32[]{:S(2)}, u32[]{:S(2)}) collective-permute-start(bf16[896,384]{1,0:T(8,128)(2,1)} %get-tuple-element.175), channel_id=1, source_target_pairs={{0,1},{1,0},{2,3},{3,2},{4,5},{5,4},{6,7},{7,6},{8,9},{9,8},{10,11... | collective-permute-start | bytes 2064392 | tf_op jit(solution)/shard_map/ppermute | solution.py:1080
  298.9 38.8 %collective-permute-start.39 = (bf16[896,384]{1,0:T(8,128)(2,1)}, bf16[896,384]{1,0:T(8,128)(2,1)}, u32[]{:S(2)}, u32[]{:S(2)}) collective-permute-start(bf16[896,384]{1,0:T(8,128)(2,1)} %get-tuple-element.177), channel_id=1, source_target_pairs={{0,1},{1,0},{2,3},{3,2},{4,5},{5,4},{6,7},{7,6},{8,9},{9,8},{10,11... | collective-permute-start | bytes 2064392 | tf_op jit(solution)/shard_map/ppermute | solution.py:1080
  339.9 51.4 %collective-permute-start.42 = (bf16[4,224,384]{2,1,0:T(8,128)(2,1)}, bf16[4,224,384]{2,1,0:T(8,128)(2,1)}, u32[]{:S(2)}, u32[]{:S(2)}) collective-permute-start(bf16[4,224,384]{2,1,0:T(8,128)(2,1)} %bitcast.61), channel_id=1, source_target_pairs={{0,4},{2,6},{4,0},{6,2},{1,5},{3,7},{5,1},{7,3},{8,12},{10,14},{12... | collective-permute-start | bytes 2064392 | tf_op jit(solution)/shard_map/ppermute | solution.py:1080
  372.3 54.4 %collective-permute-start.48 = (bf16[3,192,1024]{2,1,0:T(8,128)(2,1)}, bf16[3,192,1024]{2,1,0:T(8,128)(2,1)}, u32[]{:S(2)}, u32[]{:S(2)}) collective-permute-start(bf16[3,192,1024]{2,1,0:T(8,128)(2,1)} %fusion.13), channel_id=1, source_target_pairs={{0,4},{2,6},{4,0},{6,2},{1,5},{3,7},{5,1},{7,3},{8,12},{10,14},{12... | collective-permute-start | bytes 3538952 | tf_op jit(solution)/shard_map/ppermute | solution.py:1080
  429.7 30.6 %collective-permute-start.53 = (bf16[640,768]{1,0:T(8,128)(2,1)}, bf16[640,768]{1,0:T(8,128)(2,1)}, u32[]{:S(2)}, u32[]{:S(2)}) collective-permute-start(bf16[640,768]{1,0:T(8,128)(2,1)} %fusion.17), channel_id=1, source_target_pairs={{4,2},{6,4},{5,3},{7,5},{12,10},{14,12},{13,11},{15,13},{20,18},{2... | collective-permute-start | bytes 2949128 | tf_op jit(solution)/shard_map/ppermute | solution.py:1379
  437.8 29.9 %collective-permute-start.58 = (bf16[4,208,384]{2,1,0:T(8,128)(2,1)}, bf16[4,208,384]{2,1,0:T(8,128)(2,1)}, u32[]{:S(2)}, u32[]{:S(2)}) collective-permute-start(bf16[4,208,384]{2,1,0:T(8,128)(2,1)} %get-tuple-element.296), channel_id=1, source_target_pairs={{0,24},{8,16},{16,8},{24,0},{1,25},{9,17},{17,9},{25,1},{2,26},{10... | collective-permute-start | bytes 1916936 | tf_op jit(solution)/shard_map/ppermute | solution.py:1080
  439.3 29.7 %collective-permute-start.57 = (bf16[4,208,384]{2,1,0:T(8,128)(2,1)S(1)}, bf16[4,208,384]{2,1,0:T(8,128)(2,1)}, u32[]{:S(2)}, u32[]{:S(2)}) collective-permute-start(bf16[4,208,384]{2,1,0:T(8,128)(2,1)S(1)} %get-tuple-element.295), channel_id=1, source_target_pairs={{0,16},{8,24},{16,0},{24,8},{1,17},{9,25},{17,1},{25,9},{2,18},{10... | collective-permute-start | bytes 1916936 | tf_op jit(solution)/shard_map/ppermute | solution.py:1080
  462.4 26.6 %collective-permute-start.54 = (bf16[640,768]{1,0:T(8,128)(2,1)S(1)}, bf16[640,768]{1,0:T(8,128)(2,1)S(1)}, u32[]{:S(2)}, u32[]{:S(2)}) collective-permute-start(bf16[640,768]{1,0:T(8,128)(2,1)S(1)} %pad_select_fusion), channel_id=1, source_target_pairs={{2,0},{4,2},{6,4},{3,1},{5,3},{7,5},{10,8},{12,10},{14,12},{11,9},... | collective-permute-start | bytes 2949128 | tf_op jit(solution)/shard_map/ppermute | solution.py:1379
  471.1 30.9 %collective-permute-start.61 = (bf16[208,384]{1,0:T(8,128)(2,1)S(1)}, bf16[208,384]{1,0:T(8,128)(2,1)S(1)}, u32[]{:S(2)}, u32[]{:S(2)}) collective-permute-start(bf16[208,384]{1,0:T(8,128)(2,1)S(1)} %get-tuple-element.345), channel_id=1, source_target_pairs={{0,6},{2,0},{4,2},{6,4},{1,7},{3,1},{5,3},{7,5},{8,14},{10,8},{12,... | collective-permute-start | bytes 479240 | tf_op jit(solution)/shard_map/ppermute | solution.py:1096
  474.2 27.9 %collective-permute-start.60 = (bf16[208,384]{1,0:T(8,128)(2,1)S(1)}, bf16[208,384]{1,0:T(8,128)(2,1)S(1)}, u32[]{:S(2)}, u32[]{:S(2)}) collective-permute-start(bf16[208,384]{1,0:T(8,128)(2,1)S(1)} %get-tuple-element.346), channel_id=1, source_target_pairs={{0,4},{2,6},{4,0},{6,2},{1,5},{3,7},{5,1},{7,3},{8,12},{10,14},{12... | collective-permute-start | bytes 479240 | tf_op jit(solution)/shard_map/ppermute | solution.py:1096
  474.2 27.9 %collective-permute-start.59 = (bf16[208,384]{1,0:T(8,128)(2,1)S(1)}, bf16[208,384]{1,0:T(8,128)(2,1)S(1)}, u32[]{:S(2)}, u32[]{:S(2)}) collective-permute-start(bf16[208,384]{1,0:T(8,128)(2,1)S(1)} %get-tuple-element.344), channel_id=1, source_target_pairs={{0,2},{2,4},{4,6},{6,0},{1,3},{3,5},{5,7},{7,1},{8,10},{10,12},{12... | collective-permute-start | bytes 479240 | tf_op jit(solution)/shard_map/ppermute | solution.py:1096
  475.8 29.9 %collective-permute-start.52 = (f32[640,768]{1,0:T(8,128)S(1)}, f32[640,768]{1,0:T(8,128)S(1)}, u32[]{:S(2)}, u32[]{:S(2)}) collective-permute-start(f32[640,768]{1,0:T(8,128)S(1)} %multiply_add_fusion), channel_id=1, source_target_pairs={{0,1},{1,0},{2,3},{3,2},{4,5},{5,4},{6,7},{7,6},{8,9},{9,8},{10,11... | collective-permute-start | bytes 5898248 | tf_op jit(solution)/shard_map/ppermute | solution.py:1080
  (115 other events, 1697.9 us)
